TPU v7x, 32 devices: a whole 2x2x4 slice. The times are simulated.
32 devices in a mesh: dom: 8 (over y, x, core), slab: 4 (over z).
Axes of the slice: x: 2, y: 2, z: 4, core: 2. Of those that a mesh axis runs over, the one named last changes fastest.
Arguments:
- particles: bfloat16 [4096, 320, 256], P('dom', 'slab'), may hold values from -8 to 8
- blocks: int32 [4096, 2], P('dom'), may hold values from 0 to 3, as said below
- references: bfloat16 [512, 320, 256], P(None, 'slab'), may hold values from -1 to 1
- inv_noise: float32 [320], P('slab'), may hold values from 0.5 to 2
- destination: int32 [320, 512], replicated, may hold values from 0 to 31, as said below
- row_index: int32 [320, 512], replicated, may hold values from 0 to 254
- fraction: float32 [320, 512], replicated, may hold values from 0 to 1
Outputs:
- volume_data: float32 [8192, 256], P(('dom', 'slab'))
- next_slab: bfloat16 [2048, 1024], P(None, 'slab')
Inputs may be any that keep to these rules, and one draw needn't show every extreme that they name: Each particle names 2 different orientation blocks. destination is a device index in the order of the joined axes (dom, slab), dom major. Among the pieces whose group belongs to one index of slab and whose orientation belongs to one index of dom, no destination is named more than 256 times, and some destination exactly 256 times.
All inputs are finite; a program needn't handle non-finite values.
Results may differ from a plain program's by a relative error of at most 0.013.
Values may be sent and summed in bfloat16 or wider, within the bound.
No kernel may reach another device: no remote copies, remote signals or barrier semaphores. Data moves between devices by JAX's collectives and lax.ppermute only.
A program may use at most 256 MiB of HBM per device.

v0:
```python
import jax
import jax.numpy as jnp
from jax import lax
from jax.sharding import PartitionSpec as P

OB = 128
RD = 256


def spread_rows(volume_rows, targets, fractions, values):
    lower_part = (1.0 - fractions)[:, None] * values
    upper_part = fractions[:, None] * values
    return volume_rows.at[targets].add(lower_part).at[targets + 1].add(upper_part)


def shards(particles, blocks, references, inv_noise, destination, row_index, fraction):
    particle_count, groups, row_width = particles.shape
    orients = references.shape[0]
    dom_size = lax.axis_size("dom")
    slab_size = lax.axis_size("slab")
    devices = dom_size * slab_size
    slab_pos = lax.axis_index("slab")
    weighted = (references.astype(jnp.float32) * inv_noise[None, :, None]).astype(jnp.bfloat16)
    weighted = weighted.reshape(orients, groups * row_width)
    flat_rows = particles.reshape(particle_count, groups * row_width)
    partial_value = lax.dot_general(
        flat_rows, weighted, (((1,), (1,)), ((), ())), preferred_element_type=jnp.float32
    )
    scores = lax.psum(partial_value, "slab")
    block_of = jnp.arange(orients, dtype=jnp.int32) // OB
    allowed = jnp.any(blocks[:, :, None] == block_of[None, None, :], axis=1)
    masked = jnp.where(allowed, scores, -jnp.inf)
    highest = jnp.max(masked, axis=1, keepdims=True)
    weights = jnp.where(allowed, jnp.exp(masked - highest), 0.0)
    posterior = (weights / jnp.sum(weights, axis=1, keepdims=True)).astype(jnp.bfloat16)
    slices = lax.dot_general(
        posterior, flat_rows, (((0,), (0,)), ((), ())), preferred_element_type=jnp.float32
    )
    slices = slices.astype(jnp.bfloat16).reshape(orients, groups, row_width)
    my_dest = lax.dynamic_slice_in_dim(destination, slab_pos * groups, groups, 0).T
    my_rows = lax.dynamic_slice_in_dim(row_index, slab_pos * groups, groups, 0).T
    my_frac = lax.dynamic_slice_in_dim(fraction, slab_pos * groups, groups, 0).T
    targets = (my_dest * RD + my_rows).reshape(-1)
    whole = jnp.zeros((RD * devices + 1, row_width), jnp.float32)
    whole = spread_rows(whole, targets, my_frac.reshape(-1), slices.reshape(-1, row_width))[
        : RD * devices
    ]
    volume = lax.psum_scatter(whole, ("dom", "slab"), scatter_dimension=0, tiled=True)
    next_slab = lax.all_gather(volume.astype(jnp.bfloat16), "dom", axis=0, tiled=True)
    return (volume, next_slab)


def solution(mesh):
    return jax.shard_map(
        shards,
        mesh=mesh,
        in_specs=(
            P("dom", "slab", None),
            P("dom", None),
            P(None, "slab", None),
            P("slab"),
            P(),
            P(),
            P(),
        ),
        out_specs=(P(("dom", "slab"), None), P(None, "slab")),
        check_vma=False,
    )
```

profile of v0, /device:TPU:0, one launch (start us, length us, event | category | flops | bytes accessed | tf_op | source)
XLA Modules:
  0.0 893.6 jit_solution(15783648063973167933)
XLA Ops:
  7.2 21.1 %multiply_convert_fusion = bf16[512,80,256]{2,1,0:T(8,128)(2,1)} fusion(bf16[512,80,256]{2,1,0:T(8,128)(2,1)} %param.9, f32[80]{0:T(128)} %param.10), kind=kLoop, calls=%fused_computation.6 | loop fusion | flops 31457280 | bytes 41943360 | tf_op jit(solution)/shard_map/convert_element_type | solution.py:23
  28.3 27.9 %fusion.11 = f32[512,512]{0,1:T(8,128)} fusion(bf16[512,80,256]{2,1,0:T(8,128)(2,1)} %param.7, bf16[512,80,256]{2,1,0:T(8,128)(2,1)} %multiply_convert_fusion), kind=kOutput, calls=%fused_computation.16 | convolution fusion | flops 10737418240 | bytes 42991616 | tf_op jit(solution)/shard_map/dot_general | solution.py:26
  56.2 0.2 reduce-scatter.2.cloned.1.call-start
  56.5 0.2 compare_reduce_fusion
  56.7 0.3 copy.22
  57.1 20.1 %copy.23 = bf16[64,8,80,256]{3,1,2,0:T(8,128)(2,1)} copy(bf16[64,8,80,256]{3,2,1,0:T(8,128)(2,1)} %bitcast.14) | data formatting | bytes 41943040
  77.2 1.0 add_bitcast_fusion
  78.2 0.1 copy.17
  78.3 0.3 reshape.92
  78.6 0.3 compare_select_fusion
  79.0 0.1 copy.18
  79.1 0.2 reshape.93
  79.4 31.5 %all-reduce.2.cloned.1.call-done = f32[512,512]{0,1:T(8,128)} async-done(((f32[512,512]{0,1:T(8,128)}), f32[512,512]{0,1:T(8,128)}) %all-reduce.2.cloned.1.call-update) | async-done | bytes 1048592 | tf_op jit(solution)/shard_map/psum | solution.py:29
  110.9 1.4 fusion.20
  112.3 1.5 fusion.16
  113.8 24.1 %fusion.4 = f32[512,20480]{1,0:T(8,128)} fusion(bf16[512,20480]{1,0:T(8,128)(2,1)} %bitcast.13, pred[512,512]{0,1:T(32,128)(4,1)S(1)} %copy.22, f32[512]{0:T(512)S(1)} %fusion.16, f32[512]{0:T(512)S(1)} %fusion.20, f32[512,512]{0,1:T(8,128)} %all-reduce.2.cloned.1.call-done), kind=kOutput, calls=%fused_computation.8 | convolution fusion | flops 10759700480 | bytes 64229376 | tf_op jit(solution)/shard_map/dot_general | solution.py:36
  137.9 40.6 %reshape.95 = f32[40960,256]{1,0:T(8,128)} reshape(f32[512,20480]{1,0:T(8,128)} %fusion.4) | data formatting | bytes 83886080 | tf_op jit(solution)/shard_map/convert_element_type | solution.py:11
  178.5 243.5 %scatter_custom_fusion = f32[8193,256]{1,0:T(8,128)} fusion(s32[40960]{0:T(1024)S(1)} %bitcast.16, f32[40960,256]{1,0:T(8,128)} %reshape.95, f32[40960]{0:T(1024)S(1)} %broadcast_subtract_fusion, f32[]{:T(128)} %constant.15.clone.1), kind=kCustom, calls=%fused_computation.4 | custom fusion | flops 20971520 | bytes 50496516 | tf_op jit(solution)/shard_map/scatter-add | solution.py:13
  422.0 246.4 %scatter_custom_fusion.1 = f32[8193,256]{1,0:T(8,128)} fusion(f32[8193,256]{1,0:T(8,128)} %scatter_custom_fusion, s32[40960]{0:T(1024)S(1)} %bitcast.15, f32[40960,256]{1,0:T(8,128)} %reshape.95, f32[40960]{0:T(1024)S(1)} %reshape.93), kind=kCustom, calls=%fused_computation.2 | custom fusion | flops 20971520 | bytes 50496512 | tf_op jit(solution)/shard_map/scatter-add | solution.py:13
  668.4 7.1 slice.4
  675.6 185.3 %reduce-scatter.2.cloned.1.call-done = f32[256,256]{1,0:T(8,128)} async-done(((f32[8192,256]{1,0:T(8,128)}), f32[256,256]{1,0:T(8,128)}) %reduce-scatter.2.cloned.1.call-update) | async-done | bytes 262160 | tf_op jit(solution)/shard_map/reduce_scatter | solution.py:48
  860.9 1.6 convert_element_type.28
  862.6 22.2 %all-gather.2.cloned.1.call-done = bf16[2048,256]{1,0:T(8,128)(2,1)} async-done(((bf16[256,256]{1,0:T(8,128)(2,1)}), bf16[2048,256]{1,0:T(8,128)(2,1)}) %all-gather.2.cloned.1.call-update) | async-done | bytes 1048592 | tf_op jit(solution)/shard_map/all_gather | solution.py:49
  884.8 2.3 copy.38
  (14 shorter events, 0.2 us)
Async XLA Ops:
  7.2 71.8 %copy-start = (f32[320,512]{1,0:T(8,128)S(1)}, f32[320,512]{1,0:T(8,128)}, u32[]{:S(2)}) copy-start(f32[320,512]{1,0:T(8,128)} %param.13) | copy-start | bytes 1966084
  7.2 103.7 %all-reduce.2.cloned.1.call-start = ((), (), s32[]{:S(2)}) async-start(), calls=%async_computation.1 | async-start | bytes 2097152 | tf_op jit(solution)/shard_map/psum | solution.py:29
  28.3 28.2 %copy-start.2 = (s32[512,2]{0,1:T(2,128)S(1)}, s32[512,2]{0,1:T(2,128)}, u32[]{:S(2)}) copy-start(s32[512,2]{0,1:T(2,128)} %param.8) | copy-start | bytes 12292
  56.2 804.7 %reduce-scatter.2.cloned.1.call-start = ((), (), s32[]{:S(2)}) async-start(), calls=%async_computation.2 | async-start | bytes 8650752 | tf_op jit(solution)/shard_map/reduce_scatter | solution.py:48
  422.0 465.0 %copy-start.1 = (f32[320,512]{1,0:T(8,128)S(1)}, f32[320,512]{1,0:T(8,128)}, u32[]{:S(2)}) copy-start(f32[320,512]{1,0:T(8,128)} %param.13) | copy-start | bytes 1966084
  675.6 209.2 %all-gather.2.cloned.1.call-start = ((), (), s32[]{:S(2)}) async-start(), calls=%async_computation.3 | async-start | bytes 1179648 | tf_op jit(solution)/shard_map/all_gather | solution.py:49
Sparse Core Ops, SparseCore 0:
  56.4 54.5 all-reduce.1
  675.7 185.1 reduce-scatter.1
  863.6 21.1 all-gather.1
where the time goes:
time: 895 us; the launch traced here: 894 us
  other arithmetic  517 us (58%)
  waiting for transfers between devices  239 us (27%)
  local copies, waits for them, and re-layouts  71.2 us (8%)
  matrix products  52 us (6%)
  between operations  13.9 us (2%)
    scatter-add x2, other arithmetic, spread_rows(): volume_rows.at[targets].add(lower_part).at[targets + 1].add(upper_part)  490 us
    reduce_scatter x1, waiting for transfers between devices, shards(): lax.psum_scatter(whole, ('dom', 'slab'), scatter_dimension=0, tiled=True)  185 us
    convert_element_type x1, local copies, waits for them, and re-layouts, spread_rows(): lower_part = (1.0 - fractions)[:, None] * values  40.6 us
    psum x1, waiting for transfers between devices, shards(): scores = lax.psum(partial_value, 'slab')  31.5 us
    dot_general x1, matrix products, shards(): lax.dot_general(flat_rows, weighted, (((1,), (1,)), ((), ())), preferred_...  27.9 us
    dot_general x1, matrix products, shards(): lax.dot_general(posterior, flat_rows, (((0,), (0,)), ((), ())), preferred...  24.1 us
    unnamed x8, local copies, waits for them, and re-layouts  22.4 us
    all_gather x1, waiting for transfers between devices, shards(): lax.all_gather(volume.astype(jnp.bfloat16), 'dom', axis=0, tiled=True)  22.2 us
  transfers between devices with their start and end apart: 3, of which 3 were waited for; matrix products, arithmetic and copies ran while one was open for 3% of the time, Pallas kernels for 0%

commit v1 on v0

v1 whole, which is shorter than its diff:
```python
import functools

import jax
import jax.numpy as jnp
from jax import lax
from jax.experimental import pallas as pl
from jax.experimental.pallas import tpu as pltpu
from jax.sharding import PartitionSpec as P

OB = 128
RD = 256
MB = 2**20
F32 = jnp.float32
BF16 = jnp.bfloat16


def group_block(groups):
    return 16 if groups % 16 == 0 else 8


def score_kernel(me_ref, noise_ref, perm_ref, x_ref, r_ref, blk_ref, flat_ref, *rest):
    *out_refs, w_ref, acc_ref = rest
    step = pl.program_id(0)
    particles, gb, width = x_ref.shape
    orients = r_ref.shape[0]

    @pl.when(step == 0)
    def _():
        acc_ref[...] = jnp.zeros_like(acc_ref)

    perm = perm_ref[...]

    def regroup(src_ref, dst_ref, scaled):
        def body(i, carry):
            at = pl.multiple_of(i * 16, 16)
            tile = src_ref[pl.ds(at, 16)].reshape(16 * gb, width)
            moved = jnp.dot(perm, tile, preferred_element_type=F32)
            for g in range(gb):
                part = moved[g * 16 : (g + 1) * 16]
                if scaled:
                    part = part * noise_ref[step * gb + g]
                dst_ref[pl.ds(at, 16), g * width : (g + 1) * width] = part.astype(BF16)
            return carry

        lax.fori_loop(0, src_ref.shape[0] // 16, body, 0, unroll=2)

    regroup(r_ref, w_ref, True)
    regroup(x_ref, flat_ref, False)
    half = min(256, orients)

    def product(n, carry):
        at = pl.multiple_of(n * half, half)
        acc_ref[n] += lax.dot_general(
            flat_ref[...],
            w_ref[pl.ds(at, half), :],
            (((1,), (1,)), ((), ())),
            preferred_element_type=F32,
        )
        return carry

    lax.fori_loop(0, orients // half, product, 0)

    @pl.when(step == pl.num_programs(0) - 1)
    def _():
        me = me_ref[0]
        share = particles // len(out_refs)
        per = half // OB
        for k, out_ref in enumerate(out_refs):
            at = pl.multiple_of((me ^ k) * share, share)
            for j in range(2):
                wanted = blk_ref[pl.ds(at, share), j : j + 1]
                chosen = jnp.zeros((share, OB), F32)
                for b in range(orients // OB):
                    lane = (b % per) * OB
                    chosen = jnp.where(
                        wanted == b, acc_ref[b // per, pl.ds(at, share), lane : lane + OB], chosen
                    )
                out_ref[:, j * OB : (j + 1) * OB] = chosen


def score_call(me, inv_noise, particles, references, blocks, slab_size):
    count, groups, width = particles.shape
    orients = references.shape[0]
    gb = group_block(groups)
    side = 16 * gb
    row = jnp.arange(side, dtype=jnp.int32)[:, None]
    col = jnp.arange(side, dtype=jnp.int32)[None, :]
    perm = ((row // 16 == col % gb) & (row % 16 == col // gb)).astype(BF16)
    share = count // slab_size
    half = min(256, orients)
    smem = pl.BlockSpec(memory_space=pltpu.SMEM)
    return pl.pallas_call(
        score_kernel,
        grid=(groups // gb,),
        out_shape=[jax.ShapeDtypeStruct((count, groups * width), BF16)]
        + [jax.ShapeDtypeStruct((share, 2 * OB), F32)] * slab_size,
        in_specs=[
            smem,
            smem,
            pl.BlockSpec((side, side), lambda i: (0, 0)),
            pl.BlockSpec((count, gb, width), lambda i: (0, i, 0)),
            pl.BlockSpec((orients, gb, width), lambda i: (0, i, 0)),
            pl.BlockSpec((count, 2), lambda i: (0, 0)),
        ],
        out_specs=[pl.BlockSpec((count, gb * width), lambda i: (0, i))]
        + [pl.BlockSpec((share, 2 * OB), lambda i: (0, 0))] * slab_size,
        scratch_shapes=[
            pltpu.VMEM((orients, gb * width), BF16),
            pltpu.VMEM((orients // half, count, half), F32),
        ],
        compiler_params=pltpu.CompilerParams(vmem_limit_bytes=56 * MB),
        cost_estimate=pl.CostEstimate(
            flops=4 * count * orients * groups * width,
            bytes_accessed=6 * count * groups * width,
            transcendentals=0,
        ),
    )(me, inv_noise, perm, particles, references, blocks)


def softmax_kernel(*refs):
    *parts, out_ref = refs
    total = parts[0][...]
    for part in parts[1:]:
        total = total + part[...]
    highest = jnp.max(total, axis=1, keepdims=True)
    weights = jnp.exp(total - highest)
    out_ref[...] = (weights / jnp.sum(weights, axis=1, keepdims=True)).astype(BF16)


def softmax_call(parts):
    return pl.pallas_call(
        softmax_kernel, out_shape=jax.ShapeDtypeStruct(parts[0].shape, BF16)
    )(*parts)


def insert_kernel(me_ref, row_ref, x_ref, frac_ref, blk_ref, *rest, share_count, copies):
    post_refs = rest[:share_count]
    send_ref, keep_ref = rest[share_count : share_count + 2]
    post_t, spread_ref, quad_ref = rest[share_count + 2 : share_count + 5]
    volumes = rest[share_count + 5 :]
    step = pl.program_id(0)
    count = x_ref.shape[0]
    orients = post_t.shape[0]
    gb = frac_ref.shape[2]
    width = x_ref.shape[1] // gb
    share = count // share_count

    @pl.when(step == 0)
    def _():
        for volume in volumes:
            volume[...] = jnp.zeros_like(volume)
        me = me_ref[0]
        for k, post_ref in enumerate(post_refs):
            at = pl.multiple_of((me ^ k) * share, share)
            post = post_ref[...].astype(F32)
            first = blk_ref[pl.ds(at, share), 0:1]
            second = blk_ref[pl.ds(at, share), 1:2]
            for b in range(orients // OB):
                spread = jnp.where(
                    first == b, post[:, :OB], jnp.where(second == b, post[:, OB:], 0.0)
                )
                spread_ref[pl.ds(at, share), b * OB : (b + 1) * OB] = spread
        for b in range(orients // OB):
            post_t[b * OB : (b + 1) * OB] = spread_ref[:, b * OB : (b + 1) * OB].T.astype(BF16)

    lanes = lax.broadcasted_iota(jnp.int32, (1, gb), 1)

    def one_group(g, carry):
        piece = jnp.dot(
            post_t[...],
            x_ref[:, pl.ds(pl.multiple_of(g * width, width), width)],
            preferred_element_type=F32,
        )
        upper = jnp.sum(jnp.where(lanes == g, frac_ref[0], 0.0), axis=1, keepdims=True)
        lower = 1.0 - upper
        quad_ref[pl.ds(0, orients, 4), :] = piece[:, :OB] * lower
        quad_ref[pl.ds(1, orients, 4), :] = piece[:, OB:] * lower
        quad_ref[pl.ds(2, orients, 4), :] = piece[:, :OB] * upper
        quad_ref[pl.ds(3, orients, 4), :] = piece[:, OB:] * upper
        burst = 32

        def rows(i, c):
            for u in range(burst):
                at = row_ref[0, g, i * burst + u]
                src = quad_ref[pl.ds(pl.multiple_of(i * (4 * burst), 4 * burst) + 4 * u, 4), :]
                volume = volumes[u % copies]
                volume[pl.ds(at, 4), :] = volume[pl.ds(at, 4), :] + src
            return c

        lax.fori_loop(0, orients // burst, rows, 0)
        return carry

    lax.fori_loop(0, gb, one_group, 0)

    @pl.when(step == pl.num_programs(0) - 1)
    def _():
        half = keep_ref.shape[0]
        tile = min(512, half)
        for base, out_ref in ((half, send_ref), (0, keep_ref)):
            def finish(i, carry, base=base, out_ref=out_ref):
                at = pl.multiple_of(i * tile, tile)
                for lane in range(2):
                    total = volumes[0][pl.ds(2 * (base + at) + lane, tile, 2), :]
                    for volume in volumes[1:]:
                        total = total + volume[pl.ds(2 * (base + at) + lane, tile, 2), :]
                    out_ref[pl.ds(at, tile), lane * OB : (lane + 1) * OB] = total.astype(BF16)
                return carry

            lax.fori_loop(0, half // tile, finish, 0)


def insert_call(me, rows, flat, fraction, blocks, posts, devices):
    count = flat.shape[0]
    steps, gb, orients = rows.shape
    width = flat.shape[1] // (steps * gb)
    total = devices * RD
    copies = max(1, min(4, 32 * MB // (total * width * 4)))
    smem = pl.BlockSpec(memory_space=pltpu.SMEM)
    share = posts[0].shape[0]
    return pl.pallas_call(
        functools.partial(insert_kernel, share_count=len(posts), copies=copies),
        grid=(steps,),
        out_shape=[jax.ShapeDtypeStruct((total // 2, width), BF16)] * 2,
        in_specs=[
            smem,
            pl.BlockSpec((1, gb, orients), lambda i: (i, 0, 0), memory_space=pltpu.SMEM),
            pl.BlockSpec((count, gb * width), lambda i: (0, i)),
            pl.BlockSpec((1, orients, gb), lambda i: (i, 0, 0)),
            pl.BlockSpec((count, 2), lambda i: (0, 0)),
        ]
        + [pl.BlockSpec((share, 2 * OB), lambda i: (0, 0))] * len(posts),
        out_specs=[pl.BlockSpec((total // 2, width), lambda i: (0, 0))] * 2,
        scratch_shapes=[
            pltpu.VMEM((orients, count), BF16),
            pltpu.VMEM((count, orients), F32),
            pltpu.VMEM((4 * orients, OB), F32),
        ]
        + [pltpu.VMEM((2 * total, OB), F32)] * copies,
        compiler_params=pltpu.CompilerParams(vmem_limit_bytes=60 * MB),
        cost_estimate=pl.CostEstimate(
            flops=2 * count * orients * steps * gb * width,
            bytes_accessed=2 * count * steps * gb * width,
            transcendentals=0,
        ),
    )(me, rows, flat, fraction, blocks, *posts)


def flip(value, axis, bit):
    size = lax.axis_size(axis)
    return lax.ppermute(value, axis, [(i, i ^ bit) for i in range(size)])


def shards(particles, blocks, references, inv_noise, destination, row_index, fraction):
    groups, width = particles.shape[1:]
    orients = references.shape[0]
    dom_size = lax.axis_size("dom")
    slab_size = lax.axis_size("slab")
    devices = dom_size * slab_size
    dom_pos = lax.axis_index("dom")
    slab_pos = lax.axis_index("slab")
    slab_me = slab_pos.astype(jnp.int32).reshape(1)
    dom_bits = [1 << i for i in range((dom_size - 1).bit_length())]
    slab_bits = [1 << i for i in range((slab_size - 1).bit_length())]

    flat, *scores = score_call(slab_me, inv_noise, particles, references, blocks, slab_size)
    parts = [scores[0]] + [flip(scores[k], "slab", k) for k in range(1, slab_size)]
    post = softmax_call(parts)
    posts = [post] + [flip(post, "slab", k) for k in range(1, slab_size)]

    gb = group_block(groups)
    steps = groups // gb
    take = lambda table: lax.dynamic_slice_in_dim(table, slab_pos * groups, groups, 0)
    owner = take(destination)
    dom_off = (owner // slab_size) ^ dom_pos
    slab_off = (owner % slab_size) ^ slab_pos
    place = jnp.zeros_like(owner)
    for bit in dom_bits:
        place = place * 2 + jnp.where(dom_off & bit != 0, 1, 0)
    for bit in slab_bits:
        place = place * 2 + jnp.where(slab_off & bit != 0, 1, 0)
    rows = ((place * RD + take(row_index)) * 2).reshape(steps, gb, orients)
    mine = take(fraction).reshape(steps, gb, orients).transpose(0, 2, 1)
    send, keep = insert_call(slab_me, rows, flat, mine, blocks, posts, devices)

    def merge(kept, got):
        return kept.astype(F32) + got.astype(F32)

    total = merge(keep, flip(send, "dom", dom_bits[0]))
    rest = dom_bits[1:]
    total = total.reshape((2,) * len(rest) + (slab_size * RD, width))
    halves = []
    for part, order in ((0, rest), (1, rest[::-1])):
        value = total[..., part * OB : (part + 1) * OB]
        axes = list(rest)
        for bit in order:
            axis = axes.index(bit)
            axes.pop(axis)
            kept = lax.index_in_dim(value, 0, axis, keepdims=False)
            sent = lax.index_in_dim(value, 1, axis, keepdims=False)
            value = merge(kept, flip(sent.astype(BF16), "dom", bit))
        halves.append(value)
    value = jnp.concatenate(halves, axis=1)
    for bit in slab_bits:
        near, far = jnp.split(value, 2, axis=0)
        value = merge(near, flip(far.astype(BF16), "slab", bit))
    volume = value

    own = volume.astype(BF16)
    columns = []
    for part, order in ((0, rest), (1, rest[::-1])):
        value = own[:, part * OB : (part + 1) * OB]
        done = []
        for bit in order:
            got = flip(value, "dom", bit)
            axis = len([b for b in done if b > bit])
            done.append(bit)
            mine_low = dom_pos & bit == 0
            value = jnp.where(
                mine_low, jnp.stack([value, got], axis), jnp.stack([got, value], axis)
            )
        columns.append(value)
    value = jnp.concatenate(columns, axis=-1)
    got = flip(value, "dom", dom_bits[0])
    value = jnp.where(
        dom_pos & dom_bits[0] == 0,
        jnp.stack([value, got], len(rest)),
        jnp.stack([got, value], len(rest)),
    )
    return volume, value.reshape(dom_size * RD, width)


def solution(mesh):
    return jax.shard_map(
        shards,
        mesh=mesh,
        in_specs=(
            P("dom", "slab", None),
            P("dom", None),
            P(None, "slab", None),
            P("slab"),
            P(),
            P(),
            P(),
        ),
        out_specs=(P(("dom", "slab"), None), P(None, "slab")),
        check_vma=False,
    )
```

time: 895 us -> 290 us (0.32)
  other arithmetic: 517 us -> 6.26 us
  Pallas kernels: 0 us -> 201 us
  waiting for transfers between devices: 239 us -> 51.8 us
  local copies, waits for them, and re-layouts: 71.2 us -> 5.78 us
  matrix products: 52 us -> 0 us
  starting transfers between devices: 0.3 us -> 24.2 us
  between operations: 13.9 us -> 0.8 us
    scatter-add x2 -> x0, other arithmetic: 490 us -> none  [spread_rows(): volume_rows.at[targets].add(lower_part).at[targets + 1].add(upper_part)]
    pallas_call x0 -> x3, Pallas kernels: none -> 201 us  [the longest x1 141 us: insert_call(): pl.pallas_call(functools.partial(insert_kernel, share_count=len(posts), c...]
    reduce_scatter x1 -> x0, waiting for transfers between devices: 185 us -> none  [shards(): lax.psum_scatter(whole, ('dom', 'slab'), scatter_dimension=0, tiled=True)]
    dot_general x2 -> x0, matrix products: 52 us -> none  [the longest x1 27.9 us: shards(): lax.dot_general(flat_rows, weighted, (((1,), (1,)), ((), ())), preferred_...]
    ppermute x0 -> x18, waiting for transfers between devices: none -> 51.8 us  [flip(): return lax.ppermute(value, axis, [(i, i ^ bit) for i in range(size)])]
    convert_element_type x1 -> x4, local copies, waits for them, and re-layouts: 40.6 us -> 0.2 us  [shards(): value = merge(kept, flip(sent.astype(BF16), 'dom', bit))]
    psum x1 -> x0, waiting for transfers between devices: 31.5 us -> none  [shards(): scores = lax.psum(partial_value, 'slab')]
    ppermute x0 -> x18, starting transfers between devices: none -> 24.2 us  [flip(): return lax.ppermute(value, axis, [(i, i ^ bit) for i in range(size)])]
  transfers between devices with their start and end apart: 3 -> 18, of which waited for: 3 -> 15; matrix products, arithmetic and copies ran while one was open for 3% -> 1% of each run, Pallas kernels for 0% -> 0%
where the time goes in v1:
time: 290 us
  Pallas kernels  201 us (69%)
  waiting for transfers between devices  51.8 us (18%)
  starting transfers between devices  24.2 us (8%)
  other arithmetic  6.26 us (2%)
  local copies, waits for them, and re-layouts  5.78 us (2%)
    pallas_call x1, Pallas kernels, insert_call(): pl.pallas_call(functools.partial(insert_kernel, share_count=len(posts), c...  141 us
    pallas_call x1, Pallas kernels, score_call(): pl.pallas_call(score_kernel, grid=(groups // gb,), out_shape=[jax.ShapeDt...  58.1 us
    ppermute x18, waiting for transfers between devices, flip(): return lax.ppermute(value, axis, [(i, i ^ bit) for i in range(size)])  51.8 us
    ppermute x18, starting transfers between devices, flip(): return lax.ppermute(value, axis, [(i, i ^ bit) for i in range(size)])  24.2 us
  transfers between devices with their start and end apart: 18, of which 15 were waited for; matrix products, arithmetic and copies ran while one was open for 1% of the time, Pallas kernels for 0%

profile of v1, /device:TPU:0, one launch (start us, length us, event | category | flops | bytes accessed | tf_op | source)
XLA Modules:
  0.0 290.2 jit_solution(18412442726531806954)
XLA Ops:
  0.7 1.6 copy.15.blk_ref
  3.1 58.1 %shard_map.86 = (bf16[512,20480]{1,0:T(8,128)(2,1)}, f32[128,256]{1,0:T(8,128)}, f32[128,256]{1,0:T(8,128)}, f32[128,256]{1,0:T(8,128)}, f32[128,256]{1,0:T(8,128)}) custom-call(s32[1]{0:T(128)} %bitcast.me_ref, f32[80]{0:T(128)} %noise_ref.1, bf16[256,256]{1,0:T(8,128)(2,1)} %and_convert_fusion.perm_ref, bf16[512,80,256]{2,1,0:T(8,128)(2,1)} %x_ref.1, ...), custom_call_target="tpu_custom_call" | custom-call | flops 21474836480 | bytes 62914560 | tf_op jit(solution)/shard_map/pallas_call | solution.py:92
  61.2 3.1 %collective-permute-start = (f32[128,256]{1,0:T(8,128)}, f32[128,256]{1,0:T(8,128)S(1)}, u32[]{:S(2)}, u32[]{:S(2)}) collective-permute-start(f32[128,256]{1,0:T(8,128)} %get-tuple-element.11), channel_id=1, source_target_pairs={{0,1},{1,0},{2,3},{3,2},{4,5},{5,4},{6,7},{7,6},{8,9},{9,8},{10,11... | collective-permute-start | bytes 393224 | tf_op jit(solution)/shard_map/ppermute | solution.py:250
  64.3 2.6 collective-permute-start.1
  69.5 7.9 %collective-permute-done.1.refs_2_ = f32[128,256]{1,0:T(8,128)S(1)} collective-permute-done((f32[128,256]{1,0:T(8,128)}, f32[128,256]{1,0:T(8,128)S(1)}, u32[]{:S(2)}, u32[]{:S(2)}) %collective-permute-start.1) | collective-permute-done | bytes 131104 | tf_op jit(solution)/shard_map/ppermute | solution.py:250
  78.1 1.9 shard_map.87.rest_0_
  80.1 1.9 collective-permute-start.3
  84.4 2.0 add_multiply_fusion
  86.4 2.1 collective-permute-done.4.rest_2_
  89.9 141.2 %shard_map.88 = (bf16[4096,256]{1,0:T(8,128)(2,1)}, bf16[4096,256]{1,0:T(8,128)(2,1)}) custom-call(s32[1]{0:T(128)} %bitcast.me_ref, s32[5,16,512]{2,1,0:T(8,128)} %bitcast.66, bf16[512,20480]{1,0:T(8,128)(2,1)} %get-tuple-element.9.x_ref, f32[5,512,16]{2,1,0:T(8,128)} %bitcast.58, s32[512,2]{1,0:T(8,128)} %copy.15.blk_ref, ...), custom_call_target="tpu_custom_call" | custom-call | flops 10737418240 | bytes 20971520 | tf_op jit(solution)/shard_map/pallas_call | solution.py:220
  231.2 4.4 %collective-permute-done.6 = bf16[4096,256]{1,0:T(8,128)(2,1)S(1)} collective-permute-done((bf16[4096,256]{1,0:T(8,128)(2,1)}, bf16[4096,256]{1,0:T(8,128)(2,1)S(1)}, u32[]{:S(2)}, u32[]{:S(2)}) %collective-permute-start.6) | collective-permute-done | bytes 2097184 | tf_op jit(solution)/shard_map/ppermute | solution.py:250
  235.5 2.0 convert_add_fusion
  237.7 1.5 collective-permute-start.7
  239.2 1.5 collective-permute-start.9
  240.8 11.0 %collective-permute-done.7 = bf16[2,1024,128]{2,1,0:T(8,128)(2,1)S(1)} collective-permute-done((bf16[2,1024,128]{2,1,0:T(8,128)(2,1)S(1)}, bf16[2,1024,128]{2,1,0:T(8,128)(2,1)S(1)}, u32[]{:S(2)}, u32[]{:S(2)}) %collective-permute-start.7) | collective-permute-done | bytes 524320 | tf_op jit(solution)/shard_map/ppermute | solution.py:250
  253.8 1.6 collective-permute-start.8
  255.4 5.0 %collective-permute-done.10 = bf16[1024,128]{1,0:T(8,128)(2,1)S(1)} collective-permute-done((bf16[1024,128]{1,0:T(8,128)(2,1)S(1)}, bf16[1024,128]{1,0:T(8,128)(2,1)S(1)}, u32[]{:S(2)}, u32[]{:S(2)}) %collective-permute-start.10) | collective-permute-done | bytes 262176 | tf_op jit(solution)/shard_map/ppermute | solution.py:250
  262.2 5.2 %collective-permute-done.11 = bf16[512,256]{1,0:T(8,128)(2,1)S(1)} collective-permute-done((bf16[512,256]{1,0:T(8,128)(2,1)S(1)}, bf16[512,256]{1,0:T(8,128)(2,1)S(1)}, u32[]{:S(2)}, u32[]{:S(2)}) %collective-permute-start.11) | collective-permute-done | bytes 262176 | tf_op jit(solution)/shard_map/ppermute | solution.py:250
  267.5 2.2 collective-permute-start.12
  269.7 5.1 %collective-permute-done.12 = bf16[256,256]{1,0:T(8,128)(2,1)S(1)} collective-permute-done((bf16[256,256]{1,0:T(8,128)(2,1)S(1)}, bf16[256,256]{1,0:T(8,128)(2,1)S(1)}, u32[]{:S(2)}, u32[]{:S(2)}) %collective-permute-start.12) | collective-permute-done | bytes 131104 | tf_op jit(solution)/shard_map/ppermute | solution.py:250
  277.1 1.5 collective-permute-start.15
  278.6 2.0 collective-permute-done.13
  283.1 2.6 collective-permute-done.14
  287.0 1.9 collective-permute-done.17
  (59 shorter events, 19.4 us)
Async XLA Ops:
  0.6 66.2 %copy-start = (f32[320,512]{1,0:T(8,128)S(1)}, f32[320,512]{1,0:T(8,128)}, u32[]{:S(2)}) copy-start(f32[320,512]{1,0:T(8,128)} %param.13) | copy-start | bytes 1966084
  61.2 8.3 %collective-permute-start = (f32[128,256]{1,0:T(8,128)}, f32[128,256]{1,0:T(8,128)S(1)}, u32[]{:S(2)}, u32[]{:S(2)}) collective-permute-start(f32[128,256]{1,0:T(8,128)} %get-tuple-element.11), channel_id=1, source_target_pairs={{0,1},{1,0},{2,3},{3,2},{4,5},{5,4},{6,7},{7,6},{8,9},{9,8},{10,11... | collective-permute-start | bytes 393224 | tf_op jit(solution)/shard_map/ppermute | solution.py:250
  64.3 13.1 %collective-permute-start.1 = (f32[128,256]{1,0:T(8,128)}, f32[128,256]{1,0:T(8,128)S(1)}, u32[]{:S(2)}, u32[]{:S(2)}) collective-permute-start(f32[128,256]{1,0:T(8,128)} %get-tuple-element.12), channel_id=1, source_target_pairs={{0,2},{1,3},{2,0},{3,1},{4,6},{5,7},{6,4},{7,5},{8,10},{9,11},{10,... | collective-permute-start | bytes 393224 | tf_op jit(solution)/shard_map/ppermute | solution.py:250
  66.9 10.6 %collective-permute-start.2 = (f32[128,256]{1,0:T(8,128)}, f32[128,256]{1,0:T(8,128)S(1)}, u32[]{:S(2)}, u32[]{:S(2)}) collective-permute-start(f32[128,256]{1,0:T(8,128)} %get-tuple-element.13), channel_id=1, source_target_pairs={{0,3},{1,2},{2,1},{3,0},{4,7},{5,6},{6,5},{7,4},{8,11},{9,10},{10,... | collective-permute-start | bytes 393224 | tf_op jit(solution)/shard_map/ppermute | solution.py:250
  69.5 7.9 %copy-start.2 = (f32[128,256]{1,0:T(8,128)}, f32[128,256]{1,0:T(8,128)S(1)}, u32[]{:S(2)}) copy-start(f32[128,256]{1,0:T(8,128)S(1)} %collective-permute-done.refs_1_) | copy-start | bytes 393220
  77.4 0.7 copy-start.4
  80.1 6.3 %collective-permute-start.3 = (bf16[128,256]{1,0:T(8,128)(2,1)}, bf16[128,256]{1,0:T(8,128)(2,1)S(1)}, u32[]{:S(2)}, u32[]{:S(2)}) collective-permute-start(bf16[128,256]{1,0:T(8,128)(2,1)} %shard_map.87.rest_0_), channel_id=1, source_target_pairs={{0,1},{1,0},{2,3},{3,2},{4,5},{5,4},{6,7},{7,6},{8,9},{9,8},{10,11... | collective-permute-start | bytes 196616 | tf_op jit(solution)/shard_map/ppermute | solution.py:250
  82.0 6.6 %collective-permute-start.4 = (bf16[128,256]{1,0:T(8,128)(2,1)}, bf16[128,256]{1,0:T(8,128)(2,1)S(1)}, u32[]{:S(2)}, u32[]{:S(2)}) collective-permute-start(bf16[128,256]{1,0:T(8,128)(2,1)} %shard_map.87.rest_0_), channel_id=1, source_target_pairs={{0,2},{1,3},{2,0},{3,1},{4,6},{5,7},{6,4},{7,5},{8,10},{9,11},{10,... | collective-permute-start | bytes 196616 | tf_op jit(solution)/shard_map/ppermute | solution.py:250
  83.0 6.3 %collective-permute-start.5 = (bf16[128,256]{1,0:T(8,128)(2,1)}, bf16[128,256]{1,0:T(8,128)(2,1)S(1)}, u32[]{:S(2)}, u32[]{:S(2)}) collective-permute-start(bf16[128,256]{1,0:T(8,128)(2,1)} %shard_map.87.rest_0_), channel_id=1, source_target_pairs={{0,3},{1,2},{2,1},{3,0},{4,7},{5,6},{6,5},{7,4},{8,11},{9,10},{10,... | collective-permute-start | bytes 196616 | tf_op jit(solution)/shard_map/ppermute | solution.py:250
  86.4 2.9 %copy-start.5 = (bf16[128,256]{1,0:T(8,128)(2,1)}, bf16[128,256]{1,0:T(8,128)(2,1)S(1)}, u32[]{:S(2)}) copy-start(bf16[128,256]{1,0:T(8,128)(2,1)S(1)} %collective-permute-done.3.rest_1_) | copy-start | bytes 196612
  88.5 0.8 copy-start.6
  231.2 4.4 %collective-permute-start.6 = (bf16[4096,256]{1,0:T(8,128)(2,1)}, bf16[4096,256]{1,0:T(8,128)(2,1)S(1)}, u32[]{:S(2)}, u32[]{:S(2)}) collective-permute-start(bf16[4096,256]{1,0:T(8,128)(2,1)} %get-tuple-element.15), channel_id=1, source_target_pairs={{0,4},{4,0},{8,12},{12,8},{16,20},{20,16},{24,28},{28,24},{1,5},{5... | collective-permute-start | bytes 6291464 | tf_op jit(solution)/shard_map/ppermute | solution.py:250
  237.7 14.0 %collective-permute-start.7 = (bf16[2,1024,128]{2,1,0:T(8,128)(2,1)S(1)}, bf16[2,1024,128]{2,1,0:T(8,128)(2,1)S(1)}, u32[]{:S(2)}, u32[]{:S(2)}) collective-permute-start(bf16[2,1024,128]{2,1,0:T(8,128)(2,1)S(1)} %slice_bitcast_fusion.5), channel_id=1, source_target_pairs={{0,8},{4,12},{8,0},{12,4},{16,24},{20,28},{24,16},{28,20},{1,9},{5... | collective-permute-start | bytes 1572872 | tf_op jit(solution)/shard_map/ppermute | solution.py:250
  239.2 13.7 %collective-permute-start.9 = (bf16[2,1024,128]{2,1,0:T(8,128)(2,1)S(1)}, bf16[2,1024,128]{2,1,0:T(8,128)(2,1)S(1)}, u32[]{:S(2)}, u32[]{:S(2)}) collective-permute-start(bf16[2,1024,128]{2,1,0:T(8,128)(2,1)S(1)} %slice_bitcast_fusion.3), channel_id=1, source_target_pairs={{0,16},{4,20},{8,24},{12,28},{16,0},{20,4},{24,8},{28,12},{1,17},{... | collective-permute-start | bytes 1572872 | tf_op jit(solution)/shard_map/ppermute | solution.py:250
  253.2 7.3 %collective-permute-start.10 = (bf16[1024,128]{1,0:T(8,128)(2,1)S(1)}, bf16[1024,128]{1,0:T(8,128)(2,1)S(1)}, u32[]{:S(2)}, u32[]{:S(2)}) collective-permute-start(bf16[1024,128]{1,0:T(8,128)(2,1)S(1)} %fusion.8), channel_id=1, source_target_pairs={{0,8},{4,12},{8,0},{12,4},{16,24},{20,28},{24,16},{28,20},{1,9},{5... | collective-permute-start | bytes 786440 | tf_op jit(solution)/shard_map/ppermute | solution.py:250
  253.8 7.0 %collective-permute-start.8 = (bf16[1024,128]{1,0:T(8,128)(2,1)S(1)}, bf16[1024,128]{1,0:T(8,128)(2,1)S(1)}, u32[]{:S(2)}, u32[]{:S(2)}) collective-permute-start(bf16[1024,128]{1,0:T(8,128)(2,1)S(1)} %fusion.7), channel_id=1, source_target_pairs={{0,16},{4,20},{8,24},{12,28},{16,0},{20,4},{24,8},{28,12},{1,17},{... | collective-permute-start | bytes 786440 | tf_op jit(solution)/shard_map/ppermute | solution.py:250
  260.9 6.4 %collective-permute-start.11 = (bf16[512,256]{1,0:T(8,128)(2,1)S(1)}, bf16[512,256]{1,0:T(8,128)(2,1)S(1)}, u32[]{:S(2)}, u32[]{:S(2)}) collective-permute-start(bf16[512,256]{1,0:T(8,128)(2,1)S(1)} %fusion.4), channel_id=1, source_target_pairs={{0,1},{1,0},{2,3},{3,2},{4,5},{5,4},{6,7},{7,6},{8,9},{9,8},{10,11... | collective-permute-start | bytes 786440 | tf_op jit(solution)/shard_map/ppermute | solution.py:250
  267.5 7.3 %collective-permute-start.12 = (bf16[256,256]{1,0:T(8,128)(2,1)S(1)}, bf16[256,256]{1,0:T(8,128)(2,1)S(1)}, u32[]{:S(2)}, u32[]{:S(2)}) collective-permute-start(bf16[256,256]{1,0:T(8,128)(2,1)S(1)} %split.32), channel_id=1, source_target_pairs={{0,2},{1,3},{2,0},{3,1},{4,6},{5,7},{6,4},{7,5},{8,10},{9,11},{10,... | collective-permute-start | bytes 393224 | tf_op jit(solution)/shard_map/ppermute | solution.py:250
  275.5 14.6 %copy-start.1 = (f32[320,512]{1,0:T(8,128)S(1)}, f32[320,512]{1,0:T(8,128)}, u32[]{:S(2)}) copy-start(f32[320,512]{1,0:T(8,128)} %param.13) | copy-start | bytes 1966084
  275.6 5.0 %collective-permute-start.13 = (bf16[256,128]{1,0:T(8,128)(2,1)S(1)}, bf16[256,128]{1,0:T(8,128)(2,1)S(1)}, u32[]{:S(2)}, u32[]{:S(2)}) collective-permute-start(bf16[256,128]{1,0:T(8,128)(2,1)S(1)} %get-tuple-element.27), channel_id=1, source_target_pairs={{0,8},{4,12},{8,0},{12,4},{16,24},{20,28},{24,16},{28,20},{1,9},{5... | collective-permute-start | bytes 196616 | tf_op jit(solution)/shard_map/ppermute | solution.py:250
  277.1 4.7 %collective-permute-start.15 = (bf16[256,128]{1,0:T(8,128)(2,1)S(1)}, bf16[256,128]{1,0:T(8,128)(2,1)S(1)}, u32[]{:S(2)}, u32[]{:S(2)}) collective-permute-start(bf16[256,128]{1,0:T(8,128)(2,1)S(1)} %get-tuple-element.26), channel_id=1, source_target_pairs={{0,16},{4,20},{8,24},{12,28},{16,0},{20,4},{24,8},{28,12},{1,17},{... | collective-permute-start | bytes 196616 | tf_op jit(solution)/shard_map/ppermute | solution.py:250
  280.6 5.0 %collective-permute-start.14 = (bf16[2,256,128]{2,1,0:T(8,128)(2,1)S(1)}, bf16[2,256,128]{2,1,0:T(8,128)(2,1)S(1)}, u32[]{:S(2)}, u32[]{:S(2)}) collective-permute-start(bf16[2,256,128]{2,1,0:T(8,128)(2,1)S(1)} %maximum_select_fusion.3), channel_id=1, source_target_pairs={{0,16},{4,20},{8,24},{12,28},{16,0},{20,4},{24,8},{28,12},{1,17},{... | collective-permute-start | bytes 393224 | tf_op jit(solution)/shard_map/ppermute | solution.py:250
  281.8 5.0 %collective-permute-start.16 = (bf16[2,256,128]{2,1,0:T(8,128)(2,1)S(1)}, bf16[2,256,128]{2,1,0:T(8,128)(2,1)S(1)}, u32[]{:S(2)}, u32[]{:S(2)}) collective-permute-start(bf16[2,256,128]{2,1,0:T(8,128)(2,1)S(1)} %maximum_select_fusion.5), channel_id=1, source_target_pairs={{0,8},{4,12},{8,0},{12,4},{16,24},{20,28},{24,16},{28,20},{1,9},{5... | collective-permute-start | bytes 393224 | tf_op jit(solution)/shard_map/ppermute | solution.py:250
  287.0 2.0 collective-permute-start.17
  (2 other events, 1.3 us)

commit v2 on v1

--- a/solution.py
+++ b/solution.py
@@ -42,7 +42,7 @@
                 dst_ref[pl.ds(at, 16), g * width : (g + 1) * width] = part.astype(BF16)
             return carry
 
-        lax.fori_loop(0, src_ref.shape[0] // 16, body, 0, unroll=2)
+        lax.fori_loop(0, src_ref.shape[0] // 16, body, 0, unroll=8)
 
     regroup(r_ref, w_ref, True)
     regroup(x_ref, flat_ref, False)
@@ -133,22 +133,120 @@
     )(*parts)
 
 
-def insert_kernel(me_ref, row_ref, x_ref, frac_ref, blk_ref, *rest, share_count, copies):
-    post_refs = rest[:share_count]
-    send_ref, keep_ref = rest[share_count : share_count + 2]
-    post_t, spread_ref, quad_ref = rest[share_count + 2 : share_count + 5]
-    volumes = rest[share_count + 5 :]
+def plan_kernel(place_ref, pos_ref, addr_ref, item_ref, hot_ref, count_ref, *, owners):
+    _, gb, orients = place_ref.shape
+    lanes = addr_ref.shape[2]
+    owner = lax.broadcasted_iota(jnp.int32, (owners, 1), 0)
+    for g in range(gb):
+        hot = jnp.where(place_ref[0, g : g + 1, :] == owner, 1.0, 0.0)
+        hot_ref[g * owners : (g + 1) * owners, :] = hot.astype(BF16)
+    before = lax.broadcasted_iota(jnp.int32, (orients, orients), 0)
+    after = lax.broadcasted_iota(jnp.int32, (orients, orients), 1)
+    upto = jnp.where(before <= after, 1.0, 0.0).astype(BF16)
+    count_ref[...] = jnp.dot(hot_ref[...], upto, preferred_element_type=F32)
+
+    exact = functools.partial(
+        jnp.dot, preferred_element_type=F32, precision=lax.Precision.HIGHEST
+    )
+    tri = lambda n, lower: jnp.where(
+        (lax.broadcasted_iota(jnp.int32, (n, n), 0) > lax.broadcasted_iota(jnp.int32, (n, n), 1))
+        == lower,
+        1.0,
+        0.0,
+    )
+    below = tri(owners, True)
+    row = lax.broadcasted_iota(jnp.int32, (OB, OB), 0)
+    col = lax.broadcasted_iota(jnp.int32, (OB, OB), 1)
+    earlier = jnp.where(row < col, 1.0, 0.0)
+    lane = lax.broadcasted_iota(jnp.int32, (owners, OB), 1)
+    sizes = jnp.zeros((owners, OB), F32)
+    for g in range(gb):
+        size = count_ref[g * owners : (g + 1) * owners, orients - 1 : orients]
+        size = jnp.floor((size + 7.0) * 0.125) * 8.0
+        sizes = jnp.where(lane == g, size, sizes)
+    base = exact(below, sizes)
+    ahead = exact(sizes, earlier)
+    total = jnp.sum(sizes, axis=1, keepdims=True)
+    start = exact(below, jnp.broadcast_to(total, (owners, OB)))[:, :1]
+    blocks = jnp.floor((total + (RD - 1.0)) * (1.0 / RD))
+    first = exact(below, jnp.broadcast_to(blocks, (owners, OB)))[:, :1]
+    owner_f = owner.astype(F32)
+
+    slot = (lax.broadcasted_iota(jnp.int32, (1, lanes), 1) * 8).astype(F32)
+    is_last = lax.broadcasted_iota(jnp.int32, (1, lanes), 1) == lanes - 1
+    rows = gb * (orients + 7 * owners)
+    for g in range(gb):
+        low, size = base[:, g : g + 1], sizes[:, g : g + 1]
+        hot = hot_ref[g * owners : (g + 1) * owners, :].astype(F32)
+        rank = count_ref[g * owners : (g + 1) * owners, :] - 1.0 + low
+        pos_ref[0, g : g + 1, :] = jnp.sum(hot * rank, axis=0, keepdims=True).astype(jnp.int32)
+        inside = (slot >= low) & (slot < low + size)
+        goal = jnp.where(inside, start + ahead[:, g : g + 1] - low + slot - rows, 0.0)
+        goal = jnp.sum(goal, axis=0, keepdims=True) + rows
+        used = jnp.sum(size, axis=0, keepdims=True)
+        addr_ref[0, g : g + 1, :] = jnp.where(is_last, used, goal).astype(jnp.int32)
+
+    wide = item_ref.shape[2]
+    number = lax.broadcasted_iota(jnp.int32, (1, wide), 1).astype(F32)
+    inside = (number >= first) & (number < first + blocks)
+    done = (number - first) * RD
+    pick = lambda value: jnp.sum(jnp.where(inside, value, 0.0), axis=0, keepdims=True)
+    item_ref[0, 0:1, :] = pick(jnp.broadcast_to(owner_f, (owners, wide))).astype(jnp.int32)
+    item_ref[0, 1:2, :] = pick(start + done).astype(jnp.int32)
+    item_ref[0, 2:3, :] = pick(total - done).astype(jnp.int32)
+    items = jnp.sum(jnp.broadcast_to(blocks, (owners, wide)), axis=0, keepdims=True)
+    item_ref[0, 3:4, :] = items.astype(jnp.int32)
+
+
+def up_to(value, step):
+    return -(-value // step) * step
+
+
+def plan_call(place, owners):
+    steps, gb, orients = place.shape
+    slots = orients + 7 * owners
+    lanes = up_to(slots // 8 + 17, 128)
+    wide = up_to(owners + gb * slots // RD + 4, 128)
+    block = lambda *shape: pl.BlockSpec((1,) + shape, lambda i: (i, 0, 0))
+    return pl.pallas_call(
+        functools.partial(plan_kernel, owners=owners),
+        grid=(steps,),
+        out_shape=[
+            jax.ShapeDtypeStruct((steps, gb, orients), jnp.int32),
+            jax.ShapeDtypeStruct((steps, gb, lanes), jnp.int32),
+            jax.ShapeDtypeStruct((steps, 4, wide), jnp.int32),
+        ],
+        in_specs=[block(gb, orients)],
+        out_specs=[block(gb, orients), block(gb, lanes), block(4, wide)],
+        scratch_shapes=[
+            pltpu.VMEM((gb * owners, orients), BF16),
+            pltpu.VMEM((gb * owners, orients), F32),
+        ],
+        compiler_params=pltpu.CompilerParams(vmem_limit_bytes=40 * MB),
+        cost_estimate=pl.CostEstimate(
+            flops=8 * steps * gb * owners * orients * orients,
+            bytes_accessed=8 * steps * gb * orients,
+            transcendentals=0,
+        ),
+    )(place)
+
+
+def insert_kernel(me_ref, addr_ref, item_ref, x_ref, pos_ref, rowf_ref, blk_ref, *rest):
+    *post_refs, send_ref, keep_ref = rest[:-8]
+    post_t, spread_ref, slice_ref, buf_s, buf_t, volume, stage, sem = rest[-8:]
     step = pl.program_id(0)
     count = x_ref.shape[0]
     orients = post_t.shape[0]
-    gb = frac_ref.shape[2]
+    gb = pos_ref.shape[1]
     width = x_ref.shape[1] // gb
-    share = count // share_count
+    share = count // len(post_refs)
+    lanes = addr_ref.shape[2]
 
     @pl.when(step == 0)
     def _():
-        for volume in volumes:
-            volume[...] = jnp.zeros_like(volume)
+        volume[...] = jnp.zeros_like(volume)
+        buf_s[...] = jnp.zeros_like(buf_s)
+        buf_t[...] = jnp.zeros_like(buf_t)
         me = me_ref[0]
         for k, post_ref in enumerate(post_refs):
             at = pl.multiple_of((me ^ k) * share, share)
@@ -163,86 +261,136 @@
         for b in range(orients // OB):
             post_t[b * OB : (b + 1) * OB] = spread_ref[:, b * OB : (b + 1) * OB].T.astype(BF16)
 
-    lanes = lax.broadcasted_iota(jnp.int32, (1, gb), 1)
+    def one_slice(g, carry):
+        at = pl.ds(pl.multiple_of(g * width, width), width)
+        value = jnp.dot(post_t[...], x_ref[:, at], preferred_element_type=F32)
+        slice_ref[:, at] = value.astype(BF16)
+        return carry
+
+    lax.fori_loop(0, gb, one_slice, 0, unroll=2)
+
+    bins = lax.broadcasted_iota(jnp.int32, (RD, 1), 0).astype(F32)
 
     def one_group(g, carry):
-        piece = jnp.dot(
-            post_t[...],
-            x_ref[:, pl.ds(pl.multiple_of(g * width, width), width)],
-            preferred_element_type=F32,
-        )
-        upper = jnp.sum(jnp.where(lanes == g, frac_ref[0], 0.0), axis=1, keepdims=True)
-        lower = 1.0 - upper
-        quad_ref[pl.ds(0, orients, 4), :] = piece[:, :OB] * lower
-        quad_ref[pl.ds(1, orients, 4), :] = piece[:, OB:] * lower
-        quad_ref[pl.ds(2, orients, 4), :] = piece[:, :OB] * upper
-        quad_ref[pl.ds(3, orients, 4), :] = piece[:, OB:] * upper
-        burst = 32
-
-        def rows(i, c):
-            for u in range(burst):
-                at = row_ref[0, g, i * burst + u]
-                src = quad_ref[pl.ds(pl.multiple_of(i * (4 * burst), 4 * burst) + 4 * u, 4), :]
-                volume = volumes[u % copies]
-                volume[pl.ds(at, 4), :] = volume[pl.ds(at, 4), :] + src
+        pos = pos_ref[0, pl.ds(g, 1), :]
+        tent = jnp.maximum(1.0 - jnp.abs(bins - rowf_ref[0, pl.ds(g, 1), :]), 0.0).astype(BF16)
+        piece = slice_ref[:, pl.ds(pl.multiple_of(g * width, width), width)]
+
+        def emit(base, size):
+            slot = lax.broadcasted_iota(jnp.int32, (size, 1), 0) + base
+            order = jnp.where(slot == pos, 1.0, 0.0).astype(BF16)
+            rows = jnp.dot(order, piece, preferred_element_type=F32)
+            weights = lax.dot_general(
+                order, tent, (((1,), (1,)), ((), ())), preferred_element_type=F32
+            )
+            for i in range(size // 8):
+                at = pl.multiple_of(addr_ref[0, g, base // 8 + i], 8)
+                buf_s[pl.ds(at, 8), :] = rows[8 * i : 8 * i + 8]
+                buf_t[pl.ds(at, 8), :] = weights[8 * i : 8 * i + 8]
+
+        sure = orients + 128
+        emit(0, sure)
+
+        def more(e, c):
+            emit(sure + e * 128, 128)
             return c
 
-        lax.fori_loop(0, orients // burst, rows, 0)
+        used = addr_ref[0, g, lanes - 1]
+        lax.fori_loop(0, lax.div(jnp.maximum(used - sure, 0) + 127, 128), more, 0)
         return carry
 
     lax.fori_loop(0, gb, one_group, 0)
+
+    line = lax.broadcasted_iota(jnp.int32, (RD, 1), 0)
+
+    def some_items(q, carry):
+        for u in range(4):
+            j = q * 4 + u
+            owner, at, left = item_ref[0, 0, j], item_ref[0, 1, j], item_ref[0, 2, j]
+            span = pl.ds(pl.multiple_of(at, 8), RD)
+            weights = jnp.where(line < left, buf_t[span, :], 0.0).T.astype(BF16)
+            goal = pl.ds(pl.multiple_of(owner * RD, RD), RD)
+            volume[goal, :] += jnp.dot(
+                weights, buf_s[span, :].astype(BF16), preferred_element_type=F32
+            )
+        return carry
+
+    lax.fori_loop(0, lax.div(item_ref[0, 3, 0] + 3, 4), some_items, 0)
 
     @pl.when(step == pl.num_programs(0) - 1)
     def _():
         half = keep_ref.shape[0]
-        tile = min(512, half)
+        tile = stage.shape[1]
+        copies = []
+        number = 0
         for base, out_ref in ((half, send_ref), (0, keep_ref)):
-            def finish(i, carry, base=base, out_ref=out_ref):
-                at = pl.multiple_of(i * tile, tile)
-                for lane in range(2):
-                    total = volumes[0][pl.ds(2 * (base + at) + lane, tile, 2), :]
-                    for volume in volumes[1:]:
-                        total = total + volume[pl.ds(2 * (base + at) + lane, tile, 2), :]
-                    out_ref[pl.ds(at, tile), lane * OB : (lane + 1) * OB] = total.astype(BF16)
-                return carry
-
-            lax.fori_loop(0, half // tile, finish, 0)
-
-
-def insert_call(me, rows, flat, fraction, blocks, posts, devices):
+            for at in range(0, half, tile):
+                slot = number % 2
+                if number >= 2:
+                    copies[number - 2].wait()
+                stage[slot] = volume[base + at : base + at + tile, :].astype(BF16)
+                copy = pltpu.make_async_copy(
+                    stage.at[slot], out_ref.at[pl.ds(at, tile)], sem.at[slot]
+                )
+                copy.start()
+                copies.append(copy)
+                number += 1
+        for copy in copies[-2:]:
+            copy.wait()
+
+
+def insert_block(groups, orients, owners, count, width):
+    room = 58 * MB - owners * RD * width * 4 - 6 * MB
+    best = 1
+    for gb in range(1, groups + 1):
+        rows = gb * (orients + 7 * owners) + RD + 8
+        need = rows * width * 8 + 4 * count * gb * width + 2 * orients * gb * width
+        if groups % gb == 0 and need <= room:
+            best = gb
+    return best
+
+
+def insert_call(me, addr, items, flat, pos, rowf, blocks, posts, owners):
     count = flat.shape[0]
-    steps, gb, orients = rows.shape
+    steps, gb, orients = pos.shape
     width = flat.shape[1] // (steps * gb)
-    total = devices * RD
-    copies = max(1, min(4, 32 * MB // (total * width * 4)))
+    total = owners * RD
+    share = posts[0].shape[0]
+    rows = gb * (orients + 7 * owners) + RD + 8
     smem = pl.BlockSpec(memory_space=pltpu.SMEM)
-    share = posts[0].shape[0]
+    block = lambda shape, **kw: pl.BlockSpec((1,) + shape[1:], lambda i: (i, 0, 0), **kw)
     return pl.pallas_call(
-        functools.partial(insert_kernel, share_count=len(posts), copies=copies),
+        insert_kernel,
         grid=(steps,),
         out_shape=[jax.ShapeDtypeStruct((total // 2, width), BF16)] * 2,
         in_specs=[
             smem,
-            pl.BlockSpec((1, gb, orients), lambda i: (i, 0, 0), memory_space=pltpu.SMEM),
+            block(addr.shape, memory_space=pltpu.SMEM),
+            block(items.shape, memory_space=pltpu.SMEM),
             pl.BlockSpec((count, gb * width), lambda i: (0, i)),
-            pl.BlockSpec((1, orients, gb), lambda i: (i, 0, 0)),
+            block(pos.shape),
+            block(rowf.shape),
             pl.BlockSpec((count, 2), lambda i: (0, 0)),
         ]
         + [pl.BlockSpec((share, 2 * OB), lambda i: (0, 0))] * len(posts),
-        out_specs=[pl.BlockSpec((total // 2, width), lambda i: (0, 0))] * 2,
+        out_specs=[pl.BlockSpec(memory_space=pl.ANY)] * 2,
         scratch_shapes=[
             pltpu.VMEM((orients, count), BF16),
             pltpu.VMEM((count, orients), F32),
-            pltpu.VMEM((4 * orients, OB), F32),
-        ]
-        + [pltpu.VMEM((2 * total, OB), F32)] * copies,
-        compiler_params=pltpu.CompilerParams(vmem_limit_bytes=60 * MB),
+            pltpu.VMEM((orients, gb * width), BF16),
+            pltpu.VMEM((rows, width), F32),
+            pltpu.VMEM((rows, RD), F32),
+            pltpu.VMEM((total, width), F32),
+            pltpu.VMEM((2, 512, width), BF16),
+            pltpu.SemaphoreType.DMA((2,)),
+        ],
+        compiler_params=pltpu.CompilerParams(vmem_limit_bytes=62 * MB),
         cost_estimate=pl.CostEstimate(
-            flops=2 * count * orients * steps * gb * width,
+            flops=8 * count * orients * steps * gb * width,
             bytes_accessed=2 * count * steps * gb * width,
             transcendentals=0,
         ),
-    )(me, rows, flat, fraction, blocks, *posts)
+    )(me, addr, items, flat, pos, rowf, blocks, *posts)
 
 
 def flip(value, axis, bit):
@@ -267,9 +415,9 @@
     post = softmax_call(parts)
     posts = [post] + [flip(post, "slab", k) for k in range(1, slab_size)]
 
-    gb = group_block(groups)
-    steps = groups // gb
-    take = lambda table: lax.dynamic_slice_in_dim(table, slab_pos * groups, groups, 0)
+    gb = insert_block(groups, orients, devices, particles.shape[0], width)
+    table = (groups // gb, gb, orients)
+    take = lambda array: lax.dynamic_slice_in_dim(array, slab_pos * groups, groups, 0)
     owner = take(destination)
     dom_off = (owner // slab_size) ^ dom_pos
     slab_off = (owner % slab_size) ^ slab_pos
@@ -278,9 +426,9 @@
         place = place * 2 + jnp.where(dom_off & bit != 0, 1, 0)
     for bit in slab_bits:
         place = place * 2 + jnp.where(slab_off & bit != 0, 1, 0)
-    rows = ((place * RD + take(row_index)) * 2).reshape(steps, gb, orients)
-    mine = take(fraction).reshape(steps, gb, orients).transpose(0, 2, 1)
-    send, keep = insert_call(slab_me, rows, flat, mine, blocks, posts, devices)
+    rowf = (take(row_index).astype(F32) + take(fraction)).reshape(table)
+    pos, addr, items = plan_call(place.reshape(table), devices)
+    send, keep = insert_call(slab_me, addr, items, flat, pos, rowf, blocks, posts, devices)
 
     def merge(kept, got):
         return kept.astype(F32) + got.astype(F32)

time: 290 us -> 238 us (0.82)
  Pallas kernels: 201 us -> 155 us
  waiting for transfers between devices: 51.8 us -> 44.8 us
    pallas_call x1 -> x2, Pallas kernels: 141 us -> 115 us  [the longest x1 108 us: insert_call(): pl.pallas_call(insert_kernel, grid=(steps,), out_shape=[jax.ShapeDtypeStr...]
    pallas_call x1, Pallas kernels: 58.1 us -> 38 us  [score_call(): pl.pallas_call(score_kernel, grid=(groups // gb,), out_shape=[jax.ShapeDt...]
    ppermute x18, waiting for transfers between devices: 51.8 us -> 44.8 us  [flip(): return lax.ppermute(value, axis, [(i, i ^ bit) for i in range(size)])]
  transfers between devices with their start and end apart: 18 -> 18, of which waited for: 15 -> 14; matrix products, arithmetic and copies ran while one was open for 1% -> 1% of each run, Pallas kernels for 0% -> 3%
where the time goes in v2:
time: 238 us
  Pallas kernels  155 us (65%)
  waiting for transfers between devices  44.8 us (19%)
  starting transfers between devices  24 us (10%)
  other arithmetic  7.18 us (3%)
  local copies, waits for them, and re-layouts  6.04 us (3%)
    pallas_call x1, Pallas kernels, insert_call(): pl.pallas_call(insert_kernel, grid=(steps,), out_shape=[jax.ShapeDtypeStr...  108 us
    ppermute x18, waiting for transfers between devices, flip(): return lax.ppermute(value, axis, [(i, i ^ bit) for i in range(size)])  44.8 us
    pallas_call x1, Pallas kernels, score_call(): pl.pallas_call(score_kernel, grid=(groups // gb,), out_shape=[jax.ShapeDt...  38 us
    ppermute x18, starting transfers between devices, flip(): return lax.ppermute(value, axis, [(i, i ^ bit) for i in range(size)])  24 us
    pallas_call x1, Pallas kernels, plan_call(): pl.pallas_call(functools.partial(plan_kernel, owners=owners), grid=(steps...  6.48 us
  transfers between devices with their start and end apart: 18, of which 14 were waited for; matrix products, arithmetic and copies ran while one was open for 1% of the time, Pallas kernels for 3%

profile of v2, /device:TPU:0, one launch (start us, length us, event | category | flops | bytes accessed | tf_op | source)
XLA Modules:
  0.0 237.6 jit_solution(8005567916509529682)
XLA Ops:
  0.6 1.5 copy.9.blk_ref
  3.0 38.0 %shard_map.87 = (bf16[512,20480]{1,0:T(8,128)(2,1)}, f32[128,256]{1,0:T(8,128)}, f32[128,256]{1,0:T(8,128)}, f32[128,256]{1,0:T(8,128)}, f32[128,256]{1,0:T(8,128)}) custom-call(s32[1]{0:T(128)} %bitcast.me_ref, f32[80]{0:T(128)} %noise_ref.1, bf16[256,256]{1,0:T(8,128)(2,1)} %and_convert_fusion.perm_ref, bf16[512,80,256]{2,1,0:T(8,128)(2,1)} %x_ref.1, ...), custom_call_target="tpu_custom_call" | custom-call | flops 21474836480 | bytes 62914560 | tf_op jit(solution)/shard_map/pallas_call | solution.py:92
  40.9 3.1 %collective-permute-start = (f32[128,256]{1,0:T(8,128)}, f32[128,256]{1,0:T(8,128)S(1)}, u32[]{:S(2)}, u32[]{:S(2)}) collective-permute-start(f32[128,256]{1,0:T(8,128)} %get-tuple-element.17), channel_id=1, source_target_pairs={{0,1},{1,0},{2,3},{3,2},{4,5},{5,4},{6,7},{7,6},{8,9},{9,8},{10,11... | collective-permute-start | bytes 393224 | tf_op jit(solution)/shard_map/ppermute | solution.py:398
  44.0 2.6 %collective-permute-start.1 = (f32[128,256]{1,0:T(8,128)}, f32[128,256]{1,0:T(8,128)S(1)}, u32[]{:S(2)}, u32[]{:S(2)}) collective-permute-start(f32[128,256]{1,0:T(8,128)} %get-tuple-element.18), channel_id=1, source_target_pairs={{0,2},{1,3},{2,0},{3,1},{4,6},{5,7},{6,4},{7,5},{8,10},{9,11},{10,... | collective-permute-start | bytes 393224 | tf_op jit(solution)/shard_map/ppermute | solution.py:398
  47.8 6.5 %shard_map.86 = (s32[5,16,512]{2,1,0:T(8,128)S(1)}, s32[5,16,128]{2,1,0:T(8,128)S(1)}, s32[5,4,128]{2,1,0:T(4,128)S(1)}) custom-call(s32[5,16,512]{2,1,0:T(8,128)S(1)} %bitcast.54), custom_call_target="tpu_custom_call" | custom-call | flops 5368709120 | bytes 327680 | tf_op jit(solution)/shard_map/pallas_call | solution.py:211
  57.9 1.9 shard_map.88.rest_0_
  59.8 1.9 collective-permute-start.3
  61.7 1.6 collective-permute-start.4
  64.2 1.7 dynamic-slice_add_fusion
  65.9 2.5 %collective-permute-done.4.rest_2_ = bf16[128,256]{1,0:T(8,128)(2,1)S(1)} collective-permute-done((bf16[128,256]{1,0:T(8,128)(2,1)}, bf16[128,256]{1,0:T(8,128)(2,1)S(1)}, u32[]{:S(2)}, u32[]{:S(2)}) %collective-permute-start.4) | collective-permute-done | bytes 65568 | tf_op jit(solution)/shard_map/ppermute | solution.py:398
  70.3 108.4 %shard_map.89 = (bf16[4096,256]{1,0:T(8,128)(2,1)}, bf16[4096,256]{1,0:T(8,128)(2,1)}) custom-call(s32[1]{0:T(128)} %bitcast.me_ref, s32[5,16,128]{2,1,0:T(8,128)} %copy-done.1, s32[5,4,128]{2,1,0:T(4,128)} %copy-done.2, bf16[512,20480]{1,0:T(8,128)(2,1)} %get-tuple-element.14.x_ref, s32[5,16,512]{2,1,0:T(8,128)} %copy-done, f32[5,16,512]{2,1,0:T(8,128)} %bitcast.64, ...), custom_call_target="tpu_custom_call" | custom-call | flops 42949672960 | bytes 20971520 | tf_op jit(solution)/shard_map/pallas_call | solution.py:362
  178.8 4.4 %collective-permute-done.6 = bf16[4096,256]{1,0:T(8,128)(2,1)S(1)} collective-permute-done((bf16[4096,256]{1,0:T(8,128)(2,1)}, bf16[4096,256]{1,0:T(8,128)(2,1)S(1)}, u32[]{:S(2)}, u32[]{:S(2)}) %collective-permute-start.6) | collective-permute-done | bytes 2097184 | tf_op jit(solution)/shard_map/ppermute | solution.py:398
  183.1 2.0 convert_add_fusion
  186.6 1.6 collective-permute-start.9
  188.2 11.1 %collective-permute-done.7 = bf16[2,1024,128]{2,1,0:T(8,128)(2,1)S(1)} collective-permute-done((bf16[2,1024,128]{2,1,0:T(8,128)(2,1)S(1)}, bf16[2,1024,128]{2,1,0:T(8,128)(2,1)S(1)}, u32[]{:S(2)}, u32[]{:S(2)}) %collective-permute-start.7) | collective-permute-done | bytes 524320 | tf_op jit(solution)/shard_map/ppermute | solution.py:398
  201.4 1.6 collective-permute-start.8
  203.0 4.9 %collective-permute-done.10 = bf16[1024,128]{1,0:T(8,128)(2,1)S(1)} collective-permute-done((bf16[1024,128]{1,0:T(8,128)(2,1)S(1)}, bf16[1024,128]{1,0:T(8,128)(2,1)S(1)}, u32[]{:S(2)}, u32[]{:S(2)}) %collective-permute-start.10) | collective-permute-done | bytes 262176 | tf_op jit(solution)/shard_map/ppermute | solution.py:398
  209.6 5.3 %collective-permute-done.11 = bf16[512,256]{1,0:T(8,128)(2,1)S(1)} collective-permute-done((bf16[512,256]{1,0:T(8,128)(2,1)S(1)}, bf16[512,256]{1,0:T(8,128)(2,1)S(1)}, u32[]{:S(2)}, u32[]{:S(2)}) %collective-permute-start.11) | collective-permute-done | bytes 262176 | tf_op jit(solution)/shard_map/ppermute | solution.py:398
  215.0 2.1 collective-permute-start.12
  217.1 5.2 %collective-permute-done.12 = bf16[256,256]{1,0:T(8,128)(2,1)S(1)} collective-permute-done((bf16[256,256]{1,0:T(8,128)(2,1)S(1)}, bf16[256,256]{1,0:T(8,128)(2,1)S(1)}, u32[]{:S(2)}, u32[]{:S(2)}) %collective-permute-start.12) | collective-permute-done | bytes 131104 | tf_op jit(solution)/shard_map/ppermute | solution.py:398
  224.5 1.6 collective-permute-start.15
  226.1 2.1 collective-permute-done.13
  230.6 2.6 %collective-permute-done.14 = bf16[2,256,128]{2,1,0:T(8,128)(2,1)S(1)} collective-permute-done((bf16[2,256,128]{2,1,0:T(8,128)(2,1)S(1)}, bf16[2,256,128]{2,1,0:T(8,128)(2,1)S(1)}, u32[]{:S(2)}, u32[]{:S(2)}) %collective-permute-start.14) | collective-permute-done | bytes 131104 | tf_op jit(solution)/shard_map/ppermute | solution.py:398
  234.5 1.9 collective-permute-done.17
  (61 shorter events, 20.9 us)
Async XLA Ops:
  40.9 15.3 %collective-permute-start = (f32[128,256]{1,0:T(8,128)}, f32[128,256]{1,0:T(8,128)S(1)}, u32[]{:S(2)}, u32[]{:S(2)}) collective-permute-start(f32[128,256]{1,0:T(8,128)} %get-tuple-element.17), channel_id=1, source_target_pairs={{0,1},{1,0},{2,3},{3,2},{4,5},{5,4},{6,7},{7,6},{8,9},{9,8},{10,11... | collective-permute-start | bytes 393224 | tf_op jit(solution)/shard_map/ppermute | solution.py:398
  44.0 13.2 %collective-permute-start.1 = (f32[128,256]{1,0:T(8,128)}, f32[128,256]{1,0:T(8,128)S(1)}, u32[]{:S(2)}, u32[]{:S(2)}) collective-permute-start(f32[128,256]{1,0:T(8,128)} %get-tuple-element.18), channel_id=1, source_target_pairs={{0,2},{1,3},{2,0},{3,1},{4,6},{5,7},{6,4},{7,5},{8,10},{9,11},{10,... | collective-permute-start | bytes 393224 | tf_op jit(solution)/shard_map/ppermute | solution.py:398
  46.6 10.5 %collective-permute-start.2 = (f32[128,256]{1,0:T(8,128)}, f32[128,256]{1,0:T(8,128)S(1)}, u32[]{:S(2)}, u32[]{:S(2)}) collective-permute-start(f32[128,256]{1,0:T(8,128)} %get-tuple-element.19), channel_id=1, source_target_pairs={{0,3},{1,2},{2,1},{3,0},{4,7},{5,6},{6,5},{7,4},{8,11},{9,10},{10,... | collective-permute-start | bytes 393224 | tf_op jit(solution)/shard_map/ppermute | solution.py:398
  54.3 0.7 copy-start
  56.2 1.0 copy-start.3
  57.2 0.7 copy-start.4
  57.2 0.7 copy-start.5
  59.8 6.1 %collective-permute-start.3 = (bf16[128,256]{1,0:T(8,128)(2,1)}, bf16[128,256]{1,0:T(8,128)(2,1)S(1)}, u32[]{:S(2)}, u32[]{:S(2)}) collective-permute-start(bf16[128,256]{1,0:T(8,128)(2,1)} %shard_map.88.rest_0_), channel_id=1, source_target_pairs={{0,1},{1,0},{2,3},{3,2},{4,5},{5,4},{6,7},{7,6},{8,9},{9,8},{10,11... | collective-permute-start | bytes 196616 | tf_op jit(solution)/shard_map/ppermute | solution.py:398
  61.7 6.7 %collective-permute-start.4 = (bf16[128,256]{1,0:T(8,128)(2,1)}, bf16[128,256]{1,0:T(8,128)(2,1)S(1)}, u32[]{:S(2)}, u32[]{:S(2)}) collective-permute-start(bf16[128,256]{1,0:T(8,128)(2,1)} %shard_map.88.rest_0_), channel_id=1, source_target_pairs={{0,2},{1,3},{2,0},{3,1},{4,6},{5,7},{6,4},{7,5},{8,10},{9,11},{10,... | collective-permute-start | bytes 196616 | tf_op jit(solution)/shard_map/ppermute | solution.py:398
  63.3 6.4 %collective-permute-start.5 = (bf16[128,256]{1,0:T(8,128)(2,1)}, bf16[128,256]{1,0:T(8,128)(2,1)S(1)}, u32[]{:S(2)}, u32[]{:S(2)}) collective-permute-start(bf16[128,256]{1,0:T(8,128)(2,1)} %shard_map.88.rest_0_), channel_id=1, source_target_pairs={{0,3},{1,2},{2,1},{3,0},{4,7},{5,6},{6,5},{7,4},{8,11},{9,10},{10,... | collective-permute-start | bytes 196616 | tf_op jit(solution)/shard_map/ppermute | solution.py:398
  65.9 3.8 %copy-start.6 = (bf16[128,256]{1,0:T(8,128)(2,1)}, bf16[128,256]{1,0:T(8,128)(2,1)S(1)}, u32[]{:S(2)}) copy-start(bf16[128,256]{1,0:T(8,128)(2,1)S(1)} %collective-permute-done.3.rest_1_) | copy-start | bytes 196612
  68.4 1.3 copy-start.7
  178.7 4.4 %collective-permute-start.6 = (bf16[4096,256]{1,0:T(8,128)(2,1)}, bf16[4096,256]{1,0:T(8,128)(2,1)S(1)}, u32[]{:S(2)}, u32[]{:S(2)}) collective-permute-start(bf16[4096,256]{1,0:T(8,128)(2,1)} %get-tuple-element.21), channel_id=1, source_target_pairs={{0,4},{4,0},{8,12},{12,8},{16,20},{20,16},{24,28},{28,24},{1,5},{5... | collective-permute-start | bytes 6291464 | tf_op jit(solution)/shard_map/ppermute | solution.py:398
  185.3 14.0 %collective-permute-start.7 = (bf16[2,1024,128]{2,1,0:T(8,128)(2,1)S(1)}, bf16[2,1024,128]{2,1,0:T(8,128)(2,1)S(1)}, u32[]{:S(2)}, u32[]{:S(2)}) collective-permute-start(bf16[2,1024,128]{2,1,0:T(8,128)(2,1)S(1)} %slice_bitcast_fusion.5), channel_id=1, source_target_pairs={{0,8},{4,12},{8,0},{12,4},{16,24},{20,28},{24,16},{28,20},{1,9},{5... | collective-permute-start | bytes 1572872 | tf_op jit(solution)/shard_map/ppermute | solution.py:398
  186.6 13.7 %collective-permute-start.9 = (bf16[2,1024,128]{2,1,0:T(8,128)(2,1)S(1)}, bf16[2,1024,128]{2,1,0:T(8,128)(2,1)S(1)}, u32[]{:S(2)}, u32[]{:S(2)}) collective-permute-start(bf16[2,1024,128]{2,1,0:T(8,128)(2,1)S(1)} %slice_bitcast_fusion.3), channel_id=1, source_target_pairs={{0,16},{4,20},{8,24},{12,28},{16,0},{20,4},{24,8},{28,12},{1,17},{... | collective-permute-start | bytes 1572872 | tf_op jit(solution)/shard_map/ppermute | solution.py:398
  200.6 7.3 %collective-permute-start.10 = (bf16[1024,128]{1,0:T(8,128)(2,1)S(1)}, bf16[1024,128]{1,0:T(8,128)(2,1)S(1)}, u32[]{:S(2)}, u32[]{:S(2)}) collective-permute-start(bf16[1024,128]{1,0:T(8,128)(2,1)S(1)} %fusion.8), channel_id=1, source_target_pairs={{0,8},{4,12},{8,0},{12,4},{16,24},{20,28},{24,16},{28,20},{1,9},{5... | collective-permute-start | bytes 786440 | tf_op jit(solution)/shard_map/ppermute | solution.py:398
  201.4 7.0 %collective-permute-start.8 = (bf16[1024,128]{1,0:T(8,128)(2,1)S(1)}, bf16[1024,128]{1,0:T(8,128)(2,1)S(1)}, u32[]{:S(2)}, u32[]{:S(2)}) collective-permute-start(bf16[1024,128]{1,0:T(8,128)(2,1)S(1)} %fusion.7), channel_id=1, source_target_pairs={{0,16},{4,20},{8,24},{12,28},{16,0},{20,4},{24,8},{28,12},{1,17},{... | collective-permute-start | bytes 786440 | tf_op jit(solution)/shard_map/ppermute | solution.py:398
  208.5 6.4 %collective-permute-start.11 = (bf16[512,256]{1,0:T(8,128)(2,1)S(1)}, bf16[512,256]{1,0:T(8,128)(2,1)S(1)}, u32[]{:S(2)}, u32[]{:S(2)}) collective-permute-start(bf16[512,256]{1,0:T(8,128)(2,1)S(1)} %fusion.4), channel_id=1, source_target_pairs={{0,1},{1,0},{2,3},{3,2},{4,5},{5,4},{6,7},{7,6},{8,9},{9,8},{10,11... | collective-permute-start | bytes 786440 | tf_op jit(solution)/shard_map/ppermute | solution.py:398
  215.0 7.3 %collective-permute-start.12 = (bf16[256,256]{1,0:T(8,128)(2,1)S(1)}, bf16[256,256]{1,0:T(8,128)(2,1)S(1)}, u32[]{:S(2)}, u32[]{:S(2)}) collective-permute-start(bf16[256,256]{1,0:T(8,128)(2,1)S(1)} %split.32), channel_id=1, source_target_pairs={{0,2},{1,3},{2,0},{3,1},{4,6},{5,7},{6,4},{7,5},{8,10},{9,11},{10,... | collective-permute-start | bytes 393224 | tf_op jit(solution)/shard_map/ppermute | solution.py:398
  223.1 5.0 %collective-permute-start.13 = (bf16[256,128]{1,0:T(8,128)(2,1)S(1)}, bf16[256,128]{1,0:T(8,128)(2,1)S(1)}, u32[]{:S(2)}, u32[]{:S(2)}) collective-permute-start(bf16[256,128]{1,0:T(8,128)(2,1)S(1)} %get-tuple-element.33), channel_id=1, source_target_pairs={{0,8},{4,12},{8,0},{12,4},{16,24},{20,28},{24,16},{28,20},{1,9},{5... | collective-permute-start | bytes 196616 | tf_op jit(solution)/shard_map/ppermute | solution.py:398
  224.5 4.8 %collective-permute-start.15 = (bf16[256,128]{1,0:T(8,128)(2,1)S(1)}, bf16[256,128]{1,0:T(8,128)(2,1)S(1)}, u32[]{:S(2)}, u32[]{:S(2)}) collective-permute-start(bf16[256,128]{1,0:T(8,128)(2,1)S(1)} %get-tuple-element.32), channel_id=1, source_target_pairs={{0,16},{4,20},{8,24},{12,28},{16,0},{20,4},{24,8},{28,12},{1,17},{... | collective-permute-start | bytes 196616 | tf_op jit(solution)/shard_map/ppermute | solution.py:398
  228.1 5.0 %collective-permute-start.14 = (bf16[2,256,128]{2,1,0:T(8,128)(2,1)S(1)}, bf16[2,256,128]{2,1,0:T(8,128)(2,1)S(1)}, u32[]{:S(2)}, u32[]{:S(2)}) collective-permute-start(bf16[2,256,128]{2,1,0:T(8,128)(2,1)S(1)} %maximum_select_fusion.3), channel_id=1, source_target_pairs={{0,16},{4,20},{8,24},{12,28},{16,0},{20,4},{24,8},{28,12},{1,17},{... | collective-permute-start | bytes 393224 | tf_op jit(solution)/shard_map/ppermute | solution.py:398
  229.3 5.0 %collective-permute-start.16 = (bf16[2,256,128]{2,1,0:T(8,128)(2,1)S(1)}, bf16[2,256,128]{2,1,0:T(8,128)(2,1)S(1)}, u32[]{:S(2)}, u32[]{:S(2)}) collective-permute-start(bf16[2,256,128]{2,1,0:T(8,128)(2,1)S(1)} %maximum_select_fusion.5), channel_id=1, source_target_pairs={{0,8},{4,12},{8,0},{12,4},{16,24},{20,28},{24,16},{28,20},{1,9},{5... | collective-permute-start | bytes 393224 | tf_op jit(solution)/shard_map/ppermute | solution.py:398
  234.4 2.0 collective-permute-start.17
  (3 other events, 1.8 us)

commit v3 on v2

--- a/solution.py
+++ b/solution.py
@@ -30,22 +30,32 @@
 
     perm = perm_ref[...]
 
-    def regroup(src_ref, dst_ref, scaled):
+    def regroup(src_ref, dst_ref, scaled, i):
+        at = pl.multiple_of(i * 16, 16)
+        tile = src_ref[pl.ds(at, 16)].reshape(16 * gb, width)
+        moved = jnp.dot(perm, tile, preferred_element_type=F32)
+        for g in range(gb):
+            part = moved[g * 16 : (g + 1) * 16]
+            if scaled:
+                part = part * noise_ref[step * gb + g]
+            dst_ref[pl.ds(at, 16), g * width : (g + 1) * width] = part.astype(BF16)
+
+    def tiles(i, carry):
+        regroup(r_ref, w_ref, True, i)
+        regroup(x_ref, flat_ref, False, i)
+        return carry
+
+    def more_tiles(src_ref, dst_ref, scaled):
         def body(i, carry):
-            at = pl.multiple_of(i * 16, 16)
-            tile = src_ref[pl.ds(at, 16)].reshape(16 * gb, width)
-            moved = jnp.dot(perm, tile, preferred_element_type=F32)
-            for g in range(gb):
-                part = moved[g * 16 : (g + 1) * 16]
-                if scaled:
-                    part = part * noise_ref[step * gb + g]
-                dst_ref[pl.ds(at, 16), g * width : (g + 1) * width] = part.astype(BF16)
+            regroup(src_ref, dst_ref, scaled, i)
             return carry
 
-        lax.fori_loop(0, src_ref.shape[0] // 16, body, 0, unroll=8)
-
-    regroup(r_ref, w_ref, True)
-    regroup(x_ref, flat_ref, False)
+        lax.fori_loop(both, src_ref.shape[0] // 16, body, 0)
+
+    both = min(particles, orients) // 16
+    lax.fori_loop(0, both, tiles, 0, unroll=8)
+    more_tiles(r_ref, w_ref, True)
+    more_tiles(x_ref, flat_ref, False)
     half = min(256, orients)
 
     def product(n, carry):
@@ -133,7 +143,9 @@
     )(*parts)
 
 
-def plan_kernel(place_ref, pos_ref, addr_ref, item_ref, hot_ref, count_ref, *, owners):
+def plan_kernel(
+    place_ref, rowf_ref, pos_ref, addr_ref, item_ref, meta_ref, hot_ref, count_ref, *, owners
+):
     _, gb, orients = place_ref.shape
     lanes = addr_ref.shape[2]
     owner = lax.broadcasted_iota(jnp.int32, (owners, 1), 0)
@@ -173,16 +185,33 @@
     owner_f = owner.astype(F32)
 
     slot = (lax.broadcasted_iota(jnp.int32, (1, lanes), 1) * 8).astype(F32)
+    eighth = lax.broadcasted_iota(jnp.int32, (meta_ref.shape[2], 1), 0).astype(F32)
+    lane_of = (lax.broadcasted_iota(jnp.int32, (OB, 1), 0) % 8).astype(F32)
     is_last = lax.broadcasted_iota(jnp.int32, (1, lanes), 1) == lanes - 1
     rows = gb * (orients + 7 * owners)
     for g in range(gb):
         low, size = base[:, g : g + 1], sizes[:, g : g + 1]
         hot = hot_ref[g * owners : (g + 1) * owners, :].astype(F32)
         rank = count_ref[g * owners : (g + 1) * owners, :] - 1.0 + low
-        pos_ref[0, g : g + 1, :] = jnp.sum(hot * rank, axis=0, keepdims=True).astype(jnp.int32)
+        pos = jnp.sum(hot * rank, axis=0, keepdims=True)
+        pos_ref[0, g : g + 1, :] = pos.astype(jnp.int32)
+        block = jnp.floor(pos * 0.125)
+        value = rowf_ref[0, g : g + 1, :]
+        coarse = value.astype(BF16).astype(F32)
+        here = lane_of == pos - 8.0 * block
+        spots = jnp.where(eighth == block, 1.0, 0.0).astype(BF16)
+        meta = jnp.zeros((meta_ref.shape[2], OB), F32)
+        for term in (coarse, value - coarse):
+            meta = meta + lax.dot_general(
+                spots,
+                jnp.where(here, term, 0.0).astype(BF16),
+                (((1,), (1,)), ((), ())),
+                preferred_element_type=F32,
+            )
+        meta_ref[0, g] = meta
         inside = (slot >= low) & (slot < low + size)
-        goal = jnp.where(inside, start + ahead[:, g : g + 1] - low + slot - rows, 0.0)
-        goal = jnp.sum(goal, axis=0, keepdims=True) + rows
+        goal = jnp.where(inside, start + ahead[:, g : g + 1] - low + slot - rows, 0.0) * 0.125
+        goal = jnp.sum(goal, axis=0, keepdims=True) + rows // 8
         used = jnp.sum(size, axis=0, keepdims=True)
         addr_ref[0, g : g + 1, :] = jnp.where(is_last, used, goal).astype(jnp.int32)
 
@@ -192,7 +221,7 @@
     done = (number - first) * RD
     pick = lambda value: jnp.sum(jnp.where(inside, value, 0.0), axis=0, keepdims=True)
     item_ref[0, 0:1, :] = pick(jnp.broadcast_to(owner_f, (owners, wide))).astype(jnp.int32)
-    item_ref[0, 1:2, :] = pick(start + done).astype(jnp.int32)
+    item_ref[0, 1:2, :] = pick((start + done) * 0.125).astype(jnp.int32)
     item_ref[0, 2:3, :] = pick(total - done).astype(jnp.int32)
     items = jnp.sum(jnp.broadcast_to(blocks, (owners, wide)), axis=0, keepdims=True)
     item_ref[0, 3:4, :] = items.astype(jnp.int32)
@@ -202,12 +231,21 @@
     return -(-value // step) * step
 
 
-def plan_call(place, owners):
+def sort_sizes(orients, owners):
+    slots = orients + 7 * owners
+    sure = orients + 144
+    blocks = up_to((sure + up_to(max(0, slots - sure), 128)) // 8, 8)
+    return slots, sure, blocks
+
+
+def plan_call(place, rowf, owners):
     steps, gb, orients = place.shape
-    slots = orients + 7 * owners
-    lanes = up_to(slots // 8 + 17, 128)
-    wide = up_to(owners + gb * slots // RD + 4, 128)
-    block = lambda *shape: pl.BlockSpec((1,) + shape, lambda i: (i, 0, 0))
+    slots, _, blocks = sort_sizes(orients, owners)
+    lanes = up_to(blocks + 1, 128)
+    wide = up_to(owners + gb * slots // RD + 8, 128)
+    block = lambda *shape: pl.BlockSpec(
+        (1,) + shape, lambda i, n=len(shape): (i,) + (0,) * n
+    )
     return pl.pallas_call(
         functools.partial(plan_kernel, owners=owners),
         grid=(steps,),
@@ -215,9 +253,10 @@
             jax.ShapeDtypeStruct((steps, gb, orients), jnp.int32),
             jax.ShapeDtypeStruct((steps, gb, lanes), jnp.int32),
             jax.ShapeDtypeStruct((steps, 4, wide), jnp.int32),
+            jax.ShapeDtypeStruct((steps, gb, blocks, OB), F32),
         ],
-        in_specs=[block(gb, orients)],
-        out_specs=[block(gb, orients), block(gb, lanes), block(4, wide)],
+        in_specs=[block(gb, orients)] * 2,
+        out_specs=[block(gb, orients), block(gb, lanes), block(4, wide), block(gb, blocks, OB)],
         scratch_shapes=[
             pltpu.VMEM((gb * owners, orients), BF16),
             pltpu.VMEM((gb * owners, orients), F32),
@@ -228,12 +267,12 @@
             bytes_accessed=8 * steps * gb * orients,
             transcendentals=0,
         ),
-    )(place)
-
-
-def insert_kernel(me_ref, addr_ref, item_ref, x_ref, pos_ref, rowf_ref, blk_ref, *rest):
+    )(place, rowf)
+
+
+def insert_kernel(me_ref, addr_ref, item_ref, x_ref, pos_ref, meta_ref, blk_ref, *rest):
     *post_refs, send_ref, keep_ref = rest[:-8]
-    post_t, spread_ref, slice_ref, buf_s, buf_t, volume, stage, sem = rest[-8:]
+    post_t, spread_ref, slice_ref, buf_s, buf_m, volume, stage, sem = rest[-8:]
     step = pl.program_id(0)
     count = x_ref.shape[0]
     orients = post_t.shape[0]
@@ -241,12 +280,13 @@
     width = x_ref.shape[1] // gb
     share = count // len(post_refs)
     lanes = addr_ref.shape[2]
+    unroll = 4 if gb % 4 == 0 else 1
 
     @pl.when(step == 0)
     def _():
         volume[...] = jnp.zeros_like(volume)
         buf_s[...] = jnp.zeros_like(buf_s)
-        buf_t[...] = jnp.zeros_like(buf_t)
+        buf_m[...] = jnp.zeros_like(buf_m)
         me = me_ref[0]
         for k, post_ref in enumerate(post_refs):
             at = pl.multiple_of((me ^ k) * share, share)
@@ -267,55 +307,66 @@
         slice_ref[:, at] = value.astype(BF16)
         return carry
 
-    lax.fori_loop(0, gb, one_slice, 0, unroll=2)
+    lax.fori_loop(0, gb, one_slice, 0, unroll=unroll)
+
+    def emit(g, base, size):
+        pos = pos_ref[0, pl.ds(g, 1), :]
+        piece = slice_ref[:, pl.ds(pl.multiple_of(g * width, width), width)]
+        slot = lax.broadcasted_iota(jnp.int32, (size, 1), 0) + base
+        order = jnp.where(slot == pos, 1.0, 0.0).astype(BF16)
+        rows = jnp.dot(order, piece, preferred_element_type=F32)
+        for i in range(size // 8):
+            at = addr_ref[0, g, base // 8 + i]
+            buf_s[pl.ds(pl.multiple_of(at * 8, 8), 8), :] = rows[8 * i : 8 * i + 8]
+            buf_m[pl.ds(at, 1), :] = meta_ref[0, g, pl.ds(base // 8 + i, 1), :]
+
+    slots, sure, _ = sort_sizes(orients, volume.shape[0] // RD)
+
+    def one_group(g, carry):
+        emit(g, 0, sure)
+        return carry
+
+    lax.fori_loop(0, gb, one_group, 0, unroll=unroll)
+
+    def rest_of_group(g, carry):
+        def more(e, c):
+            emit(g, sure + e * 128, 128)
+            return c
+
+        used = addr_ref[0, g, lanes - 1]
+        return lax.fori_loop(0, lax.div(jnp.maximum(used - sure, 0) + 127, 128), more, carry)
+
+    if slots > sure:
+        lax.fori_loop(0, gb, rest_of_group, 0)
 
     bins = lax.broadcasted_iota(jnp.int32, (RD, 1), 0).astype(F32)
-
-    def one_group(g, carry):
-        pos = pos_ref[0, pl.ds(g, 1), :]
-        tent = jnp.maximum(1.0 - jnp.abs(bins - rowf_ref[0, pl.ds(g, 1), :]), 0.0).astype(BF16)
-        piece = slice_ref[:, pl.ds(pl.multiple_of(g * width, width), width)]
-
-        def emit(base, size):
-            slot = lax.broadcasted_iota(jnp.int32, (size, 1), 0) + base
-            order = jnp.where(slot == pos, 1.0, 0.0).astype(BF16)
-            rows = jnp.dot(order, piece, preferred_element_type=F32)
-            weights = lax.dot_general(
-                order, tent, (((1,), (1,)), ((), ())), preferred_element_type=F32
-            )
-            for i in range(size // 8):
-                at = pl.multiple_of(addr_ref[0, g, base // 8 + i], 8)
-                buf_s[pl.ds(at, 8), :] = rows[8 * i : 8 * i + 8]
-                buf_t[pl.ds(at, 8), :] = weights[8 * i : 8 * i + 8]
-
-        sure = orients + 128
-        emit(0, sure)
-
-        def more(e, c):
-            emit(sure + e * 128, 128)
-            return c
-
-        used = addr_ref[0, g, lanes - 1]
-        lax.fori_loop(0, lax.div(jnp.maximum(used - sure, 0) + 127, 128), more, 0)
+    side = RD // 2
+    at_lane = lax.broadcasted_iota(jnp.int32, (side // 8, side), 1) // 8
+    own_lane = at_lane == lax.broadcasted_iota(jnp.int32, (side // 8, side), 0)
+    line = lax.broadcasted_iota(jnp.int32, (1, RD), 1)
+    together = 8
+
+    def some_items(q, carry):
+        for u in range(together):
+            j = q * together + u
+            owner, at, left = item_ref[0, 0, j], item_ref[0, 1, j], item_ref[0, 2, j]
+            places = [
+                jnp.sum(
+                    jnp.where(own_lane, buf_m[pl.ds(at + h * (side // 8), side // 8), :], 0.0),
+                    axis=0,
+                    keepdims=True,
+                )
+                for h in range(2)
+            ]
+            place = jnp.where(line < left, jnp.concatenate(places, axis=1), -9.0)
+            weights = jnp.maximum(1.0 - jnp.abs(bins - place), 0.0).astype(BF16)
+            values = buf_s[pl.ds(pl.multiple_of(at * 8, 8), RD), :].astype(BF16)
+            goal = pl.ds(pl.multiple_of(owner * RD, RD), RD)
+            volume[goal, :] += jnp.dot(weights, values, preferred_element_type=F32)
         return carry
 
-    lax.fori_loop(0, gb, one_group, 0)
-
-    line = lax.broadcasted_iota(jnp.int32, (RD, 1), 0)
-
-    def some_items(q, carry):
-        for u in range(4):
-            j = q * 4 + u
-            owner, at, left = item_ref[0, 0, j], item_ref[0, 1, j], item_ref[0, 2, j]
-            span = pl.ds(pl.multiple_of(at, 8), RD)
-            weights = jnp.where(line < left, buf_t[span, :], 0.0).T.astype(BF16)
-            goal = pl.ds(pl.multiple_of(owner * RD, RD), RD)
-            volume[goal, :] += jnp.dot(
-                weights, buf_s[span, :].astype(BF16), preferred_element_type=F32
-            )
-        return carry
-
-    lax.fori_loop(0, lax.div(item_ref[0, 3, 0] + 3, 4), some_items, 0)
+    count_items = lax.div(item_ref[0, 3, 0] + together - 1, together)
+    lax.fori_loop(0, count_items, some_items, 0)
 
     @pl.when(step == pl.num_programs(0) - 1)
     def _():
@@ -344,13 +395,13 @@
     best = 1
     for gb in range(1, groups + 1):
         rows = gb * (orients + 7 * owners) + RD + 8
-        need = rows * width * 8 + 4 * count * gb * width + 2 * orients * gb * width
+        need = rows * width * 4 + rows * OB // 2 + 4 * count * gb * width + 2 * orients * gb * width
         if groups % gb == 0 and need <= room:
             best = gb
     return best
 
 
-def insert_call(me, addr, items, flat, pos, rowf, blocks, posts, owners):
+def insert_call(me, addr, items, flat, pos, meta, blocks, posts, owners):
     count = flat.shape[0]
     steps, gb, orients = pos.shape
     width = flat.shape[1] // (steps * gb)
@@ -358,7 +409,7 @@
     share = posts[0].shape[0]
     rows = gb * (orients + 7 * owners) + RD + 8
     smem = pl.BlockSpec(memory_space=pltpu.SMEM)
-    block = lambda shape, **kw: pl.BlockSpec((1,) + shape[1:], lambda i: (i, 0, 0), **kw)
+    block = lambda shape, **kw: pl.BlockSpec((1,) + shape[1:], lambda i: (i,) + (0,) * (len(shape) - 1), **kw)
     return pl.pallas_call(
         insert_kernel,
         grid=(steps,),
@@ -369,7 +420,7 @@
             block(items.shape, memory_space=pltpu.SMEM),
             pl.BlockSpec((count, gb * width), lambda i: (0, i)),
             block(pos.shape),
-            block(rowf.shape),
+            block(meta.shape),
             pl.BlockSpec((count, 2), lambda i: (0, 0)),
         ]
         + [pl.BlockSpec((share, 2 * OB), lambda i: (0, 0))] * len(posts),
@@ -379,7 +430,7 @@
             pltpu.VMEM((count, orients), F32),
             pltpu.VMEM((orients, gb * width), BF16),
             pltpu.VMEM((rows, width), F32),
-            pltpu.VMEM((rows, RD), F32),
+            pltpu.VMEM((rows // 8, OB), F32),
             pltpu.VMEM((total, width), F32),
             pltpu.VMEM((2, 512, width), BF16),
             pltpu.SemaphoreType.DMA((2,)),
@@ -390,7 +441,7 @@
             bytes_accessed=2 * count * steps * gb * width,
             transcendentals=0,
         ),
-    )(me, addr, items, flat, pos, rowf, blocks, *posts)
+    )(me, addr, items, flat, pos, meta, blocks, *posts)
 
 
 def flip(value, axis, bit):
@@ -427,8 +478,8 @@
     for bit in slab_bits:
         place = place * 2 + jnp.where(slab_off & bit != 0, 1, 0)
     rowf = (take(row_index).astype(F32) + take(fraction)).reshape(table)
-    pos, addr, items = plan_call(place.reshape(table), devices)
-    send, keep = insert_call(slab_me, addr, items, flat, pos, rowf, blocks, posts, devices)
+    pos, addr, items, meta = plan_call(place.reshape(table), rowf, devices)
+    send, keep = insert_call(slab_me, addr, items, flat, pos, meta, blocks, posts, devices)
 
     def merge(kept, got):
         return kept.astype(F32) + got.astype(F32)

time: 238 us -> 218 us (0.916)
  Pallas kernels: 155 us -> 130 us
  waiting for transfers between devices: 44.8 us -> 47.9 us
    pallas_call x1, Pallas kernels: 108 us -> 82.6 us  [insert_call(): pl.pallas_call(insert_kernel, grid=(steps,), out_shape=[jax.ShapeDtypeStr...]
    pallas_call x1, Pallas kernels: 6.48 us -> 11 us  [plan_call(): pl.pallas_call(functools.partial(plan_kernel, owners=owners), grid=(steps...]
    pallas_call x1, Pallas kernels: 38 us -> 34.1 us  [score_call(): pl.pallas_call(score_kernel, grid=(groups // gb,), out_shape=[jax.ShapeDt...]
    ppermute x18, waiting for transfers between devices: 44.8 us -> 47.9 us  [flip(): return lax.ppermute(value, axis, [(i, i ^ bit) for i in range(size)])]
    unnamed x19 -> x21, local copies, waits for them, and re-layouts: 4.74 us -> 6.83 us
  transfers between devices with their start and end apart: 18 -> 18, of which waited for: 14 -> 13; matrix products, arithmetic and copies ran while one was open for 1% -> 1% of each run, Pallas kernels for 3% -> 5%
where the time goes in v3:
time: 218 us
  Pallas kernels  130 us (60%)
  waiting for transfers between devices  47.9 us (22%)
  starting transfers between devices  24.7 us (11%)
  local copies, waits for them, and re-layouts  8.17 us (4%)
  other arithmetic  6.52 us (3%)
    pallas_call x1, Pallas kernels, insert_call(): pl.pallas_call(insert_kernel, grid=(steps,), out_shape=[jax.ShapeDtypeStr...  82.6 us
    ppermute x18, waiting for transfers between devices, flip(): return lax.ppermute(value, axis, [(i, i ^ bit) for i in range(size)])  47.9 us
    pallas_call x1, Pallas kernels, score_call(): pl.pallas_call(score_kernel, grid=(groups // gb,), out_shape=[jax.ShapeDt...  34.1 us
    ppermute x18, starting transfers between devices, flip(): return lax.ppermute(value, axis, [(i, i ^ bit) for i in range(size)])  24.7 us
    pallas_call x1, Pallas kernels, plan_call(): pl.pallas_call(functools.partial(plan_kernel, owners=owners), grid=(steps...  11 us
    unnamed x21, local copies, waits for them, and re-layouts  6.83 us
  transfers between devices with their start and end apart: 18, of which 13 were waited for; matrix products, arithmetic and copies ran while one was open for 1% of the time, Pallas kernels for 5%

profile of v3, /device:TPU:0, one launch (start us, length us, event | category | flops | bytes accessed | tf_op | source)
XLA Modules:
  0.0 217.7 jit_solution(17233815633044514674)
XLA Ops:
  0.6 1.5 copy.15.blk_ref
  3.0 34.1 %shard_map.87 = (bf16[512,20480]{1,0:T(8,128)(2,1)}, f32[128,256]{1,0:T(8,128)}, f32[128,256]{1,0:T(8,128)}, f32[128,256]{1,0:T(8,128)}, f32[128,256]{1,0:T(8,128)}) custom-call(s32[1]{0:T(128)} %bitcast.me_ref, f32[80]{0:T(128)} %noise_ref.1, bf16[256,256]{1,0:T(8,128)(2,1)} %and_convert_fusion.perm_ref, bf16[512,80,256]{2,1,0:T(8,128)(2,1)} %x_ref.1, ...), custom_call_target="tpu_custom_call" | custom-call | flops 21474836480 | bytes 62914560 | tf_op jit(solution)/shard_map/pallas_call | solution.py:102
  37.1 3.1 %collective-permute-start = (f32[128,256]{1,0:T(8,128)}, f32[128,256]{1,0:T(8,128)S(1)}, u32[]{:S(2)}, u32[]{:S(2)}) collective-permute-start(f32[128,256]{1,0:T(8,128)} %get-tuple-element.19), channel_id=1, source_target_pairs={{0,1},{1,0},{2,3},{3,2},{4,5},{5,4},{6,7},{7,6},{8,9},{9,8},{10,11... | collective-permute-start | bytes 393224 | tf_op jit(solution)/shard_map/ppermute | solution.py:449
  40.2 2.6 %collective-permute-start.1 = (f32[128,256]{1,0:T(8,128)}, f32[128,256]{1,0:T(8,128)S(1)}, u32[]{:S(2)}, u32[]{:S(2)}) collective-permute-start(f32[128,256]{1,0:T(8,128)} %get-tuple-element.20), channel_id=1, source_target_pairs={{0,2},{1,3},{2,0},{3,1},{4,6},{5,7},{6,4},{7,5},{8,10},{9,11},{10,... | collective-permute-start | bytes 393224 | tf_op jit(solution)/shard_map/ppermute | solution.py:449
  45.4 7.9 %collective-permute-done.1.refs_2_ = f32[128,256]{1,0:T(8,128)S(1)} collective-permute-done((f32[128,256]{1,0:T(8,128)}, f32[128,256]{1,0:T(8,128)S(1)}, u32[]{:S(2)}, u32[]{:S(2)}) %collective-permute-start.1) | collective-permute-done | bytes 131104 | tf_op jit(solution)/shard_map/ppermute | solution.py:449
  54.0 1.9 shard_map.88.rest_0_
  55.9 1.9 collective-permute-start.3
  60.3 11.0 %shard_map.86 = (s32[4,20,512]{2,1,0:T(8,128)S(1)}, s32[4,20,128]{2,1,0:T(8,128)S(1)}, s32[4,4,128]{2,1,0:T(4,128)S(1)}, f32[4,20,104,128]{3,2,1,0:T(8,128)S(1)}) custom-call(s32[4,20,512]{2,1,0:T(8,128)S(1)} %reshape.248.place_ref, f32[4,20,512]{2,1,0:T(8,128)S(1)} %reshape.249.rowf_ref), custom_call_target="tpu_custom_call" | custom-call | flops 5368709120 | bytes 327680 | tf_op jit(solution)/shard_map/pallas_call | solution.py:249
  71.3 2.0 copy-done
  75.9 82.6 %shard_map.89 = (bf16[4096,256]{1,0:T(8,128)(2,1)}, bf16[4096,256]{1,0:T(8,128)(2,1)}) custom-call(s32[1]{0:T(128)} %bitcast.me_ref, s32[4,20,128]{2,1,0:T(8,128)} %copy-done.2, s32[4,4,128]{2,1,0:T(4,128)} %copy-done.3, bf16[512,20480]{1,0:T(8,128)(2,1)} %get-tuple-element.15.x_ref, s32[4,20,512]{2,1,0:T(8,128)} %copy-done.1, f32[4,20,104,128]{3,2,1,0:T(8,128)} %copy-done, ...), custom_call_target="tpu_custom_call" | custom-call | flops 42949672960 | bytes 20971520 | tf_op jit(solution)/shard_map/pallas_call | solution.py:413
  158.6 4.4 %collective-permute-done.6 = bf16[4096,256]{1,0:T(8,128)(2,1)S(1)} collective-permute-done((bf16[4096,256]{1,0:T(8,128)(2,1)}, bf16[4096,256]{1,0:T(8,128)(2,1)S(1)}, u32[]{:S(2)}, u32[]{:S(2)}) %collective-permute-start.6) | collective-permute-done | bytes 2097184 | tf_op jit(solution)/shard_map/ppermute | solution.py:449
  163.0 2.0 convert_add_fusion
  165.2 1.5 collective-permute-start.7
  166.7 1.6 collective-permute-start.9
  168.3 10.9 %collective-permute-done.7 = bf16[2,1024,128]{2,1,0:T(8,128)(2,1)S(1)} collective-permute-done((bf16[2,1024,128]{2,1,0:T(8,128)(2,1)S(1)}, bf16[2,1024,128]{2,1,0:T(8,128)(2,1)S(1)}, u32[]{:S(2)}, u32[]{:S(2)}) %collective-permute-start.7) | collective-permute-done | bytes 524320 | tf_op jit(solution)/shard_map/ppermute | solution.py:449
  181.3 1.6 collective-permute-start.8
  182.9 5.0 %collective-permute-done.10 = bf16[1024,128]{1,0:T(8,128)(2,1)S(1)} collective-permute-done((bf16[1024,128]{1,0:T(8,128)(2,1)S(1)}, bf16[1024,128]{1,0:T(8,128)(2,1)S(1)}, u32[]{:S(2)}, u32[]{:S(2)}) %collective-permute-start.10) | collective-permute-done | bytes 262176 | tf_op jit(solution)/shard_map/ppermute | solution.py:449
  189.3 5.5 %collective-permute-done.11 = bf16[512,256]{1,0:T(8,128)(2,1)S(1)} collective-permute-done((bf16[512,256]{1,0:T(8,128)(2,1)S(1)}, bf16[512,256]{1,0:T(8,128)(2,1)S(1)}, u32[]{:S(2)}, u32[]{:S(2)}) %collective-permute-start.11) | collective-permute-done | bytes 262176 | tf_op jit(solution)/shard_map/ppermute | solution.py:449
  194.9 2.5 %collective-permute-start.12 = (bf16[256,256]{1,0:T(8,128)(2,1)S(1)}, bf16[256,256]{1,0:T(8,128)(2,1)S(1)}, u32[]{:S(2)}, u32[]{:S(2)}) collective-permute-start(bf16[256,256]{1,0:T(8,128)(2,1)S(1)} %split.32), channel_id=1, source_target_pairs={{0,2},{1,3},{2,0},{3,1},{4,6},{5,7},{6,4},{7,5},{8,10},{9,11},{10,... | collective-permute-start | bytes 393224 | tf_op jit(solution)/shard_map/ppermute | solution.py:449
  197.5 4.8 %collective-permute-done.12 = bf16[256,256]{1,0:T(8,128)(2,1)S(1)} collective-permute-done((bf16[256,256]{1,0:T(8,128)(2,1)S(1)}, bf16[256,256]{1,0:T(8,128)(2,1)S(1)}, u32[]{:S(2)}, u32[]{:S(2)}) %collective-permute-start.12) | collective-permute-done | bytes 131104 | tf_op jit(solution)/shard_map/ppermute | solution.py:449
  204.5 1.6 collective-permute-start.15
  206.2 1.9 collective-permute-done.13
  210.6 2.4 %collective-permute-done.14 = bf16[2,256,128]{2,1,0:T(8,128)(2,1)S(1)} collective-permute-done((bf16[2,256,128]{2,1,0:T(8,128)(2,1)S(1)}, bf16[2,256,128]{2,1,0:T(8,128)(2,1)S(1)}, u32[]{:S(2)}, u32[]{:S(2)}) %collective-permute-start.14) | collective-permute-done | bytes 131104 | tf_op jit(solution)/shard_map/ppermute | solution.py:449
  214.6 1.9 collective-permute-done.17
  (65 shorter events, 20.5 us)
Async XLA Ops:
  37.1 8.3 %collective-permute-start = (f32[128,256]{1,0:T(8,128)}, f32[128,256]{1,0:T(8,128)S(1)}, u32[]{:S(2)}, u32[]{:S(2)}) collective-permute-start(f32[128,256]{1,0:T(8,128)} %get-tuple-element.19), channel_id=1, source_target_pairs={{0,1},{1,0},{2,3},{3,2},{4,5},{5,4},{6,7},{7,6},{8,9},{9,8},{10,11... | collective-permute-start | bytes 393224 | tf_op jit(solution)/shard_map/ppermute | solution.py:449
  40.2 13.1 %collective-permute-start.1 = (f32[128,256]{1,0:T(8,128)}, f32[128,256]{1,0:T(8,128)S(1)}, u32[]{:S(2)}, u32[]{:S(2)}) collective-permute-start(f32[128,256]{1,0:T(8,128)} %get-tuple-element.20), channel_id=1, source_target_pairs={{0,2},{1,3},{2,0},{3,1},{4,6},{5,7},{6,4},{7,5},{8,10},{9,11},{10,... | collective-permute-start | bytes 393224 | tf_op jit(solution)/shard_map/ppermute | solution.py:449
  42.8 10.6 %collective-permute-start.2 = (f32[128,256]{1,0:T(8,128)}, f32[128,256]{1,0:T(8,128)S(1)}, u32[]{:S(2)}, u32[]{:S(2)}) collective-permute-start(f32[128,256]{1,0:T(8,128)} %get-tuple-element.21), channel_id=1, source_target_pairs={{0,3},{1,2},{2,1},{3,0},{4,7},{5,6},{6,5},{7,4},{8,11},{9,10},{10,... | collective-permute-start | bytes 393224 | tf_op jit(solution)/shard_map/ppermute | solution.py:449
  45.4 7.9 %copy-start.4 = (f32[128,256]{1,0:T(8,128)}, f32[128,256]{1,0:T(8,128)S(1)}, u32[]{:S(2)}) copy-start(f32[128,256]{1,0:T(8,128)S(1)} %collective-permute-done.refs_1_) | copy-start | bytes 393220
  53.3 0.6 copy-start.5
  53.3 0.7 copy-start.6
  55.9 19.3 %collective-permute-start.3 = (bf16[128,256]{1,0:T(8,128)(2,1)}, bf16[128,256]{1,0:T(8,128)(2,1)S(1)}, u32[]{:S(2)}, u32[]{:S(2)}) collective-permute-start(bf16[128,256]{1,0:T(8,128)(2,1)} %shard_map.88.rest_0_), channel_id=1, source_target_pairs={{0,1},{1,0},{2,3},{3,2},{4,5},{5,4},{6,7},{7,6},{8,9},{9,8},{10,11... | collective-permute-start | bytes 196616 | tf_op jit(solution)/shard_map/ppermute | solution.py:449
  57.8 17.4 %collective-permute-start.4 = (bf16[128,256]{1,0:T(8,128)(2,1)}, bf16[128,256]{1,0:T(8,128)(2,1)S(1)}, u32[]{:S(2)}, u32[]{:S(2)}) collective-permute-start(bf16[128,256]{1,0:T(8,128)(2,1)} %shard_map.88.rest_0_), channel_id=1, source_target_pairs={{0,2},{1,3},{2,0},{3,1},{4,6},{5,7},{6,4},{7,5},{8,10},{9,11},{10,... | collective-permute-start | bytes 196616 | tf_op jit(solution)/shard_map/ppermute | solution.py:449
  58.9 16.4 %collective-permute-start.5 = (bf16[128,256]{1,0:T(8,128)(2,1)}, bf16[128,256]{1,0:T(8,128)(2,1)S(1)}, u32[]{:S(2)}, u32[]{:S(2)}) collective-permute-start(bf16[128,256]{1,0:T(8,128)(2,1)} %shard_map.88.rest_0_), channel_id=1, source_target_pairs={{0,3},{1,2},{2,1},{3,0},{4,7},{5,6},{6,5},{7,4},{8,11},{9,10},{10,... | collective-permute-start | bytes 196616 | tf_op jit(solution)/shard_map/ppermute | solution.py:449
  71.3 2.1 copy-start
  73.3 0.7 copy-start.1
  75.3 0.7 copy-start.9
  158.6 4.4 %collective-permute-start.6 = (bf16[4096,256]{1,0:T(8,128)(2,1)}, bf16[4096,256]{1,0:T(8,128)(2,1)S(1)}, u32[]{:S(2)}, u32[]{:S(2)}) collective-permute-start(bf16[4096,256]{1,0:T(8,128)(2,1)} %get-tuple-element.23), channel_id=1, source_target_pairs={{0,4},{4,0},{8,12},{12,8},{16,20},{20,16},{24,28},{28,24},{1,5},{5... | collective-permute-start | bytes 6291464 | tf_op jit(solution)/shard_map/ppermute | solution.py:449
  165.2 14.0 %collective-permute-start.7 = (bf16[2,1024,128]{2,1,0:T(8,128)(2,1)S(1)}, bf16[2,1024,128]{2,1,0:T(8,128)(2,1)S(1)}, u32[]{:S(2)}, u32[]{:S(2)}) collective-permute-start(bf16[2,1024,128]{2,1,0:T(8,128)(2,1)S(1)} %slice_bitcast_fusion.5), channel_id=1, source_target_pairs={{0,8},{4,12},{8,0},{12,4},{16,24},{20,28},{24,16},{28,20},{1,9},{5... | collective-permute-start | bytes 1572872 | tf_op jit(solution)/shard_map/ppermute | solution.py:449
  166.7 13.7 %collective-permute-start.9 = (bf16[2,1024,128]{2,1,0:T(8,128)(2,1)S(1)}, bf16[2,1024,128]{2,1,0:T(8,128)(2,1)S(1)}, u32[]{:S(2)}, u32[]{:S(2)}) collective-permute-start(bf16[2,1024,128]{2,1,0:T(8,128)(2,1)S(1)} %slice_bitcast_fusion.3), channel_id=1, source_target_pairs={{0,16},{4,20},{8,24},{12,28},{16,0},{20,4},{24,8},{28,12},{1,17},{... | collective-permute-start | bytes 1572872 | tf_op jit(solution)/shard_map/ppermute | solution.py:449
  180.6 7.3 %collective-permute-start.10 = (bf16[1024,128]{1,0:T(8,128)(2,1)S(1)}, bf16[1024,128]{1,0:T(8,128)(2,1)S(1)}, u32[]{:S(2)}, u32[]{:S(2)}) collective-permute-start(bf16[1024,128]{1,0:T(8,128)(2,1)S(1)} %fusion.8), channel_id=1, source_target_pairs={{0,8},{4,12},{8,0},{12,4},{16,24},{20,28},{24,16},{28,20},{1,9},{5... | collective-permute-start | bytes 786440 | tf_op jit(solution)/shard_map/ppermute | solution.py:449
  181.3 7.0 %collective-permute-start.8 = (bf16[1024,128]{1,0:T(8,128)(2,1)S(1)}, bf16[1024,128]{1,0:T(8,128)(2,1)S(1)}, u32[]{:S(2)}, u32[]{:S(2)}) collective-permute-start(bf16[1024,128]{1,0:T(8,128)(2,1)S(1)} %fusion.7), channel_id=1, source_target_pairs={{0,16},{4,20},{8,24},{12,28},{16,0},{20,4},{24,8},{28,12},{1,17},{... | collective-permute-start | bytes 786440 | tf_op jit(solution)/shard_map/ppermute | solution.py:449
  188.4 6.4 %collective-permute-start.11 = (bf16[512,256]{1,0:T(8,128)(2,1)S(1)}, bf16[512,256]{1,0:T(8,128)(2,1)S(1)}, u32[]{:S(2)}, u32[]{:S(2)}) collective-permute-start(bf16[512,256]{1,0:T(8,128)(2,1)S(1)} %fusion.4), channel_id=1, source_target_pairs={{0,1},{1,0},{2,3},{3,2},{4,5},{5,4},{6,7},{7,6},{8,9},{9,8},{10,11... | collective-permute-start | bytes 786440 | tf_op jit(solution)/shard_map/ppermute | solution.py:449
  194.9 7.3 %collective-permute-start.12 = (bf16[256,256]{1,0:T(8,128)(2,1)S(1)}, bf16[256,256]{1,0:T(8,128)(2,1)S(1)}, u32[]{:S(2)}, u32[]{:S(2)}) collective-permute-start(bf16[256,256]{1,0:T(8,128)(2,1)S(1)} %split.32), channel_id=1, source_target_pairs={{0,2},{1,3},{2,0},{3,1},{4,6},{5,7},{6,4},{7,5},{8,10},{9,11},{10,... | collective-permute-start | bytes 393224 | tf_op jit(solution)/shard_map/ppermute | solution.py:449
  203.1 5.0 %collective-permute-start.13 = (bf16[256,128]{1,0:T(8,128)(2,1)S(1)}, bf16[256,128]{1,0:T(8,128)(2,1)S(1)}, u32[]{:S(2)}, u32[]{:S(2)}) collective-permute-start(bf16[256,128]{1,0:T(8,128)(2,1)S(1)} %get-tuple-element.35), channel_id=1, source_target_pairs={{0,8},{4,12},{8,0},{12,4},{16,24},{20,28},{24,16},{28,20},{1,9},{5... | collective-permute-start | bytes 196616 | tf_op jit(solution)/shard_map/ppermute | solution.py:449
  204.5 4.8 %collective-permute-start.15 = (bf16[256,128]{1,0:T(8,128)(2,1)S(1)}, bf16[256,128]{1,0:T(8,128)(2,1)S(1)}, u32[]{:S(2)}, u32[]{:S(2)}) collective-permute-start(bf16[256,128]{1,0:T(8,128)(2,1)S(1)} %get-tuple-element.34), channel_id=1, source_target_pairs={{0,16},{4,20},{8,24},{12,28},{16,0},{20,4},{24,8},{28,12},{1,17},{... | collective-permute-start | bytes 196616 | tf_op jit(solution)/shard_map/ppermute | solution.py:449
  208.0 5.0 %collective-permute-start.14 = (bf16[2,256,128]{2,1,0:T(8,128)(2,1)S(1)}, bf16[2,256,128]{2,1,0:T(8,128)(2,1)S(1)}, u32[]{:S(2)}, u32[]{:S(2)}) collective-permute-start(bf16[2,256,128]{2,1,0:T(8,128)(2,1)S(1)} %maximum_select_fusion.3), channel_id=1, source_target_pairs={{0,16},{4,20},{8,24},{12,28},{16,0},{20,4},{24,8},{28,12},{1,17},{... | collective-permute-start | bytes 393224 | tf_op jit(solution)/shard_map/ppermute | solution.py:449
  209.4 5.0 %collective-permute-start.16 = (bf16[2,256,128]{2,1,0:T(8,128)(2,1)S(1)}, bf16[2,256,128]{2,1,0:T(8,128)(2,1)S(1)}, u32[]{:S(2)}, u32[]{:S(2)}) collective-permute-start(bf16[2,256,128]{2,1,0:T(8,128)(2,1)S(1)} %maximum_select_fusion.5), channel_id=1, source_target_pairs={{0,8},{4,12},{8,0},{12,4},{16,24},{20,28},{24,16},{28,20},{1,9},{5... | collective-permute-start | bytes 393224 | tf_op jit(solution)/shard_map/ppermute | solution.py:449
  214.5 2.0 collective-permute-start.17
  (4 other events, 2.5 us)

commit v4 on v3

--- a/solution.py
+++ b/solution.py
@@ -18,73 +18,76 @@
     return 16 if groups % 16 == 0 else 8
 
 
-def score_kernel(me_ref, noise_ref, perm_ref, x_ref, r_ref, blk_ref, flat_ref, *rest):
-    *out_refs, w_ref, acc_ref = rest
+def spread_columns(blk_ref, cols_ref):
+    count = blk_ref.shape[1]
+    for j in range(2):
+        for at in range(0, count, OB):
+            line = blk_ref[j : j + 1, at : at + OB].astype(F32)
+            cols_ref[j, at : at + OB, :] = jnp.broadcast_to(line, (OB, OB)).T
+
+
+def score_kernel(me_ref, noise_ref, x_ref, r_ref, blk_ref, flat_ref, *rest):
+    *out_refs, w_ref, acc_ref, perm_ref, cols_ref = rest
     step = pl.program_id(0)
     particles, gb, width = x_ref.shape
     orients = r_ref.shape[0]
+    side = 16 * gb
 
     @pl.when(step == 0)
     def _():
+        row = lax.broadcasted_iota(jnp.int32, (side, side), 0)
+        col = lax.broadcasted_iota(jnp.int32, (side, side), 1)
+        same = ((row // 16) == (col % gb)) & ((row % 16) == (col // gb))
+        perm_ref[...] = jnp.where(same, 1.0, 0.0).astype(BF16)
         acc_ref[...] = jnp.zeros_like(acc_ref)
+        spread_columns(blk_ref, cols_ref)
 
     perm = perm_ref[...]
 
-    def regroup(src_ref, dst_ref, scaled, i):
-        at = pl.multiple_of(i * 16, 16)
-        tile = src_ref[pl.ds(at, 16)].reshape(16 * gb, width)
-        moved = jnp.dot(perm, tile, preferred_element_type=F32)
+    def regroup(src_ref, dst_ref, scaled, first, number):
+        at = pl.multiple_of(first * 16, 16)
+        tile = src_ref[pl.ds(at, 16 * number)].reshape(number, side, width)
+        wide = jnp.concatenate([tile[t] for t in range(number)], axis=1)
+        moved = jnp.dot(perm, wide, preferred_element_type=F32)
         for g in range(gb):
-            part = moved[g * 16 : (g + 1) * 16]
-            if scaled:
-                part = part * noise_ref[step * gb + g]
-            dst_ref[pl.ds(at, 16), g * width : (g + 1) * width] = part.astype(BF16)
+            for t in range(number):
+                part = moved[g * 16 : (g + 1) * 16, t * width : (t + 1) * width]
+                if scaled:
+                    part = part * noise_ref[step * gb + g]
+                dst_ref[pl.ds(at + 16 * t, 16), g * width : (g + 1) * width] = part.astype(BF16)
 
     def tiles(i, carry):
-        regroup(r_ref, w_ref, True, i)
-        regroup(x_ref, flat_ref, False, i)
+        regroup(r_ref, w_ref, True, i * 4, 4)
+        regroup(x_ref, flat_ref, False, i * 4, 4)
         return carry
 
     def more_tiles(src_ref, dst_ref, scaled):
         def body(i, carry):
-            regroup(src_ref, dst_ref, scaled, i)
+            regroup(src_ref, dst_ref, scaled, i, 1)
             return carry
 
-        lax.fori_loop(both, src_ref.shape[0] // 16, body, 0)
-
-    both = min(particles, orients) // 16
-    lax.fori_loop(0, both, tiles, 0, unroll=8)
+        lax.fori_loop(both * 4, src_ref.shape[0] // 16, body, 0)
+
+    both = min(particles, orients) // 64
+    lax.fori_loop(0, both, tiles, 0, unroll=2)
     more_tiles(r_ref, w_ref, True)
     more_tiles(x_ref, flat_ref, False)
-    half = min(256, orients)
-
-    def product(n, carry):
-        at = pl.multiple_of(n * half, half)
-        acc_ref[n] += lax.dot_general(
-            flat_ref[...],
-            w_ref[pl.ds(at, half), :],
-            (((1,), (1,)), ((), ())),
-            preferred_element_type=F32,
-        )
-        return carry
-
-    lax.fori_loop(0, orients // half, product, 0)
+    acc_ref[...] += lax.dot_general(
+        flat_ref[...], w_ref[...], (((1,), (1,)), ((), ())), preferred_element_type=F32
+    )
 
     @pl.when(step == pl.num_programs(0) - 1)
     def _():
         me = me_ref[0]
         share = particles // len(out_refs)
-        per = half // OB
         for k, out_ref in enumerate(out_refs):
             at = pl.multiple_of((me ^ k) * share, share)
             for j in range(2):
-                wanted = blk_ref[pl.ds(at, share), j : j + 1]
+                wanted = cols_ref[j, pl.ds(at, share), :]
                 chosen = jnp.zeros((share, OB), F32)
                 for b in range(orients // OB):
-                    lane = (b % per) * OB
-                    chosen = jnp.where(
-                        wanted == b, acc_ref[b // per, pl.ds(at, share), lane : lane + OB], chosen
-                    )
+                    value = acc_ref[pl.ds(at, share), b * OB : (b + 1) * OB]
+                    chosen = jnp.where(wanted == b, value, chosen)
                 out_ref[:, j * OB : (j + 1) * OB] = chosen
 
 
@@ -93,11 +96,7 @@
     orients = references.shape[0]
     gb = group_block(groups)
     side = 16 * gb
-    row = jnp.arange(side, dtype=jnp.int32)[:, None]
-    col = jnp.arange(side, dtype=jnp.int32)[None, :]
-    perm = ((row // 16 == col % gb) & (row % 16 == col // gb)).astype(BF16)
     share = count // slab_size
-    half = min(256, orients)
     smem = pl.BlockSpec(memory_space=pltpu.SMEM)
     return pl.pallas_call(
         score_kernel,
@@ -107,16 +106,17 @@
         in_specs=[
             smem,
             smem,
-            pl.BlockSpec((side, side), lambda i: (0, 0)),
             pl.BlockSpec((count, gb, width), lambda i: (0, i, 0)),
             pl.BlockSpec((orients, gb, width), lambda i: (0, i, 0)),
-            pl.BlockSpec((count, 2), lambda i: (0, 0)),
+            pl.BlockSpec((2, count), lambda i: (0, 0)),
         ],
         out_specs=[pl.BlockSpec((count, gb * width), lambda i: (0, i))]
         + [pl.BlockSpec((share, 2 * OB), lambda i: (0, 0))] * slab_size,
         scratch_shapes=[
             pltpu.VMEM((orients, gb * width), BF16),
-            pltpu.VMEM((orients // half, count, half), F32),
+            pltpu.VMEM((count, orients), F32),
+            pltpu.VMEM((side, side), BF16),
+            pltpu.VMEM((2, count, OB), F32),
         ],
         compiler_params=pltpu.CompilerParams(vmem_limit_bytes=56 * MB),
         cost_estimate=pl.CostEstimate(
@@ -124,7 +124,7 @@
             bytes_accessed=6 * count * groups * width,
             transcendentals=0,
         ),
-    )(me, inv_noise, perm, particles, references, blocks)
+    )(me, inv_noise, particles, references, blocks)
 
 
 def softmax_kernel(*refs):
@@ -139,7 +139,9 @@
 
 def softmax_call(parts):
     return pl.pallas_call(
-        softmax_kernel, out_shape=jax.ShapeDtypeStruct(parts[0].shape, BF16)
+        softmax_kernel,
+        out_shape=jax.ShapeDtypeStruct(parts[0].shape, BF16),
+        compiler_params=pltpu.CompilerParams(vmem_limit_bytes=8 * MB),
     )(*parts)
 
 
@@ -261,7 +263,7 @@
             pltpu.VMEM((gb * owners, orients), BF16),
             pltpu.VMEM((gb * owners, orients), F32),
         ],
-        compiler_params=pltpu.CompilerParams(vmem_limit_bytes=40 * MB),
+        compiler_params=pltpu.CompilerParams(vmem_limit_bytes=60 * MB),
         cost_estimate=pl.CostEstimate(
             flops=8 * steps * gb * owners * orients * orients,
             bytes_accessed=8 * steps * gb * orients,
@@ -271,8 +273,8 @@
 
 
 def insert_kernel(me_ref, addr_ref, item_ref, x_ref, pos_ref, meta_ref, blk_ref, *rest):
-    *post_refs, send_ref, keep_ref = rest[:-8]
-    post_t, spread_ref, slice_ref, buf_s, buf_m, volume, stage, sem = rest[-8:]
+    *post_refs, send_ref, keep_ref = rest[:-9]
+    post_t, spread_ref, cols_ref, slice_ref, buf_s, buf_m, volume, stage, sem = rest[-9:]
     step = pl.program_id(0)
     count = x_ref.shape[0]
     orients = post_t.shape[0]
@@ -288,11 +290,12 @@
         buf_s[...] = jnp.zeros_like(buf_s)
         buf_m[...] = jnp.zeros_like(buf_m)
         me = me_ref[0]
+        spread_columns(blk_ref, cols_ref)
         for k, post_ref in enumerate(post_refs):
             at = pl.multiple_of((me ^ k) * share, share)
             post = post_ref[...].astype(F32)
-            first = blk_ref[pl.ds(at, share), 0:1]
-            second = blk_ref[pl.ds(at, share), 1:2]
+            first = cols_ref[0, pl.ds(at, share), :]
+            second = cols_ref[1, pl.ds(at, share), :]
             for b in range(orients // OB):
                 spread = jnp.where(
                     first == b, post[:, :OB], jnp.where(second == b, post[:, OB:], 0.0)
@@ -301,19 +304,27 @@
         for b in range(orients // OB):
             post_t[b * OB : (b + 1) * OB] = spread_ref[:, b * OB : (b + 1) * OB].T.astype(BF16)
 
-    def one_slice(g, carry):
-        at = pl.ds(pl.multiple_of(g * width, width), width)
+    def some_slices(q, carry):
+        span = unroll * width
+        at = pl.ds(pl.multiple_of(q * span, span), span)
         value = jnp.dot(post_t[...], x_ref[:, at], preferred_element_type=F32)
         slice_ref[:, at] = value.astype(BF16)
         return carry
 
-    lax.fori_loop(0, gb, one_slice, 0, unroll=unroll)
+    lax.fori_loop(0, gb // unroll, some_slices, 0)
+
+    one, none = jnp.bfloat16(1.0), jnp.bfloat16(0.0)
 
     def emit(g, base, size):
         pos = pos_ref[0, pl.ds(g, 1), :]
         piece = slice_ref[:, pl.ds(pl.multiple_of(g * width, width), width)]
-        slot = lax.broadcasted_iota(jnp.int32, (size, 1), 0) + base
-        order = jnp.where(slot == pos, 1.0, 0.0).astype(BF16)
+        parts = []
+        for at in range(0, size, 128):
+            high = min(128, size - at)
+            slot = lax.broadcasted_iota(jnp.int32, (high, orients), 0).astype(F32).astype(BF16)
+            near = jnp.clip(pos - (base + at), -1, 128).astype(F32).astype(BF16)
+            parts.append(jnp.where(slot == near, one, none))
+        order = jnp.concatenate(parts, axis=0)
         rows = jnp.dot(order, piece, preferred_element_type=F32)
         for i in range(size // 8):
             at = addr_ref[0, g, base // 8 + i]
@@ -339,7 +350,7 @@
     if slots > sure:
         lax.fori_loop(0, gb, rest_of_group, 0)
 
-    bins = lax.broadcasted_iota(jnp.int32, (RD, 1), 0).astype(F32)
+    bins = lax.broadcasted_iota(jnp.int32, (RD, RD), 0).astype(F32).astype(BF16)
     side = RD // 2
     at_lane = lax.broadcasted_iota(jnp.int32, (side // 8, side), 1) // 8
     own_lane = at_lane == lax.broadcasted_iota(jnp.int32, (side // 8, side), 0)
@@ -359,7 +370,9 @@
                 for h in range(2)
             ]
             place = jnp.where(line < left, jnp.concatenate(places, axis=1), -9.0)
-            weights = jnp.maximum(1.0 - jnp.abs(bins - place), 0.0).astype(BF16)
+            whole = jnp.floor(place)
+            apart = (bins - whole.astype(BF16)) - (place - whole).astype(BF16)
+            weights = jnp.maximum(one - jnp.abs(apart), none)
             values = buf_s[pl.ds(pl.multiple_of(at * 8, 8), RD), :].astype(BF16)
             goal = pl.ds(pl.multiple_of(owner * RD, RD), RD)
             volume[goal, :] += jnp.dot(weights, values, preferred_element_type=F32)
@@ -421,13 +434,14 @@
             pl.BlockSpec((count, gb * width), lambda i: (0, i)),
             block(pos.shape),
             block(meta.shape),
-            pl.BlockSpec((count, 2), lambda i: (0, 0)),
+            pl.BlockSpec((2, count), lambda i: (0, 0)),
         ]
         + [pl.BlockSpec((share, 2 * OB), lambda i: (0, 0))] * len(posts),
         out_specs=[pl.BlockSpec(memory_space=pl.ANY)] * 2,
         scratch_shapes=[
             pltpu.VMEM((orients, count), BF16),
             pltpu.VMEM((count, orients), F32),
+            pltpu.VMEM((2, count, OB), F32),
             pltpu.VMEM((orients, gb * width), BF16),
             pltpu.VMEM((rows, width), F32),
             pltpu.VMEM((rows // 8, OB), F32),
@@ -461,11 +475,8 @@
     dom_bits = [1 << i for i in range((dom_size - 1).bit_length())]
     slab_bits = [1 << i for i in range((slab_size - 1).bit_length())]
 
+    blocks = blocks.T
     flat, *scores = score_call(slab_me, inv_noise, particles, references, blocks, slab_size)
-    parts = [scores[0]] + [flip(scores[k], "slab", k) for k in range(1, slab_size)]
-    post = softmax_call(parts)
-    posts = [post] + [flip(post, "slab", k) for k in range(1, slab_size)]
-
     gb = insert_block(groups, orients, devices, particles.shape[0], width)
     table = (groups // gb, gb, orients)
     take = lambda array: lax.dynamic_slice_in_dim(array, slab_pos * groups, groups, 0)
@@ -478,7 +489,14 @@
     for bit in slab_bits:
         place = place * 2 + jnp.where(slab_off & bit != 0, 1, 0)
     rowf = (take(row_index).astype(F32) + take(fraction)).reshape(table)
-    pos, addr, items, meta = plan_call(place.reshape(table), rowf, devices)
+    place, own = lax.optimization_barrier((place.reshape(table), scores[0]))
+    plan = plan_call(place, rowf, devices)
+    own, *plan = lax.optimization_barrier((own, *plan))
+    pos, addr, items, meta = plan
+
+    parts = [own] + [flip(scores[k], "slab", k) for k in range(1, slab_size)]
+    post = softmax_call(parts)
+    posts = [post] + [flip(post, "slab", k) for k in range(1, slab_size)]
     send, keep = insert_call(slab_me, addr, items, flat, pos, meta, blocks, posts, devices)
 
     def merge(kept, got):

time: 218 us -> 201 us (0.922)
  Pallas kernels: 130 us -> 120 us
  local copies, waits for them, and re-layouts: 8.17 us -> 3.31 us
  starting transfers between devices: 24.7 us -> 22.2 us
    pallas_call x1, Pallas kernels: 82.6 us -> 73.5 us  [insert_call(): pl.pallas_call(insert_kernel, grid=(steps,), out_shape=[jax.ShapeDtypeStr...]
    unnamed x21 -> x10, local copies, waits for them, and re-layouts: 6.83 us -> 0.62 us
    ppermute x18, starting transfers between devices: 24.7 us -> 22.2 us  [flip(): return lax.ppermute(value, axis, [(i, i ^ bit) for i in range(size)])]
    pallas_call x1, Pallas kernels: 11 us -> 13.3 us  [plan_call(): pl.pallas_call(functools.partial(plan_kernel, owners=owners), grid=(steps...]
  transfers between devices with their start and end apart: 18 -> 18, of which waited for: 13 -> 14; matrix products, arithmetic and copies ran while one was open for 1% -> 2% of each run, Pallas kernels for 5% -> 7%
where the time goes in v4:
time: 201 us; the launch traced here: 200 us
  Pallas kernels  120 us (60%)
  waiting for transfers between devices  47.9 us (24%)
  starting transfers between devices  22.2 us (11%)
  other arithmetic  5.71 us (3%)
  local copies, waits for them, and re-layouts  3.31 us (2%)
    pallas_call x1, Pallas kernels, insert_call(): pl.pallas_call(insert_kernel, grid=(steps,), out_shape=[jax.ShapeDtypeStr...  73.5 us
    ppermute x18, waiting for transfers between devices, flip(): return lax.ppermute(value, axis, [(i, i ^ bit) for i in range(size)])  47.9 us
    pallas_call x1, Pallas kernels, score_call(): pl.pallas_call(score_kernel, grid=(groups // gb,), out_shape=[jax.ShapeDt...  32.6 us
    ppermute x18, starting transfers between devices, flip(): return lax.ppermute(value, axis, [(i, i ^ bit) for i in range(size)])  22.2 us
    pallas_call x1, Pallas kernels, plan_call(): pl.pallas_call(functools.partial(plan_kernel, owners=owners), grid=(steps...  13.3 us
  transfers between devices with their start and end apart: 18, of which 14 were waited for; matrix products, arithmetic and copies ran while one was open for 2% of the time, Pallas kernels for 7%

profile of v4, /device:TPU:0, one launch (start us, length us, event | category | flops | bytes accessed | tf_op | source)
XLA Modules:
  0.0 199.6 jit_solution(518866229233531349)
XLA Ops:
  0.6 32.6 %shard_map.86 = (bf16[512,20480]{1,0:T(8,128)(2,1)}, f32[128,256]{1,0:T(8,128)}, f32[128,256]{1,0:T(8,128)}, f32[128,256]{1,0:T(8,128)}, f32[128,256]{1,0:T(8,128)}) custom-call(s32[1]{0:T(128)} %bitcast.me_ref, f32[80]{0:T(128)} %noise_ref.1, bf16[512,80,256]{2,1,0:T(8,128)(2,1)} %x_ref.1, bf16[512,80,256]{2,1,0:T(8,128)(2,1)} %r_ref.1, s32[2,512]{1,0:T(2,128)} %bitcast.64), custom_call_target="tpu_custom_call" | custom-call | flops 21474836480 | bytes 62914560 | tf_op jit(solution)/shard_map/pallas_call | solution.py:101
  33.3 3.1 %collective-permute-start = (f32[128,256]{1,0:T(8,128)}, f32[128,256]{1,0:T(8,128)S(1)}, u32[]{:S(2)}, u32[]{:S(2)}) collective-permute-start(f32[128,256]{1,0:T(8,128)} %get-tuple-element.33), channel_id=1, source_target_pairs={{0,1},{1,0},{2,3},{3,2},{4,5},{5,4},{6,7},{7,6},{8,9},{9,8},{10,11... | collective-permute-start | bytes 393224 | tf_op jit(solution)/shard_map/ppermute | solution.py:463
  36.3 2.6 %collective-permute-start.1 = (f32[128,256]{1,0:T(8,128)}, f32[128,256]{1,0:T(8,128)S(1)}, u32[]{:S(2)}, u32[]{:S(2)}) collective-permute-start(f32[128,256]{1,0:T(8,128)} %get-tuple-element.34), channel_id=1, source_target_pairs={{0,2},{1,3},{2,0},{3,1},{4,6},{5,7},{6,4},{7,5},{8,10},{9,11},{10,... | collective-permute-start | bytes 393224 | tf_op jit(solution)/shard_map/ppermute | solution.py:463
  42.5 13.3 %shard_map.87 = (s32[4,20,512]{2,1,0:T(8,128)}, s32[4,20,128]{2,1,0:T(8,128)}, s32[4,4,128]{2,1,0:T(4,128)}, f32[4,20,104,128]{3,2,1,0:T(8,128)}) custom-call(s32[4,20,512]{2,1,0:T(8,128)} %reshape.144.place_ref, f32[4,20,512]{2,1,0:T(8,128)} %reshape.145.rowf_ref), custom_call_target="tpu_custom_call" | custom-call | flops 5368709120 | bytes 327680 | tf_op jit(solution)/shard_map/pallas_call | solution.py:251
  57.0 3.5 %collective-permute-start.4 = (bf16[128,256]{1,0:T(8,128)(2,1)S(1)}, bf16[128,256]{1,0:T(8,128)(2,1)S(1)}, u32[]{:S(2)}, u32[]{:S(2)}) collective-permute-start(bf16[128,256]{1,0:T(8,128)(2,1)S(1)} %shard_map.88.rest_0_), channel_id=1, source_target_pairs={{0,2},{1,3},{2,0},{3,1},{4,6},{5,7},{6,4},{7,5},{8,10},{9,11},{10,... | collective-permute-start | bytes 196616 | tf_op jit(solution)/shard_map/ppermute | solution.py:463
  61.0 3.4 %collective-permute-done.4.rest_2_ = bf16[128,256]{1,0:T(8,128)(2,1)S(1)} collective-permute-done((bf16[128,256]{1,0:T(8,128)(2,1)S(1)}, bf16[128,256]{1,0:T(8,128)(2,1)S(1)}, u32[]{:S(2)}, u32[]{:S(2)}) %collective-permute-start.4) | collective-permute-done | bytes 65568 | tf_op jit(solution)/shard_map/ppermute | solution.py:463
  64.3 2.3 %collective-permute-done.5.rest_3_ = bf16[128,256]{1,0:T(8,128)(2,1)S(1)} collective-permute-done((bf16[128,256]{1,0:T(8,128)(2,1)S(1)}, bf16[128,256]{1,0:T(8,128)(2,1)S(1)}, u32[]{:S(2)}, u32[]{:S(2)}) %collective-permute-start.5) | collective-permute-done | bytes 65568 | tf_op jit(solution)/shard_map/ppermute | solution.py:463
  67.3 73.5 %shard_map.89 = (bf16[4096,256]{1,0:T(8,128)(2,1)}, bf16[4096,256]{1,0:T(8,128)(2,1)}) custom-call(s32[1]{0:T(128)} %bitcast.me_ref, s32[4,20,128]{2,1,0:T(8,128)} %get-tuple-element.27.addr_ref, s32[4,4,128]{2,1,0:T(4,128)} %get-tuple-element.28.item_ref, bf16[512,20480]{1,0:T(8,128)(2,1)} %get-tuple-element.29.x_ref, ...), custom_call_target="tpu_custom_call" | custom-call | flops 42949672960 | bytes 20971520 | tf_op jit(solution)/shard_map/pallas_call | solution.py:426
  140.8 4.4 %collective-permute-done.6 = bf16[4096,256]{1,0:T(8,128)(2,1)S(1)} collective-permute-done((bf16[4096,256]{1,0:T(8,128)(2,1)}, bf16[4096,256]{1,0:T(8,128)(2,1)S(1)}, u32[]{:S(2)}, u32[]{:S(2)}) %collective-permute-start.6) | collective-permute-done | bytes 2097184 | tf_op jit(solution)/shard_map/ppermute | solution.py:463
  145.2 2.0 %convert_add_fusion = f32[4096,256]{1,0:T(8,128)S(1)} fusion(bf16[4096,256]{1,0:T(8,128)(2,1)S(1)} %collective-permute-done.6, bf16[4096,256]{1,0:T(8,128)(2,1)} %get-tuple-element.36), kind=kLoop, calls=%fused_computation.1 | loop fusion | flops 3145728 | bytes 8388608 | tf_op jit(solution)/shard_map/add | solution.py:503
  147.3 1.5 collective-permute-start.7
  148.8 1.5 collective-permute-start.9
  150.4 11.0 %collective-permute-done.7 = bf16[2,1024,128]{2,1,0:T(8,128)(2,1)S(1)} collective-permute-done((bf16[2,1024,128]{2,1,0:T(8,128)(2,1)S(1)}, bf16[2,1024,128]{2,1,0:T(8,128)(2,1)S(1)}, u32[]{:S(2)}, u32[]{:S(2)}) %collective-permute-start.7) | collective-permute-done | bytes 524320 | tf_op jit(solution)/shard_map/ppermute | solution.py:463
  163.4 1.6 collective-permute-start.8
  165.0 5.0 %collective-permute-done.10 = bf16[1024,128]{1,0:T(8,128)(2,1)S(1)} collective-permute-done((bf16[1024,128]{1,0:T(8,128)(2,1)S(1)}, bf16[1024,128]{1,0:T(8,128)(2,1)S(1)}, u32[]{:S(2)}, u32[]{:S(2)}) %collective-permute-start.10) | collective-permute-done | bytes 262176 | tf_op jit(solution)/shard_map/ppermute | solution.py:463
  170.6 6.4 %collective-permute-done.11 = bf16[512,256]{1,0:T(8,128)(2,1)S(1)} collective-permute-done((bf16[512,256]{1,0:T(8,128)(2,1)S(1)}, bf16[512,256]{1,0:T(8,128)(2,1)S(1)}, u32[]{:S(2)}, u32[]{:S(2)}) %collective-permute-start.11) | collective-permute-done | bytes 262176 | tf_op jit(solution)/shard_map/ppermute | solution.py:463
  178.1 5.7 %collective-permute-done.12 = bf16[256,256]{1,0:T(8,128)(2,1)S(1)} collective-permute-done((bf16[256,256]{1,0:T(8,128)(2,1)S(1)}, bf16[256,256]{1,0:T(8,128)(2,1)S(1)}, u32[]{:S(2)}, u32[]{:S(2)}) %collective-permute-start.12) | collective-permute-done | bytes 131104 | tf_op jit(solution)/shard_map/ppermute | solution.py:463
  184.6 1.5 collective-permute-start.13
  186.1 1.5 collective-permute-start.15
  187.6 2.0 %collective-permute-done.13 = bf16[256,128]{1,0:T(8,128)(2,1)S(1)} collective-permute-done((bf16[256,128]{1,0:T(8,128)(2,1)S(1)}, bf16[256,128]{1,0:T(8,128)(2,1)S(1)}, u32[]{:S(2)}, u32[]{:S(2)}) %collective-permute-start.13) | collective-permute-done | bytes 65568 | tf_op jit(solution)/shard_map/ppermute | solution.py:463
  189.7 1.6 collective-permute-start.14
  192.2 2.5 %collective-permute-done.14 = bf16[2,256,128]{2,1,0:T(8,128)(2,1)S(1)} collective-permute-done((bf16[2,256,128]{2,1,0:T(8,128)(2,1)S(1)}, bf16[2,256,128]{2,1,0:T(8,128)(2,1)S(1)}, u32[]{:S(2)}, u32[]{:S(2)}) %collective-permute-start.14) | collective-permute-done | bytes 131104 | tf_op jit(solution)/shard_map/ppermute | solution.py:463
  194.7 1.6 collective-permute-done.16
  196.5 1.9 collective-permute-done.17
  (52 shorter events, 12.9 us)
Async XLA Ops:
  33.3 22.6 %collective-permute-start = (f32[128,256]{1,0:T(8,128)}, f32[128,256]{1,0:T(8,128)S(1)}, u32[]{:S(2)}, u32[]{:S(2)}) collective-permute-start(f32[128,256]{1,0:T(8,128)} %get-tuple-element.33), channel_id=1, source_target_pairs={{0,1},{1,0},{2,3},{3,2},{4,5},{5,4},{6,7},{7,6},{8,9},{9,8},{10,11... | collective-permute-start | bytes 393224 | tf_op jit(solution)/shard_map/ppermute | solution.py:463
  36.3 19.5 %collective-permute-start.1 = (f32[128,256]{1,0:T(8,128)}, f32[128,256]{1,0:T(8,128)S(1)}, u32[]{:S(2)}, u32[]{:S(2)}) collective-permute-start(f32[128,256]{1,0:T(8,128)} %get-tuple-element.34), channel_id=1, source_target_pairs={{0,2},{1,3},{2,0},{3,1},{4,6},{5,7},{6,4},{7,5},{8,10},{9,11},{10,... | collective-permute-start | bytes 393224 | tf_op jit(solution)/shard_map/ppermute | solution.py:463
  38.9 16.9 %collective-permute-start.2 = (f32[128,256]{1,0:T(8,128)}, f32[128,256]{1,0:T(8,128)S(1)}, u32[]{:S(2)}, u32[]{:S(2)}) collective-permute-start(f32[128,256]{1,0:T(8,128)} %get-tuple-element.35), channel_id=1, source_target_pairs={{0,3},{1,2},{2,1},{3,0},{4,7},{5,6},{6,5},{7,4},{8,11},{9,10},{10,... | collective-permute-start | bytes 393224 | tf_op jit(solution)/shard_map/ppermute | solution.py:463
  42.5 13.3 %copy-start = (f32[128,256]{1,0:T(8,128)S(1)}, f32[128,256]{1,0:T(8,128)}, u32[]{:S(2)}) copy-start(f32[128,256]{1,0:T(8,128)} %get-tuple-element.32.refs_0_) | copy-start | bytes 393220
  56.1 10.6 %copy-start.1 = (bf16[128,256]{1,0:T(8,128)(2,1)}, bf16[128,256]{1,0:T(8,128)(2,1)S(1)}, u32[]{:S(2)}) copy-start(bf16[128,256]{1,0:T(8,128)(2,1)S(1)} %shard_map.88.rest_0_) | copy-start | bytes 196612
  56.1 4.9 %collective-permute-start.3 = (bf16[128,256]{1,0:T(8,128)(2,1)S(1)}, bf16[128,256]{1,0:T(8,128)(2,1)S(1)}, u32[]{:S(2)}, u32[]{:S(2)}) collective-permute-start(bf16[128,256]{1,0:T(8,128)(2,1)S(1)} %shard_map.88.rest_0_), channel_id=1, source_target_pairs={{0,1},{1,0},{2,3},{3,2},{4,5},{5,4},{6,7},{7,6},{8,9},{9,8},{10,11... | collective-permute-start | bytes 196616 | tf_op jit(solution)/shard_map/ppermute | solution.py:463
  57.0 7.3 %collective-permute-start.4 = (bf16[128,256]{1,0:T(8,128)(2,1)S(1)}, bf16[128,256]{1,0:T(8,128)(2,1)S(1)}, u32[]{:S(2)}, u32[]{:S(2)}) collective-permute-start(bf16[128,256]{1,0:T(8,128)(2,1)S(1)} %shard_map.88.rest_0_), channel_id=1, source_target_pairs={{0,2},{1,3},{2,0},{3,1},{4,6},{5,7},{6,4},{7,5},{8,10},{9,11},{10,... | collective-permute-start | bytes 196616 | tf_op jit(solution)/shard_map/ppermute | solution.py:463
  60.6 6.1 %collective-permute-start.5 = (bf16[128,256]{1,0:T(8,128)(2,1)S(1)}, bf16[128,256]{1,0:T(8,128)(2,1)S(1)}, u32[]{:S(2)}, u32[]{:S(2)}) collective-permute-start(bf16[128,256]{1,0:T(8,128)(2,1)S(1)} %shard_map.88.rest_0_), channel_id=1, source_target_pairs={{0,3},{1,2},{2,1},{3,0},{4,7},{5,6},{6,5},{7,4},{8,11},{9,10},{10,... | collective-permute-start | bytes 196616 | tf_op jit(solution)/shard_map/ppermute | solution.py:463
  61.0 5.7 %copy-start.2 = (bf16[128,256]{1,0:T(8,128)(2,1)}, bf16[128,256]{1,0:T(8,128)(2,1)S(1)}, u32[]{:S(2)}) copy-start(bf16[128,256]{1,0:T(8,128)(2,1)S(1)} %collective-permute-done.3.rest_1_) | copy-start | bytes 196612
  64.3 2.3 %copy-start.3 = (bf16[128,256]{1,0:T(8,128)(2,1)}, bf16[128,256]{1,0:T(8,128)(2,1)S(1)}, u32[]{:S(2)}) copy-start(bf16[128,256]{1,0:T(8,128)(2,1)S(1)} %collective-permute-done.4.rest_2_) | copy-start | bytes 196612
  66.6 0.6 copy-start.4
  140.7 4.4 %collective-permute-start.6 = (bf16[4096,256]{1,0:T(8,128)(2,1)}, bf16[4096,256]{1,0:T(8,128)(2,1)S(1)}, u32[]{:S(2)}, u32[]{:S(2)}) collective-permute-start(bf16[4096,256]{1,0:T(8,128)(2,1)} %get-tuple-element.37), channel_id=1, source_target_pairs={{0,4},{4,0},{8,12},{12,8},{16,20},{20,16},{24,28},{28,24},{1,5},{5... | collective-permute-start | bytes 6291464 | tf_op jit(solution)/shard_map/ppermute | solution.py:463
  147.3 14.0 %collective-permute-start.7 = (bf16[2,1024,128]{2,1,0:T(8,128)(2,1)S(1)}, bf16[2,1024,128]{2,1,0:T(8,128)(2,1)S(1)}, u32[]{:S(2)}, u32[]{:S(2)}) collective-permute-start(bf16[2,1024,128]{2,1,0:T(8,128)(2,1)S(1)} %slice_bitcast_fusion.5), channel_id=1, source_target_pairs={{0,8},{4,12},{8,0},{12,4},{16,24},{20,28},{24,16},{28,20},{1,9},{5... | collective-permute-start | bytes 1572872 | tf_op jit(solution)/shard_map/ppermute | solution.py:463
  148.8 13.7 %collective-permute-start.9 = (bf16[2,1024,128]{2,1,0:T(8,128)(2,1)S(1)}, bf16[2,1024,128]{2,1,0:T(8,128)(2,1)S(1)}, u32[]{:S(2)}, u32[]{:S(2)}) collective-permute-start(bf16[2,1024,128]{2,1,0:T(8,128)(2,1)S(1)} %slice_bitcast_fusion.3), channel_id=1, source_target_pairs={{0,16},{4,20},{8,24},{12,28},{16,0},{20,4},{24,8},{28,12},{1,17},{... | collective-permute-start | bytes 1572872 | tf_op jit(solution)/shard_map/ppermute | solution.py:463
  162.7 7.3 %collective-permute-start.10 = (bf16[1024,128]{1,0:T(8,128)(2,1)S(1)}, bf16[1024,128]{1,0:T(8,128)(2,1)S(1)}, u32[]{:S(2)}, u32[]{:S(2)}) collective-permute-start(bf16[1024,128]{1,0:T(8,128)(2,1)S(1)} %fusion.8), channel_id=1, source_target_pairs={{0,8},{4,12},{8,0},{12,4},{16,24},{20,28},{24,16},{28,20},{1,9},{5... | collective-permute-start | bytes 786440 | tf_op jit(solution)/shard_map/ppermute | solution.py:463
  163.4 7.0 %collective-permute-start.8 = (bf16[1024,128]{1,0:T(8,128)(2,1)S(1)}, bf16[1024,128]{1,0:T(8,128)(2,1)S(1)}, u32[]{:S(2)}, u32[]{:S(2)}) collective-permute-start(bf16[1024,128]{1,0:T(8,128)(2,1)S(1)} %fusion.7), channel_id=1, source_target_pairs={{0,16},{4,20},{8,24},{12,28},{16,0},{20,4},{24,8},{28,12},{1,17},{... | collective-permute-start | bytes 786440 | tf_op jit(solution)/shard_map/ppermute | solution.py:463
  170.5 6.4 %collective-permute-start.11 = (bf16[512,256]{1,0:T(8,128)(2,1)S(1)}, bf16[512,256]{1,0:T(8,128)(2,1)S(1)}, u32[]{:S(2)}, u32[]{:S(2)}) collective-permute-start(bf16[512,256]{1,0:T(8,128)(2,1)S(1)} %fusion.4), channel_id=1, source_target_pairs={{0,1},{1,0},{2,3},{3,2},{4,5},{5,4},{6,7},{7,6},{8,9},{9,8},{10,11... | collective-permute-start | bytes 786440 | tf_op jit(solution)/shard_map/ppermute | solution.py:463
  177.0 6.8 %collective-permute-start.12 = (bf16[256,256]{1,0:T(8,128)(2,1)S(1)}, bf16[256,256]{1,0:T(8,128)(2,1)S(1)}, u32[]{:S(2)}, u32[]{:S(2)}) collective-permute-start(bf16[256,256]{1,0:T(8,128)(2,1)S(1)} %split.32), channel_id=1, source_target_pairs={{0,2},{1,3},{2,0},{3,1},{4,6},{5,7},{6,4},{7,5},{8,10},{9,11},{10,... | collective-permute-start | bytes 393224 | tf_op jit(solution)/shard_map/ppermute | solution.py:463
  184.6 5.0 %collective-permute-start.13 = (bf16[256,128]{1,0:T(8,128)(2,1)S(1)}, bf16[256,128]{1,0:T(8,128)(2,1)S(1)}, u32[]{:S(2)}, u32[]{:S(2)}) collective-permute-start(bf16[256,128]{1,0:T(8,128)(2,1)S(1)} %get-tuple-element.49), channel_id=1, source_target_pairs={{0,8},{4,12},{8,0},{12,4},{16,24},{20,28},{24,16},{28,20},{1,9},{5... | collective-permute-start | bytes 196616 | tf_op jit(solution)/shard_map/ppermute | solution.py:463
  186.1 5.1 %collective-permute-start.15 = (bf16[256,128]{1,0:T(8,128)(2,1)S(1)}, bf16[256,128]{1,0:T(8,128)(2,1)S(1)}, u32[]{:S(2)}, u32[]{:S(2)}) collective-permute-start(bf16[256,128]{1,0:T(8,128)(2,1)S(1)} %get-tuple-element.48), channel_id=1, source_target_pairs={{0,16},{4,20},{8,24},{12,28},{16,0},{20,4},{24,8},{28,12},{1,17},{... | collective-permute-start | bytes 196616 | tf_op jit(solution)/shard_map/ppermute | solution.py:463
  189.7 5.0 %collective-permute-start.14 = (bf16[2,256,128]{2,1,0:T(8,128)(2,1)S(1)}, bf16[2,256,128]{2,1,0:T(8,128)(2,1)S(1)}, u32[]{:S(2)}, u32[]{:S(2)}) collective-permute-start(bf16[2,256,128]{2,1,0:T(8,128)(2,1)S(1)} %maximum_select_fusion.3), channel_id=1, source_target_pairs={{0,16},{4,20},{8,24},{12,28},{16,0},{20,4},{24,8},{28,12},{1,17},{... | collective-permute-start | bytes 393224 | tf_op jit(solution)/shard_map/ppermute | solution.py:463
  191.3 5.0 %collective-permute-start.16 = (bf16[2,256,128]{2,1,0:T(8,128)(2,1)S(1)}, bf16[2,256,128]{2,1,0:T(8,128)(2,1)S(1)}, u32[]{:S(2)}, u32[]{:S(2)}) collective-permute-start(bf16[2,256,128]{2,1,0:T(8,128)(2,1)S(1)} %maximum_select_fusion.5), channel_id=1, source_target_pairs={{0,8},{4,12},{8,0},{12,4},{16,24},{20,28},{24,16},{28,20},{1,9},{5... | collective-permute-start | bytes 393224 | tf_op jit(solution)/shard_map/ppermute | solution.py:463
  196.4 2.0 collective-permute-start.17

commit v5 on v4

--- a/solution.py
+++ b/solution.py
@@ -146,63 +146,111 @@
 
 
 def plan_kernel(
-    place_ref, rowf_ref, pos_ref, addr_ref, item_ref, meta_ref, hot_ref, count_ref, *, owners
+    here_ref, dest_ref, pos_ref, addr_ref, item_ref, place_ref, hot_ref, count_ref, *, sizes
 ):
-    _, gb, orients = place_ref.shape
+    step = pl.program_id(0)
+    dom_size, slab_size = sizes
+    owners = dom_size * slab_size
+    _, units, half = pos_ref.shape
     lanes = addr_ref.shape[2]
+    parts = dest_ref.shape[1] // half
+    gb = units // parts
+    dom_log, slab_log = (dom_size - 1).bit_length(), (slab_size - 1).bit_length()
+
+    @pl.when(step == 0)
+    def _():
+        off = dest_ref[...] ^ (here_ref[0] * slab_size + here_ref[1])
+        place = jnp.zeros_like(off)
+        for bit in list(range(slab_log, slab_log + dom_log)) + list(range(slab_log)):
+            place = place * 2 + (lax.shift_right_logical(off, bit) & 1)
+        place_ref[...] = place
+
     owner = lax.broadcasted_iota(jnp.int32, (owners, 1), 0)
-    for g in range(gb):
-        hot = jnp.where(place_ref[0, g : g + 1, :] == owner, 1.0, 0.0)
-        hot_ref[g * owners : (g + 1) * owners, :] = hot.astype(BF16)
-    before = lax.broadcasted_iota(jnp.int32, (orients, orients), 0)
-    after = lax.broadcasted_iota(jnp.int32, (orients, orients), 1)
+    for u in range(units):
+        g, h = u // parts, u % parts
+        line = place_ref[pl.ds(step * gb + g, 1), h * half : (h + 1) * half]
+        hot = jnp.where(line == owner, 1.0, 0.0)
+        hot_ref[u * owners : (u + 1) * owners, :] = hot.astype(BF16)
+    before = lax.broadcasted_iota(jnp.int32, (half, half), 0)
+    after = lax.broadcasted_iota(jnp.int32, (half, half), 1)
     upto = jnp.where(before <= after, 1.0, 0.0).astype(BF16)
     count_ref[...] = jnp.dot(hot_ref[...], upto, preferred_element_type=F32)
 
     exact = functools.partial(
         jnp.dot, preferred_element_type=F32, precision=lax.Precision.HIGHEST
     )
-    tri = lambda n, lower: jnp.where(
-        (lax.broadcasted_iota(jnp.int32, (n, n), 0) > lax.broadcasted_iota(jnp.int32, (n, n), 1))
-        == lower,
-        1.0,
-        0.0,
-    )
-    below = tri(owners, True)
+    row = lax.broadcasted_iota(jnp.int32, (owners, owners), 0)
+    col = lax.broadcasted_iota(jnp.int32, (owners, owners), 1)
+    below = jnp.where(row > col, 1.0, 0.0)
     row = lax.broadcasted_iota(jnp.int32, (OB, OB), 0)
     col = lax.broadcasted_iota(jnp.int32, (OB, OB), 1)
     earlier = jnp.where(row < col, 1.0, 0.0)
     lane = lax.broadcasted_iota(jnp.int32, (owners, OB), 1)
-    sizes = jnp.zeros((owners, OB), F32)
-    for g in range(gb):
-        size = count_ref[g * owners : (g + 1) * owners, orients - 1 : orients]
-        size = jnp.floor((size + 7.0) * 0.125) * 8.0
-        sizes = jnp.where(lane == g, size, sizes)
-    base = exact(below, sizes)
-    ahead = exact(sizes, earlier)
-    total = jnp.sum(sizes, axis=1, keepdims=True)
+    runs = jnp.zeros((owners, OB), F32)
+    for u in range(units):
+        size = count_ref[u * owners : (u + 1) * owners, half - 1 : half]
+        runs = jnp.where(lane == u, size, runs)
+    runs = jnp.floor((runs + 7.0) * 0.125) * 8.0
+    base = exact(below, runs)
+    ahead = exact(runs, earlier)
+    total = jnp.sum(runs, axis=1, keepdims=True)
     start = exact(below, jnp.broadcast_to(total, (owners, OB)))[:, :1]
     blocks = jnp.floor((total + (RD - 1.0)) * (1.0 / RD))
     first = exact(below, jnp.broadcast_to(blocks, (owners, OB)))[:, :1]
-    owner_f = owner.astype(F32)
+    shift = start + ahead - base
+    used = jnp.sum(runs, axis=0, keepdims=True)
 
     slot = (lax.broadcasted_iota(jnp.int32, (1, lanes), 1) * 8).astype(F32)
-    eighth = lax.broadcasted_iota(jnp.int32, (meta_ref.shape[2], 1), 0).astype(F32)
-    lane_of = (lax.broadcasted_iota(jnp.int32, (OB, 1), 0) % 8).astype(F32)
     is_last = lax.broadcasted_iota(jnp.int32, (1, lanes), 1) == lanes - 1
-    rows = gb * (orients + 7 * owners)
-    for g in range(gb):
-        low, size = base[:, g : g + 1], sizes[:, g : g + 1]
-        hot = hot_ref[g * owners : (g + 1) * owners, :].astype(F32)
-        rank = count_ref[g * owners : (g + 1) * owners, :] - 1.0 + low
-        pos = jnp.sum(hot * rank, axis=0, keepdims=True)
-        pos_ref[0, g : g + 1, :] = pos.astype(jnp.int32)
-        block = jnp.floor(pos * 0.125)
-        value = rowf_ref[0, g : g + 1, :]
+    rows = units * (half + 7 * owners)
+    for u in range(units):
+        low, size = base[:, u : u + 1], runs[:, u : u + 1]
+        hot = hot_ref[u * owners : (u + 1) * owners, :].astype(F32)
+        rank = count_ref[u * owners : (u + 1) * owners, :] + (low - 1.0)
+        pos_ref[0, u : u + 1, :] = jnp.sum(hot * rank, axis=0, keepdims=True).astype(jnp.int32)
+        inside = (slot >= low) & (slot < low + size)
+        goal = jnp.where(inside, shift[:, u : u + 1] + slot - rows, 0.0)
+        goal = (jnp.sum(goal, axis=0, keepdims=True) + rows) * 0.125
+        addr_ref[0, u : u + 1, :] = jnp.where(is_last, used[:, u : u + 1], goal).astype(jnp.int32)
+
+    wide = item_ref.shape[2]
+    number = lax.broadcasted_iota(jnp.int32, (1, wide), 1).astype(F32)
+    inside = (number >= first) & (number < first + blocks)
+    done = (number - first) * RD
+    pick = lambda value: jnp.sum(jnp.where(inside, value, 0.0), axis=0, keepdims=True)
+    every = lambda value: jnp.sum(
+        jnp.broadcast_to(value, (owners, wide)), axis=0, keepdims=True
+    )
+    lines = (
+        pick(jnp.broadcast_to(owner.astype(F32), (owners, wide))),
+        pick((start + done) * 0.125),
+        pick(total - done),
+        every(blocks),
+        every(total * 0.125),
+    )
+    for i, value in enumerate(lines):
+        item_ref[0, i : i + 1, :] = value.astype(jnp.int32)
+
+
+def meta_kernel(here_ref, index_ref, frac_ref, pos_ref, meta_ref):
+    step = pl.program_id(0)
+    _, units, half = pos_ref.shape
+    parts = index_ref.shape[1] // half
+    gb = units // parts
+    blocks = meta_ref.shape[2]
+    eighth = lax.broadcasted_iota(jnp.int32, (blocks, 1), 0)
+    lane_of = lax.broadcasted_iota(jnp.int32, (OB, 1), 0) % 8
+    for u in range(units):
+        g, h = u // parts, u % parts
+        line = pl.ds(step * gb + g, 1)
+        span = slice(h * half, (h + 1) * half)
+        value = index_ref[line, span].astype(F32) + frac_ref[line, span]
         coarse = value.astype(BF16).astype(F32)
-        here = lane_of == pos - 8.0 * block
+        pos = pos_ref[0, u : u + 1, :]
+        block = lax.shift_right_logical(pos, 3)
+        here = lane_of == (pos & 7)
         spots = jnp.where(eighth == block, 1.0, 0.0).astype(BF16)
-        meta = jnp.zeros((meta_ref.shape[2], OB), F32)
+        meta = jnp.zeros((blocks, OB), F32)
         for term in (coarse, value - coarse):
             meta = meta + lax.dot_general(
                 spots,
@@ -210,23 +258,7 @@
                 (((1,), (1,)), ((), ())),
                 preferred_element_type=F32,
             )
-        meta_ref[0, g] = meta
-        inside = (slot >= low) & (slot < low + size)
-        goal = jnp.where(inside, start + ahead[:, g : g + 1] - low + slot - rows, 0.0) * 0.125
-        goal = jnp.sum(goal, axis=0, keepdims=True) + rows // 8
-        used = jnp.sum(size, axis=0, keepdims=True)
-        addr_ref[0, g : g + 1, :] = jnp.where(is_last, used, goal).astype(jnp.int32)
-
-    wide = item_ref.shape[2]
-    number = lax.broadcasted_iota(jnp.int32, (1, wide), 1).astype(F32)
-    inside = (number >= first) & (number < first + blocks)
-    done = (number - first) * RD
-    pick = lambda value: jnp.sum(jnp.where(inside, value, 0.0), axis=0, keepdims=True)
-    item_ref[0, 0:1, :] = pick(jnp.broadcast_to(owner_f, (owners, wide))).astype(jnp.int32)
-    item_ref[0, 1:2, :] = pick((start + done) * 0.125).astype(jnp.int32)
-    item_ref[0, 2:3, :] = pick(total - done).astype(jnp.int32)
-    items = jnp.sum(jnp.broadcast_to(blocks, (owners, wide)), axis=0, keepdims=True)
-    item_ref[0, 3:4, :] = items.astype(jnp.int32)
+        meta_ref[0, u] = meta
 
 
 def up_to(value, step):
@@ -240,55 +272,85 @@
     return slots, sure, blocks
 
 
-def plan_call(place, rowf, owners):
-    steps, gb, orients = place.shape
-    slots, _, blocks = sort_sizes(orients, owners)
-    lanes = up_to(blocks + 1, 128)
-    wide = up_to(owners + gb * slots // RD + 8, 128)
-    block = lambda *shape: pl.BlockSpec(
-        (1,) + shape, lambda i, n=len(shape): (i,) + (0,) * n
-    )
+def planned(shape):
+    return pl.BlockSpec((1,) + shape[1:], lambda i, here: (i,) + (0,) * (len(shape) - 1))
+
+
+def plan_call(here, destination, groups, gb, mesh_sizes):
+    orients = destination.shape[1]
+    half = min(256, orients)
+    owners = mesh_sizes[0] * mesh_sizes[1]
+    steps, units = groups // gb, gb * (orients // half)
+    slots, _, blocks = sort_sizes(half, owners)
+    shapes = [
+        (steps, units, half),
+        (steps, units, up_to(blocks + 1, 128)),
+        (steps, 5, up_to(owners + units * slots // RD + 8, 128)),
+    ]
     return pl.pallas_call(
-        functools.partial(plan_kernel, owners=owners),
-        grid=(steps,),
-        out_shape=[
-            jax.ShapeDtypeStruct((steps, gb, orients), jnp.int32),
-            jax.ShapeDtypeStruct((steps, gb, lanes), jnp.int32),
-            jax.ShapeDtypeStruct((steps, 4, wide), jnp.int32),
-            jax.ShapeDtypeStruct((steps, gb, blocks, OB), F32),
-        ],
-        in_specs=[block(gb, orients)] * 2,
-        out_specs=[block(gb, orients), block(gb, lanes), block(4, wide), block(gb, blocks, OB)],
-        scratch_shapes=[
-            pltpu.VMEM((gb * owners, orients), BF16),
-            pltpu.VMEM((gb * owners, orients), F32),
-        ],
+        functools.partial(plan_kernel, sizes=mesh_sizes),
+        grid_spec=pltpu.PrefetchScalarGridSpec(
+            num_scalar_prefetch=1,
+            grid=(steps,),
+            in_specs=[pl.BlockSpec((groups, orients), lambda i, here: (here[1], 0))],
+            out_specs=[planned(shape) for shape in shapes],
+            scratch_shapes=[
+                pltpu.VMEM((groups, orients), jnp.int32),
+                pltpu.VMEM((units * owners, half), BF16),
+                pltpu.VMEM((units * owners, half), F32),
+            ],
+        ),
+        out_shape=[jax.ShapeDtypeStruct(shape, jnp.int32) for shape in shapes],
         compiler_params=pltpu.CompilerParams(vmem_limit_bytes=60 * MB),
         cost_estimate=pl.CostEstimate(
-            flops=8 * steps * gb * owners * orients * orients,
-            bytes_accessed=8 * steps * gb * orients,
+            flops=8 * steps * units * owners * half * half,
+            bytes_accessed=8 * groups * orients,
             transcendentals=0,
         ),
-    )(place, rowf)
+    )(here, destination)
+
+
+def meta_call(here, row_index, fraction, pos, owners):
+    steps, units, half = pos.shape
+    orients = row_index.shape[1]
+    groups = steps * units * half // orients
+    blocks = sort_sizes(half, owners)[2]
+    shape = (steps, units, blocks, OB)
+    table = pl.BlockSpec((groups, orients), lambda i, here: (here[1], 0))
+    return pl.pallas_call(
+        meta_kernel,
+        grid_spec=pltpu.PrefetchScalarGridSpec(
+            num_scalar_prefetch=1,
+            grid=(steps,),
+            in_specs=[table, table, planned(pos.shape)],
+            out_specs=planned(shape),
+        ),
+        out_shape=jax.ShapeDtypeStruct(shape, F32),
+        compiler_params=pltpu.CompilerParams(vmem_limit_bytes=60 * MB),
+        cost_estimate=pl.CostEstimate(
+            flops=8 * steps * units * blocks * half * OB,
+            bytes_accessed=8 * steps * units * blocks * OB,
+            transcendentals=0,
+        ),
+    )(here, row_index, fraction, pos)
 
 
 def insert_kernel(me_ref, addr_ref, item_ref, x_ref, pos_ref, meta_ref, blk_ref, *rest):
-    *post_refs, send_ref, keep_ref = rest[:-9]
-    post_t, spread_ref, cols_ref, slice_ref, buf_s, buf_m, volume, stage, sem = rest[-9:]
+    *post_refs, send_ref, keep_ref = rest[:-10]
+    post_t, spread_ref, cols_ref, slice_a, slice_b, buf_s, buf_m, volume, stage, sem = rest[-10:]
     step = pl.program_id(0)
     count = x_ref.shape[0]
     orients = post_t.shape[0]
-    gb = pos_ref.shape[1]
+    units, half = pos_ref.shape[1:]
+    parts = orients // half
+    gb = units // parts
     width = x_ref.shape[1] // gb
     share = count // len(post_refs)
     lanes = addr_ref.shape[2]
-    unroll = 4 if gb % 4 == 0 else 1
 
     @pl.when(step == 0)
     def _():
         volume[...] = jnp.zeros_like(volume)
-        buf_s[...] = jnp.zeros_like(buf_s)
-        buf_m[...] = jnp.zeros_like(buf_m)
         me = me_ref[0]
         spread_columns(blk_ref, cols_ref)
         for k, post_ref in enumerate(post_refs):
@@ -304,51 +366,81 @@
         for b in range(orients // OB):
             post_t[b * OB : (b + 1) * OB] = spread_ref[:, b * OB : (b + 1) * OB].T.astype(BF16)
 
-    def some_slices(q, carry):
-        span = unroll * width
-        at = pl.ds(pl.multiple_of(q * span, span), span)
+    tail = pl.ds(pl.multiple_of(item_ref[0, 4, 0] * 8, 8), RD)
+    buf_s[tail, :] = jnp.zeros((RD, width), F32)
+    one, none = jnp.bfloat16(1.0), jnp.bfloat16(0.0)
+    slots, sure, _ = sort_sizes(half, volume.shape[0] // RD)
+    per = slice_a.shape[1] // width
+    number = gb // per
+
+    def slices(q, dst_ref):
+        at = pl.ds(pl.multiple_of(q * (per * width), per * width), per * width)
         value = jnp.dot(post_t[...], x_ref[:, at], preferred_element_type=F32)
-        slice_ref[:, at] = value.astype(BF16)
-        return carry
-
-    lax.fori_loop(0, gb // unroll, some_slices, 0)
-
-    one, none = jnp.bfloat16(1.0), jnp.bfloat16(0.0)
-
-    def emit(g, base, size):
-        pos = pos_ref[0, pl.ds(g, 1), :]
-        piece = slice_ref[:, pl.ds(pl.multiple_of(g * width, width), width)]
-        parts = []
+        dst_ref[...] = value.astype(BF16)
+
+    def emit(u, piece, base, size):
+        pos = pos_ref[0, pl.ds(u, 1), :]
+        order = []
         for at in range(0, size, 128):
             high = min(128, size - at)
-            slot = lax.broadcasted_iota(jnp.int32, (high, orients), 0).astype(F32).astype(BF16)
+            slot = lax.broadcasted_iota(jnp.int32, (high, half), 0).astype(F32).astype(BF16)
             near = jnp.clip(pos - (base + at), -1, 128).astype(F32).astype(BF16)
-            parts.append(jnp.where(slot == near, one, none))
-        order = jnp.concatenate(parts, axis=0)
+            order.append(jnp.where(slot == near, one, none))
+        order = jnp.concatenate(order, axis=0)
         rows = jnp.dot(order, piece, preferred_element_type=F32)
         for i in range(size // 8):
-            at = addr_ref[0, g, base // 8 + i]
+            at = addr_ref[0, u, base // 8 + i]
             buf_s[pl.ds(pl.multiple_of(at * 8, 8), 8), :] = rows[8 * i : 8 * i + 8]
-            buf_m[pl.ds(at, 1), :] = meta_ref[0, g, pl.ds(base // 8 + i, 1), :]
-
-    slots, sure, _ = sort_sizes(orients, volume.shape[0] // RD)
-
-    def one_group(g, carry):
-        emit(g, 0, sure)
+            buf_m[pl.ds(at, 1), :] = meta_ref[0, u, pl.ds(base // 8 + i, 1), :]
+
+    def sort(q, src_ref):
+        for g in range(per):
+            for h in range(parts):
+                piece = src_ref[h * half : (h + 1) * half, g * width : (g + 1) * width]
+                emit((q * per + g) * parts + h, piece, 0, sure)
+
+    def rest_of(q, src_ref):
+        for g in range(per):
+            for h in range(parts):
+                u = (q * per + g) * parts + h
+
+                def more(e, c, u=u, g=g, h=h):
+                    piece = src_ref[h * half : (h + 1) * half, g * width : (g + 1) * width]
+                    emit(u, piece, sure + e * 128, 128)
+                    return c
+
+                used = addr_ref[0, u, lanes - 1]
+                lax.fori_loop(0, lax.div(jnp.maximum(used - sure, 0) + 127, 128), more, 0)
+
+    def most_used(q):
+        most = addr_ref[0, q * per * parts, lanes - 1]
+        for u in range(1, per * parts):
+            most = jnp.maximum(most, addr_ref[0, q * per * parts + u, lanes - 1])
+        return most
+
+    def two(j, carry):
+        q = j * 2
+        sort(q, slice_a)
+        slices(q + 1, slice_b)
+
+        @pl.when(most_used(q) > sure)
+        def _():
+            rest_of(q, slice_a)
+
+        sort(q + 1, slice_b)
+        slices(jnp.minimum(q + 2, number - 1), slice_a)
+
+        @pl.when(most_used(q + 1) > sure)
+        def _():
+            rest_of(q + 1, slice_b)
+
         return carry
 
-    lax.fori_loop(0, gb, one_group, 0, unroll=unroll)
-
-    def rest_of_group(g, carry):
-        def more(e, c):
-            emit(g, sure + e * 128, 128)
-            return c
-
-        used = addr_ref[0, g, lanes - 1]
-        return lax.fori_loop(0, lax.div(jnp.maximum(used - sure, 0) + 127, 128), more, carry)
-
-    if slots > sure:
-        lax.fori_loop(0, gb, rest_of_group, 0)
+    slices(0, slice_a)
+    lax.fori_loop(0, number // 2, two, 0)
+    if number % 2:
+        sort(number - 1, slice_a)
+        rest_of(number - 1, slice_a)
 
     bins = lax.broadcasted_iota(jnp.int32, (RD, RD), 0).astype(F32).astype(BF16)
     side = RD // 2
@@ -403,26 +495,36 @@
             copy.wait()
 
 
+def group_pair(gb):
+    return 2 if gb % 4 == 0 else 1
+
+
 def insert_block(groups, orients, owners, count, width):
-    room = 58 * MB - owners * RD * width * 4 - 6 * MB
+    half = min(256, orients)
+    slots, _, blocks = sort_sizes(half, owners)
+    room = 52 * MB - owners * RD * width * 4
     best = 1
     for gb in range(1, groups + 1):
-        rows = gb * (orients + 7 * owners) + RD + 8
-        need = rows * width * 4 + rows * OB // 2 + 4 * count * gb * width + 2 * orients * gb * width
+        units = gb * (orients // half)
+        rows = units * slots + RD + 8
+        need = rows * (width * 4 + OB // 2) + 4 * count * gb * width + units * blocks * OB * 8
         if groups % gb == 0 and need <= room:
             best = gb
     return best
 
 
-def insert_call(me, addr, items, flat, pos, meta, blocks, posts, owners):
-    count = flat.shape[0]
-    steps, gb, orients = pos.shape
-    width = flat.shape[1] // (steps * gb)
+def insert_call(me, addr, items, flat, pos, meta, blocks, posts, orients, owners):
+    count, length = flat.shape
+    steps, units, half = pos.shape
+    gb = units * half // orients
+    width = length // (steps * gb)
     total = owners * RD
     share = posts[0].shape[0]
-    rows = gb * (orients + 7 * owners) + RD + 8
+    rows = units * sort_sizes(half, owners)[0] + RD + 8
     smem = pl.BlockSpec(memory_space=pltpu.SMEM)
-    block = lambda shape, **kw: pl.BlockSpec((1,) + shape[1:], lambda i: (i,) + (0,) * (len(shape) - 1), **kw)
+    block = lambda shape, **kw: pl.BlockSpec(
+        (1,) + shape[1:], lambda i: (i,) + (0,) * (len(shape) - 1), **kw
+    )
     return pl.pallas_call(
         insert_kernel,
         grid=(steps,),
@@ -442,7 +544,8 @@
             pltpu.VMEM((orients, count), BF16),
             pltpu.VMEM((count, orients), F32),
             pltpu.VMEM((2, count, OB), F32),
-            pltpu.VMEM((orients, gb * width), BF16),
+            pltpu.VMEM((orients, group_pair(gb) * width), BF16),
+            pltpu.VMEM((orients, group_pair(gb) * width), BF16),
             pltpu.VMEM((rows, width), F32),
             pltpu.VMEM((rows // 8, OB), F32),
             pltpu.VMEM((total, width), F32),
@@ -451,8 +554,8 @@
         ],
         compiler_params=pltpu.CompilerParams(vmem_limit_bytes=62 * MB),
         cost_estimate=pl.CostEstimate(
-            flops=8 * count * orients * steps * gb * width,
-            bytes_accessed=2 * count * steps * gb * width,
+            flops=8 * count * orients * length,
+            bytes_accessed=2 * count * length,
             transcendentals=0,
         ),
     )(me, addr, items, flat, pos, meta, blocks, *posts)
@@ -471,33 +574,26 @@
     devices = dom_size * slab_size
     dom_pos = lax.axis_index("dom")
     slab_pos = lax.axis_index("slab")
-    slab_me = slab_pos.astype(jnp.int32).reshape(1)
+    here = jnp.stack([dom_pos, slab_pos]).astype(jnp.int32)
+    slab_me = here[1:]
     dom_bits = [1 << i for i in range((dom_size - 1).bit_length())]
     slab_bits = [1 << i for i in range((slab_size - 1).bit_length())]
 
     blocks = blocks.T
     flat, *scores = score_call(slab_me, inv_noise, particles, references, blocks, slab_size)
     gb = insert_block(groups, orients, devices, particles.shape[0], width)
-    table = (groups // gb, gb, orients)
-    take = lambda array: lax.dynamic_slice_in_dim(array, slab_pos * groups, groups, 0)
-    owner = take(destination)
-    dom_off = (owner // slab_size) ^ dom_pos
-    slab_off = (owner % slab_size) ^ slab_pos
-    place = jnp.zeros_like(owner)
-    for bit in dom_bits:
-        place = place * 2 + jnp.where(dom_off & bit != 0, 1, 0)
-    for bit in slab_bits:
-        place = place * 2 + jnp.where(slab_off & bit != 0, 1, 0)
-    rowf = (take(row_index).astype(F32) + take(fraction)).reshape(table)
-    place, own = lax.optimization_barrier((place.reshape(table), scores[0]))
-    plan = plan_call(place, rowf, devices)
+    here, own = lax.optimization_barrier((here, scores[0]))
+    plan = plan_call(here, destination, groups, gb, (dom_size, slab_size))
     own, *plan = lax.optimization_barrier((own, *plan))
-    pos, addr, items, meta = plan
-
+    pos, addr, items = plan
     parts = [own] + [flip(scores[k], "slab", k) for k in range(1, slab_size)]
     post = softmax_call(parts)
+    post, pos = lax.optimization_barrier((post, pos))
+    meta = meta_call(here, row_index, fraction, pos, devices)
     posts = [post] + [flip(post, "slab", k) for k in range(1, slab_size)]
-    send, keep = insert_call(slab_me, addr, items, flat, pos, meta, blocks, posts, devices)
+    send, keep = insert_call(
+        slab_me, addr, items, flat, pos, meta, blocks, posts, orients, devices
+    )
 
     def merge(kept, got):
         return kept.astype(F32) + got.astype(F32)

time: 201 us -> 190 us (0.945); the launches traced: 200 us -> 191 us
  waiting for transfers between devices: 47.9 us -> 39.8 us
  starting transfers between devices: 22.2 us -> 24.6 us
    ppermute x18, waiting for transfers between devices: 47.9 us -> 39.8 us  [flip(): return lax.ppermute(value, axis, [(i, i ^ bit) for i in range(size)])]
    pallas_call x1, Pallas kernels: 73.5 us -> 66.3 us  [insert_call(): pl.pallas_call(insert_kernel, grid=(steps,), out_shape=[jax.ShapeDtypeStr...]
    pallas_call x1 -> x2, Pallas kernels: 13.3 us -> 20.4 us  [the longest x1 10.7 us: meta_call(): pl.pallas_call(meta_kernel, grid_spec=pltpu.PrefetchScalarGridSpec(num_sc...]
    ppermute x18, starting transfers between devices: 22.2 us -> 24.6 us  [flip(): return lax.ppermute(value, axis, [(i, i ^ bit) for i in range(size)])]
    add x2 -> x0, other arithmetic: 2.21 us -> none  [the longest x1 1.19 us: shards(): place = place * 2 + jnp.where(slab_off & bit != 0, 1, 0)]
  transfers between devices with their start and end apart: 18 -> 18, of which waited for: 14 -> 12; matrix products, arithmetic and copies ran while one was open for 2% -> 0% of each run, Pallas kernels for 7% -> 11%
where the time goes in v5:
time: 190 us; the launch traced here: 191 us
  Pallas kernels  119 us (63%)
  waiting for transfers between devices  39.8 us (21%)
  starting transfers between devices  24.6 us (13%)
  other arithmetic  4.17 us (2%)
  local copies, waits for them, and re-layouts  1.95 us (1%)
    pallas_call x1, Pallas kernels, insert_call(): pl.pallas_call(insert_kernel, grid=(steps,), out_shape=[jax.ShapeDtypeStr...  66.3 us
    ppermute x18, waiting for transfers between devices, flip(): return lax.ppermute(value, axis, [(i, i ^ bit) for i in range(size)])  39.8 us
    pallas_call x1, Pallas kernels, score_call(): pl.pallas_call(score_kernel, grid=(groups // gb,), out_shape=[jax.ShapeDt...  32.6 us
    ppermute x18, starting transfers between devices, flip(): return lax.ppermute(value, axis, [(i, i ^ bit) for i in range(size)])  24.6 us
    pallas_call x1, Pallas kernels, meta_call(): pl.pallas_call(meta_kernel, grid_spec=pltpu.PrefetchScalarGridSpec(num_sc...  10.7 us
    pallas_call x1, Pallas kernels, plan_call(): pl.pallas_call(functools.partial(plan_kernel, sizes=mesh_sizes), grid_spe...  9.71 us
  transfers between devices with their start and end apart: 18, of which 12 were waited for; matrix products, arithmetic and copies ran while one was open for 0% of the time, Pallas kernels for 11%

profile of v5, /device:TPU:0, one launch (start us, length us, event | category | flops | bytes accessed | tf_op | source)
XLA Modules:
  0.0 190.8 jit_solution(11319395024712257739)
XLA Ops:
  0.6 32.6 %shard_map.86 = (bf16[512,20480]{1,0:T(8,128)(2,1)}, f32[128,256]{1,0:T(8,128)}, f32[128,256]{1,0:T(8,128)}, f32[128,256]{1,0:T(8,128)}, f32[128,256]{1,0:T(8,128)}) custom-call(s32[1]{0:T(128)} %bitcast.me_ref, f32[80]{0:T(128)} %noise_ref.1, bf16[512,80,256]{2,1,0:T(8,128)(2,1)} %x_ref.1, bf16[512,80,256]{2,1,0:T(8,128)(2,1)} %r_ref.1, s32[2,512]{1,0:T(2,128)} %bitcast.65), custom_call_target="tpu_custom_call" | custom-call | flops 21474836480 | bytes 62914560 | tf_op jit(solution)/shard_map/pallas_call | solution.py:101
  33.2 3.1 %collective-permute-start = (f32[128,256]{1,0:T(8,128)}, f32[128,256]{1,0:T(8,128)S(1)}, u32[]{:S(2)}, u32[]{:S(2)}) collective-permute-start(f32[128,256]{1,0:T(8,128)} %get-tuple-element.30), channel_id=1, source_target_pairs={{0,1},{1,0},{2,3},{3,2},{4,5},{5,4},{6,7},{7,6},{8,9},{9,8},{10,11... | collective-permute-start | bytes 393224 | tf_op jit(solution)/shard_map/ppermute | solution.py:566
  36.3 2.6 %collective-permute-start.1 = (f32[128,256]{1,0:T(8,128)}, f32[128,256]{1,0:T(8,128)S(1)}, u32[]{:S(2)}, u32[]{:S(2)}) collective-permute-start(f32[128,256]{1,0:T(8,128)} %get-tuple-element.31), channel_id=1, source_target_pairs={{0,2},{1,3},{2,0},{3,1},{4,6},{5,7},{6,4},{7,5},{8,10},{9,11},{10,... | collective-permute-start | bytes 393224 | tf_op jit(solution)/shard_map/ppermute | solution.py:566
  39.5 9.7 %shard_map.87 = (s32[4,40,256]{2,1,0:T(8,128)}, s32[4,40,128]{2,1,0:T(8,128)}, s32[4,5,128]{2,1,0:T(8,128)}) custom-call(s32[2]{0:T(128)} %pad_add_fusion.here_ref, s32[320,512]{1,0:T(8,128)} %dest_ref.1), custom_call_target="tpu_custom_call" | custom-call | flops 2684354560 | bytes 327680 | tf_op jit(solution)/shard_map/pallas_call | solution.py:290
  49.6 2.0 %collective-permute-start.3 = (bf16[128,256]{1,0:T(8,128)(2,1)S(1)}, bf16[128,256]{1,0:T(8,128)(2,1)S(1)}, u32[]{:S(2)}, u32[]{:S(2)}) collective-permute-start(bf16[128,256]{1,0:T(8,128)(2,1)S(1)} %shard_map.88.rest_0_), channel_id=1, source_target_pairs={{0,1},{1,0},{2,3},{3,2},{4,5},{5,4},{6,7},{7,6},{8,9},{9,8},{10,11... | collective-permute-start | bytes 196616 | tf_op jit(solution)/shard_map/ppermute | solution.py:566
  51.7 2.3 %collective-permute-start.4 = (bf16[128,256]{1,0:T(8,128)(2,1)S(1)}, bf16[128,256]{1,0:T(8,128)(2,1)S(1)}, u32[]{:S(2)}, u32[]{:S(2)}) collective-permute-start(bf16[128,256]{1,0:T(8,128)(2,1)S(1)} %shard_map.88.rest_0_), channel_id=1, source_target_pairs={{0,2},{1,3},{2,0},{3,1},{4,6},{5,7},{6,4},{7,5},{8,10},{9,11},{10,... | collective-permute-start | bytes 196616 | tf_op jit(solution)/shard_map/ppermute | solution.py:566
  54.1 10.7 %shard_map.89.meta_ref = f32[4,40,72,128]{3,2,1,0:T(8,128)} custom-call(s32[2]{0:T(128)} %pad_add_fusion.here_ref, s32[320,512]{1,0:T(8,128)} %index_ref.1, f32[320,512]{1,0:T(8,128)} %frac_ref.1, s32[4,40,256]{2,1,0:T(8,128)} %get-tuple-element.34.pos_ref), custom_call_target="tpu_custom_call" | custom-call | flops 3019898880 | bytes 11796480 | tf_op jit(solution)/shard_map/pallas_call | solution.py:320
  65.5 66.3 %shard_map.90 = (bf16[4096,256]{1,0:T(8,128)(2,1)}, bf16[4096,256]{1,0:T(8,128)(2,1)}) custom-call(s32[1]{0:T(128)} %bitcast.me_ref, s32[4,40,128]{2,1,0:T(8,128)} %get-tuple-element.26.addr_ref, s32[4,5,128]{2,1,0:T(8,128)} %get-tuple-element.27.item_ref, bf16[512,20480]{1,0:T(8,128)(2,1)} %get-tuple-element.28.x_ref, ...), custom_call_target="tpu_custom_call" | custom-call | flops 42949672960 | bytes 20971520 | tf_op jit(solution)/shard_map/pallas_call | solution.py:528
  131.9 4.4 %collective-permute-done.6 = bf16[4096,256]{1,0:T(8,128)(2,1)S(1)} collective-permute-done((bf16[4096,256]{1,0:T(8,128)(2,1)}, bf16[4096,256]{1,0:T(8,128)(2,1)S(1)}, u32[]{:S(2)}, u32[]{:S(2)}) %collective-permute-start.6) | collective-permute-done | bytes 2097184 | tf_op jit(solution)/shard_map/ppermute | solution.py:566
  136.2 2.0 %convert_add_fusion = f32[4096,256]{1,0:T(8,128)S(1)} fusion(bf16[4096,256]{1,0:T(8,128)(2,1)S(1)} %collective-permute-done.6, bf16[4096,256]{1,0:T(8,128)(2,1)} %get-tuple-element.36), kind=kLoop, calls=%fused_computation.1 | loop fusion | flops 3145728 | bytes 8388608 | tf_op jit(solution)/shard_map/add | solution.py:599
  138.4 1.5 collective-permute-start.7
  139.9 1.5 collective-permute-start.9
  141.4 11.0 %collective-permute-done.7 = bf16[2,1024,128]{2,1,0:T(8,128)(2,1)S(1)} collective-permute-done((bf16[2,1024,128]{2,1,0:T(8,128)(2,1)S(1)}, bf16[2,1024,128]{2,1,0:T(8,128)(2,1)S(1)}, u32[]{:S(2)}, u32[]{:S(2)}) %collective-permute-start.7) | collective-permute-done | bytes 524320 | tf_op jit(solution)/shard_map/ppermute | solution.py:566
  154.5 1.6 collective-permute-start.8
  156.1 5.0 %collective-permute-done.10 = bf16[1024,128]{1,0:T(8,128)(2,1)S(1)} collective-permute-done((bf16[1024,128]{1,0:T(8,128)(2,1)S(1)}, bf16[1024,128]{1,0:T(8,128)(2,1)S(1)}, u32[]{:S(2)}, u32[]{:S(2)}) %collective-permute-start.10) | collective-permute-done | bytes 262176 | tf_op jit(solution)/shard_map/ppermute | solution.py:566
  162.7 5.4 %collective-permute-done.11 = bf16[512,256]{1,0:T(8,128)(2,1)S(1)} collective-permute-done((bf16[512,256]{1,0:T(8,128)(2,1)S(1)}, bf16[512,256]{1,0:T(8,128)(2,1)S(1)}, u32[]{:S(2)}, u32[]{:S(2)}) %collective-permute-start.11) | collective-permute-done | bytes 262176 | tf_op jit(solution)/shard_map/ppermute | solution.py:566
  168.1 2.4 %collective-permute-start.12 = (bf16[256,256]{1,0:T(8,128)(2,1)S(1)}, bf16[256,256]{1,0:T(8,128)(2,1)S(1)}, u32[]{:S(2)}, u32[]{:S(2)}) collective-permute-start(bf16[256,256]{1,0:T(8,128)(2,1)S(1)} %split.32), channel_id=1, source_target_pairs={{0,2},{1,3},{2,0},{3,1},{4,6},{5,7},{6,4},{7,5},{8,10},{9,11},{10,... | collective-permute-start | bytes 393224 | tf_op jit(solution)/shard_map/ppermute | solution.py:566
  170.6 4.9 %collective-permute-done.12 = bf16[256,256]{1,0:T(8,128)(2,1)S(1)} collective-permute-done((bf16[256,256]{1,0:T(8,128)(2,1)S(1)}, bf16[256,256]{1,0:T(8,128)(2,1)S(1)}, u32[]{:S(2)}, u32[]{:S(2)}) %collective-permute-start.12) | collective-permute-done | bytes 131104 | tf_op jit(solution)/shard_map/ppermute | solution.py:566
  176.3 1.5 collective-permute-start.13
  177.7 1.5 collective-permute-start.15
  179.3 1.9 %collective-permute-done.13 = bf16[256,128]{1,0:T(8,128)(2,1)S(1)} collective-permute-done((bf16[256,128]{1,0:T(8,128)(2,1)S(1)}, bf16[256,128]{1,0:T(8,128)(2,1)S(1)}, u32[]{:S(2)}, u32[]{:S(2)}) %collective-permute-start.13) | collective-permute-done | bytes 65568 | tf_op jit(solution)/shard_map/ppermute | solution.py:566
  182.5 1.2 collective-permute-start.16
  183.8 2.5 %collective-permute-done.14 = bf16[2,256,128]{2,1,0:T(8,128)(2,1)S(1)} collective-permute-done((bf16[2,256,128]{2,1,0:T(8,128)(2,1)S(1)}, bf16[2,256,128]{2,1,0:T(8,128)(2,1)S(1)}, u32[]{:S(2)}, u32[]{:S(2)}) %collective-permute-start.14) | collective-permute-done | bytes 131104 | tf_op jit(solution)/shard_map/ppermute | solution.py:566
  187.7 1.9 collective-permute-done.17
  (50 shorter events, 10.5 us)
Async XLA Ops:
  33.2 16.0 %collective-permute-start = (f32[128,256]{1,0:T(8,128)}, f32[128,256]{1,0:T(8,128)S(1)}, u32[]{:S(2)}, u32[]{:S(2)}) collective-permute-start(f32[128,256]{1,0:T(8,128)} %get-tuple-element.30), channel_id=1, source_target_pairs={{0,1},{1,0},{2,3},{3,2},{4,5},{5,4},{6,7},{7,6},{8,9},{9,8},{10,11... | collective-permute-start | bytes 393224 | tf_op jit(solution)/shard_map/ppermute | solution.py:566
  36.3 13.1 %collective-permute-start.1 = (f32[128,256]{1,0:T(8,128)}, f32[128,256]{1,0:T(8,128)S(1)}, u32[]{:S(2)}, u32[]{:S(2)}) collective-permute-start(f32[128,256]{1,0:T(8,128)} %get-tuple-element.31), channel_id=1, source_target_pairs={{0,2},{1,3},{2,0},{3,1},{4,6},{5,7},{6,4},{7,5},{8,10},{9,11},{10,... | collective-permute-start | bytes 393224 | tf_op jit(solution)/shard_map/ppermute | solution.py:566
  38.9 10.5 %collective-permute-start.2 = (f32[128,256]{1,0:T(8,128)}, f32[128,256]{1,0:T(8,128)S(1)}, u32[]{:S(2)}, u32[]{:S(2)}) collective-permute-start(f32[128,256]{1,0:T(8,128)} %get-tuple-element.32), channel_id=1, source_target_pairs={{0,3},{1,2},{2,1},{3,0},{4,7},{5,6},{6,5},{7,4},{8,11},{9,10},{10,... | collective-permute-start | bytes 393224 | tf_op jit(solution)/shard_map/ppermute | solution.py:566
  39.5 9.9 %copy-start = (f32[128,256]{1,0:T(8,128)S(1)}, f32[128,256]{1,0:T(8,128)}, u32[]{:S(2)}) copy-start(f32[128,256]{1,0:T(8,128)} %get-tuple-element.29.refs_0_) | copy-start | bytes 393220
  49.6 15.2 %copy-start.1 = (bf16[128,256]{1,0:T(8,128)(2,1)}, bf16[128,256]{1,0:T(8,128)(2,1)S(1)}, u32[]{:S(2)}) copy-start(bf16[128,256]{1,0:T(8,128)(2,1)S(1)} %shard_map.88.rest_0_) | copy-start | bytes 196612
  49.6 15.2 %collective-permute-start.3 = (bf16[128,256]{1,0:T(8,128)(2,1)S(1)}, bf16[128,256]{1,0:T(8,128)(2,1)S(1)}, u32[]{:S(2)}, u32[]{:S(2)}) collective-permute-start(bf16[128,256]{1,0:T(8,128)(2,1)S(1)} %shard_map.88.rest_0_), channel_id=1, source_target_pairs={{0,1},{1,0},{2,3},{3,2},{4,5},{5,4},{6,7},{7,6},{8,9},{9,8},{10,11... | collective-permute-start | bytes 196616 | tf_op jit(solution)/shard_map/ppermute | solution.py:566
  51.7 13.2 %collective-permute-start.4 = (bf16[128,256]{1,0:T(8,128)(2,1)S(1)}, bf16[128,256]{1,0:T(8,128)(2,1)S(1)}, u32[]{:S(2)}, u32[]{:S(2)}) collective-permute-start(bf16[128,256]{1,0:T(8,128)(2,1)S(1)} %shard_map.88.rest_0_), channel_id=1, source_target_pairs={{0,2},{1,3},{2,0},{3,1},{4,6},{5,7},{6,4},{7,5},{8,10},{9,11},{10,... | collective-permute-start | bytes 196616 | tf_op jit(solution)/shard_map/ppermute | solution.py:566
  53.9 10.9 %collective-permute-start.5 = (bf16[128,256]{1,0:T(8,128)(2,1)S(1)}, bf16[128,256]{1,0:T(8,128)(2,1)S(1)}, u32[]{:S(2)}, u32[]{:S(2)}) collective-permute-start(bf16[128,256]{1,0:T(8,128)(2,1)S(1)} %shard_map.88.rest_0_), channel_id=1, source_target_pairs={{0,3},{1,2},{2,1},{3,0},{4,7},{5,6},{6,5},{7,4},{8,11},{9,10},{10,... | collective-permute-start | bytes 196616 | tf_op jit(solution)/shard_map/ppermute | solution.py:566
  64.8 0.6 copy-start.2
  64.8 0.6 copy-start.3
  64.9 0.6 copy-start.4
  131.8 4.4 %collective-permute-start.6 = (bf16[4096,256]{1,0:T(8,128)(2,1)}, bf16[4096,256]{1,0:T(8,128)(2,1)S(1)}, u32[]{:S(2)}, u32[]{:S(2)}) collective-permute-start(bf16[4096,256]{1,0:T(8,128)(2,1)} %get-tuple-element.37), channel_id=1, source_target_pairs={{0,4},{4,0},{8,12},{12,8},{16,20},{20,16},{24,28},{28,24},{1,5},{5... | collective-permute-start | bytes 6291464 | tf_op jit(solution)/shard_map/ppermute | solution.py:566
  138.4 14.0 %collective-permute-start.7 = (bf16[2,1024,128]{2,1,0:T(8,128)(2,1)S(1)}, bf16[2,1024,128]{2,1,0:T(8,128)(2,1)S(1)}, u32[]{:S(2)}, u32[]{:S(2)}) collective-permute-start(bf16[2,1024,128]{2,1,0:T(8,128)(2,1)S(1)} %slice_bitcast_fusion.5), channel_id=1, source_target_pairs={{0,8},{4,12},{8,0},{12,4},{16,24},{20,28},{24,16},{28,20},{1,9},{5... | collective-permute-start | bytes 1572872 | tf_op jit(solution)/shard_map/ppermute | solution.py:566
  139.9 13.7 %collective-permute-start.9 = (bf16[2,1024,128]{2,1,0:T(8,128)(2,1)S(1)}, bf16[2,1024,128]{2,1,0:T(8,128)(2,1)S(1)}, u32[]{:S(2)}, u32[]{:S(2)}) collective-permute-start(bf16[2,1024,128]{2,1,0:T(8,128)(2,1)S(1)} %slice_bitcast_fusion.3), channel_id=1, source_target_pairs={{0,16},{4,20},{8,24},{12,28},{16,0},{20,4},{24,8},{28,12},{1,17},{... | collective-permute-start | bytes 1572872 | tf_op jit(solution)/shard_map/ppermute | solution.py:566
  153.8 7.3 %collective-permute-start.10 = (bf16[1024,128]{1,0:T(8,128)(2,1)S(1)}, bf16[1024,128]{1,0:T(8,128)(2,1)S(1)}, u32[]{:S(2)}, u32[]{:S(2)}) collective-permute-start(bf16[1024,128]{1,0:T(8,128)(2,1)S(1)} %fusion.8), channel_id=1, source_target_pairs={{0,8},{4,12},{8,0},{12,4},{16,24},{20,28},{24,16},{28,20},{1,9},{5... | collective-permute-start | bytes 786440 | tf_op jit(solution)/shard_map/ppermute | solution.py:566
  154.5 7.0 %collective-permute-start.8 = (bf16[1024,128]{1,0:T(8,128)(2,1)S(1)}, bf16[1024,128]{1,0:T(8,128)(2,1)S(1)}, u32[]{:S(2)}, u32[]{:S(2)}) collective-permute-start(bf16[1024,128]{1,0:T(8,128)(2,1)S(1)} %fusion.7), channel_id=1, source_target_pairs={{0,16},{4,20},{8,24},{12,28},{16,0},{20,4},{24,8},{28,12},{1,17},{... | collective-permute-start | bytes 786440 | tf_op jit(solution)/shard_map/ppermute | solution.py:566
  161.6 6.4 %collective-permute-start.11 = (bf16[512,256]{1,0:T(8,128)(2,1)S(1)}, bf16[512,256]{1,0:T(8,128)(2,1)S(1)}, u32[]{:S(2)}, u32[]{:S(2)}) collective-permute-start(bf16[512,256]{1,0:T(8,128)(2,1)S(1)} %fusion.4), channel_id=1, source_target_pairs={{0,1},{1,0},{2,3},{3,2},{4,5},{5,4},{6,7},{7,6},{8,9},{9,8},{10,11... | collective-permute-start | bytes 786440 | tf_op jit(solution)/shard_map/ppermute | solution.py:566
  168.1 7.3 %collective-permute-start.12 = (bf16[256,256]{1,0:T(8,128)(2,1)S(1)}, bf16[256,256]{1,0:T(8,128)(2,1)S(1)}, u32[]{:S(2)}, u32[]{:S(2)}) collective-permute-start(bf16[256,256]{1,0:T(8,128)(2,1)S(1)} %split.32), channel_id=1, source_target_pairs={{0,2},{1,3},{2,0},{3,1},{4,6},{5,7},{6,4},{7,5},{8,10},{9,11},{10,... | collective-permute-start | bytes 393224 | tf_op jit(solution)/shard_map/ppermute | solution.py:566
  176.3 5.0 %collective-permute-start.13 = (bf16[256,128]{1,0:T(8,128)(2,1)S(1)}, bf16[256,128]{1,0:T(8,128)(2,1)S(1)}, u32[]{:S(2)}, u32[]{:S(2)}) collective-permute-start(bf16[256,128]{1,0:T(8,128)(2,1)S(1)} %get-tuple-element.49), channel_id=1, source_target_pairs={{0,8},{4,12},{8,0},{12,4},{16,24},{20,28},{24,16},{28,20},{1,9},{5... | collective-permute-start | bytes 196616 | tf_op jit(solution)/shard_map/ppermute | solution.py:566
  177.7 4.7 %collective-permute-start.15 = (bf16[256,128]{1,0:T(8,128)(2,1)S(1)}, bf16[256,128]{1,0:T(8,128)(2,1)S(1)}, u32[]{:S(2)}, u32[]{:S(2)}) collective-permute-start(bf16[256,128]{1,0:T(8,128)(2,1)S(1)} %get-tuple-element.48), channel_id=1, source_target_pairs={{0,16},{4,20},{8,24},{12,28},{16,0},{20,4},{24,8},{28,12},{1,17},{... | collective-permute-start | bytes 196616 | tf_op jit(solution)/shard_map/ppermute | solution.py:566
  181.2 5.0 %collective-permute-start.14 = (bf16[2,256,128]{2,1,0:T(8,128)(2,1)S(1)}, bf16[2,256,128]{2,1,0:T(8,128)(2,1)S(1)}, u32[]{:S(2)}, u32[]{:S(2)}) collective-permute-start(bf16[2,256,128]{2,1,0:T(8,128)(2,1)S(1)} %maximum_select_fusion.3), channel_id=1, source_target_pairs={{0,16},{4,20},{8,24},{12,28},{16,0},{20,4},{24,8},{28,12},{1,17},{... | collective-permute-start | bytes 393224 | tf_op jit(solution)/shard_map/ppermute | solution.py:566
  182.5 5.0 %collective-permute-start.16 = (bf16[2,256,128]{2,1,0:T(8,128)(2,1)S(1)}, bf16[2,256,128]{2,1,0:T(8,128)(2,1)S(1)}, u32[]{:S(2)}, u32[]{:S(2)}) collective-permute-start(bf16[2,256,128]{2,1,0:T(8,128)(2,1)S(1)} %maximum_select_fusion.5), channel_id=1, source_target_pairs={{0,8},{4,12},{8,0},{12,4},{16,24},{20,28},{24,16},{28,20},{1,9},{5... | collective-permute-start | bytes 393224 | tf_op jit(solution)/shard_map/ppermute | solution.py:566
  187.6 2.0 %collective-permute-start.17 = (bf16[2,2,256,256]{3,2,0,1:T(8,128)(2,1)S(1)}, bf16[2,2,256,256]{3,2,0,1:T(8,128)(2,1)S(1)}, u32[]{:S(2)}, u32[]{:S(2)}) collective-permute-start(bf16[2,2,256,256]{3,2,0,1:T(8,128)(2,1)S(1)} %get-tuple-element.43), channel_id=1, source_target_pairs={{0,4},{4,0},{8,12},{12,8},{16,20},{20,16},{24,28},{28,24},{1,5},{5... | collective-permute-start | bytes 1572872 | tf_op jit(solution)/shard_map/ppermute | solution.py:566

commit v6 on v5

--- a/solution.py
+++ b/solution.py
@@ -46,6 +46,12 @@
 
     def regroup(src_ref, dst_ref, scaled, first, number):
         at = pl.multiple_of(first * 16, 16)
+        if not scaled:
+            for t in range(number):
+                turned = jnp.swapaxes(src_ref[pl.ds(at + 16 * t, 16)], 0, 1)
+                for g in range(gb):
+                    dst_ref[pl.ds(at + 16 * t, 16), g * width : (g + 1) * width] = turned[g]
+            return
         tile = src_ref[pl.ds(at, 16 * number)].reshape(number, side, width)
         wide = jnp.concatenate([tile[t] for t in range(number)], axis=1)
         moved = jnp.dot(perm, wide, preferred_element_type=F32)
@@ -195,7 +201,7 @@
     ahead = exact(runs, earlier)
     total = jnp.sum(runs, axis=1, keepdims=True)
     start = exact(below, jnp.broadcast_to(total, (owners, OB)))[:, :1]
-    blocks = jnp.floor((total + (RD - 1.0)) * (1.0 / RD))
+    blocks = jnp.floor((total + (2 * RD - 1.0)) * (0.5 / RD))
     first = exact(below, jnp.broadcast_to(blocks, (owners, OB)))[:, :1]
     shift = start + ahead - base
     used = jnp.sum(runs, axis=0, keepdims=True)
@@ -216,7 +222,7 @@
     wide = item_ref.shape[2]
     number = lax.broadcasted_iota(jnp.int32, (1, wide), 1).astype(F32)
     inside = (number >= first) & (number < first + blocks)
-    done = (number - first) * RD
+    done = (number - first) * (2 * RD)
     pick = lambda value: jnp.sum(jnp.where(inside, value, 0.0), axis=0, keepdims=True)
     every = lambda value: jnp.sum(
         jnp.broadcast_to(value, (owners, wide)), axis=0, keepdims=True
@@ -232,33 +238,40 @@
         item_ref[0, i : i + 1, :] = value.astype(jnp.int32)
 
 
-def meta_kernel(here_ref, index_ref, frac_ref, pos_ref, meta_ref):
+def meta_kernel(here_ref, index_ref, frac_ref, pos_ref, addr_ref, table_ref, meta_ref):
     step = pl.program_id(0)
     _, units, half = pos_ref.shape
     parts = index_ref.shape[1] // half
     gb = units // parts
-    blocks = meta_ref.shape[2]
-    eighth = lax.broadcasted_iota(jnp.int32, (blocks, 1), 0)
-    lane_of = lax.broadcasted_iota(jnp.int32, (OB, 1), 0) % 8
+    blocks = meta_ref.shape[1]
+    low = lambda value: value.astype(F32).astype(BF16)
+    eighth = low(lax.broadcasted_iota(jnp.int32, (blocks, half), 0))
+    lane_of = low(lax.broadcasted_iota(jnp.int32, (OB, half), 0) % 8)
+    one, none = jnp.bfloat16(1.0), jnp.bfloat16(0.0)
     for u in range(units):
         g, h = u // parts, u % parts
         line = pl.ds(step * gb + g, 1)
         span = slice(h * half, (h + 1) * half)
-        value = index_ref[line, span].astype(F32) + frac_ref[line, span]
-        coarse = value.astype(BF16).astype(F32)
         pos = pos_ref[0, u : u + 1, :]
-        block = lax.shift_right_logical(pos, 3)
-        here = lane_of == (pos & 7)
-        spots = jnp.where(eighth == block, 1.0, 0.0).astype(BF16)
-        meta = jnp.zeros((blocks, OB), F32)
-        for term in (coarse, value - coarse):
-            meta = meta + lax.dot_general(
-                spots,
-                jnp.where(here, term, 0.0).astype(BF16),
-                (((1,), (1,)), ((), ())),
-                preferred_element_type=F32,
-            )
-        meta_ref[0, u] = meta
+        here = lane_of == low(pos & 7)
+        spots = jnp.where(eighth == low(lax.shift_right_logical(pos, 3)), one, none)
+        terms = [
+            jnp.where(here, low(index_ref[line, span]), none),
+            jnp.where(here, low(frac_ref[line, span]), none),
+        ]
+        meta_ref[u] = lax.dot_general(
+            jnp.concatenate([spots, spots], axis=1),
+            jnp.concatenate(terms, axis=1),
+            (((1,), (1,)), ((), ())),
+            preferred_element_type=F32,
+        )
+
+    def move(u, carry):
+        for i in range(blocks):
+            table_ref[0, pl.ds(addr_ref[0, u, i], 1), :] = meta_ref[u, i : i + 1, :]
+        return carry
+
+    lax.fori_loop(0, units, move, 0)
 
 
 def up_to(value, step):
@@ -310,20 +323,32 @@
     )(here, destination)
 
 
-def meta_call(here, row_index, fraction, pos, owners):
+def table_rows(units, half, owners):
+    return up_to((units * sort_sizes(half, owners)[0] + 2 * RD + 8) // 8, 8)
+
+
+def meta_call(here, row_index, fraction, pos, addr, owners):
     steps, units, half = pos.shape
     orients = row_index.shape[1]
     groups = steps * units * half // orients
     blocks = sort_sizes(half, owners)[2]
-    shape = (steps, units, blocks, OB)
+    shape = (steps, table_rows(units, half, owners), OB)
     table = pl.BlockSpec((groups, orients), lambda i, here: (here[1], 0))
     return pl.pallas_call(
         meta_kernel,
         grid_spec=pltpu.PrefetchScalarGridSpec(
             num_scalar_prefetch=1,
             grid=(steps,),
-            in_specs=[table, table, planned(pos.shape)],
+            in_specs=[
+                table,
+                table,
+                planned(pos.shape),
+                pl.BlockSpec(
+                    (1,) + addr.shape[1:], lambda i, here: (i, 0, 0), memory_space=pltpu.SMEM
+                ),
+            ],
             out_specs=planned(shape),
+            scratch_shapes=[pltpu.VMEM((units, blocks, OB), F32)],
         ),
         out_shape=jax.ShapeDtypeStruct(shape, F32),
         compiler_params=pltpu.CompilerParams(vmem_limit_bytes=60 * MB),
@@ -332,12 +357,12 @@
             bytes_accessed=8 * steps * units * blocks * OB,
             transcendentals=0,
         ),
-    )(here, row_index, fraction, pos)
+    )(here, row_index, fraction, pos, addr)
 
 
 def insert_kernel(me_ref, addr_ref, item_ref, x_ref, pos_ref, meta_ref, blk_ref, *rest):
-    *post_refs, send_ref, keep_ref = rest[:-10]
-    post_t, spread_ref, cols_ref, slice_a, slice_b, buf_s, buf_m, volume, stage, sem = rest[-10:]
+    *post_refs, send_ref, keep_ref = rest[:-9]
+    post_t, spread_ref, cols_ref, slice_a, slice_b, buf_s, volume, stage, sem = rest[-9:]
     step = pl.program_id(0)
     count = x_ref.shape[0]
     orients = post_t.shape[0]
@@ -366,8 +391,8 @@
         for b in range(orients // OB):
             post_t[b * OB : (b + 1) * OB] = spread_ref[:, b * OB : (b + 1) * OB].T.astype(BF16)
 
-    tail = pl.ds(pl.multiple_of(item_ref[0, 4, 0] * 8, 8), RD)
-    buf_s[tail, :] = jnp.zeros((RD, width), F32)
+    tail = pl.ds(pl.multiple_of(item_ref[0, 4, 0] * 8, 8), 2 * RD)
+    buf_s[tail, :] = jnp.zeros((2 * RD, width), F32)
     one, none = jnp.bfloat16(1.0), jnp.bfloat16(0.0)
     slots, sure, _ = sort_sizes(half, volume.shape[0] // RD)
     per = slice_a.shape[1] // width
@@ -391,7 +416,6 @@
         for i in range(size // 8):
             at = addr_ref[0, u, base // 8 + i]
             buf_s[pl.ds(pl.multiple_of(at * 8, 8), 8), :] = rows[8 * i : 8 * i + 8]
-            buf_m[pl.ds(at, 1), :] = meta_ref[0, u, pl.ds(base // 8 + i, 1), :]
 
     def sort(q, src_ref):
         for g in range(per):
@@ -442,12 +466,12 @@
         sort(number - 1, slice_a)
         rest_of(number - 1, slice_a)
 
-    bins = lax.broadcasted_iota(jnp.int32, (RD, RD), 0).astype(F32).astype(BF16)
+    bins = lax.broadcasted_iota(jnp.int32, (RD, 2 * RD), 0).astype(F32).astype(BF16)
     side = RD // 2
     at_lane = lax.broadcasted_iota(jnp.int32, (side // 8, side), 1) // 8
     own_lane = at_lane == lax.broadcasted_iota(jnp.int32, (side // 8, side), 0)
-    line = lax.broadcasted_iota(jnp.int32, (1, RD), 1)
-    together = 8
+    line = lax.broadcasted_iota(jnp.int32, (1, 2 * RD), 1)
+    together = 4
 
     def some_items(q, carry):
         for u in range(together):
@@ -455,17 +479,17 @@
             owner, at, left = item_ref[0, 0, j], item_ref[0, 1, j], item_ref[0, 2, j]
             places = [
                 jnp.sum(
-                    jnp.where(own_lane, buf_m[pl.ds(at + h * (side // 8), side // 8), :], 0.0),
+                    jnp.where(own_lane, meta_ref[0, pl.ds(at + h * (side // 8), side // 8), :], 0.0),
                     axis=0,
                     keepdims=True,
                 )
-                for h in range(2)
+                for h in range(4)
             ]
             place = jnp.where(line < left, jnp.concatenate(places, axis=1), -9.0)
             whole = jnp.floor(place)
             apart = (bins - whole.astype(BF16)) - (place - whole).astype(BF16)
             weights = jnp.maximum(one - jnp.abs(apart), none)
-            values = buf_s[pl.ds(pl.multiple_of(at * 8, 8), RD), :].astype(BF16)
+            values = buf_s[pl.ds(pl.multiple_of(at * 8, 8), 2 * RD), :].astype(BF16)
             goal = pl.ds(pl.multiple_of(owner * RD, RD), RD)
             volume[goal, :] += jnp.dot(weights, values, preferred_element_type=F32)
         return carry
@@ -506,8 +530,8 @@
     best = 1
     for gb in range(1, groups + 1):
         units = gb * (orients // half)
-        rows = units * slots + RD + 8
-        need = rows * (width * 4 + OB // 2) + 4 * count * gb * width + units * blocks * OB * 8
+        rows = units * slots + 2 * RD + 8
+        need = rows * (width * 4 + OB) + 4 * count * gb * width
         if groups % gb == 0 and need <= room:
             best = gb
     return best
@@ -520,7 +544,7 @@
     width = length // (steps * gb)
     total = owners * RD
     share = posts[0].shape[0]
-    rows = units * sort_sizes(half, owners)[0] + RD + 8
+    rows = units * sort_sizes(half, owners)[0] + 2 * RD + 8
     smem = pl.BlockSpec(memory_space=pltpu.SMEM)
     block = lambda shape, **kw: pl.BlockSpec(
         (1,) + shape[1:], lambda i: (i,) + (0,) * (len(shape) - 1), **kw
@@ -547,7 +571,6 @@
             pltpu.VMEM((orients, group_pair(gb) * width), BF16),
             pltpu.VMEM((orients, group_pair(gb) * width), BF16),
             pltpu.VMEM((rows, width), F32),
-            pltpu.VMEM((rows // 8, OB), F32),
             pltpu.VMEM((total, width), F32),
             pltpu.VMEM((2, 512, width), BF16),
             pltpu.SemaphoreType.DMA((2,)),
@@ -589,55 +612,50 @@
     parts = [own] + [flip(scores[k], "slab", k) for k in range(1, slab_size)]
     post = softmax_call(parts)
     post, pos = lax.optimization_barrier((post, pos))
-    meta = meta_call(here, row_index, fraction, pos, devices)
+    meta = meta_call(here, row_index, fraction, pos, addr, devices)
     posts = [post] + [flip(post, "slab", k) for k in range(1, slab_size)]
     send, keep = insert_call(
         slab_me, addr, items, flat, pos, meta, blocks, posts, orients, devices
     )
 
-    def merge(kept, got):
-        return kept.astype(F32) + got.astype(F32)
-
-    total = merge(keep, flip(send, "dom", dom_bits[0]))
+    def added(terms):
+        return functools.reduce(jnp.add, [term.astype(F32) for term in terms])
+
+    def halve(terms, axis_name, axis, bit):
+        size = terms[0].shape[axis] // 2
+        pick = lambda term, at: lax.slice_in_dim(term, at, at + size, axis=axis)
+        sent = added([pick(term, size) for term in terms]).astype(BF16)
+        return [pick(term, 0) for term in terms] + [flip(sent, axis_name, bit)]
+
+    terms = [keep, flip(send, "dom", dom_bits[0])]
     rest = dom_bits[1:]
-    total = total.reshape((2,) * len(rest) + (slab_size * RD, width))
-    halves = []
-    for part, order in ((0, rest), (1, rest[::-1])):
-        value = total[..., part * OB : (part + 1) * OB]
-        axes = list(rest)
-        for bit in order:
-            axis = axes.index(bit)
-            axes.pop(axis)
-            kept = lax.index_in_dim(value, 0, axis, keepdims=False)
-            sent = lax.index_in_dim(value, 1, axis, keepdims=False)
-            value = merge(kept, flip(sent.astype(BF16), "dom", bit))
-        halves.append(value)
-    value = jnp.concatenate(halves, axis=1)
+    terms = [term.reshape((2,) * len(rest) + (slab_size * RD, width)) for term in terms]
+    columns = [[term[..., part * OB : (part + 1) * OB] for term in terms] for part in range(2)]
+    for stage in range(len(rest)):
+        for part in range(2):
+            axis = stage if part == 0 else len(rest) - 1 - stage
+            columns[part] = halve(columns[part], "dom", axis, rest[axis])
+    columns = [[term.reshape(slab_size * RD, OB) for term in terms] for terms in columns]
+    terms = [jnp.concatenate(pair, axis=1) for pair in zip(*columns)]
     for bit in slab_bits:
-        near, far = jnp.split(value, 2, axis=0)
-        value = merge(near, flip(far.astype(BF16), "slab", bit))
-    volume = value
+        terms = halve(terms, "slab", 0, bit)
+    volume = added(terms)
 
     own = volume.astype(BF16)
-    columns = []
-    for part, order in ((0, rest), (1, rest[::-1])):
-        value = own[:, part * OB : (part + 1) * OB]
-        done = []
-        for bit in order:
-            got = flip(value, "dom", bit)
-            axis = len([b for b in done if b > bit])
-            done.append(bit)
-            mine_low = dom_pos & bit == 0
-            value = jnp.where(
-                mine_low, jnp.stack([value, got], axis), jnp.stack([got, value], axis)
-            )
-        columns.append(value)
-    value = jnp.concatenate(columns, axis=-1)
+    plane = [own] + [flip(own, "dom", 2 * k) for k in range(1, dom_size // 2)]
+    chip = dom_pos // 2
+    placed = []
+    for k in range(dom_size // 2):
+        value = plane[0]
+        for j in range(1, dom_size // 2):
+            value = jnp.where(chip ^ j == k, plane[j], value)
+        placed.append(value)
+    value = jnp.stack(placed)
     got = flip(value, "dom", dom_bits[0])
     value = jnp.where(
         dom_pos & dom_bits[0] == 0,
-        jnp.stack([value, got], len(rest)),
-        jnp.stack([got, value], len(rest)),
+        jnp.stack([value, got], 1),
+        jnp.stack([got, value], 1),
     )
     return volume, value.reshape(dom_size * RD, width)
 

time: 190 us -> 191 us (level)
  Pallas kernels: 119 us -> 123 us
    pallas_call x1, Pallas kernels: 10.7 us -> 20.7 us  [meta_call(): pl.pallas_call(meta_kernel, grid_spec=pltpu.PrefetchScalarGridSpec(num_sc...]
    pallas_call x1, Pallas kernels: 66.3 us -> 61.7 us  [insert_call(): pl.pallas_call(insert_kernel, grid=(steps,), out_shape=[jax.ShapeDtypeStr...]
    convert_element_type x0 -> x5, other arithmetic: none -> 2.85 us  [halve(): sent = added([pick(term, size) for term in terms]).astype(BF16)]
    add x5 -> x0, other arithmetic: 2.38 us -> none  [merge(): return kept.astype(F32) + got.astype(F32)]
    ppermute x18 -> x17, starting transfers between devices: 24.6 us -> 22.7 us  [flip(): return lax.ppermute(value, axis, [(i, i ^ bit) for i in range(size)])]
    ppermute x18 -> x17, waiting for transfers between devices: 39.8 us -> 38.6 us  [flip(): return lax.ppermute(value, axis, [(i, i ^ bit) for i in range(size)])]
  transfers between devices with their start and end apart: 18 -> 17, of which waited for: 12 -> 12; matrix products, arithmetic and copies ran while one was open for 0% -> 0% of each run, Pallas kernels for 11% -> 16%
where the time goes in v6:
time: 191 us; the launch traced here: 192 us
  Pallas kernels  123 us (64%)
  waiting for transfers between devices  38.6 us (20%)
  starting transfers between devices  22.7 us (12%)
  other arithmetic  4.62 us (2%)
    pallas_call x1, Pallas kernels, insert_call(): pl.pallas_call(insert_kernel, grid=(steps,), out_shape=[jax.ShapeDtypeStr...  61.7 us
    ppermute x17, waiting for transfers between devices, flip(): return lax.ppermute(value, axis, [(i, i ^ bit) for i in range(size)])  38.6 us
    pallas_call x1, Pallas kernels, score_call(): pl.pallas_call(score_kernel, grid=(groups // gb,), out_shape=[jax.ShapeDt...  30.9 us
    ppermute x17, starting transfers between devices, flip(): return lax.ppermute(value, axis, [(i, i ^ bit) for i in range(size)])  22.7 us
    pallas_call x1, Pallas kernels, meta_call(): pl.pallas_call(meta_kernel, grid_spec=pltpu.PrefetchScalarGridSpec(num_sc...  20.7 us
    pallas_call x1, Pallas kernels, plan_call(): pl.pallas_call(functools.partial(plan_kernel, sizes=mesh_sizes), grid_spe...  9.71 us
  transfers between devices with their start and end apart: 17, of which 12 were waited for; matrix products, arithmetic and copies ran while one was open for 0% of the time, Pallas kernels for 16%

profile of v6, /device:TPU:0, one launch (start us, length us, event | category | flops | bytes accessed | tf_op | source)
XLA Modules:
  0.0 191.5 jit_solution(3079333591782868332)
XLA Ops:
  0.6 30.9 %shard_map.86 = (bf16[512,20480]{1,0:T(8,128)(2,1)}, f32[128,256]{1,0:T(8,128)}, f32[128,256]{1,0:T(8,128)}, f32[128,256]{1,0:T(8,128)}, f32[128,256]{1,0:T(8,128)}) custom-call(s32[1]{0:T(128)} %bitcast.me_ref, f32[80]{0:T(128)} %noise_ref.1, bf16[512,80,256]{2,1,0:T(8,128)(2,1)} %x_ref.1, bf16[512,80,256]{2,1,0:T(8,128)(2,1)} %r_ref.1, s32[2,512]{1,0:T(2,128)} %bitcast.47), custom_call_target="tpu_custom_call" | custom-call | flops 21474836480 | bytes 62914560 | tf_op jit(solution)/shard_map/pallas_call | solution.py:107
  31.5 3.1 %collective-permute-start = (f32[128,256]{1,0:T(8,128)}, f32[128,256]{1,0:T(8,128)S(1)}, u32[]{:S(2)}, u32[]{:S(2)}) collective-permute-start(f32[128,256]{1,0:T(8,128)} %get-tuple-element.30), channel_id=1, source_target_pairs={{0,1},{1,0},{2,3},{3,2},{4,5},{5,4},{6,7},{7,6},{8,9},{9,8},{10,11... | collective-permute-start | bytes 393224 | tf_op jit(solution)/shard_map/ppermute | solution.py:589
  34.6 2.6 %collective-permute-start.1 = (f32[128,256]{1,0:T(8,128)}, f32[128,256]{1,0:T(8,128)S(1)}, u32[]{:S(2)}, u32[]{:S(2)}) collective-permute-start(f32[128,256]{1,0:T(8,128)} %get-tuple-element.31), channel_id=1, source_target_pairs={{0,2},{1,3},{2,0},{3,1},{4,6},{5,7},{6,4},{7,5},{8,10},{9,11},{10,... | collective-permute-start | bytes 393224 | tf_op jit(solution)/shard_map/ppermute | solution.py:589
  37.8 9.7 %shard_map.87 = (s32[4,40,256]{2,1,0:T(8,128)}, s32[4,40,128]{2,1,0:T(8,128)}, s32[4,5,128]{2,1,0:T(8,128)}) custom-call(s32[2]{0:T(128)} %pad_add_fusion.here_ref, s32[320,512]{1,0:T(8,128)} %dest_ref.1), custom_call_target="tpu_custom_call" | custom-call | flops 2684354560 | bytes 327680 | tf_op jit(solution)/shard_map/pallas_call | solution.py:303
  47.9 2.0 %collective-permute-start.3 = (bf16[128,256]{1,0:T(8,128)(2,1)S(1)}, bf16[128,256]{1,0:T(8,128)(2,1)S(1)}, u32[]{:S(2)}, u32[]{:S(2)}) collective-permute-start(bf16[128,256]{1,0:T(8,128)(2,1)S(1)} %shard_map.88.rest_0_), channel_id=1, source_target_pairs={{0,1},{1,0},{2,3},{3,2},{4,5},{5,4},{6,7},{7,6},{8,9},{9,8},{10,11... | collective-permute-start | bytes 196616 | tf_op jit(solution)/shard_map/ppermute | solution.py:589
  50.0 2.2 %collective-permute-start.4 = (bf16[128,256]{1,0:T(8,128)(2,1)S(1)}, bf16[128,256]{1,0:T(8,128)(2,1)S(1)}, u32[]{:S(2)}, u32[]{:S(2)}) collective-permute-start(bf16[128,256]{1,0:T(8,128)(2,1)S(1)} %shard_map.88.rest_0_), channel_id=1, source_target_pairs={{0,2},{1,3},{2,0},{3,1},{4,6},{5,7},{6,4},{7,5},{8,10},{9,11},{10,... | collective-permute-start | bytes 196616 | tf_op jit(solution)/shard_map/ppermute | solution.py:589
  52.4 20.7 %shard_map.89.meta_ref = f32[4,2472,128]{2,1,0:T(8,128)} custom-call(s32[2]{0:T(128)} %pad_add_fusion.here_ref, s32[320,512]{1,0:T(8,128)} %index_ref.1, f32[320,512]{1,0:T(8,128)} %frac_ref.1, s32[4,40,256]{2,1,0:T(8,128)} %get-tuple-element.34.pos_ref, s32[4,40,128]{2,1,0:T(8,128)} %get-tuple-element.26.addr_ref), custom_call_target="tpu_custom_call" | custom-call | flops 3019898880 | bytes 11796480 | tf_op jit(solution)/shard_map/pallas_call | solution.py:337
  73.8 61.7 %shard_map.90 = (bf16[4096,256]{1,0:T(8,128)(2,1)}, bf16[4096,256]{1,0:T(8,128)(2,1)}) custom-call(s32[1]{0:T(128)} %bitcast.me_ref, s32[4,40,128]{2,1,0:T(8,128)} %get-tuple-element.26.addr_ref, s32[4,5,128]{2,1,0:T(8,128)} %get-tuple-element.27.item_ref, bf16[512,20480]{1,0:T(8,128)(2,1)} %get-tuple-element.28.x_ref, ...), custom_call_target="tpu_custom_call" | custom-call | flops 42949672960 | bytes 20971520 | tf_op jit(solution)/shard_map/pallas_call | solution.py:552
  135.5 4.4 %collective-permute-done.6 = bf16[4096,256]{1,0:T(8,128)(2,1)S(1)} collective-permute-done((bf16[4096,256]{1,0:T(8,128)(2,1)}, bf16[4096,256]{1,0:T(8,128)(2,1)S(1)}, u32[]{:S(2)}, u32[]{:S(2)}) %collective-permute-start.6) | collective-permute-done | bytes 2097184 | tf_op jit(solution)/shard_map/ppermute | solution.py:589
  141.1 1.2 add_convert_fusion
  142.3 1.6 collective-permute-start.7
  143.9 1.5 collective-permute-start.8
  145.4 10.9 %collective-permute-done.7 = bf16[1,2,1024,128]{3,2,1,0:T(8,128)(2,1)S(1)} collective-permute-done((bf16[1,2,1024,128]{3,2,1,0:T(8,128)(2,1)S(1)}, bf16[1,2,1024,128]{3,2,1,0:T(8,128)(2,1)S(1)}, u32[]{:S(2)}, u32[]{:S(2)}) %collective-permute-start.7) | collective-permute-done | bytes 524320 | tf_op jit(solution)/shard_map/ppermute | solution.py:589
  156.3 1.3 collective-permute-done.8
  157.8 1.5 collective-permute-start.9
  159.9 5.1 %collective-permute-done.9 = bf16[1,1,1024,128]{3,2,1,0:T(8,128)(2,1)S(1)} collective-permute-done((bf16[1,1,1024,128]{3,2,1,0:T(8,128)(2,1)S(1)}, bf16[1,1,1024,128]{3,2,1,0:T(8,128)(2,1)S(1)}, u32[]{:S(2)}, u32[]{:S(2)}) %collective-permute-start.9) | collective-permute-done | bytes 262176 | tf_op jit(solution)/shard_map/ppermute | solution.py:589
  165.0 1.2 collective-permute-done.10
  167.6 5.3 %collective-permute-done.11 = bf16[512,256]{1,0:T(8,128)(2,1)S(1)} collective-permute-done((bf16[512,256]{1,0:T(8,128)(2,1)S(1)}, bf16[512,256]{1,0:T(8,128)(2,1)S(1)}, u32[]{:S(2)}, u32[]{:S(2)}) %collective-permute-start.11) | collective-permute-done | bytes 262176 | tf_op jit(solution)/shard_map/ppermute | solution.py:589
  173.0 2.5 %collective-permute-start.12 = (bf16[256,256]{1,0:T(8,128)(2,1)S(1)}, bf16[256,256]{1,0:T(8,128)(2,1)S(1)}, u32[]{:S(2)}, u32[]{:S(2)}) collective-permute-start(bf16[256,256]{1,0:T(8,128)(2,1)S(1)} %add_convert_fusion.5), channel_id=1, source_target_pairs={{0,2},{1,3},{2,0},{3,1},{4,6},{5,7},{6,4},{7,5},{8,10},{9,11},{10,... | collective-permute-start | bytes 393224 | tf_op jit(solution)/shard_map/ppermute | solution.py:589
  175.5 4.8 %collective-permute-done.12 = bf16[256,256]{1,0:T(8,128)(2,1)S(1)} collective-permute-done((bf16[256,256]{1,0:T(8,128)(2,1)S(1)}, bf16[256,256]{1,0:T(8,128)(2,1)S(1)}, u32[]{:S(2)}, u32[]{:S(2)}) %collective-permute-start.12) | collective-permute-done | bytes 131104 | tf_op jit(solution)/shard_map/ppermute | solution.py:589
  181.7 1.5 collective-permute-start.14
  183.2 1.4 collective-permute-start.15
  184.6 2.5 %collective-permute-done.13 = bf16[256,256]{1,0:T(8,128)(2,1)S(1)} collective-permute-done((bf16[256,256]{1,0:T(8,128)(2,1)S(1)}, bf16[256,256]{1,0:T(8,128)(2,1)S(1)}, u32[]{:S(2)}, u32[]{:S(2)}) %collective-permute-start.13) | collective-permute-done | bytes 131104 | tf_op jit(solution)/shard_map/ppermute | solution.py:589
  188.4 1.9 collective-permute-done.16
  (42 shorter events, 9.5 us)
Async XLA Ops:
  31.5 16.0 %collective-permute-start = (f32[128,256]{1,0:T(8,128)}, f32[128,256]{1,0:T(8,128)S(1)}, u32[]{:S(2)}, u32[]{:S(2)}) collective-permute-start(f32[128,256]{1,0:T(8,128)} %get-tuple-element.30), channel_id=1, source_target_pairs={{0,1},{1,0},{2,3},{3,2},{4,5},{5,4},{6,7},{7,6},{8,9},{9,8},{10,11... | collective-permute-start | bytes 393224 | tf_op jit(solution)/shard_map/ppermute | solution.py:589
  34.6 13.1 %collective-permute-start.1 = (f32[128,256]{1,0:T(8,128)}, f32[128,256]{1,0:T(8,128)S(1)}, u32[]{:S(2)}, u32[]{:S(2)}) collective-permute-start(f32[128,256]{1,0:T(8,128)} %get-tuple-element.31), channel_id=1, source_target_pairs={{0,2},{1,3},{2,0},{3,1},{4,6},{5,7},{6,4},{7,5},{8,10},{9,11},{10,... | collective-permute-start | bytes 393224 | tf_op jit(solution)/shard_map/ppermute | solution.py:589
  37.2 10.6 %collective-permute-start.2 = (f32[128,256]{1,0:T(8,128)}, f32[128,256]{1,0:T(8,128)S(1)}, u32[]{:S(2)}, u32[]{:S(2)}) collective-permute-start(f32[128,256]{1,0:T(8,128)} %get-tuple-element.32), channel_id=1, source_target_pairs={{0,3},{1,2},{2,1},{3,0},{4,7},{5,6},{6,5},{7,4},{8,11},{9,10},{10,... | collective-permute-start | bytes 393224 | tf_op jit(solution)/shard_map/ppermute | solution.py:589
  37.8 9.9 %copy-start = (f32[128,256]{1,0:T(8,128)S(1)}, f32[128,256]{1,0:T(8,128)}, u32[]{:S(2)}) copy-start(f32[128,256]{1,0:T(8,128)} %get-tuple-element.29.refs_0_) | copy-start | bytes 393220
  47.9 25.2 %copy-start.1 = (bf16[128,256]{1,0:T(8,128)(2,1)}, bf16[128,256]{1,0:T(8,128)(2,1)S(1)}, u32[]{:S(2)}) copy-start(bf16[128,256]{1,0:T(8,128)(2,1)S(1)} %shard_map.88.rest_0_) | copy-start | bytes 196612
  47.9 25.2 %collective-permute-start.3 = (bf16[128,256]{1,0:T(8,128)(2,1)S(1)}, bf16[128,256]{1,0:T(8,128)(2,1)S(1)}, u32[]{:S(2)}, u32[]{:S(2)}) collective-permute-start(bf16[128,256]{1,0:T(8,128)(2,1)S(1)} %shard_map.88.rest_0_), channel_id=1, source_target_pairs={{0,1},{1,0},{2,3},{3,2},{4,5},{5,4},{6,7},{7,6},{8,9},{9,8},{10,11... | collective-permute-start | bytes 196616 | tf_op jit(solution)/shard_map/ppermute | solution.py:589
  50.0 23.1 %collective-permute-start.4 = (bf16[128,256]{1,0:T(8,128)(2,1)S(1)}, bf16[128,256]{1,0:T(8,128)(2,1)S(1)}, u32[]{:S(2)}, u32[]{:S(2)}) collective-permute-start(bf16[128,256]{1,0:T(8,128)(2,1)S(1)} %shard_map.88.rest_0_), channel_id=1, source_target_pairs={{0,2},{1,3},{2,0},{3,1},{4,6},{5,7},{6,4},{7,5},{8,10},{9,11},{10,... | collective-permute-start | bytes 196616 | tf_op jit(solution)/shard_map/ppermute | solution.py:589
  52.2 20.9 %collective-permute-start.5 = (bf16[128,256]{1,0:T(8,128)(2,1)S(1)}, bf16[128,256]{1,0:T(8,128)(2,1)S(1)}, u32[]{:S(2)}, u32[]{:S(2)}) collective-permute-start(bf16[128,256]{1,0:T(8,128)(2,1)S(1)} %shard_map.88.rest_0_), channel_id=1, source_target_pairs={{0,3},{1,2},{2,1},{3,0},{4,7},{5,6},{6,5},{7,4},{8,11},{9,10},{10,... | collective-permute-start | bytes 196616 | tf_op jit(solution)/shard_map/ppermute | solution.py:589
  73.1 0.6 copy-start.3
  73.1 0.6 copy-start.4
  73.1 0.6 copy-start.5
  135.4 9.9 %copy-start.2 = (bf16[4096,256]{1,0:T(8,128)(2,1)S(1)}, bf16[4096,256]{1,0:T(8,128)(2,1)}, u32[]{:S(2)}) copy-start(bf16[4096,256]{1,0:T(8,128)(2,1)} %get-tuple-element.36) | copy-start | bytes 6291460
  135.5 4.4 %collective-permute-start.6 = (bf16[4096,256]{1,0:T(8,128)(2,1)}, bf16[4096,256]{1,0:T(8,128)(2,1)S(1)}, u32[]{:S(2)}, u32[]{:S(2)}) collective-permute-start(bf16[4096,256]{1,0:T(8,128)(2,1)} %get-tuple-element.37), channel_id=1, source_target_pairs={{0,4},{4,0},{8,12},{12,8},{16,20},{20,16},{24,28},{28,24},{1,5},{5... | collective-permute-start | bytes 6291464 | tf_op jit(solution)/shard_map/ppermute | solution.py:589
  142.3 14.0 %collective-permute-start.7 = (bf16[1,2,1024,128]{3,2,1,0:T(8,128)(2,1)S(1)}, bf16[1,2,1024,128]{3,2,1,0:T(8,128)(2,1)S(1)}, u32[]{:S(2)}, u32[]{:S(2)}) collective-permute-start(bf16[1,2,1024,128]{3,2,1,0:T(8,128)(2,1)S(1)} %add_convert_fusion.1), channel_id=1, source_target_pairs={{0,8},{4,12},{8,0},{12,4},{16,24},{20,28},{24,16},{28,20},{1,9},{5... | collective-permute-start | bytes 1572872 | tf_op jit(solution)/shard_map/ppermute | solution.py:589
  143.9 13.7 %collective-permute-start.8 = (bf16[2,1,1024,128]{3,2,1,0:T(8,128)(2,1)S(1)}, bf16[2,1,1024,128]{3,2,1,0:T(8,128)(2,1)S(1)}, u32[]{:S(2)}, u32[]{:S(2)}) collective-permute-start(bf16[2,1,1024,128]{3,2,1,0:T(8,128)(2,1)S(1)} %add_convert_fusion), channel_id=1, source_target_pairs={{0,16},{4,20},{8,24},{12,28},{16,0},{20,4},{24,8},{28,12},{1,17},{... | collective-permute-start | bytes 1572872 | tf_op jit(solution)/shard_map/ppermute | solution.py:589
  157.8 7.3 %collective-permute-start.9 = (bf16[1,1,1024,128]{3,2,1,0:T(8,128)(2,1)S(1)}, bf16[1,1,1024,128]{3,2,1,0:T(8,128)(2,1)S(1)}, u32[]{:S(2)}, u32[]{:S(2)}) collective-permute-start(bf16[1,1,1024,128]{3,2,1,0:T(8,128)(2,1)S(1)} %get-tuple-element.41), channel_id=1, source_target_pairs={{0,16},{4,20},{8,24},{12,28},{16,0},{20,4},{24,8},{28,12},{1,17},{... | collective-permute-start | bytes 786440 | tf_op jit(solution)/shard_map/ppermute | solution.py:589
  159.3 6.9 %collective-permute-start.10 = (bf16[1,1,1024,128]{3,2,1,0:T(8,128)(2,1)S(1)}, bf16[1,1,1024,128]{3,2,1,0:T(8,128)(2,1)S(1)}, u32[]{:S(2)}, u32[]{:S(2)}) collective-permute-start(bf16[1,1,1024,128]{3,2,1,0:T(8,128)(2,1)S(1)} %get-tuple-element.40), channel_id=1, source_target_pairs={{0,8},{4,12},{8,0},{12,4},{16,24},{20,28},{24,16},{28,20},{1,9},{5... | collective-permute-start | bytes 786440 | tf_op jit(solution)/shard_map/ppermute | solution.py:589
  166.4 6.4 %collective-permute-start.11 = (bf16[512,256]{1,0:T(8,128)(2,1)S(1)}, bf16[512,256]{1,0:T(8,128)(2,1)S(1)}, u32[]{:S(2)}, u32[]{:S(2)}) collective-permute-start(bf16[512,256]{1,0:T(8,128)(2,1)S(1)} %add_convert_fusion.2), channel_id=1, source_target_pairs={{0,1},{1,0},{2,3},{3,2},{4,5},{5,4},{6,7},{7,6},{8,9},{9,8},{10,11... | collective-permute-start | bytes 786440 | tf_op jit(solution)/shard_map/ppermute | solution.py:589
  173.0 7.3 %collective-permute-start.12 = (bf16[256,256]{1,0:T(8,128)(2,1)S(1)}, bf16[256,256]{1,0:T(8,128)(2,1)S(1)}, u32[]{:S(2)}, u32[]{:S(2)}) collective-permute-start(bf16[256,256]{1,0:T(8,128)(2,1)S(1)} %add_convert_fusion.5), channel_id=1, source_target_pairs={{0,2},{1,3},{2,0},{3,1},{4,6},{5,7},{6,4},{7,5},{8,10},{9,11},{10,... | collective-permute-start | bytes 393224 | tf_op jit(solution)/shard_map/ppermute | solution.py:589
  181.1 6.0 %collective-permute-start.13 = (bf16[256,256]{1,0:T(8,128)(2,1)S(1)}, bf16[256,256]{1,0:T(8,128)(2,1)S(1)}, u32[]{:S(2)}, u32[]{:S(2)}) collective-permute-start(bf16[256,256]{1,0:T(8,128)(2,1)S(1)} %get-tuple-element.38), channel_id=1, source_target_pairs={{0,24},{4,28},{8,16},{12,20},{16,8},{20,12},{24,0},{28,4},{1,25},{... | collective-permute-start | bytes 393224 | tf_op jit(solution)/shard_map/ppermute | solution.py:589
  181.7 6.4 %collective-permute-start.14 = (bf16[256,256]{1,0:T(8,128)(2,1)S(1)}, bf16[256,256]{1,0:T(8,128)(2,1)S(1)}, u32[]{:S(2)}, u32[]{:S(2)}) collective-permute-start(bf16[256,256]{1,0:T(8,128)(2,1)S(1)} %get-tuple-element.38), channel_id=1, source_target_pairs={{0,16},{4,20},{8,24},{12,28},{16,0},{20,4},{24,8},{28,12},{1,17},{... | collective-permute-start | bytes 393224 | tf_op jit(solution)/shard_map/ppermute | solution.py:589
  183.2 5.0 %collective-permute-start.15 = (bf16[256,256]{1,0:T(8,128)(2,1)S(1)}, bf16[256,256]{1,0:T(8,128)(2,1)S(1)}, u32[]{:S(2)}, u32[]{:S(2)}) collective-permute-start(bf16[256,256]{1,0:T(8,128)(2,1)S(1)} %get-tuple-element.38), channel_id=1, source_target_pairs={{0,8},{4,12},{8,0},{12,4},{16,24},{20,28},{24,16},{28,20},{1,9},{5... | collective-permute-start | bytes 393224 | tf_op jit(solution)/shard_map/ppermute | solution.py:589
  188.3 2.0 %collective-permute-start.16 = (bf16[4,256,256]{2,1,0:T(8,128)(2,1)S(1)}, bf16[4,256,256]{2,1,0:T(8,128)(2,1)S(1)}, u32[]{:S(2)}, u32[]{:S(2)}) collective-permute-start(bf16[4,256,256]{2,1,0:T(8,128)(2,1)S(1)} %get-tuple-element.47), channel_id=1, source_target_pairs={{0,4},{4,0},{8,12},{12,8},{16,20},{20,16},{24,28},{28,24},{1,5},{5... | collective-permute-start | bytes 1572872 | tf_op jit(solution)/shard_map/ppermute | solution.py:589

commit v7 on v6

--- a/solution.py
+++ b/solution.py
@@ -10,6 +10,8 @@
 OB = 128
 RD = 256
 MB = 2**20
+OUT_SLOTS = 8
+OUT_TILE = 1024
 F32 = jnp.float32
 BF16 = jnp.bfloat16
 
@@ -44,32 +46,33 @@
 
     perm = perm_ref[...]
 
-    def regroup(src_ref, dst_ref, scaled, first, number):
-        at = pl.multiple_of(first * 16, 16)
-        if not scaled:
-            for t in range(number):
-                turned = jnp.swapaxes(src_ref[pl.ds(at + 16 * t, 16)], 0, 1)
-                for g in range(gb):
-                    dst_ref[pl.ds(at + 16 * t, 16), g * width : (g + 1) * width] = turned[g]
-            return
-        tile = src_ref[pl.ds(at, 16 * number)].reshape(number, side, width)
-        wide = jnp.concatenate([tile[t] for t in range(number)], axis=1)
-        moved = jnp.dot(perm, wide, preferred_element_type=F32)
+    def regroup(jobs):
+        at = [pl.multiple_of(first * 16, 16) for _, _, _, first in jobs]
+        wide = [job[0][pl.ds(a, 16)].reshape(side, width) for job, a in zip(jobs, at)]
+        moved = jnp.dot(perm, jnp.concatenate(wide, axis=1), preferred_element_type=F32)
         for g in range(gb):
-            for t in range(number):
+            for t, (_, dst_ref, scaled, _) in enumerate(jobs):
                 part = moved[g * 16 : (g + 1) * 16, t * width : (t + 1) * width]
                 if scaled:
                     part = part * noise_ref[step * gb + g]
-                dst_ref[pl.ds(at + 16 * t, 16), g * width : (g + 1) * width] = part.astype(BF16)
+                dst_ref[pl.ds(at[t], 16), g * width : (g + 1) * width] = part.astype(BF16)
+
+    def turn(src_ref, dst_ref, first):
+        at = pl.ds(pl.multiple_of(first * 16, 16), 16)
+        turned = jnp.swapaxes(src_ref[at], 0, 1)
+        for g in range(gb):
+            dst_ref[at, g * width : (g + 1) * width] = turned[g]
 
     def tiles(i, carry):
-        regroup(r_ref, w_ref, True, i * 4, 4)
-        regroup(x_ref, flat_ref, False, i * 4, 4)
+        jobs = [(r_ref, w_ref, True, i * 4 + t) for t in range(4)]
+        regroup(jobs + [(x_ref, flat_ref, False, i * 4)])
+        for t in range(1, 4):
+            turn(x_ref, flat_ref, i * 4 + t)
         return carry
 
     def more_tiles(src_ref, dst_ref, scaled):
         def body(i, carry):
-            regroup(src_ref, dst_ref, scaled, i, 1)
+            regroup([(src_ref, dst_ref, scaled, i)])
             return carry
 
         lax.fori_loop(both * 4, src_ref.shape[0] // 16, body, 0)
@@ -238,12 +241,12 @@
         item_ref[0, i : i + 1, :] = value.astype(jnp.int32)
 
 
-def meta_kernel(here_ref, index_ref, frac_ref, pos_ref, addr_ref, table_ref, meta_ref):
+def meta_kernel(here_ref, index_ref, frac_ref, pos_ref, meta_ref):
     step = pl.program_id(0)
     _, units, half = pos_ref.shape
     parts = index_ref.shape[1] // half
     gb = units // parts
-    blocks = meta_ref.shape[1]
+    blocks = meta_ref.shape[2]
     low = lambda value: value.astype(F32).astype(BF16)
     eighth = low(lax.broadcasted_iota(jnp.int32, (blocks, half), 0))
     lane_of = low(lax.broadcasted_iota(jnp.int32, (OB, half), 0) % 8)
@@ -259,19 +262,12 @@
             jnp.where(here, low(index_ref[line, span]), none),
             jnp.where(here, low(frac_ref[line, span]), none),
         ]
-        meta_ref[u] = lax.dot_general(
+        meta_ref[0, u] = lax.dot_general(
             jnp.concatenate([spots, spots], axis=1),
             jnp.concatenate(terms, axis=1),
             (((1,), (1,)), ((), ())),
             preferred_element_type=F32,
         )
-
-    def move(u, carry):
-        for i in range(blocks):
-            table_ref[0, pl.ds(addr_ref[0, u, i], 1), :] = meta_ref[u, i : i + 1, :]
-        return carry
-
-    lax.fori_loop(0, units, move, 0)
 
 
 def up_to(value, step):
@@ -323,32 +319,20 @@
     )(here, destination)
 
 
-def table_rows(units, half, owners):
-    return up_to((units * sort_sizes(half, owners)[0] + 2 * RD + 8) // 8, 8)
-
-
-def meta_call(here, row_index, fraction, pos, addr, owners):
+def meta_call(here, row_index, fraction, pos, owners):
     steps, units, half = pos.shape
     orients = row_index.shape[1]
     groups = steps * units * half // orients
     blocks = sort_sizes(half, owners)[2]
-    shape = (steps, table_rows(units, half, owners), OB)
+    shape = (steps, units, blocks, OB)
     table = pl.BlockSpec((groups, orients), lambda i, here: (here[1], 0))
     return pl.pallas_call(
         meta_kernel,
         grid_spec=pltpu.PrefetchScalarGridSpec(
             num_scalar_prefetch=1,
             grid=(steps,),
-            in_specs=[
-                table,
-                table,
-                planned(pos.shape),
-                pl.BlockSpec(
-                    (1,) + addr.shape[1:], lambda i, here: (i, 0, 0), memory_space=pltpu.SMEM
-                ),
-            ],
+            in_specs=[table, table, planned(pos.shape)],
             out_specs=planned(shape),
-            scratch_shapes=[pltpu.VMEM((units, blocks, OB), F32)],
         ),
         out_shape=jax.ShapeDtypeStruct(shape, F32),
         compiler_params=pltpu.CompilerParams(vmem_limit_bytes=60 * MB),
@@ -357,12 +341,12 @@
             bytes_accessed=8 * steps * units * blocks * OB,
             transcendentals=0,
         ),
-    )(here, row_index, fraction, pos, addr)
+    )(here, row_index, fraction, pos)
 
 
 def insert_kernel(me_ref, addr_ref, item_ref, x_ref, pos_ref, meta_ref, blk_ref, *rest):
-    *post_refs, send_ref, keep_ref = rest[:-9]
-    post_t, spread_ref, cols_ref, slice_a, slice_b, buf_s, volume, stage, sem = rest[-9:]
+    *post_refs, send_ref, keep_ref = rest[:-10]
+    post_t, spread_ref, cols_ref, slice_a, slice_b, buf_s, buf_m, volume, stage, sem = rest[-10:]
     step = pl.program_id(0)
     count = x_ref.shape[0]
     orients = post_t.shape[0]
@@ -416,6 +400,7 @@
         for i in range(size // 8):
             at = addr_ref[0, u, base // 8 + i]
             buf_s[pl.ds(pl.multiple_of(at * 8, 8), 8), :] = rows[8 * i : 8 * i + 8]
+            buf_m[pl.ds(at, 1), :] = meta_ref[0, u, pl.ds(base // 8 + i, 1), :]
 
     def sort(q, src_ref):
         for g in range(per):
@@ -479,7 +464,7 @@
             owner, at, left = item_ref[0, 0, j], item_ref[0, 1, j], item_ref[0, 2, j]
             places = [
                 jnp.sum(
-                    jnp.where(own_lane, meta_ref[0, pl.ds(at + h * (side // 8), side // 8), :], 0.0),
+                    jnp.where(own_lane, buf_m[pl.ds(at + h * (side // 8), side // 8), :], 0.0),
                     axis=0,
                     keepdims=True,
                 )
@@ -499,23 +484,23 @@
 
     @pl.when(step == pl.num_programs(0) - 1)
     def _():
-        half = keep_ref.shape[0]
-        tile = stage.shape[1]
+        side_rows = keep_ref.shape[1]
+        slots_out, _, tile, _ = stage.shape
         copies = []
-        number = 0
-        for base, out_ref in ((half, send_ref), (0, keep_ref)):
-            for at in range(0, half, tile):
-                slot = number % 2
-                if number >= 2:
-                    copies[number - 2].wait()
-                stage[slot] = volume[base + at : base + at + tile, :].astype(BF16)
+        for base, out_ref in ((side_rows, send_ref), (0, keep_ref)):
+            for at in range(0, side_rows, tile):
+                slot = len(copies) % slots_out
+                if len(copies) >= slots_out:
+                    copies[len(copies) - slots_out].wait()
+                value = volume[base + at : base + at + tile, :].astype(BF16)
+                for c in range(2):
+                    stage[slot, c] = value[:, c * OB : (c + 1) * OB]
                 copy = pltpu.make_async_copy(
-                    stage.at[slot], out_ref.at[pl.ds(at, tile)], sem.at[slot]
+                    stage.at[slot], out_ref.at[:, pl.ds(at, tile)], sem.at[slot]
                 )
                 copy.start()
                 copies.append(copy)
-                number += 1
-        for copy in copies[-2:]:
+        for copy in copies[-slots_out:]:
             copy.wait()
 
 
@@ -526,12 +511,12 @@
 def insert_block(groups, orients, owners, count, width):
     half = min(256, orients)
     slots, _, blocks = sort_sizes(half, owners)
-    room = 52 * MB - owners * RD * width * 4
+    room = 50 * MB - owners * RD * width * 4
     best = 1
     for gb in range(1, groups + 1):
         units = gb * (orients // half)
         rows = units * slots + 2 * RD + 8
-        need = rows * (width * 4 + OB) + 4 * count * gb * width
+        need = rows * (width * 4 + OB // 2) + 4 * count * gb * width + units * blocks * OB * 8
         if groups % gb == 0 and need <= room:
             best = gb
     return best
@@ -552,7 +537,7 @@
     return pl.pallas_call(
         insert_kernel,
         grid=(steps,),
-        out_shape=[jax.ShapeDtypeStruct((total // 2, width), BF16)] * 2,
+        out_shape=[jax.ShapeDtypeStruct((2, total // 2, OB), BF16)] * 2,
         in_specs=[
             smem,
             block(addr.shape, memory_space=pltpu.SMEM),
@@ -571,9 +556,10 @@
             pltpu.VMEM((orients, group_pair(gb) * width), BF16),
             pltpu.VMEM((orients, group_pair(gb) * width), BF16),
             pltpu.VMEM((rows, width), F32),
+            pltpu.VMEM((rows // 8, OB), F32),
             pltpu.VMEM((total, width), F32),
-            pltpu.VMEM((2, 512, width), BF16),
-            pltpu.SemaphoreType.DMA((2,)),
+            pltpu.VMEM((OUT_SLOTS, 2, OUT_TILE, OB), BF16),
+            pltpu.SemaphoreType.DMA((OUT_SLOTS,)),
         ],
         compiler_params=pltpu.CompilerParams(vmem_limit_bytes=62 * MB),
         cost_estimate=pl.CostEstimate(
@@ -612,7 +598,7 @@
     parts = [own] + [flip(scores[k], "slab", k) for k in range(1, slab_size)]
     post = softmax_call(parts)
     post, pos = lax.optimization_barrier((post, pos))
-    meta = meta_call(here, row_index, fraction, pos, addr, devices)
+    meta = meta_call(here, row_index, fraction, pos, devices)
     posts = [post] + [flip(post, "slab", k) for k in range(1, slab_size)]
     send, keep = insert_call(
         slab_me, addr, items, flat, pos, meta, blocks, posts, orients, devices
@@ -629,17 +615,19 @@
 
     terms = [keep, flip(send, "dom", dom_bits[0])]
     rest = dom_bits[1:]
-    terms = [term.reshape((2,) * len(rest) + (slab_size * RD, width)) for term in terms]
-    columns = [[term[..., part * OB : (part + 1) * OB] for term in terms] for part in range(2)]
+    columns = []
+    for part in range(2):
+        columns.append(
+            [term[part].reshape((2,) * len(rest) + (slab_size * RD, OB)) for term in terms]
+        )
     for stage in range(len(rest)):
         for part in range(2):
             axis = stage if part == 0 else len(rest) - 1 - stage
             columns[part] = halve(columns[part], "dom", axis, rest[axis])
-    columns = [[term.reshape(slab_size * RD, OB) for term in terms] for terms in columns]
-    terms = [jnp.concatenate(pair, axis=1) for pair in zip(*columns)]
+    terms = [jnp.stack([t.reshape(slab_size * RD, OB) for t in pair]) for pair in zip(*columns)]
     for bit in slab_bits:
-        terms = halve(terms, "slab", 0, bit)
-    volume = added(terms)
+        terms = halve(terms, "slab", 1, bit)
+    volume = jnp.concatenate([added([term[part] for term in terms]) for part in range(2)], axis=1)
 
     own = volume.astype(BF16)
     plane = [own] + [flip(own, "dom", 2 * k) for k in range(1, dom_size // 2)]

time: 191 us -> 179 us (0.937)
  Pallas kernels: 123 us -> 113 us
  waiting for transfers between devices: 38.6 us -> 35.3 us
  other arithmetic: 4.62 us -> 2.53 us
  local copies, waits for them, and re-layouts: 1.79 us -> 3.75 us
    pallas_call x1, Pallas kernels: 20.7 us -> 10.5 us  [meta_call(): pl.pallas_call(meta_kernel, grid_spec=pltpu.PrefetchScalarGridSpec(num_sc...]
    ppermute x17, waiting for transfers between devices: 38.6 us -> 35.3 us  [flip(): return lax.ppermute(value, axis, [(i, i ^ bit) for i in range(size)])]
    convert_element_type x5 -> x6, other arithmetic: 2.85 us -> 0.72 us  [halve(): sent = added([pick(term, size) for term in terms]).astype(BF16)]
  transfers between devices with their start and end apart: 17 -> 17, of which waited for: 12 -> 11; matrix products, arithmetic and copies ran while one was open for 0% -> 1% of each run, Pallas kernels for 16% -> 11%
where the time goes in v7:
time: 179 us
  Pallas kernels  113 us (63%)
  waiting for transfers between devices  35.3 us (20%)
  starting transfers between devices  23.6 us (13%)
  local copies, waits for them, and re-layouts  3.75 us (2%)
  other arithmetic  2.53 us (1%)
    pallas_call x1, Pallas kernels, insert_call(): pl.pallas_call(insert_kernel, grid=(steps,), out_shape=[jax.ShapeDtypeStr...  61.6 us
    ppermute x17, waiting for transfers between devices, flip(): return lax.ppermute(value, axis, [(i, i ^ bit) for i in range(size)])  35.3 us
    pallas_call x1, Pallas kernels, score_call(): pl.pallas_call(score_kernel, grid=(groups // gb,), out_shape=[jax.ShapeDt...  30.6 us
    ppermute x17, starting transfers between devices, flip(): return lax.ppermute(value, axis, [(i, i ^ bit) for i in range(size)])  23.6 us
    pallas_call x1, Pallas kernels, meta_call(): pl.pallas_call(meta_kernel, grid_spec=pltpu.PrefetchScalarGridSpec(num_sc...  10.5 us
    pallas_call x1, Pallas kernels, plan_call(): pl.pallas_call(functools.partial(plan_kernel, sizes=mesh_sizes), grid_spe...  9.71 us
  transfers between devices with their start and end apart: 17, of which 11 were waited for; matrix products, arithmetic and copies ran while one was open for 1% of the time, Pallas kernels for 11%

profile of v7, /device:TPU:0, one launch (start us, length us, event | category | flops | bytes accessed | tf_op | source)
XLA Modules:
  0.0 178.6 jit_solution(11078751205730649890)
XLA Ops:
  0.6 30.6 %shard_map.86 = (bf16[512,20480]{1,0:T(8,128)(2,1)}, f32[128,256]{1,0:T(8,128)}, f32[128,256]{1,0:T(8,128)}, f32[128,256]{1,0:T(8,128)}, f32[128,256]{1,0:T(8,128)}) custom-call(s32[1]{0:T(128)} %bitcast.me_ref, f32[80]{0:T(128)} %noise_ref.1, bf16[512,80,256]{2,1,0:T(8,128)(2,1)} %x_ref.1, bf16[512,80,256]{2,1,0:T(8,128)(2,1)} %r_ref.1, s32[2,512]{1,0:T(2,128)} %bitcast.57), custom_call_target="tpu_custom_call" | custom-call | flops 21474836480 | bytes 62914560 | tf_op jit(solution)/shard_map/pallas_call | solution.py:110
  31.2 3.1 %collective-permute-start = (f32[128,256]{1,0:T(8,128)}, f32[128,256]{1,0:T(8,128)S(1)}, u32[]{:S(2)}, u32[]{:S(2)}) collective-permute-start(f32[128,256]{1,0:T(8,128)} %get-tuple-element.30), channel_id=1, source_target_pairs={{0,1},{1,0},{2,3},{3,2},{4,5},{5,4},{6,7},{7,6},{8,9},{9,8},{10,11... | collective-permute-start | bytes 393224 | tf_op jit(solution)/shard_map/ppermute | solution.py:575
  34.3 2.6 %collective-permute-start.1 = (f32[128,256]{1,0:T(8,128)}, f32[128,256]{1,0:T(8,128)S(1)}, u32[]{:S(2)}, u32[]{:S(2)}) collective-permute-start(f32[128,256]{1,0:T(8,128)} %get-tuple-element.31), channel_id=1, source_target_pairs={{0,2},{1,3},{2,0},{3,1},{4,6},{5,7},{6,4},{7,5},{8,10},{9,11},{10,... | collective-permute-start | bytes 393224 | tf_op jit(solution)/shard_map/ppermute | solution.py:575
  37.5 9.7 %shard_map.87 = (s32[4,40,256]{2,1,0:T(8,128)}, s32[4,40,128]{2,1,0:T(8,128)}, s32[4,5,128]{2,1,0:T(8,128)}) custom-call(s32[2]{0:T(128)} %pad_add_fusion.here_ref, s32[320,512]{1,0:T(8,128)} %dest_ref.1), custom_call_target="tpu_custom_call" | custom-call | flops 2684354560 | bytes 327680 | tf_op jit(solution)/shard_map/pallas_call | solution.py:299
  47.6 2.0 %collective-permute-start.3 = (bf16[128,256]{1,0:T(8,128)(2,1)S(1)}, bf16[128,256]{1,0:T(8,128)(2,1)S(1)}, u32[]{:S(2)}, u32[]{:S(2)}) collective-permute-start(bf16[128,256]{1,0:T(8,128)(2,1)S(1)} %shard_map.88.rest_0_), channel_id=1, source_target_pairs={{0,1},{1,0},{2,3},{3,2},{4,5},{5,4},{6,7},{7,6},{8,9},{9,8},{10,11... | collective-permute-start | bytes 196616 | tf_op jit(solution)/shard_map/ppermute | solution.py:575
  49.7 2.2 %collective-permute-start.4 = (bf16[128,256]{1,0:T(8,128)(2,1)S(1)}, bf16[128,256]{1,0:T(8,128)(2,1)S(1)}, u32[]{:S(2)}, u32[]{:S(2)}) collective-permute-start(bf16[128,256]{1,0:T(8,128)(2,1)S(1)} %shard_map.88.rest_0_), channel_id=1, source_target_pairs={{0,2},{1,3},{2,0},{3,1},{4,6},{5,7},{6,4},{7,5},{8,10},{9,11},{10,... | collective-permute-start | bytes 196616 | tf_op jit(solution)/shard_map/ppermute | solution.py:575
  52.1 10.5 %shard_map.89.meta_ref = f32[4,40,72,128]{3,2,1,0:T(8,128)} custom-call(s32[2]{0:T(128)} %pad_add_fusion.here_ref, s32[320,512]{1,0:T(8,128)} %index_ref.1, f32[320,512]{1,0:T(8,128)} %frac_ref.1, s32[4,40,256]{2,1,0:T(8,128)} %get-tuple-element.34.pos_ref), custom_call_target="tpu_custom_call" | custom-call | flops 3019898880 | bytes 11796480 | tf_op jit(solution)/shard_map/pallas_call | solution.py:329
  63.3 61.6 %shard_map.90 = (bf16[2,4096,128]{2,1,0:T(8,128)(2,1)}, bf16[2,4096,128]{2,1,0:T(8,128)(2,1)}) custom-call(s32[1]{0:T(128)} %bitcast.me_ref, s32[4,40,128]{2,1,0:T(8,128)} %get-tuple-element.26.addr_ref, s32[4,5,128]{2,1,0:T(8,128)} %get-tuple-element.27.item_ref, bf16[512,20480]{1,0:T(8,128)(2,1)} %get-tuple-element.28.x_ref, ...), custom_call_target="tpu_custom_call" | custom-call | flops 42949672960 | bytes 20971520 | tf_op jit(solution)/shard_map/pallas_call | solution.py:537
  125.0 1.4 slice.194
  126.9 2.5 %collective-permute-done.6 = bf16[2,4096,128]{2,1,0:T(8,128)(2,1)S(1)} collective-permute-done((bf16[2,4096,128]{2,1,0:T(8,128)(2,1)}, bf16[2,4096,128]{2,1,0:T(8,128)(2,1)S(1)}, u32[]{:S(2)}, u32[]{:S(2)}) %collective-permute-start.6) | collective-permute-done | bytes 2097184 | tf_op jit(solution)/shard_map/ppermute | solution.py:575
  129.6 1.6 collective-permute-start.9
  131.4 1.5 collective-permute-start.7
  133.0 10.6 %collective-permute-done.9 = bf16[2,1,1024,128]{3,2,1,0:T(8,128)(2,1)S(1)} collective-permute-done((bf16[2,1,1024,128]{3,2,1,0:T(8,128)(2,1)S(1)}, bf16[2,1,1024,128]{3,2,1,0:T(8,128)(2,1)S(1)}, u32[]{:S(2)}, u32[]{:S(2)}) %collective-permute-start.9) | collective-permute-done | bytes 524320 | tf_op jit(solution)/shard_map/ppermute | solution.py:575
  143.7 1.6 collective-permute-start.10
  145.4 1.6 collective-permute-start.8
  147.0 4.3 %collective-permute-done.10 = bf16[1,1,1024,128]{3,2,1,0:T(8,128)(2,1)S(1)} collective-permute-done((bf16[1,1,1024,128]{3,2,1,0:T(8,128)(2,1)S(1)}, bf16[1,1,1024,128]{3,2,1,0:T(8,128)(2,1)S(1)}, u32[]{:S(2)}, u32[]{:S(2)}) %collective-permute-start.10) | collective-permute-done | bytes 262176 | tf_op jit(solution)/shard_map/ppermute | solution.py:575
  151.3 1.4 collective-permute-done.8
  153.9 5.4 %collective-permute-done.11 = bf16[2,512,128]{2,1,0:T(8,128)(2,1)S(1)} collective-permute-done((bf16[2,512,128]{2,1,0:T(8,128)(2,1)S(1)}, bf16[2,512,128]{2,1,0:T(8,128)(2,1)S(1)}, u32[]{:S(2)}, u32[]{:S(2)}) %collective-permute-start.11) | collective-permute-done | bytes 262176 | tf_op jit(solution)/shard_map/ppermute | solution.py:575
  159.4 2.5 %collective-permute-start.12 = (bf16[2,256,128]{2,1,0:T(8,128)(2,1)S(1)}, bf16[2,256,128]{2,1,0:T(8,128)(2,1)S(1)}, u32[]{:S(2)}, u32[]{:S(2)}) collective-permute-start(bf16[2,256,128]{2,1,0:T(8,128)(2,1)S(1)} %add_convert_fusion.5), channel_id=1, source_target_pairs={{0,2},{1,3},{2,0},{3,1},{4,6},{5,7},{6,4},{7,5},{8,10},{9,11},{10,... | collective-permute-start | bytes 393224 | tf_op jit(solution)/shard_map/ppermute | solution.py:575
  161.9 4.9 %collective-permute-done.12 = bf16[2,256,128]{2,1,0:T(8,128)(2,1)S(1)} collective-permute-done((bf16[2,256,128]{2,1,0:T(8,128)(2,1)S(1)}, bf16[2,256,128]{2,1,0:T(8,128)(2,1)S(1)}, u32[]{:S(2)}, u32[]{:S(2)}) %collective-permute-start.12) | collective-permute-done | bytes 131104 | tf_op jit(solution)/shard_map/ppermute | solution.py:575
  167.6 1.5 collective-permute-start.13
  171.1 2.5 %collective-permute-done.13 = bf16[256,256]{1,0:T(8,128)(2,1)S(1)} collective-permute-done((bf16[256,256]{1,0:T(8,128)(2,1)S(1)}, bf16[256,256]{1,0:T(8,128)(2,1)S(1)}, u32[]{:S(2)}, u32[]{:S(2)}) %collective-permute-start.13) | collective-permute-done | bytes 131104 | tf_op jit(solution)/shard_map/ppermute | solution.py:575
  173.5 1.3 collective-permute-done.14
  175.5 1.9 %collective-permute-done.16 = bf16[4,256,256]{2,1,0:T(8,128)(2,1)S(1)} collective-permute-done((bf16[4,256,256]{2,1,0:T(8,128)(2,1)S(1)}, bf16[4,256,256]{2,1,0:T(8,128)(2,1)S(1)}, u32[]{:S(2)}, u32[]{:S(2)}) %collective-permute-start.16) | collective-permute-done | bytes 524320 | tf_op jit(solution)/shard_map/ppermute | solution.py:575
  (48 shorter events, 9.0 us)
Async XLA Ops:
  31.2 16.0 %collective-permute-start = (f32[128,256]{1,0:T(8,128)}, f32[128,256]{1,0:T(8,128)S(1)}, u32[]{:S(2)}, u32[]{:S(2)}) collective-permute-start(f32[128,256]{1,0:T(8,128)} %get-tuple-element.30), channel_id=1, source_target_pairs={{0,1},{1,0},{2,3},{3,2},{4,5},{5,4},{6,7},{7,6},{8,9},{9,8},{10,11... | collective-permute-start | bytes 393224 | tf_op jit(solution)/shard_map/ppermute | solution.py:575
  34.3 13.1 %collective-permute-start.1 = (f32[128,256]{1,0:T(8,128)}, f32[128,256]{1,0:T(8,128)S(1)}, u32[]{:S(2)}, u32[]{:S(2)}) collective-permute-start(f32[128,256]{1,0:T(8,128)} %get-tuple-element.31), channel_id=1, source_target_pairs={{0,2},{1,3},{2,0},{3,1},{4,6},{5,7},{6,4},{7,5},{8,10},{9,11},{10,... | collective-permute-start | bytes 393224 | tf_op jit(solution)/shard_map/ppermute | solution.py:575
  36.9 10.6 %collective-permute-start.2 = (f32[128,256]{1,0:T(8,128)}, f32[128,256]{1,0:T(8,128)S(1)}, u32[]{:S(2)}, u32[]{:S(2)}) collective-permute-start(f32[128,256]{1,0:T(8,128)} %get-tuple-element.32), channel_id=1, source_target_pairs={{0,3},{1,2},{2,1},{3,0},{4,7},{5,6},{6,5},{7,4},{8,11},{9,10},{10,... | collective-permute-start | bytes 393224 | tf_op jit(solution)/shard_map/ppermute | solution.py:575
  37.5 9.9 %copy-start = (f32[128,256]{1,0:T(8,128)S(1)}, f32[128,256]{1,0:T(8,128)}, u32[]{:S(2)}) copy-start(f32[128,256]{1,0:T(8,128)} %get-tuple-element.29.refs_0_) | copy-start | bytes 393220
  47.6 15.0 %copy-start.1 = (bf16[128,256]{1,0:T(8,128)(2,1)}, bf16[128,256]{1,0:T(8,128)(2,1)S(1)}, u32[]{:S(2)}) copy-start(bf16[128,256]{1,0:T(8,128)(2,1)S(1)} %shard_map.88.rest_0_) | copy-start | bytes 196612
  47.6 15.0 %collective-permute-start.3 = (bf16[128,256]{1,0:T(8,128)(2,1)S(1)}, bf16[128,256]{1,0:T(8,128)(2,1)S(1)}, u32[]{:S(2)}, u32[]{:S(2)}) collective-permute-start(bf16[128,256]{1,0:T(8,128)(2,1)S(1)} %shard_map.88.rest_0_), channel_id=1, source_target_pairs={{0,1},{1,0},{2,3},{3,2},{4,5},{5,4},{6,7},{7,6},{8,9},{9,8},{10,11... | collective-permute-start | bytes 196616 | tf_op jit(solution)/shard_map/ppermute | solution.py:575
  49.7 13.0 %collective-permute-start.4 = (bf16[128,256]{1,0:T(8,128)(2,1)S(1)}, bf16[128,256]{1,0:T(8,128)(2,1)S(1)}, u32[]{:S(2)}, u32[]{:S(2)}) collective-permute-start(bf16[128,256]{1,0:T(8,128)(2,1)S(1)} %shard_map.88.rest_0_), channel_id=1, source_target_pairs={{0,2},{1,3},{2,0},{3,1},{4,6},{5,7},{6,4},{7,5},{8,10},{9,11},{10,... | collective-permute-start | bytes 196616 | tf_op jit(solution)/shard_map/ppermute | solution.py:575
  51.9 10.8 %collective-permute-start.5 = (bf16[128,256]{1,0:T(8,128)(2,1)S(1)}, bf16[128,256]{1,0:T(8,128)(2,1)S(1)}, u32[]{:S(2)}, u32[]{:S(2)}) collective-permute-start(bf16[128,256]{1,0:T(8,128)(2,1)S(1)} %shard_map.88.rest_0_), channel_id=1, source_target_pairs={{0,3},{1,2},{2,1},{3,0},{4,7},{5,6},{6,5},{7,4},{8,11},{9,10},{10,... | collective-permute-start | bytes 196616 | tf_op jit(solution)/shard_map/ppermute | solution.py:575
  62.6 0.6 copy-start.3
  62.7 0.6 copy-start.4
  62.7 0.6 copy-start.5
  124.9 1.9 %copy-start.2 = (bf16[2,4096,128]{2,1,0:T(8,128)(2,1)S(1)}, bf16[2,4096,128]{2,1,0:T(8,128)(2,1)}, u32[]{:S(2)}) copy-start(bf16[2,4096,128]{2,1,0:T(8,128)(2,1)} %get-tuple-element.36) | copy-start | bytes 6291460
  124.9 4.4 %collective-permute-start.6 = (bf16[2,4096,128]{2,1,0:T(8,128)(2,1)}, bf16[2,4096,128]{2,1,0:T(8,128)(2,1)S(1)}, u32[]{:S(2)}, u32[]{:S(2)}) collective-permute-start(bf16[2,4096,128]{2,1,0:T(8,128)(2,1)} %get-tuple-element.37), channel_id=1, source_target_pairs={{0,4},{4,0},{8,12},{12,8},{16,20},{20,16},{24,28},{28,24},{1,5},{5... | collective-permute-start | bytes 6291464 | tf_op jit(solution)/shard_map/ppermute | solution.py:575
  129.6 14.0 %collective-permute-start.9 = (bf16[2,1,1024,128]{3,2,1,0:T(8,128)(2,1)S(1)}, bf16[2,1,1024,128]{3,2,1,0:T(8,128)(2,1)S(1)}, u32[]{:S(2)}, u32[]{:S(2)}) collective-permute-start(bf16[2,1,1024,128]{3,2,1,0:T(8,128)(2,1)S(1)} %add_convert_fusion), channel_id=1, source_target_pairs={{0,16},{4,20},{8,24},{12,28},{16,0},{20,4},{24,8},{28,12},{1,17},{... | collective-permute-start | bytes 1572872 | tf_op jit(solution)/shard_map/ppermute | solution.py:575
  131.4 14.0 %collective-permute-start.7 = (bf16[1,2,1024,128]{3,2,1,0:T(8,128)(2,1)S(1)}, bf16[1,2,1024,128]{3,2,1,0:T(8,128)(2,1)S(1)}, u32[]{:S(2)}, u32[]{:S(2)}) collective-permute-start(bf16[1,2,1024,128]{3,2,1,0:T(8,128)(2,1)S(1)} %bitcast.55), channel_id=1, source_target_pairs={{0,8},{4,12},{8,0},{12,4},{16,24},{20,28},{24,16},{28,20},{1,9},{5... | collective-permute-start | bytes 1572872 | tf_op jit(solution)/shard_map/ppermute | solution.py:575
  143.7 7.6 %collective-permute-start.10 = (bf16[1,1,1024,128]{3,2,1,0:T(8,128)(2,1)S(1)}, bf16[1,1,1024,128]{3,2,1,0:T(8,128)(2,1)S(1)}, u32[]{:S(2)}, u32[]{:S(2)}) collective-permute-start(bf16[1,1,1024,128]{3,2,1,0:T(8,128)(2,1)S(1)} %add_convert_fusion.3), channel_id=1, source_target_pairs={{0,8},{4,12},{8,0},{12,4},{16,24},{20,28},{24,16},{28,20},{1,9},{5... | collective-permute-start | bytes 786440 | tf_op jit(solution)/shard_map/ppermute | solution.py:575
  145.4 7.3 %collective-permute-start.8 = (bf16[1,1,1024,128]{3,2,1,0:T(8,128)(2,1)S(1)}, bf16[1,1,1024,128]{3,2,1,0:T(8,128)(2,1)S(1)}, u32[]{:S(2)}, u32[]{:S(2)}) collective-permute-start(bf16[1,1,1024,128]{3,2,1,0:T(8,128)(2,1)S(1)} %add_convert_fusion.4), channel_id=1, source_target_pairs={{0,16},{4,20},{8,24},{12,28},{16,0},{20,4},{24,8},{28,12},{1,17},{... | collective-permute-start | bytes 786440 | tf_op jit(solution)/shard_map/ppermute | solution.py:575
  152.9 6.4 %collective-permute-start.11 = (bf16[2,512,128]{2,1,0:T(8,128)(2,1)S(1)}, bf16[2,512,128]{2,1,0:T(8,128)(2,1)S(1)}, u32[]{:S(2)}, u32[]{:S(2)}) collective-permute-start(bf16[2,512,128]{2,1,0:T(8,128)(2,1)S(1)} %add_convert_fusion.2), channel_id=1, source_target_pairs={{0,1},{1,0},{2,3},{3,2},{4,5},{5,4},{6,7},{7,6},{8,9},{9,8},{10,11... | collective-permute-start | bytes 786440 | tf_op jit(solution)/shard_map/ppermute | solution.py:575
  159.4 7.3 %collective-permute-start.12 = (bf16[2,256,128]{2,1,0:T(8,128)(2,1)S(1)}, bf16[2,256,128]{2,1,0:T(8,128)(2,1)S(1)}, u32[]{:S(2)}, u32[]{:S(2)}) collective-permute-start(bf16[2,256,128]{2,1,0:T(8,128)(2,1)S(1)} %add_convert_fusion.5), channel_id=1, source_target_pairs={{0,2},{1,3},{2,0},{3,1},{4,6},{5,7},{6,4},{7,5},{8,10},{9,11},{10,... | collective-permute-start | bytes 393224 | tf_op jit(solution)/shard_map/ppermute | solution.py:575
  167.6 5.9 %collective-permute-start.13 = (bf16[256,256]{1,0:T(8,128)(2,1)S(1)}, bf16[256,256]{1,0:T(8,128)(2,1)S(1)}, u32[]{:S(2)}, u32[]{:S(2)}) collective-permute-start(bf16[256,256]{1,0:T(8,128)(2,1)S(1)} %get-tuple-element.38), channel_id=1, source_target_pairs={{0,24},{4,28},{8,16},{12,20},{16,8},{20,12},{24,0},{28,4},{1,25},{... | collective-permute-start | bytes 393224 | tf_op jit(solution)/shard_map/ppermute | solution.py:575
  169.1 5.8 %collective-permute-start.14 = (bf16[256,256]{1,0:T(8,128)(2,1)S(1)}, bf16[256,256]{1,0:T(8,128)(2,1)S(1)}, u32[]{:S(2)}, u32[]{:S(2)}) collective-permute-start(bf16[256,256]{1,0:T(8,128)(2,1)S(1)} %get-tuple-element.38), channel_id=1, source_target_pairs={{0,16},{4,20},{8,24},{12,28},{16,0},{20,4},{24,8},{28,12},{1,17},{... | collective-permute-start | bytes 393224 | tf_op jit(solution)/shard_map/ppermute | solution.py:575
  170.2 5.0 %collective-permute-start.15 = (bf16[256,256]{1,0:T(8,128)(2,1)S(1)}, bf16[256,256]{1,0:T(8,128)(2,1)S(1)}, u32[]{:S(2)}, u32[]{:S(2)}) collective-permute-start(bf16[256,256]{1,0:T(8,128)(2,1)S(1)} %get-tuple-element.38), channel_id=1, source_target_pairs={{0,8},{4,12},{8,0},{12,4},{16,24},{20,28},{24,16},{28,20},{1,9},{5... | collective-permute-start | bytes 393224 | tf_op jit(solution)/shard_map/ppermute | solution.py:575
  175.4 2.0 %collective-permute-start.16 = (bf16[4,256,256]{2,1,0:T(8,128)(2,1)S(1)}, bf16[4,256,256]{2,1,0:T(8,128)(2,1)S(1)}, u32[]{:S(2)}, u32[]{:S(2)}) collective-permute-start(bf16[4,256,256]{2,1,0:T(8,128)(2,1)S(1)} %get-tuple-element.41), channel_id=1, source_target_pairs={{0,4},{4,0},{8,12},{12,8},{16,20},{20,16},{24,28},{28,24},{1,5},{5... | collective-permute-start | bytes 1572872 | tf_op jit(solution)/shard_map/ppermute | solution.py:575

commit v8 on v7

--- a/solution.py
+++ b/solution.py
@@ -10,7 +10,7 @@
 OB = 128
 RD = 256
 MB = 2**20
-OUT_SLOTS = 8
+OUT_SLOTS = 4
 OUT_TILE = 1024
 F32 = jnp.float32
 BF16 = jnp.bfloat16
@@ -127,7 +127,7 @@
             pltpu.VMEM((side, side), BF16),
             pltpu.VMEM((2, count, OB), F32),
         ],
-        compiler_params=pltpu.CompilerParams(vmem_limit_bytes=56 * MB),
+        compiler_params=pltpu.CompilerParams(vmem_limit_bytes=32 * MB),
         cost_estimate=pl.CostEstimate(
             flops=4 * count * orients * groups * width,
             bytes_accessed=6 * count * groups * width,
@@ -204,7 +204,7 @@
     ahead = exact(runs, earlier)
     total = jnp.sum(runs, axis=1, keepdims=True)
     start = exact(below, jnp.broadcast_to(total, (owners, OB)))[:, :1]
-    blocks = jnp.floor((total + (2 * RD - 1.0)) * (0.5 / RD))
+    blocks = jnp.floor((total + (RD - 1.0)) * (1.0 / RD))
     first = exact(below, jnp.broadcast_to(blocks, (owners, OB)))[:, :1]
     shift = start + ahead - base
     used = jnp.sum(runs, axis=0, keepdims=True)
@@ -225,7 +225,7 @@
     wide = item_ref.shape[2]
     number = lax.broadcasted_iota(jnp.int32, (1, wide), 1).astype(F32)
     inside = (number >= first) & (number < first + blocks)
-    done = (number - first) * (2 * RD)
+    done = (number - first) * RD
     pick = lambda value: jnp.sum(jnp.where(inside, value, 0.0), axis=0, keepdims=True)
     every = lambda value: jnp.sum(
         jnp.broadcast_to(value, (owners, wide)), axis=0, keepdims=True
@@ -310,7 +310,7 @@
             ],
         ),
         out_shape=[jax.ShapeDtypeStruct(shape, jnp.int32) for shape in shapes],
-        compiler_params=pltpu.CompilerParams(vmem_limit_bytes=60 * MB),
+        compiler_params=pltpu.CompilerParams(vmem_limit_bytes=16 * MB),
         cost_estimate=pl.CostEstimate(
             flops=8 * steps * units * owners * half * half,
             bytes_accessed=8 * groups * orients,
@@ -335,7 +335,7 @@
             out_specs=planned(shape),
         ),
         out_shape=jax.ShapeDtypeStruct(shape, F32),
-        compiler_params=pltpu.CompilerParams(vmem_limit_bytes=60 * MB),
+        compiler_params=pltpu.CompilerParams(vmem_limit_bytes=16 * MB),
         cost_estimate=pl.CostEstimate(
             flops=8 * steps * units * blocks * half * OB,
             bytes_accessed=8 * steps * units * blocks * OB,
@@ -375,8 +375,8 @@
         for b in range(orients // OB):
             post_t[b * OB : (b + 1) * OB] = spread_ref[:, b * OB : (b + 1) * OB].T.astype(BF16)
 
-    tail = pl.ds(pl.multiple_of(item_ref[0, 4, 0] * 8, 8), 2 * RD)
-    buf_s[tail, :] = jnp.zeros((2 * RD, width), F32)
+    tail = pl.ds(pl.multiple_of(item_ref[0, 4, 0] * 8, 8), RD)
+    buf_s[tail, :] = jnp.zeros((RD, width), F32)
     one, none = jnp.bfloat16(1.0), jnp.bfloat16(0.0)
     slots, sure, _ = sort_sizes(half, volume.shape[0] // RD)
     per = slice_a.shape[1] // width
@@ -451,12 +451,12 @@
         sort(number - 1, slice_a)
         rest_of(number - 1, slice_a)
 
-    bins = lax.broadcasted_iota(jnp.int32, (RD, 2 * RD), 0).astype(F32).astype(BF16)
+    bins = lax.broadcasted_iota(jnp.int32, (RD, RD), 0).astype(F32).astype(BF16)
     side = RD // 2
     at_lane = lax.broadcasted_iota(jnp.int32, (side // 8, side), 1) // 8
     own_lane = at_lane == lax.broadcasted_iota(jnp.int32, (side // 8, side), 0)
-    line = lax.broadcasted_iota(jnp.int32, (1, 2 * RD), 1)
-    together = 4
+    line = lax.broadcasted_iota(jnp.int32, (1, RD), 1)
+    together = 8
 
     def some_items(q, carry):
         for u in range(together):
@@ -468,13 +468,13 @@
                     axis=0,
                     keepdims=True,
                 )
-                for h in range(4)
+                for h in range(2)
             ]
             place = jnp.where(line < left, jnp.concatenate(places, axis=1), -9.0)
             whole = jnp.floor(place)
             apart = (bins - whole.astype(BF16)) - (place - whole).astype(BF16)
             weights = jnp.maximum(one - jnp.abs(apart), none)
-            values = buf_s[pl.ds(pl.multiple_of(at * 8, 8), 2 * RD), :].astype(BF16)
+            values = buf_s[pl.ds(pl.multiple_of(at * 8, 8), RD), :].astype(BF16)
             goal = pl.ds(pl.multiple_of(owner * RD, RD), RD)
             volume[goal, :] += jnp.dot(weights, values, preferred_element_type=F32)
         return carry
@@ -505,17 +505,17 @@
 
 
 def group_pair(gb):
-    return 2 if gb % 4 == 0 else 1
+    return 2 if gb % 2 == 0 else 1
 
 
 def insert_block(groups, orients, owners, count, width):
     half = min(256, orients)
     slots, _, blocks = sort_sizes(half, owners)
-    room = 50 * MB - owners * RD * width * 4
+    room = max(27 * MB - owners * RD * width * 4, 18 * MB)
     best = 1
     for gb in range(1, groups + 1):
         units = gb * (orients // half)
-        rows = units * slots + 2 * RD + 8
+        rows = units * slots + RD + 8
         need = rows * (width * 4 + OB // 2) + 4 * count * gb * width + units * blocks * OB * 8
         if groups % gb == 0 and need <= room:
             best = gb
@@ -529,7 +529,8 @@
     width = length // (steps * gb)
     total = owners * RD
     share = posts[0].shape[0]
-    rows = units * sort_sizes(half, owners)[0] + 2 * RD + 8
+    rows = units * sort_sizes(half, owners)[0] + RD + 8
+    limit = total * width * 4 // MB + 26
     smem = pl.BlockSpec(memory_space=pltpu.SMEM)
     block = lambda shape, **kw: pl.BlockSpec(
         (1,) + shape[1:], lambda i: (i,) + (0,) * (len(shape) - 1), **kw
@@ -561,7 +562,7 @@
             pltpu.VMEM((OUT_SLOTS, 2, OUT_TILE, OB), BF16),
             pltpu.SemaphoreType.DMA((OUT_SLOTS,)),
         ],
-        compiler_params=pltpu.CompilerParams(vmem_limit_bytes=62 * MB),
+        compiler_params=pltpu.CompilerParams(vmem_limit_bytes=max(34, limit) * MB),
         cost_estimate=pl.CostEstimate(
             flops=8 * count * orients * length,
             bytes_accessed=2 * count * length,

time: 179 us -> 187 us (1.045)
  local copies, waits for them, and re-layouts: 3.75 us -> 9.7 us
    unnamed x12 -> x14, local copies, waits for them, and re-layouts: 1.04 us -> 8.35 us
    pallas_call x1, Pallas kernels: 61.6 us -> 64.9 us  [insert_call(): pl.pallas_call(insert_kernel, grid=(steps,), out_shape=[jax.ShapeDtypeStr...]
  transfers between devices with their start and end apart: 17 -> 17, of which waited for: 11 -> 10; matrix products, arithmetic and copies ran while one was open for 1% -> 0% of each run, Pallas kernels for 11% -> 10%
where the time goes in v8:
time: 187 us
  Pallas kernels  114 us (61%)
  waiting for transfers between devices  36.8 us (20%)
  starting transfers between devices  23.6 us (13%)
  local copies, waits for them, and re-layouts  9.7 us (5%)
  other arithmetic  1.95 us (1%)
    pallas_call x1, Pallas kernels, insert_call(): pl.pallas_call(insert_kernel, grid=(steps,), out_shape=[jax.ShapeDtypeStr...  64.9 us
    ppermute x17, waiting for transfers between devices, flip(): return lax.ppermute(value, axis, [(i, i ^ bit) for i in range(size)])  36.8 us
    pallas_call x1, Pallas kernels, score_call(): pl.pallas_call(score_kernel, grid=(groups // gb,), out_shape=[jax.ShapeDt...  29.6 us
    ppermute x17, starting transfers between devices, flip(): return lax.ppermute(value, axis, [(i, i ^ bit) for i in range(size)])  23.6 us
    pallas_call x1, Pallas kernels, plan_call(): pl.pallas_call(functools.partial(plan_kernel, sizes=mesh_sizes), grid_spe...  10.5 us
    pallas_call x1, Pallas kernels, meta_call(): pl.pallas_call(meta_kernel, grid_spec=pltpu.PrefetchScalarGridSpec(num_sc...  8.82 us
    unnamed x14, local copies, waits for them, and re-layouts  8.35 us
  transfers between devices with their start and end apart: 17, of which 10 were waited for; matrix products, arithmetic and copies ran while one was open for 0% of the time, Pallas kernels for 10%

profile of v8, /device:TPU:0, one launch (start us, length us, event | category | flops | bytes accessed | tf_op | source)
XLA Modules:
  0.0 187.0 jit_solution(3917064994281373846)
XLA Ops:
  2.0 29.6 %shard_map.86 = (bf16[512,20480]{1,0:T(8,128)(2,1)S(1)}, f32[128,256]{1,0:T(8,128)S(1)}, f32[128,256]{1,0:T(8,128)S(1)}, f32[128,256]{1,0:T(8,128)S(1)}, f32[128,256]{1,0:T(8,128)S(1)}) custom-call(s32[1]{0:T(128)} %bitcast.me_ref, f32[80]{0:T(128)S(1)} %copy-done.5, bf16[512,80,256]{2,1,0:T(8,128)(2,1)} %x_ref.1, bf16[512,80,256]{2,1,0:T(8,128)(2,1)} %r_ref.1, ...), custom_call_target="tpu_custom_call" | custom-call | flops 21474836480 | bytes 62914560 | tf_op jit(solution)/shard_map/pallas_call | solution.py:110
  31.6 7.0 %copy-done.6 = bf16[512,20480]{1,0:T(8,128)(2,1)} copy-done((bf16[512,20480]{1,0:T(8,128)(2,1)}, bf16[512,20480]{1,0:T(8,128)(2,1)S(1)}, u32[]{:S(2)}) %copy-start.6) | copy-done | bytes 20971544
  38.6 3.0 %collective-permute-start = (f32[128,256]{1,0:T(8,128)S(1)}, f32[128,256]{1,0:T(8,128)S(1)}, u32[]{:S(2)}, u32[]{:S(2)}) collective-permute-start(f32[128,256]{1,0:T(8,128)S(1)} %get-tuple-element.30), channel_id=1, source_target_pairs={{0,1},{1,0},{2,3},{3,2},{4,5},{5,4},{6,7},{7,6},{8,9},{9,8},{10,11... | collective-permute-start | bytes 393224 | tf_op jit(solution)/shard_map/ppermute | solution.py:576
  41.6 2.6 %collective-permute-start.1 = (f32[128,256]{1,0:T(8,128)S(1)}, f32[128,256]{1,0:T(8,128)S(1)}, u32[]{:S(2)}, u32[]{:S(2)}) collective-permute-start(f32[128,256]{1,0:T(8,128)S(1)} %get-tuple-element.31), channel_id=1, source_target_pairs={{0,2},{1,3},{2,0},{3,1},{4,6},{5,7},{6,4},{7,5},{8,10},{9,11},{10,... | collective-permute-start | bytes 393224 | tf_op jit(solution)/shard_map/ppermute | solution.py:576
  44.3 10.5 %shard_map.87 = (s32[8,20,256]{2,1,0:T(8,128)S(1)}, s32[8,20,128]{2,1,0:T(8,128)S(1)}, s32[8,5,128]{2,1,0:T(8,128)S(1)}) custom-call(s32[2]{0:T(128)S(1)} %pad_add_fusion.here_ref, s32[320,512]{1,0:T(8,128)S(1)} %copy-done), custom_call_target="tpu_custom_call" | custom-call | flops 2684354560 | bytes 327680 | tf_op jit(solution)/shard_map/pallas_call | solution.py:299
  55.0 1.7 collective-permute-start.3
  56.8 2.7 %collective-permute-start.4 = (bf16[128,256]{1,0:T(8,128)(2,1)S(1)}, bf16[128,256]{1,0:T(8,128)(2,1)S(1)}, u32[]{:S(2)}, u32[]{:S(2)}) collective-permute-start(bf16[128,256]{1,0:T(8,128)(2,1)S(1)} %shard_map.88.rest_0_), channel_id=1, source_target_pairs={{0,2},{1,3},{2,0},{3,1},{4,6},{5,7},{6,4},{7,5},{8,10},{9,11},{10,... | collective-permute-start | bytes 196616 | tf_op jit(solution)/shard_map/ppermute | solution.py:576
  59.5 8.8 %shard_map.89.meta_ref = f32[8,20,72,128]{3,2,1,0:T(8,128)S(1)} custom-call(s32[2]{0:T(128)S(1)} %pad_add_fusion.here_ref, s32[320,512]{1,0:T(8,128)S(1)} %copy-done.1, f32[320,512]{1,0:T(8,128)S(1)} %copy-done.2, s32[8,20,256]{2,1,0:T(8,128)S(1)} %get-tuple-element.34.pos_ref), custom_call_target="tpu_custom_call" | custom-call | flops 3019898880 | bytes 11796480 | tf_op jit(solution)/shard_map/pallas_call | solution.py:329
  68.4 64.9 %shard_map.90 = (bf16[2,4096,128]{2,1,0:T(8,128)(2,1)S(1)}, bf16[2,4096,128]{2,1,0:T(8,128)(2,1)S(1)}) custom-call(s32[1]{0:T(128)} %bitcast.me_ref, s32[8,20,128]{2,1,0:T(8,128)S(1)} %get-tuple-element.26.addr_ref, s32[8,5,128]{2,1,0:T(8,128)S(1)} %get-tuple-element.27.item_ref, bf16[512,20480]{1,0:T(8,128)(2,1)} %copy-done.6, ...), custom_call_target="tpu_custom_call" | custom-call | flops 42949672960 | bytes 20971520 | tf_op jit(solution)/shard_map/pallas_call | solution.py:538
  133.5 4.0 %collective-permute-done.6 = bf16[2,4096,128]{2,1,0:T(8,128)(2,1)S(1)} collective-permute-done((bf16[2,4096,128]{2,1,0:T(8,128)(2,1)S(1)}, bf16[2,4096,128]{2,1,0:T(8,128)(2,1)S(1)}, u32[]{:S(2)}, u32[]{:S(2)}) %collective-permute-start.6) | collective-permute-done | bytes 2097184 | tf_op jit(solution)/shard_map/ppermute | solution.py:576
  137.7 1.8 collective-permute-start.9
  139.6 1.7 collective-permute-start.7
  141.4 10.3 %collective-permute-done.9 = bf16[2,1,1024,128]{3,2,1,0:T(8,128)(2,1)S(1)} collective-permute-done((bf16[2,1,1024,128]{3,2,1,0:T(8,128)(2,1)S(1)}, bf16[2,1,1024,128]{3,2,1,0:T(8,128)(2,1)S(1)}, u32[]{:S(2)}, u32[]{:S(2)}) %collective-permute-start.9) | collective-permute-done | bytes 524320 | tf_op jit(solution)/shard_map/ppermute | solution.py:576
  151.8 1.9 %collective-permute-start.10 = (bf16[1,1,1024,128]{3,2,1,0:T(8,128)(2,1)S(1)}, bf16[1,1,1024,128]{3,2,1,0:T(8,128)(2,1)S(1)}, u32[]{:S(2)}, u32[]{:S(2)}) collective-permute-start(bf16[1,1,1024,128]{3,2,1,0:T(8,128)(2,1)S(1)} %add_convert_fusion.3), channel_id=1, source_target_pairs={{0,8},{4,12},{8,0},{12,4},{16,24},{20,28},{24,16},{28,20},{1,9},{5... | collective-permute-start | bytes 786440 | tf_op jit(solution)/shard_map/ppermute | solution.py:576
  153.8 1.6 collective-permute-start.8
  155.4 4.1 %collective-permute-done.10 = bf16[1,1,1024,128]{3,2,1,0:T(8,128)(2,1)S(1)} collective-permute-done((bf16[1,1,1024,128]{3,2,1,0:T(8,128)(2,1)S(1)}, bf16[1,1,1024,128]{3,2,1,0:T(8,128)(2,1)S(1)}, u32[]{:S(2)}, u32[]{:S(2)}) %collective-permute-start.10) | collective-permute-done | bytes 262176 | tf_op jit(solution)/shard_map/ppermute | solution.py:576
  159.5 1.6 collective-permute-done.8
  161.9 5.9 %collective-permute-done.11 = bf16[2,512,128]{2,1,0:T(8,128)(2,1)S(1)} collective-permute-done((bf16[2,512,128]{2,1,0:T(8,128)(2,1)S(1)}, bf16[2,512,128]{2,1,0:T(8,128)(2,1)S(1)}, u32[]{:S(2)}, u32[]{:S(2)}) %collective-permute-start.11) | collective-permute-done | bytes 262176 | tf_op jit(solution)/shard_map/ppermute | solution.py:576
  167.8 2.5 %collective-permute-start.12 = (bf16[2,256,128]{2,1,0:T(8,128)(2,1)S(1)}, bf16[2,256,128]{2,1,0:T(8,128)(2,1)S(1)}, u32[]{:S(2)}, u32[]{:S(2)}) collective-permute-start(bf16[2,256,128]{2,1,0:T(8,128)(2,1)S(1)} %add_convert_fusion.5), channel_id=1, source_target_pairs={{0,2},{1,3},{2,0},{3,1},{4,6},{5,7},{6,4},{7,5},{8,10},{9,11},{10,... | collective-permute-start | bytes 393224 | tf_op jit(solution)/shard_map/ppermute | solution.py:576
  170.3 4.8 %collective-permute-done.12 = bf16[2,256,128]{2,1,0:T(8,128)(2,1)S(1)} collective-permute-done((bf16[2,256,128]{2,1,0:T(8,128)(2,1)S(1)}, bf16[2,256,128]{2,1,0:T(8,128)(2,1)S(1)}, u32[]{:S(2)}, u32[]{:S(2)}) %collective-permute-start.12) | collective-permute-done | bytes 131104 | tf_op jit(solution)/shard_map/ppermute | solution.py:576
  176.0 1.4 collective-permute-start.13
  179.5 2.5 %collective-permute-done.13 = bf16[256,256]{1,0:T(8,128)(2,1)S(1)} collective-permute-done((bf16[256,256]{1,0:T(8,128)(2,1)S(1)}, bf16[256,256]{1,0:T(8,128)(2,1)S(1)}, u32[]{:S(2)}, u32[]{:S(2)}) %collective-permute-start.13) | collective-permute-done | bytes 131104 | tf_op jit(solution)/shard_map/ppermute | solution.py:576
  181.9 1.3 collective-permute-done.14
  183.9 1.9 %collective-permute-done.16 = bf16[4,256,256]{2,1,0:T(8,128)(2,1)S(1)} collective-permute-done((bf16[4,256,256]{2,1,0:T(8,128)(2,1)S(1)}, bf16[4,256,256]{2,1,0:T(8,128)(2,1)S(1)}, u32[]{:S(2)}, u32[]{:S(2)}) %collective-permute-start.16) | collective-permute-done | bytes 524320 | tf_op jit(solution)/shard_map/ppermute | solution.py:576
  (50 shorter events, 8.1 us)
Async XLA Ops:
  0.6 0.7 copy-start.3
  1.3 0.7 copy-start.5
  2.0 42.3 %copy-start = (s32[320,512]{1,0:T(8,128)S(1)}, s32[320,512]{1,0:T(8,128)}, u32[]{:S(2)}) copy-start(s32[320,512]{1,0:T(8,128)} %dest_ref.1) | copy-start | bytes 1966084
  31.6 7.0 %copy-start.6 = (bf16[512,20480]{1,0:T(8,128)(2,1)}, bf16[512,20480]{1,0:T(8,128)(2,1)S(1)}, u32[]{:S(2)}) copy-start(bf16[512,20480]{1,0:T(8,128)(2,1)S(1)} %get-tuple-element.28.x_ref) | copy-start | bytes 62914564
  38.6 16.2 %collective-permute-start = (f32[128,256]{1,0:T(8,128)S(1)}, f32[128,256]{1,0:T(8,128)S(1)}, u32[]{:S(2)}, u32[]{:S(2)}) collective-permute-start(f32[128,256]{1,0:T(8,128)S(1)} %get-tuple-element.30), channel_id=1, source_target_pairs={{0,1},{1,0},{2,3},{3,2},{4,5},{5,4},{6,7},{7,6},{8,9},{9,8},{10,11... | collective-permute-start | bytes 393224 | tf_op jit(solution)/shard_map/ppermute | solution.py:576
  41.6 13.2 %collective-permute-start.1 = (f32[128,256]{1,0:T(8,128)S(1)}, f32[128,256]{1,0:T(8,128)S(1)}, u32[]{:S(2)}, u32[]{:S(2)}) collective-permute-start(f32[128,256]{1,0:T(8,128)S(1)} %get-tuple-element.31), channel_id=1, source_target_pairs={{0,2},{1,3},{2,0},{3,1},{4,6},{5,7},{6,4},{7,5},{8,10},{9,11},{10,... | collective-permute-start | bytes 393224 | tf_op jit(solution)/shard_map/ppermute | solution.py:576
  44.2 10.6 %collective-permute-start.2 = (f32[128,256]{1,0:T(8,128)S(1)}, f32[128,256]{1,0:T(8,128)S(1)}, u32[]{:S(2)}, u32[]{:S(2)}) collective-permute-start(f32[128,256]{1,0:T(8,128)S(1)} %get-tuple-element.32), channel_id=1, source_target_pairs={{0,3},{1,2},{2,1},{3,0},{4,7},{5,6},{6,5},{7,4},{8,11},{9,10},{10,... | collective-permute-start | bytes 393224 | tf_op jit(solution)/shard_map/ppermute | solution.py:576
  44.3 15.2 %copy-start.1 = (s32[320,512]{1,0:T(8,128)S(1)}, s32[320,512]{1,0:T(8,128)}, u32[]{:S(2)}) copy-start(s32[320,512]{1,0:T(8,128)} %index_ref.1) | copy-start | bytes 1966084
  44.3 15.2 %copy-start.2 = (f32[320,512]{1,0:T(8,128)S(1)}, f32[320,512]{1,0:T(8,128)}, u32[]{:S(2)}) copy-start(f32[320,512]{1,0:T(8,128)} %frac_ref.1) | copy-start | bytes 1966084
  55.0 13.3 %copy-start.4 = (s32[512,2]{0,1:T(2,128)S(1)}, s32[512,2]{0,1:T(2,128)}, u32[]{:S(2)}) copy-start(s32[512,2]{0,1:T(2,128)} %param.8) | copy-start | bytes 12292
  55.0 13.3 %collective-permute-start.3 = (bf16[128,256]{1,0:T(8,128)(2,1)S(1)}, bf16[128,256]{1,0:T(8,128)(2,1)S(1)}, u32[]{:S(2)}, u32[]{:S(2)}) collective-permute-start(bf16[128,256]{1,0:T(8,128)(2,1)S(1)} %shard_map.88.rest_0_), channel_id=1, source_target_pairs={{0,1},{1,0},{2,3},{3,2},{4,5},{5,4},{6,7},{7,6},{8,9},{9,8},{10,11... | collective-permute-start | bytes 196616 | tf_op jit(solution)/shard_map/ppermute | solution.py:576
  56.8 11.6 %collective-permute-start.4 = (bf16[128,256]{1,0:T(8,128)(2,1)S(1)}, bf16[128,256]{1,0:T(8,128)(2,1)S(1)}, u32[]{:S(2)}, u32[]{:S(2)}) collective-permute-start(bf16[128,256]{1,0:T(8,128)(2,1)S(1)} %shard_map.88.rest_0_), channel_id=1, source_target_pairs={{0,2},{1,3},{2,0},{3,1},{4,6},{5,7},{6,4},{7,5},{8,10},{9,11},{10,... | collective-permute-start | bytes 196616 | tf_op jit(solution)/shard_map/ppermute | solution.py:576
  59.5 8.9 %collective-permute-start.5 = (bf16[128,256]{1,0:T(8,128)(2,1)S(1)}, bf16[128,256]{1,0:T(8,128)(2,1)S(1)}, u32[]{:S(2)}, u32[]{:S(2)}) collective-permute-start(bf16[128,256]{1,0:T(8,128)(2,1)S(1)} %shard_map.88.rest_0_), channel_id=1, source_target_pairs={{0,3},{1,2},{2,1},{3,0},{4,7},{5,6},{6,5},{7,4},{8,11},{9,10},{10,... | collective-permute-start | bytes 196616 | tf_op jit(solution)/shard_map/ppermute | solution.py:576
  133.3 4.2 %collective-permute-start.6 = (bf16[2,4096,128]{2,1,0:T(8,128)(2,1)S(1)}, bf16[2,4096,128]{2,1,0:T(8,128)(2,1)S(1)}, u32[]{:S(2)}, u32[]{:S(2)}) collective-permute-start(bf16[2,4096,128]{2,1,0:T(8,128)(2,1)S(1)} %get-tuple-element.37), channel_id=1, source_target_pairs={{0,4},{4,0},{8,12},{12,8},{16,20},{20,16},{24,28},{28,24},{1,5},{5... | collective-permute-start | bytes 6291464 | tf_op jit(solution)/shard_map/ppermute | solution.py:576
  137.7 14.0 %collective-permute-start.9 = (bf16[2,1,1024,128]{3,2,1,0:T(8,128)(2,1)S(1)}, bf16[2,1,1024,128]{3,2,1,0:T(8,128)(2,1)S(1)}, u32[]{:S(2)}, u32[]{:S(2)}) collective-permute-start(bf16[2,1,1024,128]{3,2,1,0:T(8,128)(2,1)S(1)} %add_convert_fusion), channel_id=1, source_target_pairs={{0,16},{4,20},{8,24},{12,28},{16,0},{20,4},{24,8},{28,12},{1,17},{... | collective-permute-start | bytes 1572872 | tf_op jit(solution)/shard_map/ppermute | solution.py:576
  139.6 14.1 %collective-permute-start.7 = (bf16[1,2,1024,128]{3,2,1,0:T(8,128)(2,1)S(1)}, bf16[1,2,1024,128]{3,2,1,0:T(8,128)(2,1)S(1)}, u32[]{:S(2)}, u32[]{:S(2)}) collective-permute-start(bf16[1,2,1024,128]{3,2,1,0:T(8,128)(2,1)S(1)} %bitcast.57), channel_id=1, source_target_pairs={{0,8},{4,12},{8,0},{12,4},{16,24},{20,28},{24,16},{28,20},{1,9},{5... | collective-permute-start | bytes 1572872 | tf_op jit(solution)/shard_map/ppermute | solution.py:576
  151.8 7.7 %collective-permute-start.10 = (bf16[1,1,1024,128]{3,2,1,0:T(8,128)(2,1)S(1)}, bf16[1,1,1024,128]{3,2,1,0:T(8,128)(2,1)S(1)}, u32[]{:S(2)}, u32[]{:S(2)}) collective-permute-start(bf16[1,1,1024,128]{3,2,1,0:T(8,128)(2,1)S(1)} %add_convert_fusion.3), channel_id=1, source_target_pairs={{0,8},{4,12},{8,0},{12,4},{16,24},{20,28},{24,16},{28,20},{1,9},{5... | collective-permute-start | bytes 786440 | tf_op jit(solution)/shard_map/ppermute | solution.py:576
  153.8 7.3 %collective-permute-start.8 = (bf16[1,1,1024,128]{3,2,1,0:T(8,128)(2,1)S(1)}, bf16[1,1,1024,128]{3,2,1,0:T(8,128)(2,1)S(1)}, u32[]{:S(2)}, u32[]{:S(2)}) collective-permute-start(bf16[1,1,1024,128]{3,2,1,0:T(8,128)(2,1)S(1)} %add_convert_fusion.4), channel_id=1, source_target_pairs={{0,16},{4,20},{8,24},{12,28},{16,0},{20,4},{24,8},{28,12},{1,17},{... | collective-permute-start | bytes 786440 | tf_op jit(solution)/shard_map/ppermute | solution.py:576
  161.3 6.4 %collective-permute-start.11 = (bf16[2,512,128]{2,1,0:T(8,128)(2,1)S(1)}, bf16[2,512,128]{2,1,0:T(8,128)(2,1)S(1)}, u32[]{:S(2)}, u32[]{:S(2)}) collective-permute-start(bf16[2,512,128]{2,1,0:T(8,128)(2,1)S(1)} %add_convert_fusion.2), channel_id=1, source_target_pairs={{0,1},{1,0},{2,3},{3,2},{4,5},{5,4},{6,7},{7,6},{8,9},{9,8},{10,11... | collective-permute-start | bytes 786440 | tf_op jit(solution)/shard_map/ppermute | solution.py:576
  167.8 7.3 %collective-permute-start.12 = (bf16[2,256,128]{2,1,0:T(8,128)(2,1)S(1)}, bf16[2,256,128]{2,1,0:T(8,128)(2,1)S(1)}, u32[]{:S(2)}, u32[]{:S(2)}) collective-permute-start(bf16[2,256,128]{2,1,0:T(8,128)(2,1)S(1)} %add_convert_fusion.5), channel_id=1, source_target_pairs={{0,2},{1,3},{2,0},{3,1},{4,6},{5,7},{6,4},{7,5},{8,10},{9,11},{10,... | collective-permute-start | bytes 393224 | tf_op jit(solution)/shard_map/ppermute | solution.py:576
  176.0 6.0 %collective-permute-start.13 = (bf16[256,256]{1,0:T(8,128)(2,1)S(1)}, bf16[256,256]{1,0:T(8,128)(2,1)S(1)}, u32[]{:S(2)}, u32[]{:S(2)}) collective-permute-start(bf16[256,256]{1,0:T(8,128)(2,1)S(1)} %get-tuple-element.38), channel_id=1, source_target_pairs={{0,24},{4,28},{8,16},{12,20},{16,8},{20,12},{24,0},{28,4},{1,25},{... | collective-permute-start | bytes 393224 | tf_op jit(solution)/shard_map/ppermute | solution.py:576
  177.3 5.9 %collective-permute-start.14 = (bf16[256,256]{1,0:T(8,128)(2,1)S(1)}, bf16[256,256]{1,0:T(8,128)(2,1)S(1)}, u32[]{:S(2)}, u32[]{:S(2)}) collective-permute-start(bf16[256,256]{1,0:T(8,128)(2,1)S(1)} %get-tuple-element.38), channel_id=1, source_target_pairs={{0,16},{4,20},{8,24},{12,28},{16,0},{20,4},{24,8},{28,12},{1,17},{... | collective-permute-start | bytes 393224 | tf_op jit(solution)/shard_map/ppermute | solution.py:576
  178.6 5.0 %collective-permute-start.15 = (bf16[256,256]{1,0:T(8,128)(2,1)S(1)}, bf16[256,256]{1,0:T(8,128)(2,1)S(1)}, u32[]{:S(2)}, u32[]{:S(2)}) collective-permute-start(bf16[256,256]{1,0:T(8,128)(2,1)S(1)} %get-tuple-element.38), channel_id=1, source_target_pairs={{0,8},{4,12},{8,0},{12,4},{16,24},{20,28},{24,16},{28,20},{1,9},{5... | collective-permute-start | bytes 393224 | tf_op jit(solution)/shard_map/ppermute | solution.py:576
  183.8 2.0 %collective-permute-start.16 = (bf16[4,256,256]{2,1,0:T(8,128)(2,1)S(1)}, bf16[4,256,256]{2,1,0:T(8,128)(2,1)S(1)}, u32[]{:S(2)}, u32[]{:S(2)}) collective-permute-start(bf16[4,256,256]{2,1,0:T(8,128)(2,1)S(1)} %get-tuple-element.41), channel_id=1, source_target_pairs={{0,4},{4,0},{8,12},{12,8},{16,20},{20,16},{24,28},{28,24},{1,5},{5... | collective-permute-start | bytes 1572872 | tf_op jit(solution)/shard_map/ppermute | solution.py:576

commit v9 on v8

--- a/solution.py
+++ b/solution.py
@@ -28,12 +28,13 @@
             cols_ref[j, at : at + OB, :] = jnp.broadcast_to(line, (OB, OB)).T
 
 
-def score_kernel(me_ref, noise_ref, x_ref, r_ref, blk_ref, flat_ref, *rest):
+def score_kernel(here_ref, noise_ref, x_ref, r_ref, blk_ref, keep_ref, send_ref, *rest):
     *out_refs, w_ref, acc_ref, perm_ref, cols_ref = rest
     step = pl.program_id(0)
     particles, gb, width = x_ref.shape
     orients = r_ref.shape[0]
     side = 16 * gb
+    core = here_ref[0] & 1
 
     @pl.when(step == 0)
     def _():
@@ -46,48 +47,64 @@
 
     perm = perm_ref[...]
 
+    per = gb // 2
+    weighted = (w_ref.at[0], w_ref.at[1])
+
     def regroup(jobs):
         at = [pl.multiple_of(first * 16, 16) for _, _, _, first in jobs]
         wide = [job[0][pl.ds(a, 16)].reshape(side, width) for job, a in zip(jobs, at)]
         moved = jnp.dot(perm, jnp.concatenate(wide, axis=1), preferred_element_type=F32)
         for g in range(gb):
-            for t, (_, dst_ref, scaled, _) in enumerate(jobs):
+            lanes = slice(g % per * width, (g % per + 1) * width)
+            for t, (_, halves, scaled, _) in enumerate(jobs):
                 part = moved[g * 16 : (g + 1) * 16, t * width : (t + 1) * width]
                 if scaled:
                     part = part * noise_ref[step * gb + g]
-                dst_ref[pl.ds(at[t], 16), g * width : (g + 1) * width] = part.astype(BF16)
-
-    def turn(src_ref, dst_ref, first):
+                halves[g // per][pl.ds(at[t], 16), lanes] = part.astype(BF16)
+
+    def turn(src_ref, halves, first):
         at = pl.ds(pl.multiple_of(first * 16, 16), 16)
         turned = jnp.swapaxes(src_ref[at], 0, 1)
         for g in range(gb):
-            dst_ref[at, g * width : (g + 1) * width] = turned[g]
-
-    def tiles(i, carry):
-        jobs = [(r_ref, w_ref, True, i * 4 + t) for t in range(4)]
-        regroup(jobs + [(x_ref, flat_ref, False, i * 4)])
-        for t in range(1, 4):
-            turn(x_ref, flat_ref, i * 4 + t)
-        return carry
-
-    def more_tiles(src_ref, dst_ref, scaled):
-        def body(i, carry):
-            regroup([(src_ref, dst_ref, scaled, i)])
+            halves[g // per][at, g % per * width : (g % per + 1) * width] = turned[g]
+
+    both = min(particles, orients) // 64
+
+    def all_tiles(halves):
+        def tiles(i, carry):
+            jobs = [(r_ref, weighted, True, i * 4 + t) for t in range(4)]
+            regroup(jobs + [(x_ref, halves, False, i * 4)])
+            for t in range(1, 4):
+                turn(x_ref, halves, i * 4 + t)
             return carry
 
-        lax.fori_loop(both * 4, src_ref.shape[0] // 16, body, 0)
-
-    both = min(particles, orients) // 64
-    lax.fori_loop(0, both, tiles, 0, unroll=2)
-    more_tiles(r_ref, w_ref, True)
-    more_tiles(x_ref, flat_ref, False)
-    acc_ref[...] += lax.dot_general(
-        flat_ref[...], w_ref[...], (((1,), (1,)), ((), ())), preferred_element_type=F32
-    )
+        def more_tiles(src_ref, goal, scaled):
+            def body(i, carry):
+                regroup([(src_ref, goal, scaled, i)])
+                return carry
+
+            lax.fori_loop(both * 4, src_ref.shape[0] // 16, body, 0)
+
+        lax.fori_loop(0, both, tiles, 0, unroll=2)
+        more_tiles(r_ref, weighted, True)
+        more_tiles(x_ref, halves, False)
+
+    @pl.when(core == 0)
+    def _():
+        all_tiles((keep_ref, send_ref))
+
+    @pl.when(core == 1)
+    def _():
+        all_tiles((send_ref, keep_ref))
+
+    for half_ref, which in ((keep_ref, core), (send_ref, 1 - core)):
+        acc_ref[...] += lax.dot_general(
+            half_ref[...], w_ref[which], (((1,), (1,)), ((), ())), preferred_element_type=F32
+        )
 
     @pl.when(step == pl.num_programs(0) - 1)
     def _():
-        me = me_ref[0]
+        me = here_ref[1]
         share = particles // len(out_refs)
         for k, out_ref in enumerate(out_refs):
             at = pl.multiple_of((me ^ k) * share, share)
@@ -100,7 +117,7 @@
                 out_ref[:, j * OB : (j + 1) * OB] = chosen
 
 
-def score_call(me, inv_noise, particles, references, blocks, slab_size):
+def score_call(here, inv_noise, particles, references, blocks, slab_size):
     count, groups, width = particles.shape
     orients = references.shape[0]
     gb = group_block(groups)
@@ -110,7 +127,7 @@
     return pl.pallas_call(
         score_kernel,
         grid=(groups // gb,),
-        out_shape=[jax.ShapeDtypeStruct((count, groups * width), BF16)]
+        out_shape=[jax.ShapeDtypeStruct((count, groups // 2 * width), BF16)] * 2
         + [jax.ShapeDtypeStruct((share, 2 * OB), F32)] * slab_size,
         in_specs=[
             smem,
@@ -119,21 +136,21 @@
             pl.BlockSpec((orients, gb, width), lambda i: (0, i, 0)),
             pl.BlockSpec((2, count), lambda i: (0, 0)),
         ],
-        out_specs=[pl.BlockSpec((count, gb * width), lambda i: (0, i))]
+        out_specs=[pl.BlockSpec((count, gb // 2 * width), lambda i: (0, i))] * 2
         + [pl.BlockSpec((share, 2 * OB), lambda i: (0, 0))] * slab_size,
         scratch_shapes=[
-            pltpu.VMEM((orients, gb * width), BF16),
+            pltpu.VMEM((2, orients, gb // 2 * width), BF16),
             pltpu.VMEM((count, orients), F32),
             pltpu.VMEM((side, side), BF16),
             pltpu.VMEM((2, count, OB), F32),
         ],
-        compiler_params=pltpu.CompilerParams(vmem_limit_bytes=32 * MB),
+        compiler_params=pltpu.CompilerParams(vmem_limit_bytes=56 * MB),
         cost_estimate=pl.CostEstimate(
             flops=4 * count * orients * groups * width,
             bytes_accessed=6 * count * groups * width,
             transcendentals=0,
         ),
-    )(me, inv_noise, particles, references, blocks)
+    )(here, inv_noise, particles, references, blocks)
 
 
 def softmax_kernel(*refs):
@@ -154,8 +171,12 @@
     )(*parts)
 
 
+def own_row(here_ref, local, per):
+    return lax.div(local, per) * (2 * per) + (here_ref[0] & 1) * per + lax.rem(local, per)
+
+
 def plan_kernel(
-    here_ref, dest_ref, pos_ref, addr_ref, item_ref, place_ref, hot_ref, count_ref, *, sizes
+    here_ref, dest_ref, pos_ref, addr_ref, item_ref, place_ref, hot_ref, count_ref, *, sizes, per
 ):
     step = pl.program_id(0)
     dom_size, slab_size = sizes
@@ -177,7 +198,8 @@
     owner = lax.broadcasted_iota(jnp.int32, (owners, 1), 0)
     for u in range(units):
         g, h = u // parts, u % parts
-        line = place_ref[pl.ds(step * gb + g, 1), h * half : (h + 1) * half]
+        at = pl.ds(own_row(here_ref, step * gb + g, per), 1)
+        line = place_ref[at, h * half : (h + 1) * half]
         hot = jnp.where(line == owner, 1.0, 0.0)
         hot_ref[u * owners : (u + 1) * owners, :] = hot.astype(BF16)
     before = lax.broadcasted_iota(jnp.int32, (half, half), 0)
@@ -241,7 +263,7 @@
         item_ref[0, i : i + 1, :] = value.astype(jnp.int32)
 
 
-def meta_kernel(here_ref, index_ref, frac_ref, pos_ref, meta_ref):
+def meta_kernel(here_ref, index_ref, frac_ref, pos_ref, meta_ref, *, per):
     step = pl.program_id(0)
     _, units, half = pos_ref.shape
     parts = index_ref.shape[1] // half
@@ -253,7 +275,7 @@
     one, none = jnp.bfloat16(1.0), jnp.bfloat16(0.0)
     for u in range(units):
         g, h = u // parts, u % parts
-        line = pl.ds(step * gb + g, 1)
+        line = pl.ds(own_row(here_ref, step * gb + g, per), 1)
         span = slice(h * half, (h + 1) * half)
         pos = pos_ref[0, u : u + 1, :]
         here = lane_of == low(pos & 7)
@@ -289,7 +311,7 @@
     orients = destination.shape[1]
     half = min(256, orients)
     owners = mesh_sizes[0] * mesh_sizes[1]
-    steps, units = groups // gb, gb * (orients // half)
+    steps, units = groups // 2 // gb, gb * (orients // half)
     slots, _, blocks = sort_sizes(half, owners)
     shapes = [
         (steps, units, half),
@@ -297,7 +319,7 @@
         (steps, 5, up_to(owners + units * slots // RD + 8, 128)),
     ]
     return pl.pallas_call(
-        functools.partial(plan_kernel, sizes=mesh_sizes),
+        functools.partial(plan_kernel, sizes=mesh_sizes, per=group_block(groups) // 2),
         grid_spec=pltpu.PrefetchScalarGridSpec(
             num_scalar_prefetch=1,
             grid=(steps,),
@@ -310,7 +332,7 @@
             ],
         ),
         out_shape=[jax.ShapeDtypeStruct(shape, jnp.int32) for shape in shapes],
-        compiler_params=pltpu.CompilerParams(vmem_limit_bytes=16 * MB),
+        compiler_params=pltpu.CompilerParams(vmem_limit_bytes=60 * MB),
         cost_estimate=pl.CostEstimate(
             flops=8 * steps * units * owners * half * half,
             bytes_accessed=8 * groups * orients,
@@ -322,12 +344,12 @@
 def meta_call(here, row_index, fraction, pos, owners):
     steps, units, half = pos.shape
     orients = row_index.shape[1]
-    groups = steps * units * half // orients
+    groups = 2 * steps * units * half // orients
     blocks = sort_sizes(half, owners)[2]
     shape = (steps, units, blocks, OB)
     table = pl.BlockSpec((groups, orients), lambda i, here: (here[1], 0))
     return pl.pallas_call(
-        meta_kernel,
+        functools.partial(meta_kernel, per=group_block(groups) // 2),
         grid_spec=pltpu.PrefetchScalarGridSpec(
             num_scalar_prefetch=1,
             grid=(steps,),
@@ -344,12 +366,14 @@
     )(here, row_index, fraction, pos)
 
 
-def insert_kernel(me_ref, addr_ref, item_ref, x_ref, pos_ref, meta_ref, blk_ref, *rest):
-    *post_refs, send_ref, keep_ref = rest[:-10]
+def insert_kernel(
+    me_ref, addr_ref, item_ref, x_ref, y_ref, pos_ref, meta_ref, blk_ref, more_blk_ref, *rest
+):
+    *post_refs, more_ref, send_ref, keep_ref = rest[:-10]
     post_t, spread_ref, cols_ref, slice_a, slice_b, buf_s, buf_m, volume, stage, sem = rest[-10:]
     step = pl.program_id(0)
     count = x_ref.shape[0]
-    orients = post_t.shape[0]
+    orients = post_t.shape[1]
     units, half = pos_ref.shape[1:]
     parts = orients // half
     gb = units // parts
@@ -361,19 +385,22 @@
     def _():
         volume[...] = jnp.zeros_like(volume)
         me = me_ref[0]
-        spread_columns(blk_ref, cols_ref)
-        for k, post_ref in enumerate(post_refs):
-            at = pl.multiple_of((me ^ k) * share, share)
-            post = post_ref[...].astype(F32)
-            first = cols_ref[0, pl.ds(at, share), :]
-            second = cols_ref[1, pl.ds(at, share), :]
+        others = [more_ref.at[k] for k in range(len(post_refs))]
+        for who, (lists, pieces) in enumerate(((blk_ref, post_refs), (more_blk_ref, others))):
+            spread_columns(lists, cols_ref)
+            for k, post_ref in enumerate(pieces):
+                at = pl.multiple_of((me ^ k) * share, share)
+                post = post_ref[...].astype(F32)
+                first = cols_ref[0, pl.ds(at, share), :]
+                second = cols_ref[1, pl.ds(at, share), :]
+                for b in range(orients // OB):
+                    spread = jnp.where(
+                        first == b, post[:, :OB], jnp.where(second == b, post[:, OB:], 0.0)
+                    )
+                    spread_ref[pl.ds(at, share), b * OB : (b + 1) * OB] = spread
             for b in range(orients // OB):
-                spread = jnp.where(
-                    first == b, post[:, :OB], jnp.where(second == b, post[:, OB:], 0.0)
-                )
-                spread_ref[pl.ds(at, share), b * OB : (b + 1) * OB] = spread
-        for b in range(orients // OB):
-            post_t[b * OB : (b + 1) * OB] = spread_ref[:, b * OB : (b + 1) * OB].T.astype(BF16)
+                rows = slice(b * OB, (b + 1) * OB)
+                post_t[who, rows] = spread_ref[:, rows].T.astype(BF16)
 
     tail = pl.ds(pl.multiple_of(item_ref[0, 4, 0] * 8, 8), RD)
     buf_s[tail, :] = jnp.zeros((RD, width), F32)
@@ -384,7 +411,8 @@
 
     def slices(q, dst_ref):
         at = pl.ds(pl.multiple_of(q * (per * width), per * width), per * width)
-        value = jnp.dot(post_t[...], x_ref[:, at], preferred_element_type=F32)
+        value = jnp.dot(post_t[0], x_ref[:, at], preferred_element_type=F32)
+        value = value + jnp.dot(post_t[1], y_ref[:, at], preferred_element_type=F32)
         dst_ref[...] = value.astype(BF16)
 
     def emit(u, piece, base, size):
@@ -511,26 +539,26 @@
 def insert_block(groups, orients, owners, count, width):
     half = min(256, orients)
     slots, _, blocks = sort_sizes(half, owners)
-    room = max(27 * MB - owners * RD * width * 4, 18 * MB)
+    room = max(32 * MB - owners * RD * width * 4, 18 * MB)
     best = 1
     for gb in range(1, groups + 1):
         units = gb * (orients // half)
         rows = units * slots + RD + 8
-        need = rows * (width * 4 + OB // 2) + 4 * count * gb * width + units * blocks * OB * 8
+        need = rows * (width * 4 + OB // 2) + 8 * count * gb * width + units * blocks * OB * 8
         if groups % gb == 0 and need <= room:
             best = gb
     return best
 
 
-def insert_call(me, addr, items, flat, pos, meta, blocks, posts, orients, owners):
-    count, length = flat.shape
+def insert_call(me, addr, items, flats, pos, meta, blocks, posts, more, orients, owners):
+    count, length = flats[0].shape
     steps, units, half = pos.shape
     gb = units * half // orients
     width = length // (steps * gb)
     total = owners * RD
     share = posts[0].shape[0]
     rows = units * sort_sizes(half, owners)[0] + RD + 8
-    limit = total * width * 4 // MB + 26
+    limit = total * width * 4 // MB + 30
     smem = pl.BlockSpec(memory_space=pltpu.SMEM)
     block = lambda shape, **kw: pl.BlockSpec(
         (1,) + shape[1:], lambda i: (i,) + (0,) * (len(shape) - 1), **kw
@@ -544,14 +572,17 @@
             block(addr.shape, memory_space=pltpu.SMEM),
             block(items.shape, memory_space=pltpu.SMEM),
             pl.BlockSpec((count, gb * width), lambda i: (0, i)),
+            pl.BlockSpec((count, gb * width), lambda i: (0, i)),
             block(pos.shape),
             block(meta.shape),
             pl.BlockSpec((2, count), lambda i: (0, 0)),
+            pl.BlockSpec((2, count), lambda i: (0, 0)),
         ]
-        + [pl.BlockSpec((share, 2 * OB), lambda i: (0, 0))] * len(posts),
+        + [pl.BlockSpec((share, 2 * OB), lambda i: (0, 0))] * len(posts)
+        + [pl.BlockSpec(more.shape, lambda i: (0, 0, 0))],
         out_specs=[pl.BlockSpec(memory_space=pl.ANY)] * 2,
         scratch_shapes=[
-            pltpu.VMEM((orients, count), BF16),
+            pltpu.VMEM((2, orients, count), BF16),
             pltpu.VMEM((count, orients), F32),
             pltpu.VMEM((2, count, OB), F32),
             pltpu.VMEM((orients, group_pair(gb) * width), BF16),
@@ -562,13 +593,13 @@
             pltpu.VMEM((OUT_SLOTS, 2, OUT_TILE, OB), BF16),
             pltpu.SemaphoreType.DMA((OUT_SLOTS,)),
         ],
-        compiler_params=pltpu.CompilerParams(vmem_limit_bytes=max(34, limit) * MB),
+        compiler_params=pltpu.CompilerParams(vmem_limit_bytes=limit * MB),
         cost_estimate=pl.CostEstimate(
             flops=8 * count * orients * length,
             bytes_accessed=2 * count * length,
             transcendentals=0,
         ),
-    )(me, addr, items, flat, pos, meta, blocks, *posts)
+    )(me, addr, items, *flats, pos, meta, *blocks, *posts, more)
 
 
 def flip(value, axis, bit):
@@ -590,19 +621,22 @@
     slab_bits = [1 << i for i in range((slab_size - 1).bit_length())]
 
     blocks = blocks.T
-    flat, *scores = score_call(slab_me, inv_noise, particles, references, blocks, slab_size)
-    gb = insert_block(groups, orients, devices, particles.shape[0], width)
+    kept, sent, *scores = score_call(here, inv_noise, particles, references, blocks, slab_size)
+    gb = insert_block(groups // 2, orients, devices, particles.shape[0], width)
     here, own = lax.optimization_barrier((here, scores[0]))
     plan = plan_call(here, destination, groups, gb, (dom_size, slab_size))
     own, *plan = lax.optimization_barrier((own, *plan))
     pos, addr, items = plan
     parts = [own] + [flip(scores[k], "slab", k) for k in range(1, slab_size)]
+    flats = [kept, flip(sent, "dom", dom_bits[0])]
     post = softmax_call(parts)
     post, pos = lax.optimization_barrier((post, pos))
     meta = meta_call(here, row_index, fraction, pos, devices)
     posts = [post] + [flip(post, "slab", k) for k in range(1, slab_size)]
+    more = flip(jnp.stack(posts), "dom", dom_bits[0])
+    lists = [blocks, flip(blocks, "dom", dom_bits[0])]
     send, keep = insert_call(
-        slab_me, addr, items, flat, pos, meta, blocks, posts, orients, devices
+        slab_me, addr, items, flats, pos, meta, lists, posts, more, orients, devices
     )
 
     def added(terms):

time: 187 us -> 158 us (0.84)
  Pallas kernels: 114 us -> 82.4 us
  waiting for transfers between devices: 36.8 us -> 44.9 us
  local copies, waits for them, and re-layouts: 9.7 us -> 2.27 us
    pallas_call x1, Pallas kernels: 64.9 us -> 39.4 us  [insert_call(): pl.pallas_call(insert_kernel, grid=(steps,), out_shape=[jax.ShapeDtypeStr...]
    ppermute x17 -> x20, waiting for transfers between devices: 36.8 us -> 44.9 us  [flip(): return lax.ppermute(value, axis, [(i, i ^ bit) for i in range(size)])]
    unnamed x14 -> x16, local copies, waits for them, and re-layouts: 8.35 us -> 0.92 us
    pallas_call x2, Pallas kernels: 19.3 us -> 12.1 us  [the longest x1 7.41 us: plan_call(): pl.pallas_call(functools.partial(plan_kernel, sizes=mesh_sizes, per=group...]
    ppermute x17 -> x20, starting transfers between devices: 23.6 us -> 24.9 us  [flip(): return lax.ppermute(value, axis, [(i, i ^ bit) for i in range(size)])]
  transfers between devices with their start and end apart: 17 -> 20, of which waited for: 10 -> 12; matrix products, arithmetic and copies ran while one was open for 0% -> 0% of each run, Pallas kernels for 10% -> 8%
where the time goes in v9:
time: 158 us
  Pallas kernels  82.4 us (52%)
  waiting for transfers between devices  44.9 us (28%)
  starting transfers between devices  24.9 us (16%)
  other arithmetic  2.52 us (2%)
  local copies, waits for them, and re-layouts  2.27 us (1%)
    ppermute x20, waiting for transfers between devices, flip(): return lax.ppermute(value, axis, [(i, i ^ bit) for i in range(size)])  44.9 us
    pallas_call x1, Pallas kernels, insert_call(): pl.pallas_call(insert_kernel, grid=(steps,), out_shape=[jax.ShapeDtypeStr...  39.4 us
    pallas_call x1, Pallas kernels, score_call(): pl.pallas_call(score_kernel, grid=(groups // gb,), out_shape=[jax.ShapeDt...  30.8 us
    ppermute x20, starting transfers between devices, flip(): return lax.ppermute(value, axis, [(i, i ^ bit) for i in range(size)])  24.9 us
    pallas_call x1, Pallas kernels, plan_call(): pl.pallas_call(functools.partial(plan_kernel, sizes=mesh_sizes, per=group...  7.41 us
    pallas_call x1, Pallas kernels, meta_call(): pl.pallas_call(functools.partial(meta_kernel, per=group_block(groups) //...  4.69 us
  transfers between devices with their start and end apart: 20, of which 12 were waited for; matrix products, arithmetic and copies ran while one was open for 0% of the time, Pallas kernels for 8%

profile of v9, /device:TPU:0, one launch (start us, length us, event | category | flops | bytes accessed | tf_op | source)
XLA Modules:
  0.0 157.9 jit_solution(17729475379315226963)
XLA Ops:
  1.2 30.8 %shard_map.86 = (bf16[512,10240]{1,0:T(8,128)(2,1)}, bf16[512,10240]{1,0:T(8,128)(2,1)}, f32[128,256]{1,0:T(8,128)}, f32[128,256]{1,0:T(8,128)}, f32[128,256]{1,0:T(8,128)}, /*index=5*/f32[128,256]{1,0:T(8,128)}) custom-call(s32[2]{0:T(128)} %pad_add_fusion.here_ref, f32[80]{0:T(128)} %noise_ref.1, bf16[512,80,256]{2,1,0:T(8,128)(2,1)} %x_ref.1, ...), custom_call_target="tpu_custom_call" | custom-call | flops 21474836480 | bytes 62914560 | tf_op jit(solution)/shard_map/pallas_call | solution.py:127
  32.6 2.7 %collective-permute-start.1 = (f32[128,256]{1,0:T(8,128)}, f32[128,256]{1,0:T(8,128)S(1)}, u32[]{:S(2)}, u32[]{:S(2)}) collective-permute-start(f32[128,256]{1,0:T(8,128)} %get-tuple-element.32), channel_id=1, source_target_pairs={{0,1},{1,0},{2,3},{3,2},{4,5},{5,4},{6,7},{7,6},{8,9},{9,8},{10,11... | collective-permute-start | bytes 393224 | tf_op jit(solution)/shard_map/ppermute | solution.py:607
  35.2 2.6 %collective-permute-start.2 = (f32[128,256]{1,0:T(8,128)}, f32[128,256]{1,0:T(8,128)S(1)}, u32[]{:S(2)}, u32[]{:S(2)}) collective-permute-start(f32[128,256]{1,0:T(8,128)} %get-tuple-element.33), channel_id=1, source_target_pairs={{0,2},{1,3},{2,0},{3,1},{4,6},{5,7},{6,4},{7,5},{8,10},{9,11},{10,... | collective-permute-start | bytes 393224 | tf_op jit(solution)/shard_map/ppermute | solution.py:607
  37.8 7.4 %shard_map.87 = (s32[4,20,256]{2,1,0:T(8,128)}, s32[4,20,128]{2,1,0:T(8,128)}, s32[4,5,128]{2,1,0:T(8,128)}) custom-call(s32[2]{0:T(128)} %pad_add_fusion.here_ref, s32[320,512]{1,0:T(8,128)} %dest_ref.1), custom_call_target="tpu_custom_call" | custom-call | flops 1342177280 | bytes 327680 | tf_op jit(solution)/shard_map/pallas_call | solution.py:321
  45.2 3.1 %collective-permute-done.2.refs_2_ = f32[128,256]{1,0:T(8,128)S(1)} collective-permute-done((f32[128,256]{1,0:T(8,128)}, f32[128,256]{1,0:T(8,128)S(1)}, u32[]{:S(2)}, u32[]{:S(2)}) %collective-permute-start.2) | collective-permute-done | bytes 131104 | tf_op jit(solution)/shard_map/ppermute | solution.py:607
  48.5 2.7 %collective-permute-start.5 = (bf16[128,256]{1,0:T(8,128)(2,1)S(1)}, bf16[128,256]{1,0:T(8,128)(2,1)S(1)}, u32[]{:S(2)}, u32[]{:S(2)}) collective-permute-start(bf16[128,256]{1,0:T(8,128)(2,1)S(1)} %shard_map.88.rest_0_), channel_id=1, source_target_pairs={{0,1},{1,0},{2,3},{3,2},{4,5},{5,4},{6,7},{7,6},{8,9},{9,8},{10,11... | collective-permute-start | bytes 196616 | tf_op jit(solution)/shard_map/ppermute | solution.py:607
  53.7 5.0 %collective-permute-done.6.rest_2_ = bf16[128,256]{1,0:T(8,128)(2,1)S(1)} collective-permute-done((bf16[128,256]{1,0:T(8,128)(2,1)S(1)}, bf16[128,256]{1,0:T(8,128)(2,1)S(1)}, u32[]{:S(2)}, u32[]{:S(2)}) %collective-permute-start.6) | collective-permute-done | bytes 65568 | tf_op jit(solution)/shard_map/ppermute | solution.py:607
  60.2 4.7 %shard_map.89.meta_ref = f32[4,20,72,128]{3,2,1,0:T(8,128)S(1)} custom-call(s32[2]{0:T(128)S(1)} %copy-done.4, s32[320,512]{1,0:T(8,128)S(1)} %copy-done.1, f32[320,512]{1,0:T(8,128)S(1)} %copy-done.2, s32[4,20,256]{2,1,0:T(8,128)S(1)} %copy-done.5), custom_call_target="tpu_custom_call" | custom-call | flops 1509949440 | bytes 5898240 | tf_op jit(solution)/shard_map/pallas_call | solution.py:351
  65.0 39.4 %shard_map.90 = (bf16[2,4096,128]{2,1,0:T(8,128)(2,1)S(1)}, bf16[2,4096,128]{2,1,0:T(8,128)(2,1)S(1)}) custom-call(s32[1]{0:T(128)} %bitcast.me_ref, s32[4,20,128]{2,1,0:T(8,128)S(1)} %copy-done.6, s32[4,5,128]{2,1,0:T(8,128)S(1)} %copy-done.7, bf16[512,10240]{1,0:T(8,128)(2,1)} %get-tuple-element.29.x_ref, bf16[512,10240]{1,0:T(8,128)(2,1)} %collective-permute-done.y_ref, ...), custom_call_target="tpu_custom_call" | custom-call | flops 21474836480 | bytes 10485760 | tf_op jit(solution)/shard_map/pallas_call | solution.py:566
  104.5 4.0 %collective-permute-done.9 = bf16[2,4096,128]{2,1,0:T(8,128)(2,1)S(1)} collective-permute-done((bf16[2,4096,128]{2,1,0:T(8,128)(2,1)S(1)}, bf16[2,4096,128]{2,1,0:T(8,128)(2,1)S(1)}, u32[]{:S(2)}, u32[]{:S(2)}) %collective-permute-start.9) | collective-permute-done | bytes 2097184 | tf_op jit(solution)/shard_map/ppermute | solution.py:607
  108.7 1.5 collective-permute-start.10
  110.4 1.6 %collective-permute-start.12 = (bf16[2,1,1024,128]{3,2,1,0:T(8,128)(2,1)S(1)}, bf16[2,1,1024,128]{3,2,1,0:T(8,128)(2,1)S(1)}, u32[]{:S(2)}, u32[]{:S(2)}) collective-permute-start(bf16[2,1,1024,128]{3,2,1,0:T(8,128)(2,1)S(1)} %add_convert_fusion), channel_id=1, source_target_pairs={{0,16},{4,20},{8,24},{12,28},{16,0},{20,4},{24,8},{28,12},{1,17},{... | collective-permute-start | bytes 1572872 | tf_op jit(solution)/shard_map/ppermute | solution.py:607
  112.1 10.6 %collective-permute-done.10 = bf16[1,2,1024,128]{3,2,1,0:T(8,128)(2,1)S(1)} collective-permute-done((bf16[1,2,1024,128]{3,2,1,0:T(8,128)(2,1)S(1)}, bf16[1,2,1024,128]{3,2,1,0:T(8,128)(2,1)S(1)}, u32[]{:S(2)}, u32[]{:S(2)}) %collective-permute-start.10) | collective-permute-done | bytes 524320 | tf_op jit(solution)/shard_map/ppermute | solution.py:607
  122.8 1.6 collective-permute-start.11
  124.5 1.6 collective-permute-start.13
  126.1 4.3 %collective-permute-done.11 = bf16[1,1,1024,128]{3,2,1,0:T(8,128)(2,1)S(1)} collective-permute-done((bf16[1,1,1024,128]{3,2,1,0:T(8,128)(2,1)S(1)}, bf16[1,1,1024,128]{3,2,1,0:T(8,128)(2,1)S(1)}, u32[]{:S(2)}, u32[]{:S(2)}) %collective-permute-start.11) | collective-permute-done | bytes 262176 | tf_op jit(solution)/shard_map/ppermute | solution.py:607
  130.4 1.4 collective-permute-done.13
  133.3 5.1 %collective-permute-done.14 = bf16[2,512,128]{2,1,0:T(8,128)(2,1)S(1)} collective-permute-done((bf16[2,512,128]{2,1,0:T(8,128)(2,1)S(1)}, bf16[2,512,128]{2,1,0:T(8,128)(2,1)S(1)}, u32[]{:S(2)}, u32[]{:S(2)}) %collective-permute-start.14) | collective-permute-done | bytes 262176 | tf_op jit(solution)/shard_map/ppermute | solution.py:607
  138.5 2.2 %collective-permute-start.15 = (bf16[2,256,128]{2,1,0:T(8,128)(2,1)S(1)}, bf16[2,256,128]{2,1,0:T(8,128)(2,1)S(1)}, u32[]{:S(2)}, u32[]{:S(2)}) collective-permute-start(bf16[2,256,128]{2,1,0:T(8,128)(2,1)S(1)} %add_convert_fusion.5), channel_id=1, source_target_pairs={{0,2},{1,3},{2,0},{3,1},{4,6},{5,7},{6,4},{7,5},{8,10},{9,11},{10,... | collective-permute-start | bytes 393224 | tf_op jit(solution)/shard_map/ppermute | solution.py:607
  140.7 5.1 %collective-permute-done.15 = bf16[2,256,128]{2,1,0:T(8,128)(2,1)S(1)} collective-permute-done((bf16[2,256,128]{2,1,0:T(8,128)(2,1)S(1)}, bf16[2,256,128]{2,1,0:T(8,128)(2,1)S(1)}, u32[]{:S(2)}, u32[]{:S(2)}) %collective-permute-start.15) | collective-permute-done | bytes 131104 | tf_op jit(solution)/shard_map/ppermute | solution.py:607
  146.7 1.4 collective-permute-start.16
  148.1 1.5 collective-permute-start.17
  150.1 2.5 %collective-permute-done.16 = bf16[256,256]{1,0:T(8,128)(2,1)S(1)} collective-permute-done((bf16[256,256]{1,0:T(8,128)(2,1)S(1)}, bf16[256,256]{1,0:T(8,128)(2,1)S(1)}, u32[]{:S(2)}, u32[]{:S(2)}) %collective-permute-start.16) | collective-permute-done | bytes 131104 | tf_op jit(solution)/shard_map/ppermute | solution.py:607
  154.8 1.9 %collective-permute-done.19 = bf16[4,256,256]{2,1,0:T(8,128)(2,1)S(1)} collective-permute-done((bf16[4,256,256]{2,1,0:T(8,128)(2,1)S(1)}, bf16[4,256,256]{2,1,0:T(8,128)(2,1)S(1)}, u32[]{:S(2)}, u32[]{:S(2)}) %collective-permute-start.19) | collective-permute-done | bytes 524320 | tf_op jit(solution)/shard_map/ppermute | solution.py:607
  (59 shorter events, 12.6 us)
Async XLA Ops:
  32.1 32.9 %collective-permute-start = (bf16[512,10240]{1,0:T(8,128)(2,1)}, bf16[512,10240]{1,0:T(8,128)(2,1)}, u32[]{:S(2)}, u32[]{:S(2)}) collective-permute-start(bf16[512,10240]{1,0:T(8,128)(2,1)} %get-tuple-element.30), channel_id=1, source_target_pairs={{0,4},{4,0},{8,12},{12,8},{16,20},{20,16},{24,28},{28,24},{1,5},{5... | collective-permute-start | bytes 31457288 | tf_op jit(solution)/shard_map/ppermute | solution.py:607
  32.6 12.7 %collective-permute-start.1 = (f32[128,256]{1,0:T(8,128)}, f32[128,256]{1,0:T(8,128)S(1)}, u32[]{:S(2)}, u32[]{:S(2)}) collective-permute-start(f32[128,256]{1,0:T(8,128)} %get-tuple-element.32), channel_id=1, source_target_pairs={{0,1},{1,0},{2,3},{3,2},{4,5},{5,4},{6,7},{7,6},{8,9},{9,8},{10,11... | collective-permute-start | bytes 393224 | tf_op jit(solution)/shard_map/ppermute | solution.py:607
  35.2 13.1 %collective-permute-start.2 = (f32[128,256]{1,0:T(8,128)}, f32[128,256]{1,0:T(8,128)S(1)}, u32[]{:S(2)}, u32[]{:S(2)}) collective-permute-start(f32[128,256]{1,0:T(8,128)} %get-tuple-element.33), channel_id=1, source_target_pairs={{0,2},{1,3},{2,0},{3,1},{4,6},{5,7},{6,4},{7,5},{8,10},{9,11},{10,... | collective-permute-start | bytes 393224 | tf_op jit(solution)/shard_map/ppermute | solution.py:607
  37.8 10.5 %collective-permute-start.3 = (f32[128,256]{1,0:T(8,128)}, f32[128,256]{1,0:T(8,128)S(1)}, u32[]{:S(2)}, u32[]{:S(2)}) collective-permute-start(f32[128,256]{1,0:T(8,128)} %get-tuple-element.34), channel_id=1, source_target_pairs={{0,3},{1,2},{2,1},{3,0},{4,7},{5,6},{6,5},{7,4},{8,11},{9,10},{10,... | collective-permute-start | bytes 393224 | tf_op jit(solution)/shard_map/ppermute | solution.py:607
  37.8 21.0 %copy-start.3 = (s32[512,2]{0,1:T(2,128)S(1)}, s32[512,2]{0,1:T(2,128)}, u32[]{:S(2)}) copy-start(s32[512,2]{0,1:T(2,128)} %param.8) | copy-start | bytes 12292
  37.8 21.5 %copy-start.1 = (s32[320,512]{1,0:T(8,128)S(1)}, s32[320,512]{1,0:T(8,128)}, u32[]{:S(2)}) copy-start(s32[320,512]{1,0:T(8,128)} %index_ref.1) | copy-start | bytes 1966084
  37.8 21.5 %copy-start.2 = (f32[320,512]{1,0:T(8,128)S(1)}, f32[320,512]{1,0:T(8,128)}, u32[]{:S(2)}) copy-start(f32[320,512]{1,0:T(8,128)} %frac_ref.1) | copy-start | bytes 1966084
  37.8 21.5 %copy-start.4 = (s32[2]{0:T(128)S(1)}, s32[2]{0:T(128)}, u32[]{:S(2)}) copy-start(s32[2]{0:T(128)} %pad_add_fusion.here_ref) | copy-start | bytes 28
  48.5 5.1 %collective-permute-start.5 = (bf16[128,256]{1,0:T(8,128)(2,1)S(1)}, bf16[128,256]{1,0:T(8,128)(2,1)S(1)}, u32[]{:S(2)}, u32[]{:S(2)}) collective-permute-start(bf16[128,256]{1,0:T(8,128)(2,1)S(1)} %shard_map.88.rest_0_), channel_id=1, source_target_pairs={{0,1},{1,0},{2,3},{3,2},{4,5},{5,4},{6,7},{7,6},{8,9},{9,8},{10,11... | collective-permute-start | bytes 196616 | tf_op jit(solution)/shard_map/ppermute | solution.py:607
  51.2 7.5 %collective-permute-start.6 = (bf16[128,256]{1,0:T(8,128)(2,1)S(1)}, bf16[128,256]{1,0:T(8,128)(2,1)S(1)}, u32[]{:S(2)}, u32[]{:S(2)}) collective-permute-start(bf16[128,256]{1,0:T(8,128)(2,1)S(1)} %shard_map.88.rest_0_), channel_id=1, source_target_pairs={{0,2},{1,3},{2,0},{3,1},{4,6},{5,7},{6,4},{7,5},{8,10},{9,11},{10,... | collective-permute-start | bytes 196616 | tf_op jit(solution)/shard_map/ppermute | solution.py:607
  52.3 6.4 %collective-permute-start.7 = (bf16[128,256]{1,0:T(8,128)(2,1)S(1)}, bf16[128,256]{1,0:T(8,128)(2,1)S(1)}, u32[]{:S(2)}, u32[]{:S(2)}) collective-permute-start(bf16[128,256]{1,0:T(8,128)(2,1)S(1)} %shard_map.88.rest_0_), channel_id=1, source_target_pairs={{0,3},{1,2},{2,1},{3,0},{4,7},{5,6},{6,5},{7,4},{8,11},{9,10},{10,... | collective-permute-start | bytes 196616 | tf_op jit(solution)/shard_map/ppermute | solution.py:607
  58.7 6.2 %collective-permute-start.8 = (bf16[4,128,256]{2,1,0:T(8,128)(2,1)S(1)}, bf16[4,128,256]{2,1,0:T(8,128)(2,1)S(1)}, u32[]{:S(2)}, u32[]{:S(2)}) collective-permute-start(bf16[4,128,256]{2,1,0:T(8,128)(2,1)S(1)} %pad_maximum_fusion.1), channel_id=1, source_target_pairs={{0,4},{4,0},{8,12},{12,8},{16,20},{20,16},{24,28},{28,24},{1,5},{5... | collective-permute-start | bytes 786440 | tf_op jit(solution)/shard_map/ppermute | solution.py:607
  58.8 6.1 %collective-permute-start.4 = (s32[2,512]{1,0:T(2,128)S(1)}, s32[2,512]{1,0:T(2,128)S(1)}, u32[]{:S(2)}, u32[]{:S(2)}) collective-permute-start(s32[2,512]{1,0:T(2,128)S(1)} %bitcast.47), channel_id=1, source_target_pairs={{0,4},{4,0},{8,12},{12,8},{16,20},{20,16},{24,28},{28,24},{1,5},{5... | collective-permute-start | bytes 12296 | tf_op jit(solution)/shard_map/ppermute | solution.py:607
  104.3 4.2 %collective-permute-start.9 = (bf16[2,4096,128]{2,1,0:T(8,128)(2,1)S(1)}, bf16[2,4096,128]{2,1,0:T(8,128)(2,1)S(1)}, u32[]{:S(2)}, u32[]{:S(2)}) collective-permute-start(bf16[2,4096,128]{2,1,0:T(8,128)(2,1)S(1)} %get-tuple-element.39), channel_id=1, source_target_pairs={{0,4},{4,0},{8,12},{12,8},{16,20},{20,16},{24,28},{28,24},{1,5},{5... | collective-permute-start | bytes 6291464 | tf_op jit(solution)/shard_map/ppermute | solution.py:607
  108.7 14.0 %collective-permute-start.10 = (bf16[1,2,1024,128]{3,2,1,0:T(8,128)(2,1)S(1)}, bf16[1,2,1024,128]{3,2,1,0:T(8,128)(2,1)S(1)}, u32[]{:S(2)}, u32[]{:S(2)}) collective-permute-start(bf16[1,2,1024,128]{3,2,1,0:T(8,128)(2,1)S(1)} %bitcast.66), channel_id=1, source_target_pairs={{0,8},{4,12},{8,0},{12,4},{16,24},{20,28},{24,16},{28,20},{1,9},{5... | collective-permute-start | bytes 1572872 | tf_op jit(solution)/shard_map/ppermute | solution.py:607
  110.4 14.0 %collective-permute-start.12 = (bf16[2,1,1024,128]{3,2,1,0:T(8,128)(2,1)S(1)}, bf16[2,1,1024,128]{3,2,1,0:T(8,128)(2,1)S(1)}, u32[]{:S(2)}, u32[]{:S(2)}) collective-permute-start(bf16[2,1,1024,128]{3,2,1,0:T(8,128)(2,1)S(1)} %add_convert_fusion), channel_id=1, source_target_pairs={{0,16},{4,20},{8,24},{12,28},{16,0},{20,4},{24,8},{28,12},{1,17},{... | collective-permute-start | bytes 1572872 | tf_op jit(solution)/shard_map/ppermute | solution.py:607
  122.8 7.6 %collective-permute-start.11 = (bf16[1,1,1024,128]{3,2,1,0:T(8,128)(2,1)S(1)}, bf16[1,1,1024,128]{3,2,1,0:T(8,128)(2,1)S(1)}, u32[]{:S(2)}, u32[]{:S(2)}) collective-permute-start(bf16[1,1,1024,128]{3,2,1,0:T(8,128)(2,1)S(1)} %add_convert_fusion.4), channel_id=1, source_target_pairs={{0,16},{4,20},{8,24},{12,28},{16,0},{20,4},{24,8},{28,12},{1,17},{... | collective-permute-start | bytes 786440 | tf_op jit(solution)/shard_map/ppermute | solution.py:607
  124.5 7.3 %collective-permute-start.13 = (bf16[1,1,1024,128]{3,2,1,0:T(8,128)(2,1)S(1)}, bf16[1,1,1024,128]{3,2,1,0:T(8,128)(2,1)S(1)}, u32[]{:S(2)}, u32[]{:S(2)}) collective-permute-start(bf16[1,1,1024,128]{3,2,1,0:T(8,128)(2,1)S(1)} %add_convert_fusion.3), channel_id=1, source_target_pairs={{0,8},{4,12},{8,0},{12,4},{16,24},{20,28},{24,16},{28,20},{1,9},{5... | collective-permute-start | bytes 786440 | tf_op jit(solution)/shard_map/ppermute | solution.py:607
  132.0 6.4 %collective-permute-start.14 = (bf16[2,512,128]{2,1,0:T(8,128)(2,1)S(1)}, bf16[2,512,128]{2,1,0:T(8,128)(2,1)S(1)}, u32[]{:S(2)}, u32[]{:S(2)}) collective-permute-start(bf16[2,512,128]{2,1,0:T(8,128)(2,1)S(1)} %add_convert_fusion.2), channel_id=1, source_target_pairs={{0,1},{1,0},{2,3},{3,2},{4,5},{5,4},{6,7},{7,6},{8,9},{9,8},{10,11... | collective-permute-start | bytes 786440 | tf_op jit(solution)/shard_map/ppermute | solution.py:607
  138.5 7.3 %collective-permute-start.15 = (bf16[2,256,128]{2,1,0:T(8,128)(2,1)S(1)}, bf16[2,256,128]{2,1,0:T(8,128)(2,1)S(1)}, u32[]{:S(2)}, u32[]{:S(2)}) collective-permute-start(bf16[2,256,128]{2,1,0:T(8,128)(2,1)S(1)} %add_convert_fusion.5), channel_id=1, source_target_pairs={{0,2},{1,3},{2,0},{3,1},{4,6},{5,7},{6,4},{7,5},{8,10},{9,11},{10,... | collective-permute-start | bytes 393224 | tf_op jit(solution)/shard_map/ppermute | solution.py:607
  146.7 6.0 %collective-permute-start.16 = (bf16[256,256]{1,0:T(8,128)(2,1)S(1)}, bf16[256,256]{1,0:T(8,128)(2,1)S(1)}, u32[]{:S(2)}, u32[]{:S(2)}) collective-permute-start(bf16[256,256]{1,0:T(8,128)(2,1)S(1)} %get-tuple-element.40), channel_id=1, source_target_pairs={{0,24},{4,28},{8,16},{12,20},{16,8},{20,12},{24,0},{28,4},{1,25},{... | collective-permute-start | bytes 393224 | tf_op jit(solution)/shard_map/ppermute | solution.py:607
  148.1 5.9 %collective-permute-start.17 = (bf16[256,256]{1,0:T(8,128)(2,1)S(1)}, bf16[256,256]{1,0:T(8,128)(2,1)S(1)}, u32[]{:S(2)}, u32[]{:S(2)}) collective-permute-start(bf16[256,256]{1,0:T(8,128)(2,1)S(1)} %get-tuple-element.40), channel_id=1, source_target_pairs={{0,16},{4,20},{8,24},{12,28},{16,0},{20,4},{24,8},{28,12},{1,17},{... | collective-permute-start | bytes 393224 | tf_op jit(solution)/shard_map/ppermute | solution.py:607
  149.6 5.0 %collective-permute-start.18 = (bf16[256,256]{1,0:T(8,128)(2,1)S(1)}, bf16[256,256]{1,0:T(8,128)(2,1)S(1)}, u32[]{:S(2)}, u32[]{:S(2)}) collective-permute-start(bf16[256,256]{1,0:T(8,128)(2,1)S(1)} %get-tuple-element.40), channel_id=1, source_target_pairs={{0,8},{4,12},{8,0},{12,4},{16,24},{20,28},{24,16},{28,20},{1,9},{5... | collective-permute-start | bytes 393224 | tf_op jit(solution)/shard_map/ppermute | solution.py:607
  154.7 2.0 %collective-permute-start.19 = (bf16[4,256,256]{2,1,0:T(8,128)(2,1)S(1)}, bf16[4,256,256]{2,1,0:T(8,128)(2,1)S(1)}, u32[]{:S(2)}, u32[]{:S(2)}) collective-permute-start(bf16[4,256,256]{2,1,0:T(8,128)(2,1)S(1)} %get-tuple-element.43), channel_id=1, source_target_pairs={{0,4},{4,0},{8,12},{12,8},{16,20},{20,16},{24,28},{28,24},{1,5},{5... | collective-permute-start | bytes 1572872 | tf_op jit(solution)/shard_map/ppermute | solution.py:607
  (4 other events, 29.7 us)

commit v10 on v9

--- a/solution.py
+++ b/solution.py
@@ -29,12 +29,80 @@
 
 
 def score_kernel(here_ref, noise_ref, x_ref, r_ref, blk_ref, keep_ref, send_ref, *rest):
-    *out_refs, w_ref, acc_ref, perm_ref, cols_ref = rest
+    out_refs = rest[:-8]
+    flat_a, flat_b, w_a, w_b, acc_ref, perm_ref, cols_ref, sem = rest[-8:]
     step = pl.program_id(0)
+    steps = pl.num_programs(0) - 1
     particles, gb, width = x_ref.shape
     orients = r_ref.shape[0]
     side = 16 * gb
+    per = gb // 2
     core = here_ref[0] & 1
+    rounds = 4
+
+    def copies(flat_ref, slot, at_step, swap):
+        lanes = pl.ds(pl.multiple_of(at_step * (per * width), per * width), per * width)
+        goals = (send_ref, keep_ref) if swap else (keep_ref, send_ref)
+        return [
+            pltpu.make_async_copy(flat_ref.at[h], goals[h].at[:, lanes], sem.at[slot, h])
+            for h in range(2)
+        ]
+
+    def send_out(flat_ref, slot):
+        for which in range(2):
+
+            @pl.when(core == which)
+            def _(which=which):
+                for copy in copies(flat_ref, slot, step, which == 1):
+                    copy.start()
+
+    def wait_out(flat_ref, slot):
+        for copy in copies(flat_ref, slot, 0, False):
+            copy.wait()
+
+    def regroup(jobs):
+        at = [pl.multiple_of(first * 16, 16) for _, _, _, first in jobs]
+        wide = [job[0][pl.ds(a, 16)].reshape(side, width) for job, a in zip(jobs, at)]
+        moved = jnp.dot(perm_ref[...], jnp.concatenate(wide, axis=1), preferred_element_type=F32)
+        for g in range(gb):
+            lanes = slice(g % per * width, (g % per + 1) * width)
+            for t, (_, goal_ref, scaled, _) in enumerate(jobs):
+                part = moved[g * 16 : (g + 1) * 16, t * width : (t + 1) * width]
+                if scaled:
+                    part = part * noise_ref[step * gb + g]
+                goal_ref[g // per, pl.ds(at[t], 16), lanes] = part.astype(BF16)
+
+    def turn(src_ref, goal_ref, first):
+        at = pl.ds(pl.multiple_of(first * 16, 16), 16)
+        turned = jnp.swapaxes(src_ref[at], 0, 1)
+        for g in range(gb):
+            goal_ref[g // per, at, g % per * width : (g % per + 1) * width] = turned[g]
+
+    def tiles(i, flat_ref, w_ref):
+        ours, theirs = orients // 16 // rounds, particles // 16 // rounds
+        jobs = [(r_ref, w_ref, True, i * ours + t) for t in range(ours)]
+        for t in range(0, theirs, 4):
+            jobs.append((x_ref, flat_ref, False, i * theirs + t))
+        for at in range(0, len(jobs), 5):
+            regroup(jobs[at : at + 5])
+        for t in range(theirs):
+            if t % 4:
+                turn(x_ref, flat_ref, i * theirs + t)
+
+    def product(left, right):
+        acc_ref[...] += lax.dot_general(
+            left, right, (((1,), (1,)), ((), ())), preferred_element_type=F32
+        )
+
+    def both(i, flat_ref, w_ref, last_flat, last_w):
+        span = 2 * per * width // rounds
+        at = pl.ds(pl.multiple_of(lax.rem(i, rounds // 2) * span, span), span)
+        h = lax.div(i, rounds // 2)
+        product(last_flat[h, :, at], last_w[h, :, at])
+        tiles(i, flat_ref, w_ref)
+
+    def loop(body, *refs):
+        lax.fori_loop(0, rounds, lambda i, c: (body(i, *refs), c)[1], 0)
 
     @pl.when(step == 0)
     def _():
@@ -44,66 +112,29 @@
         perm_ref[...] = jnp.where(same, 1.0, 0.0).astype(BF16)
         acc_ref[...] = jnp.zeros_like(acc_ref)
         spread_columns(blk_ref, cols_ref)
-
-    perm = perm_ref[...]
-
-    per = gb // 2
-    weighted = (w_ref.at[0], w_ref.at[1])
-
-    def regroup(jobs):
-        at = [pl.multiple_of(first * 16, 16) for _, _, _, first in jobs]
-        wide = [job[0][pl.ds(a, 16)].reshape(side, width) for job, a in zip(jobs, at)]
-        moved = jnp.dot(perm, jnp.concatenate(wide, axis=1), preferred_element_type=F32)
-        for g in range(gb):
-            lanes = slice(g % per * width, (g % per + 1) * width)
-            for t, (_, halves, scaled, _) in enumerate(jobs):
-                part = moved[g * 16 : (g + 1) * 16, t * width : (t + 1) * width]
-                if scaled:
-                    part = part * noise_ref[step * gb + g]
-                halves[g // per][pl.ds(at[t], 16), lanes] = part.astype(BF16)
-
-    def turn(src_ref, halves, first):
-        at = pl.ds(pl.multiple_of(first * 16, 16), 16)
-        turned = jnp.swapaxes(src_ref[at], 0, 1)
-        for g in range(gb):
-            halves[g // per][at, g % per * width : (g % per + 1) * width] = turned[g]
-
-    both = min(particles, orients) // 64
-
-    def all_tiles(halves):
-        def tiles(i, carry):
-            jobs = [(r_ref, weighted, True, i * 4 + t) for t in range(4)]
-            regroup(jobs + [(x_ref, halves, False, i * 4)])
-            for t in range(1, 4):
-                turn(x_ref, halves, i * 4 + t)
-            return carry
-
-        def more_tiles(src_ref, goal, scaled):
-            def body(i, carry):
-                regroup([(src_ref, goal, scaled, i)])
-                return carry
-
-            lax.fori_loop(both * 4, src_ref.shape[0] // 16, body, 0)
-
-        lax.fori_loop(0, both, tiles, 0, unroll=2)
-        more_tiles(r_ref, weighted, True)
-        more_tiles(x_ref, halves, False)
-
-    @pl.when(core == 0)
+        loop(tiles, flat_a, w_a)
+        send_out(flat_a, 0)
+
+    inner = (step > 0) & (step < steps)
+
+    @pl.when(inner & (lax.rem(step, 2) == 1))
     def _():
-        all_tiles((keep_ref, send_ref))
-
-    @pl.when(core == 1)
+        @pl.when(step > 1)
+        def _():
+            wait_out(flat_b, 1)
+
+        loop(both, flat_b, w_b, flat_a, w_a)
+        send_out(flat_b, 1)
+
+    @pl.when(inner & (lax.rem(step, 2) == 0))
     def _():
-        all_tiles((send_ref, keep_ref))
-
-    for half_ref, which in ((keep_ref, core), (send_ref, 1 - core)):
-        acc_ref[...] += lax.dot_general(
-            half_ref[...], w_ref[which], (((1,), (1,)), ((), ())), preferred_element_type=F32
-        )
-
-    @pl.when(step == pl.num_programs(0) - 1)
-    def _():
+        wait_out(flat_a, 0)
+        loop(both, flat_a, w_a, flat_b, w_b)
+        send_out(flat_a, 0)
+
+    def finish(last_flat, last_w):
+        for h in range(2):
+            product(last_flat[h], last_w[h])
         me = here_ref[1]
         share = particles // len(out_refs)
         for k, out_ref in enumerate(out_refs):
@@ -115,6 +146,19 @@
                     value = acc_ref[pl.ds(at, share), b * OB : (b + 1) * OB]
                     chosen = jnp.where(wanted == b, value, chosen)
                 out_ref[:, j * OB : (j + 1) * OB] = chosen
+        wait_out(flat_a, 0)
+
+        @pl.when(steps > 1)
+        def _():
+            wait_out(flat_b, 1)
+
+    @pl.when((step == steps) & (lax.rem(step, 2) == 1))
+    def _():
+        finish(flat_a, w_a)
+
+    @pl.when((step == steps) & (lax.rem(step, 2) == 0))
+    def _():
+        finish(flat_b, w_b)
 
 
 def score_call(here, inv_noise, particles, references, blocks, slab_size):
@@ -124,25 +168,30 @@
     side = 16 * gb
     share = count // slab_size
     smem = pl.BlockSpec(memory_space=pltpu.SMEM)
+    steps = groups // gb
     return pl.pallas_call(
         score_kernel,
-        grid=(groups // gb,),
+        grid=(steps + 1,),
         out_shape=[jax.ShapeDtypeStruct((count, groups // 2 * width), BF16)] * 2
         + [jax.ShapeDtypeStruct((share, 2 * OB), F32)] * slab_size,
         in_specs=[
             smem,
             smem,
-            pl.BlockSpec((count, gb, width), lambda i: (0, i, 0)),
-            pl.BlockSpec((orients, gb, width), lambda i: (0, i, 0)),
+            pl.BlockSpec((count, gb, width), lambda i: (0, jnp.minimum(i, steps - 1), 0)),
+            pl.BlockSpec((orients, gb, width), lambda i: (0, jnp.minimum(i, steps - 1), 0)),
             pl.BlockSpec((2, count), lambda i: (0, 0)),
         ],
-        out_specs=[pl.BlockSpec((count, gb // 2 * width), lambda i: (0, i))] * 2
+        out_specs=[pl.BlockSpec(memory_space=pl.ANY)] * 2
         + [pl.BlockSpec((share, 2 * OB), lambda i: (0, 0))] * slab_size,
         scratch_shapes=[
+            pltpu.VMEM((2, count, gb // 2 * width), BF16),
+            pltpu.VMEM((2, count, gb // 2 * width), BF16),
+            pltpu.VMEM((2, orients, gb // 2 * width), BF16),
             pltpu.VMEM((2, orients, gb // 2 * width), BF16),
             pltpu.VMEM((count, orients), F32),
             pltpu.VMEM((side, side), BF16),
             pltpu.VMEM((2, count, OB), F32),
+            pltpu.SemaphoreType.DMA((2, 2)),
         ],
         compiler_params=pltpu.CompilerParams(vmem_limit_bytes=56 * MB),
         cost_estimate=pl.CostEstimate(
@@ -332,7 +381,7 @@
             ],
         ),
         out_shape=[jax.ShapeDtypeStruct(shape, jnp.int32) for shape in shapes],
-        compiler_params=pltpu.CompilerParams(vmem_limit_bytes=60 * MB),
+        compiler_params=pltpu.CompilerParams(vmem_limit_bytes=55 * MB),
         cost_estimate=pl.CostEstimate(
             flops=8 * steps * units * owners * half * half,
             bytes_accessed=8 * groups * orients,
@@ -373,7 +422,7 @@
     post_t, spread_ref, cols_ref, slice_a, slice_b, buf_s, buf_m, volume, stage, sem = rest[-10:]
     step = pl.program_id(0)
     count = x_ref.shape[0]
-    orients = post_t.shape[1]
+    orients = post_t.shape[0]
     units, half = pos_ref.shape[1:]
     parts = orients // half
     gb = units // parts
@@ -400,7 +449,7 @@
                     spread_ref[pl.ds(at, share), b * OB : (b + 1) * OB] = spread
             for b in range(orients // OB):
                 rows = slice(b * OB, (b + 1) * OB)
-                post_t[who, rows] = spread_ref[:, rows].T.astype(BF16)
+                post_t[rows, who * count : (who + 1) * count] = spread_ref[:, rows].T.astype(BF16)
 
     tail = pl.ds(pl.multiple_of(item_ref[0, 4, 0] * 8, 8), RD)
     buf_s[tail, :] = jnp.zeros((RD, width), F32)
@@ -411,8 +460,8 @@
 
     def slices(q, dst_ref):
         at = pl.ds(pl.multiple_of(q * (per * width), per * width), per * width)
-        value = jnp.dot(post_t[0], x_ref[:, at], preferred_element_type=F32)
-        value = value + jnp.dot(post_t[1], y_ref[:, at], preferred_element_type=F32)
+        images = jnp.concatenate([x_ref[:, at], y_ref[:, at]], axis=0)
+        value = jnp.dot(post_t[...], images, preferred_element_type=F32)
         dst_ref[...] = value.astype(BF16)
 
     def emit(u, piece, base, size):
@@ -582,7 +631,7 @@
         + [pl.BlockSpec(more.shape, lambda i: (0, 0, 0))],
         out_specs=[pl.BlockSpec(memory_space=pl.ANY)] * 2,
         scratch_shapes=[
-            pltpu.VMEM((2, orients, count), BF16),
+            pltpu.VMEM((orients, 2 * count), BF16),
             pltpu.VMEM((count, orients), F32),
             pltpu.VMEM((2, count, OB), F32),
             pltpu.VMEM((orients, group_pair(gb) * width), BF16),
@@ -630,11 +679,13 @@
     parts = [own] + [flip(scores[k], "slab", k) for k in range(1, slab_size)]
     flats = [kept, flip(sent, "dom", dom_bits[0])]
     post = softmax_call(parts)
-    post, pos = lax.optimization_barrier((post, pos))
-    meta = meta_call(here, row_index, fraction, pos, devices)
+    more_blocks = flip(blocks, "dom", dom_bits[0])
+    post, more_blocks, later = lax.optimization_barrier((post, more_blocks, here))
+    meta = meta_call(later, row_index, fraction, pos, devices)
     posts = [post] + [flip(post, "slab", k) for k in range(1, slab_size)]
-    more = flip(jnp.stack(posts), "dom", dom_bits[0])
-    lists = [blocks, flip(blocks, "dom", dom_bits[0])]
+    pile, meta = lax.optimization_barrier((jnp.stack(posts), meta))
+    more = flip(pile, "dom", dom_bits[0])
+    lists = [blocks, more_blocks]
     send, keep = insert_call(
         slab_me, addr, items, flats, pos, meta, lists, posts, more, orients, devices
     )

time: 158 us -> 156 us (0.987)
  waiting for transfers between devices: 44.9 us -> 41 us
    ppermute x20, waiting for transfers between devices: 44.9 us -> 41 us  [flip(): return lax.ppermute(value, axis, [(i, i ^ bit) for i in range(size)])]
where the time goes in v10:
time: 156 us; the launch traced here: 155 us
  Pallas kernels  83 us (53%)
  waiting for transfers between devices  41 us (26%)
  starting transfers between devices  25.4 us (16%)
  other arithmetic  2.52 us (2%)
  local copies, waits for them, and re-layouts  2.28 us (1%)
    ppermute x20, waiting for transfers between devices, flip(): return lax.ppermute(value, axis, [(i, i ^ bit) for i in range(size)])  41 us
    pallas_call x1, Pallas kernels, insert_call(): pl.pallas_call(insert_kernel, grid=(steps,), out_shape=[jax.ShapeDtypeStr...  39.2 us
    pallas_call x1, Pallas kernels, score_call(): pl.pallas_call(score_kernel, grid=(steps + 1,), out_shape=[jax.ShapeDtype...  31.7 us
    ppermute x20, starting transfers between devices, flip(): return lax.ppermute(value, axis, [(i, i ^ bit) for i in range(size)])  25.4 us
    pallas_call x1, Pallas kernels, plan_call(): pl.pallas_call(functools.partial(plan_kernel, sizes=mesh_sizes, per=group...  7.28 us
    pallas_call x1, Pallas kernels, meta_call(): pl.pallas_call(functools.partial(meta_kernel, per=group_block(groups) //...  4.7 us
  transfers between devices with their start and end apart: 20, of which 12 were waited for; matrix products, arithmetic and copies ran while one was open for 0% of the time, Pallas kernels for 8%

profile of v10, /device:TPU:0, one launch (start us, length us, event | category | flops | bytes accessed | tf_op | source)
XLA Modules:
  0.0 155.1 jit_solution(12189805107396559971)
XLA Ops:
  1.2 31.7 %shard_map.86 = (bf16[512,10240]{1,0:T(8,128)(2,1)}, bf16[512,10240]{1,0:T(8,128)(2,1)}, f32[128,256]{1,0:T(8,128)}, f32[128,256]{1,0:T(8,128)}, f32[128,256]{1,0:T(8,128)}, /*index=5*/f32[128,256]{1,0:T(8,128)}) custom-call(s32[2]{0:T(128)} %pad_add_fusion.here_ref, f32[80]{0:T(128)} %noise_ref.1, bf16[512,80,256]{2,1,0:T(8,128)(2,1)} %x_ref.1, ...), custom_call_target="tpu_custom_call" | custom-call | flops 21474836480 | bytes 62914560 | tf_op jit(solution)/shard_map/pallas_call | solution.py:172
  33.5 2.6 %collective-permute-start.1 = (f32[128,256]{1,0:T(8,128)}, f32[128,256]{1,0:T(8,128)S(1)}, u32[]{:S(2)}, u32[]{:S(2)}) collective-permute-start(f32[128,256]{1,0:T(8,128)} %get-tuple-element.36), channel_id=1, source_target_pairs={{0,1},{1,0},{2,3},{3,2},{4,5},{5,4},{6,7},{7,6},{8,9},{9,8},{10,11... | collective-permute-start | bytes 393224 | tf_op jit(solution)/shard_map/ppermute | solution.py:656
  36.2 2.6 %collective-permute-start.2 = (f32[128,256]{1,0:T(8,128)}, f32[128,256]{1,0:T(8,128)S(1)}, u32[]{:S(2)}, u32[]{:S(2)}) collective-permute-start(f32[128,256]{1,0:T(8,128)} %get-tuple-element.37), channel_id=1, source_target_pairs={{0,2},{1,3},{2,0},{3,1},{4,6},{5,7},{6,4},{7,5},{8,10},{9,11},{10,... | collective-permute-start | bytes 393224 | tf_op jit(solution)/shard_map/ppermute | solution.py:656
  38.8 7.3 %shard_map.87 = (s32[4,20,256]{2,1,0:T(8,128)}, s32[4,20,128]{2,1,0:T(8,128)}, s32[4,5,128]{2,1,0:T(8,128)}) custom-call(s32[2]{0:T(128)} %pad_add_fusion.here_ref, s32[320,512]{1,0:T(8,128)} %dest_ref.1), custom_call_target="tpu_custom_call" | custom-call | flops 1342177280 | bytes 327680 | tf_op jit(solution)/shard_map/pallas_call | solution.py:370
  46.0 3.2 %collective-permute-done.2.refs_2_ = f32[128,256]{1,0:T(8,128)S(1)} collective-permute-done((f32[128,256]{1,0:T(8,128)}, f32[128,256]{1,0:T(8,128)S(1)}, u32[]{:S(2)}, u32[]{:S(2)}) %collective-permute-start.2) | collective-permute-done | bytes 131104 | tf_op jit(solution)/shard_map/ppermute | solution.py:656
  49.5 4.8 %collective-permute-start.7 = (bf16[128,256]{1,0:T(8,128)(2,1)S(1)}, bf16[128,256]{1,0:T(8,128)(2,1)S(1)}, u32[]{:S(2)}, u32[]{:S(2)}) collective-permute-start(bf16[128,256]{1,0:T(8,128)(2,1)S(1)} %shard_map.88.rest_0_), channel_id=1, source_target_pairs={{0,3},{1,2},{2,1},{3,0},{4,7},{5,6},{6,5},{7,4},{8,11},{9,10},{10,... | collective-permute-start | bytes 196616 | tf_op jit(solution)/shard_map/ppermute | solution.py:656
  55.7 4.7 %shard_map.89.meta_ref = f32[4,20,72,128]{3,2,1,0:T(8,128)S(1)} custom-call(s32[2]{0:T(128)S(1)} %copy-done.4, s32[320,512]{1,0:T(8,128)S(1)} %copy-done.1, f32[320,512]{1,0:T(8,128)S(1)} %copy-done.2, s32[4,20,256]{2,1,0:T(8,128)S(1)} %copy-done.5), custom_call_target="tpu_custom_call" | custom-call | flops 1509949440 | bytes 5898240 | tf_op jit(solution)/shard_map/pallas_call | solution.py:400
  60.6 1.5 collective-permute-done.8.rest_4_
  62.1 39.2 %shard_map.90 = (bf16[2,4096,128]{2,1,0:T(8,128)(2,1)S(1)}, bf16[2,4096,128]{2,1,0:T(8,128)(2,1)S(1)}) custom-call(s32[1]{0:T(128)} %bitcast.me_ref, s32[4,20,128]{2,1,0:T(8,128)S(1)} %copy-done.6, s32[4,5,128]{2,1,0:T(8,128)S(1)} %copy-done.7, bf16[512,10240]{1,0:T(8,128)(2,1)} %get-tuple-element.32.x_ref, bf16[512,10240]{1,0:T(8,128)(2,1)} %collective-permute-done.y_ref, ...), custom_call_target="tpu_custom_call" | custom-call | flops 21474836480 | bytes 10485760 | tf_op jit(solution)/shard_map/pallas_call | solution.py:615
  101.6 3.9 %collective-permute-done.9 = bf16[2,4096,128]{2,1,0:T(8,128)(2,1)S(1)} collective-permute-done((bf16[2,4096,128]{2,1,0:T(8,128)(2,1)S(1)}, bf16[2,4096,128]{2,1,0:T(8,128)(2,1)S(1)}, u32[]{:S(2)}, u32[]{:S(2)}) %collective-permute-start.9) | collective-permute-done | bytes 2097184 | tf_op jit(solution)/shard_map/ppermute | solution.py:656
  105.7 1.8 %collective-permute-start.10 = (bf16[1,2,1024,128]{3,2,1,0:T(8,128)(2,1)S(1)}, bf16[1,2,1024,128]{3,2,1,0:T(8,128)(2,1)S(1)}, u32[]{:S(2)}, u32[]{:S(2)}) collective-permute-start(bf16[1,2,1024,128]{3,2,1,0:T(8,128)(2,1)S(1)} %bitcast.66), channel_id=1, source_target_pairs={{0,8},{4,12},{8,0},{12,4},{16,24},{20,28},{24,16},{28,20},{1,9},{5... | collective-permute-start | bytes 1572872 | tf_op jit(solution)/shard_map/ppermute | solution.py:656
  107.7 1.6 %collective-permute-start.12 = (bf16[2,1,1024,128]{3,2,1,0:T(8,128)(2,1)S(1)}, bf16[2,1,1024,128]{3,2,1,0:T(8,128)(2,1)S(1)}, u32[]{:S(2)}, u32[]{:S(2)}) collective-permute-start(bf16[2,1,1024,128]{3,2,1,0:T(8,128)(2,1)S(1)} %add_convert_fusion), channel_id=1, source_target_pairs={{0,16},{4,20},{8,24},{12,28},{16,0},{20,4},{24,8},{28,12},{1,17},{... | collective-permute-start | bytes 1572872 | tf_op jit(solution)/shard_map/ppermute | solution.py:656
  109.4 10.3 %collective-permute-done.10 = bf16[1,2,1024,128]{3,2,1,0:T(8,128)(2,1)S(1)} collective-permute-done((bf16[1,2,1024,128]{3,2,1,0:T(8,128)(2,1)S(1)}, bf16[1,2,1024,128]{3,2,1,0:T(8,128)(2,1)S(1)}, u32[]{:S(2)}, u32[]{:S(2)}) %collective-permute-start.10) | collective-permute-done | bytes 524320 | tf_op jit(solution)/shard_map/ppermute | solution.py:656
  119.8 1.8 %collective-permute-start.11 = (bf16[1,1,1024,128]{3,2,1,0:T(8,128)(2,1)S(1)}, bf16[1,1,1024,128]{3,2,1,0:T(8,128)(2,1)S(1)}, u32[]{:S(2)}, u32[]{:S(2)}) collective-permute-start(bf16[1,1,1024,128]{3,2,1,0:T(8,128)(2,1)S(1)} %add_convert_fusion.4), channel_id=1, source_target_pairs={{0,16},{4,20},{8,24},{12,28},{16,0},{20,4},{24,8},{28,12},{1,17},{... | collective-permute-start | bytes 786440 | tf_op jit(solution)/shard_map/ppermute | solution.py:656
  121.7 1.5 collective-permute-start.13
  123.3 4.1 %collective-permute-done.11 = bf16[1,1,1024,128]{3,2,1,0:T(8,128)(2,1)S(1)} collective-permute-done((bf16[1,1,1024,128]{3,2,1,0:T(8,128)(2,1)S(1)}, bf16[1,1,1024,128]{3,2,1,0:T(8,128)(2,1)S(1)}, u32[]{:S(2)}, u32[]{:S(2)}) %collective-permute-start.11) | collective-permute-done | bytes 262176 | tf_op jit(solution)/shard_map/ppermute | solution.py:656
  127.5 1.6 %collective-permute-done.13 = bf16[1,1,1024,128]{3,2,1,0:T(8,128)(2,1)S(1)} collective-permute-done((bf16[1,1,1024,128]{3,2,1,0:T(8,128)(2,1)S(1)}, bf16[1,1,1024,128]{3,2,1,0:T(8,128)(2,1)S(1)}, u32[]{:S(2)}, u32[]{:S(2)}) %collective-permute-start.13) | collective-permute-done | bytes 262176 | tf_op jit(solution)/shard_map/ppermute | solution.py:656
  130.5 5.2 %collective-permute-done.14 = bf16[2,512,128]{2,1,0:T(8,128)(2,1)S(1)} collective-permute-done((bf16[2,512,128]{2,1,0:T(8,128)(2,1)S(1)}, bf16[2,512,128]{2,1,0:T(8,128)(2,1)S(1)}, u32[]{:S(2)}, u32[]{:S(2)}) %collective-permute-start.14) | collective-permute-done | bytes 262176 | tf_op jit(solution)/shard_map/ppermute | solution.py:656
  135.8 2.6 %collective-permute-start.15 = (bf16[2,256,128]{2,1,0:T(8,128)(2,1)S(1)}, bf16[2,256,128]{2,1,0:T(8,128)(2,1)S(1)}, u32[]{:S(2)}, u32[]{:S(2)}) collective-permute-start(bf16[2,256,128]{2,1,0:T(8,128)(2,1)S(1)} %add_convert_fusion.5), channel_id=1, source_target_pairs={{0,2},{1,3},{2,0},{3,1},{4,6},{5,7},{6,4},{7,5},{8,10},{9,11},{10,... | collective-permute-start | bytes 393224 | tf_op jit(solution)/shard_map/ppermute | solution.py:656
  138.3 4.8 %collective-permute-done.15 = bf16[2,256,128]{2,1,0:T(8,128)(2,1)S(1)} collective-permute-done((bf16[2,256,128]{2,1,0:T(8,128)(2,1)S(1)}, bf16[2,256,128]{2,1,0:T(8,128)(2,1)S(1)}, u32[]{:S(2)}, u32[]{:S(2)}) %collective-permute-start.15) | collective-permute-done | bytes 131104 | tf_op jit(solution)/shard_map/ppermute | solution.py:656
  143.9 1.4 collective-permute-start.16
  145.3 1.5 collective-permute-start.17
  147.4 2.5 %collective-permute-done.16 = bf16[256,256]{1,0:T(8,128)(2,1)S(1)} collective-permute-done((bf16[256,256]{1,0:T(8,128)(2,1)S(1)}, bf16[256,256]{1,0:T(8,128)(2,1)S(1)}, u32[]{:S(2)}, u32[]{:S(2)}) %collective-permute-start.16) | collective-permute-done | bytes 131104 | tf_op jit(solution)/shard_map/ppermute | solution.py:656
  152.0 1.9 %collective-permute-done.19 = bf16[4,256,256]{2,1,0:T(8,128)(2,1)S(1)} collective-permute-done((bf16[4,256,256]{2,1,0:T(8,128)(2,1)S(1)}, bf16[4,256,256]{2,1,0:T(8,128)(2,1)S(1)}, u32[]{:S(2)}, u32[]{:S(2)}) %collective-permute-start.19) | collective-permute-done | bytes 524320 | tf_op jit(solution)/shard_map/ppermute | solution.py:656
  (59 shorter events, 10.2 us)
Async XLA Ops:
  1.2 37.5 %copy-start.3 = (s32[512,2]{0,1:T(2,128)S(1)}, s32[512,2]{0,1:T(2,128)}, u32[]{:S(2)}) copy-start(s32[512,2]{0,1:T(2,128)} %param.8) | copy-start | bytes 12292
  33.0 21.9 %copy-start.1 = (s32[320,512]{1,0:T(8,128)S(1)}, s32[320,512]{1,0:T(8,128)}, u32[]{:S(2)}) copy-start(s32[320,512]{1,0:T(8,128)} %index_ref.1) | copy-start | bytes 1966084
  33.0 21.9 %copy-start.2 = (f32[320,512]{1,0:T(8,128)S(1)}, f32[320,512]{1,0:T(8,128)}, u32[]{:S(2)}) copy-start(f32[320,512]{1,0:T(8,128)} %frac_ref.1) | copy-start | bytes 1966084
  33.0 21.9 %copy-start.4 = (s32[2]{0:T(128)S(1)}, s32[2]{0:T(128)}, u32[]{:S(2)}) copy-start(s32[2]{0:T(128)} %pad_add_fusion.here_ref) | copy-start | bytes 28
  33.0 29.1 %collective-permute-start = (bf16[512,10240]{1,0:T(8,128)(2,1)}, bf16[512,10240]{1,0:T(8,128)(2,1)}, u32[]{:S(2)}, u32[]{:S(2)}) collective-permute-start(bf16[512,10240]{1,0:T(8,128)(2,1)} %get-tuple-element.33), channel_id=1, source_target_pairs={{0,4},{4,0},{8,12},{12,8},{16,20},{20,16},{24,28},{28,24},{1,5},{5... | collective-permute-start | bytes 31457288 | tf_op jit(solution)/shard_map/ppermute | solution.py:656
  33.5 12.5 %collective-permute-start.1 = (f32[128,256]{1,0:T(8,128)}, f32[128,256]{1,0:T(8,128)S(1)}, u32[]{:S(2)}, u32[]{:S(2)}) collective-permute-start(f32[128,256]{1,0:T(8,128)} %get-tuple-element.36), channel_id=1, source_target_pairs={{0,1},{1,0},{2,3},{3,2},{4,5},{5,4},{6,7},{7,6},{8,9},{9,8},{10,11... | collective-permute-start | bytes 393224 | tf_op jit(solution)/shard_map/ppermute | solution.py:656
  36.2 13.1 %collective-permute-start.2 = (f32[128,256]{1,0:T(8,128)}, f32[128,256]{1,0:T(8,128)S(1)}, u32[]{:S(2)}, u32[]{:S(2)}) collective-permute-start(f32[128,256]{1,0:T(8,128)} %get-tuple-element.37), channel_id=1, source_target_pairs={{0,2},{1,3},{2,0},{3,1},{4,6},{5,7},{6,4},{7,5},{8,10},{9,11},{10,... | collective-permute-start | bytes 393224 | tf_op jit(solution)/shard_map/ppermute | solution.py:656
  38.8 10.5 %collective-permute-start.3 = (f32[128,256]{1,0:T(8,128)}, f32[128,256]{1,0:T(8,128)S(1)}, u32[]{:S(2)}, u32[]{:S(2)}) collective-permute-start(f32[128,256]{1,0:T(8,128)} %get-tuple-element.38), channel_id=1, source_target_pairs={{0,3},{1,2},{2,1},{3,0},{4,7},{5,6},{6,5},{7,4},{8,11},{9,10},{10,... | collective-permute-start | bytes 393224 | tf_op jit(solution)/shard_map/ppermute | solution.py:656
  38.8 10.7 %collective-permute-start.4 = (s32[2,512]{1,0:T(2,128)S(1)}, s32[2,512]{1,0:T(2,128)S(1)}, u32[]{:S(2)}, u32[]{:S(2)}) collective-permute-start(s32[2,512]{1,0:T(2,128)S(1)} %bitcast.47), channel_id=1, source_target_pairs={{0,4},{4,0},{8,12},{12,8},{16,20},{20,16},{24,28},{28,24},{1,5},{5... | collective-permute-start | bytes 12296 | tf_op jit(solution)/shard_map/ppermute | solution.py:656
  49.5 10.9 %collective-permute-start.7 = (bf16[128,256]{1,0:T(8,128)(2,1)S(1)}, bf16[128,256]{1,0:T(8,128)(2,1)S(1)}, u32[]{:S(2)}, u32[]{:S(2)}) collective-permute-start(bf16[128,256]{1,0:T(8,128)(2,1)S(1)} %shard_map.88.rest_0_), channel_id=1, source_target_pairs={{0,3},{1,2},{2,1},{3,0},{4,7},{5,6},{6,5},{7,4},{8,11},{9,10},{10,... | collective-permute-start | bytes 196616 | tf_op jit(solution)/shard_map/ppermute | solution.py:656
  54.3 6.2 %collective-permute-start.6 = (bf16[128,256]{1,0:T(8,128)(2,1)S(1)}, bf16[128,256]{1,0:T(8,128)(2,1)S(1)}, u32[]{:S(2)}, u32[]{:S(2)}) collective-permute-start(bf16[128,256]{1,0:T(8,128)(2,1)S(1)} %shard_map.88.rest_0_), channel_id=1, source_target_pairs={{0,2},{1,3},{2,0},{3,1},{4,6},{5,7},{6,4},{7,5},{8,10},{9,11},{10,... | collective-permute-start | bytes 196616 | tf_op jit(solution)/shard_map/ppermute | solution.py:656
  54.3 6.2 %collective-permute-start.5 = (bf16[128,256]{1,0:T(8,128)(2,1)S(1)}, bf16[128,256]{1,0:T(8,128)(2,1)S(1)}, u32[]{:S(2)}, u32[]{:S(2)}) collective-permute-start(bf16[128,256]{1,0:T(8,128)(2,1)S(1)} %shard_map.88.rest_0_), channel_id=1, source_target_pairs={{0,1},{1,0},{2,3},{3,2},{4,5},{5,4},{6,7},{7,6},{8,9},{9,8},{10,11... | collective-permute-start | bytes 196616 | tf_op jit(solution)/shard_map/ppermute | solution.py:656
  60.5 1.6 %collective-permute-start.8 = (bf16[4,128,256]{2,1,0:T(8,128)(2,1)S(1)}, bf16[4,128,256]{2,1,0:T(8,128)(2,1)S(1)}, u32[]{:S(2)}, u32[]{:S(2)}) collective-permute-start(bf16[4,128,256]{2,1,0:T(8,128)(2,1)S(1)} %pad_maximum_fusion.1), channel_id=1, source_target_pairs={{0,4},{4,0},{8,12},{12,8},{16,20},{20,16},{24,28},{28,24},{1,5},{5... | collective-permute-start | bytes 786440 | tf_op jit(solution)/shard_map/ppermute | solution.py:656
  101.3 4.2 %collective-permute-start.9 = (bf16[2,4096,128]{2,1,0:T(8,128)(2,1)S(1)}, bf16[2,4096,128]{2,1,0:T(8,128)(2,1)S(1)}, u32[]{:S(2)}, u32[]{:S(2)}) collective-permute-start(bf16[2,4096,128]{2,1,0:T(8,128)(2,1)S(1)} %get-tuple-element.45), channel_id=1, source_target_pairs={{0,4},{4,0},{8,12},{12,8},{16,20},{20,16},{24,28},{28,24},{1,5},{5... | collective-permute-start | bytes 6291464 | tf_op jit(solution)/shard_map/ppermute | solution.py:656
  105.7 14.0 %collective-permute-start.10 = (bf16[1,2,1024,128]{3,2,1,0:T(8,128)(2,1)S(1)}, bf16[1,2,1024,128]{3,2,1,0:T(8,128)(2,1)S(1)}, u32[]{:S(2)}, u32[]{:S(2)}) collective-permute-start(bf16[1,2,1024,128]{3,2,1,0:T(8,128)(2,1)S(1)} %bitcast.66), channel_id=1, source_target_pairs={{0,8},{4,12},{8,0},{12,4},{16,24},{20,28},{24,16},{28,20},{1,9},{5... | collective-permute-start | bytes 1572872 | tf_op jit(solution)/shard_map/ppermute | solution.py:656
  107.7 14.0 %collective-permute-start.12 = (bf16[2,1,1024,128]{3,2,1,0:T(8,128)(2,1)S(1)}, bf16[2,1,1024,128]{3,2,1,0:T(8,128)(2,1)S(1)}, u32[]{:S(2)}, u32[]{:S(2)}) collective-permute-start(bf16[2,1,1024,128]{3,2,1,0:T(8,128)(2,1)S(1)} %add_convert_fusion), channel_id=1, source_target_pairs={{0,16},{4,20},{8,24},{12,28},{16,0},{20,4},{24,8},{28,12},{1,17},{... | collective-permute-start | bytes 1572872 | tf_op jit(solution)/shard_map/ppermute | solution.py:656
  119.8 7.6 %collective-permute-start.11 = (bf16[1,1,1024,128]{3,2,1,0:T(8,128)(2,1)S(1)}, bf16[1,1,1024,128]{3,2,1,0:T(8,128)(2,1)S(1)}, u32[]{:S(2)}, u32[]{:S(2)}) collective-permute-start(bf16[1,1,1024,128]{3,2,1,0:T(8,128)(2,1)S(1)} %add_convert_fusion.4), channel_id=1, source_target_pairs={{0,16},{4,20},{8,24},{12,28},{16,0},{20,4},{24,8},{28,12},{1,17},{... | collective-permute-start | bytes 786440 | tf_op jit(solution)/shard_map/ppermute | solution.py:656
  121.7 7.4 %collective-permute-start.13 = (bf16[1,1,1024,128]{3,2,1,0:T(8,128)(2,1)S(1)}, bf16[1,1,1024,128]{3,2,1,0:T(8,128)(2,1)S(1)}, u32[]{:S(2)}, u32[]{:S(2)}) collective-permute-start(bf16[1,1,1024,128]{3,2,1,0:T(8,128)(2,1)S(1)} %add_convert_fusion.3), channel_id=1, source_target_pairs={{0,8},{4,12},{8,0},{12,4},{16,24},{20,28},{24,16},{28,20},{1,9},{5... | collective-permute-start | bytes 786440 | tf_op jit(solution)/shard_map/ppermute | solution.py:656
  129.2 6.4 %collective-permute-start.14 = (bf16[2,512,128]{2,1,0:T(8,128)(2,1)S(1)}, bf16[2,512,128]{2,1,0:T(8,128)(2,1)S(1)}, u32[]{:S(2)}, u32[]{:S(2)}) collective-permute-start(bf16[2,512,128]{2,1,0:T(8,128)(2,1)S(1)} %add_convert_fusion.2), channel_id=1, source_target_pairs={{0,1},{1,0},{2,3},{3,2},{4,5},{5,4},{6,7},{7,6},{8,9},{9,8},{10,11... | collective-permute-start | bytes 786440 | tf_op jit(solution)/shard_map/ppermute | solution.py:656
  135.8 7.3 %collective-permute-start.15 = (bf16[2,256,128]{2,1,0:T(8,128)(2,1)S(1)}, bf16[2,256,128]{2,1,0:T(8,128)(2,1)S(1)}, u32[]{:S(2)}, u32[]{:S(2)}) collective-permute-start(bf16[2,256,128]{2,1,0:T(8,128)(2,1)S(1)} %add_convert_fusion.5), channel_id=1, source_target_pairs={{0,2},{1,3},{2,0},{3,1},{4,6},{5,7},{6,4},{7,5},{8,10},{9,11},{10,... | collective-permute-start | bytes 393224 | tf_op jit(solution)/shard_map/ppermute | solution.py:656
  143.9 6.0 %collective-permute-start.16 = (bf16[256,256]{1,0:T(8,128)(2,1)S(1)}, bf16[256,256]{1,0:T(8,128)(2,1)S(1)}, u32[]{:S(2)}, u32[]{:S(2)}) collective-permute-start(bf16[256,256]{1,0:T(8,128)(2,1)S(1)} %get-tuple-element.46), channel_id=1, source_target_pairs={{0,24},{4,28},{8,16},{12,20},{16,8},{20,12},{24,0},{28,4},{1,25},{... | collective-permute-start | bytes 393224 | tf_op jit(solution)/shard_map/ppermute | solution.py:656
  145.3 5.9 %collective-permute-start.17 = (bf16[256,256]{1,0:T(8,128)(2,1)S(1)}, bf16[256,256]{1,0:T(8,128)(2,1)S(1)}, u32[]{:S(2)}, u32[]{:S(2)}) collective-permute-start(bf16[256,256]{1,0:T(8,128)(2,1)S(1)} %get-tuple-element.46), channel_id=1, source_target_pairs={{0,16},{4,20},{8,24},{12,28},{16,0},{20,4},{24,8},{28,12},{1,17},{... | collective-permute-start | bytes 393224 | tf_op jit(solution)/shard_map/ppermute | solution.py:656
  146.8 5.0 %collective-permute-start.18 = (bf16[256,256]{1,0:T(8,128)(2,1)S(1)}, bf16[256,256]{1,0:T(8,128)(2,1)S(1)}, u32[]{:S(2)}, u32[]{:S(2)}) collective-permute-start(bf16[256,256]{1,0:T(8,128)(2,1)S(1)} %get-tuple-element.46), channel_id=1, source_target_pairs={{0,8},{4,12},{8,0},{12,4},{16,24},{20,28},{24,16},{28,20},{1,9},{5... | collective-permute-start | bytes 393224 | tf_op jit(solution)/shard_map/ppermute | solution.py:656
  152.0 2.0 %collective-permute-start.19 = (bf16[4,256,256]{2,1,0:T(8,128)(2,1)S(1)}, bf16[4,256,256]{2,1,0:T(8,128)(2,1)S(1)}, u32[]{:S(2)}, u32[]{:S(2)}) collective-permute-start(bf16[4,256,256]{2,1,0:T(8,128)(2,1)S(1)} %get-tuple-element.49), channel_id=1, source_target_pairs={{0,4},{4,0},{8,12},{12,8},{16,20},{20,16},{24,28},{28,24},{1,5},{5... | collective-permute-start | bytes 1572872 | tf_op jit(solution)/shard_map/ppermute | solution.py:656
  (4 other events, 42.9 us)

commit v11 on v10

--- a/solution.py
+++ b/solution.py
@@ -11,6 +11,7 @@
 RD = 256
 MB = 2**20
 OUT_SLOTS = 4
+STREAMS = 4
 OUT_TILE = 1024
 F32 = jnp.float32
 BF16 = jnp.bfloat16
@@ -28,13 +29,15 @@
             cols_ref[j, at : at + OB, :] = jnp.broadcast_to(line, (OB, OB)).T
 
 
-def score_kernel(here_ref, noise_ref, x_ref, r_ref, blk_ref, keep_ref, send_ref, *rest):
-    out_refs = rest[:-8]
+def score_kernel(here_ref, noise_ref, blk_ref, *rest):
+    x_refs, r_refs = rest[:STREAMS], rest[STREAMS : 2 * STREAMS]
+    keep_ref, send_ref = rest[2 * STREAMS : 2 * STREAMS + 2]
+    out_refs = rest[2 * STREAMS + 2 : -8]
     flat_a, flat_b, w_a, w_b, acc_ref, perm_ref, cols_ref, sem = rest[-8:]
     step = pl.program_id(0)
     steps = pl.num_programs(0) - 1
-    particles, gb, width = x_ref.shape
-    orients = r_ref.shape[0]
+    gb, width = x_refs[0].shape[1:]
+    particles, orients = acc_ref.shape
     side = 16 * gb
     per = gb // 2
     core = here_ref[0] & 1
@@ -61,33 +64,40 @@
             copy.wait()
 
     def regroup(jobs):
-        at = [pl.multiple_of(first * 16, 16) for _, _, _, first in jobs]
-        wide = [job[0][pl.ds(a, 16)].reshape(side, width) for job, a in zip(jobs, at)]
+        wide = [ref[pl.ds(first * 16, 16)].reshape(side, width) for ref, first, *_ in jobs]
         moved = jnp.dot(perm_ref[...], jnp.concatenate(wide, axis=1), preferred_element_type=F32)
         for g in range(gb):
             lanes = slice(g % per * width, (g % per + 1) * width)
-            for t, (_, goal_ref, scaled, _) in enumerate(jobs):
+            for t, (_, first, base, goal_ref, scaled) in enumerate(jobs):
                 part = moved[g * 16 : (g + 1) * 16, t * width : (t + 1) * width]
                 if scaled:
                     part = part * noise_ref[step * gb + g]
-                goal_ref[g // per, pl.ds(at[t], 16), lanes] = part.astype(BF16)
-
-    def turn(src_ref, goal_ref, first):
-        at = pl.ds(pl.multiple_of(first * 16, 16), 16)
-        turned = jnp.swapaxes(src_ref[at], 0, 1)
+                at = pl.ds(pl.multiple_of(base + first * 16, 16), 16)
+                goal_ref[g // per, at, lanes] = part.astype(BF16)
+
+    def turn(src_ref, first, base, goal_ref):
+        turned = jnp.swapaxes(src_ref[pl.ds(first * 16, 16)], 0, 1)
+        at = pl.ds(pl.multiple_of(base + first * 16, 16), 16)
         for g in range(gb):
             goal_ref[g // per, at, g % per * width : (g % per + 1) * width] = turned[g]
 
     def tiles(i, flat_ref, w_ref):
-        ours, theirs = orients // 16 // rounds, particles // 16 // rounds
-        jobs = [(r_ref, w_ref, True, i * ours + t) for t in range(ours)]
-        for t in range(0, theirs, 4):
-            jobs.append((x_ref, flat_ref, False, i * theirs + t))
+        jobs, turns = [], []
+        for s in range(STREAMS):
+            rows = orients // STREAMS
+            for t in range(rows // 16 // rounds):
+                jobs.append((r_refs[s], i * (rows // 16 // rounds) + t, s * rows, w_ref, True))
+            rows = particles // STREAMS
+            for t in range(rows // 16 // rounds):
+                job = (x_refs[s], i * (rows // 16 // rounds) + t, s * rows, flat_ref)
+                if (s * (rows // 16 // rounds) + t) % 4:
+                    turns.append(job)
+                else:
+                    jobs.append(job + (False,))
         for at in range(0, len(jobs), 5):
             regroup(jobs[at : at + 5])
-        for t in range(theirs):
-            if t % 4:
-                turn(x_ref, flat_ref, i * theirs + t)
+        for job in turns:
+            turn(*job)
 
     def product(left, right):
         acc_ref[...] += lax.dot_general(
@@ -177,9 +187,14 @@
         in_specs=[
             smem,
             smem,
-            pl.BlockSpec((count, gb, width), lambda i: (0, jnp.minimum(i, steps - 1), 0)),
-            pl.BlockSpec((orients, gb, width), lambda i: (0, jnp.minimum(i, steps - 1), 0)),
             pl.BlockSpec((2, count), lambda i: (0, 0)),
+        ]
+        + [
+            pl.BlockSpec(
+                (rows // STREAMS, gb, width), lambda i, s=s: (s, jnp.minimum(i, steps - 1), 0)
+            )
+            for rows in (count, orients)
+            for s in range(STREAMS)
         ],
         out_specs=[pl.BlockSpec(memory_space=pl.ANY)] * 2
         + [pl.BlockSpec((share, 2 * OB), lambda i: (0, 0))] * slab_size,
@@ -199,7 +214,7 @@
             bytes_accessed=6 * count * groups * width,
             transcendentals=0,
         ),
-    )(here, inv_noise, particles, references, blocks)
+    )(here, inv_noise, blocks, *[particles] * STREAMS, *[references] * STREAMS)
 
 
 def softmax_kernel(*refs):

time: 156 us -> 156 us (level); the launches traced: 155 us -> 157 us
  Pallas kernels: 83 us -> 84.6 us
    pallas_call x1, Pallas kernels: 39.2 us -> 41.3 us  [insert_call(): pl.pallas_call(insert_kernel, grid=(steps,), out_shape=[jax.ShapeDtypeStr...]
where the time goes in v11:
time: 156 us; the launch traced here: 157 us
  Pallas kernels  84.6 us (54%)
  waiting for transfers between devices  40.2 us (26%)
  starting transfers between devices  26.2 us (17%)
  other arithmetic  2.52 us (2%)
  local copies, waits for them, and re-layouts  2.28 us (1%)
    pallas_call x1, Pallas kernels, insert_call(): pl.pallas_call(insert_kernel, grid=(steps,), out_shape=[jax.ShapeDtypeStr...  41.3 us
    ppermute x20, waiting for transfers between devices, flip(): return lax.ppermute(value, axis, [(i, i ^ bit) for i in range(size)])  40.2 us
    pallas_call x1, Pallas kernels, score_call(): pl.pallas_call(score_kernel, grid=(steps + 1,), out_shape=[jax.ShapeDtype...  31.1 us
    ppermute x20, starting transfers between devices, flip(): return lax.ppermute(value, axis, [(i, i ^ bit) for i in range(size)])  26.2 us
    pallas_call x1, Pallas kernels, plan_call(): pl.pallas_call(functools.partial(plan_kernel, sizes=mesh_sizes, per=group...  7.28 us
    pallas_call x1, Pallas kernels, meta_call(): pl.pallas_call(functools.partial(meta_kernel, per=group_block(groups) //...  4.69 us
  transfers between devices with their start and end apart: 20, of which 12 were waited for; matrix products, arithmetic and copies ran while one was open for 0% of the time, Pallas kernels for 8%

profile of v11, /device:TPU:0, one launch (start us, length us, event | category | flops | bytes accessed | tf_op | source)
XLA Modules:
  0.0 156.7 jit_solution(10860886690525081869)
XLA Ops:
  1.2 31.1 %shard_map.86 = (bf16[512,10240]{1,0:T(8,128)(2,1)}, bf16[512,10240]{1,0:T(8,128)(2,1)}, f32[128,256]{1,0:T(8,128)}, f32[128,256]{1,0:T(8,128)}, f32[128,256]{1,0:T(8,128)}, /*index=5*/f32[128,256]{1,0:T(8,128)}) custom-call(s32[2]{0:T(128)} %pad_add_fusion.here_ref, f32[80]{0:T(128)} %noise_ref.1, s32[2,512]{1,0:T(2,128)} %bitcast.46, ...), custom_call_target="tpu_custom_call" | custom-call | flops 21474836480 | bytes 62914560 | tf_op jit(solution)/shard_map/pallas_call | solution.py:182
  32.9 2.7 %collective-permute-start.1 = (f32[128,256]{1,0:T(8,128)}, f32[128,256]{1,0:T(8,128)S(1)}, u32[]{:S(2)}, u32[]{:S(2)}) collective-permute-start(f32[128,256]{1,0:T(8,128)} %get-tuple-element.36), channel_id=1, source_target_pairs={{0,1},{1,0},{2,3},{3,2},{4,5},{5,4},{6,7},{7,6},{8,9},{9,8},{10,11... | collective-permute-start | bytes 393224 | tf_op jit(solution)/shard_map/ppermute | solution.py:671
  35.6 2.6 %collective-permute-start.2 = (f32[128,256]{1,0:T(8,128)}, f32[128,256]{1,0:T(8,128)S(1)}, u32[]{:S(2)}, u32[]{:S(2)}) collective-permute-start(f32[128,256]{1,0:T(8,128)} %get-tuple-element.37), channel_id=1, source_target_pairs={{0,2},{1,3},{2,0},{3,1},{4,6},{5,7},{6,4},{7,5},{8,10},{9,11},{10,... | collective-permute-start | bytes 393224 | tf_op jit(solution)/shard_map/ppermute | solution.py:671
  38.2 7.3 %shard_map.87 = (s32[4,20,256]{2,1,0:T(8,128)}, s32[4,20,128]{2,1,0:T(8,128)}, s32[4,5,128]{2,1,0:T(8,128)}) custom-call(s32[2]{0:T(128)} %pad_add_fusion.here_ref, s32[320,512]{1,0:T(8,128)} %dest_ref.1), custom_call_target="tpu_custom_call" | custom-call | flops 1342177280 | bytes 327680 | tf_op jit(solution)/shard_map/pallas_call | solution.py:385
  45.5 3.2 %collective-permute-done.2.refs_2_ = f32[128,256]{1,0:T(8,128)S(1)} collective-permute-done((f32[128,256]{1,0:T(8,128)}, f32[128,256]{1,0:T(8,128)S(1)}, u32[]{:S(2)}, u32[]{:S(2)}) %collective-permute-start.2) | collective-permute-done | bytes 131104 | tf_op jit(solution)/shard_map/ppermute | solution.py:671
  49.0 4.8 %collective-permute-start.7 = (bf16[128,256]{1,0:T(8,128)(2,1)S(1)}, bf16[128,256]{1,0:T(8,128)(2,1)S(1)}, u32[]{:S(2)}, u32[]{:S(2)}) collective-permute-start(bf16[128,256]{1,0:T(8,128)(2,1)S(1)} %shard_map.88.rest_0_), channel_id=1, source_target_pairs={{0,3},{1,2},{2,1},{3,0},{4,7},{5,6},{6,5},{7,4},{8,11},{9,10},{10,... | collective-permute-start | bytes 196616 | tf_op jit(solution)/shard_map/ppermute | solution.py:671
  55.2 4.7 %shard_map.89.meta_ref = f32[4,20,72,128]{3,2,1,0:T(8,128)S(1)} custom-call(s32[2]{0:T(128)S(1)} %copy-done.2, s32[320,512]{1,0:T(8,128)S(1)} %copy-done.3, f32[320,512]{1,0:T(8,128)S(1)} %copy-done.4, s32[4,20,256]{2,1,0:T(8,128)S(1)} %copy-done.5), custom_call_target="tpu_custom_call" | custom-call | flops 1509949440 | bytes 5898240 | tf_op jit(solution)/shard_map/pallas_call | solution.py:415
  60.0 1.5 collective-permute-done.8.rest_4_
  61.6 41.3 %shard_map.90 = (bf16[2,4096,128]{2,1,0:T(8,128)(2,1)S(1)}, bf16[2,4096,128]{2,1,0:T(8,128)(2,1)S(1)}) custom-call(s32[1]{0:T(128)} %bitcast.me_ref, s32[4,20,128]{2,1,0:T(8,128)S(1)} %copy-done.6, s32[4,5,128]{2,1,0:T(8,128)S(1)} %copy-done.7, bf16[512,10240]{1,0:T(8,128)(2,1)} %get-tuple-element.32.x_ref, bf16[512,10240]{1,0:T(8,128)(2,1)} %collective-permute-done.y_ref, ...), custom_call_target="tpu_custom_call" | custom-call | flops 21474836480 | bytes 10485760 | tf_op jit(solution)/shard_map/pallas_call | solution.py:630
  103.2 3.9 %collective-permute-done.9 = bf16[2,4096,128]{2,1,0:T(8,128)(2,1)S(1)} collective-permute-done((bf16[2,4096,128]{2,1,0:T(8,128)(2,1)S(1)}, bf16[2,4096,128]{2,1,0:T(8,128)(2,1)S(1)}, u32[]{:S(2)}, u32[]{:S(2)}) %collective-permute-start.9) | collective-permute-done | bytes 2097184 | tf_op jit(solution)/shard_map/ppermute | solution.py:671
  107.3 1.8 %collective-permute-start.10 = (bf16[1,2,1024,128]{3,2,1,0:T(8,128)(2,1)S(1)}, bf16[1,2,1024,128]{3,2,1,0:T(8,128)(2,1)S(1)}, u32[]{:S(2)}, u32[]{:S(2)}) collective-permute-start(bf16[1,2,1024,128]{3,2,1,0:T(8,128)(2,1)S(1)} %bitcast.66), channel_id=1, source_target_pairs={{0,8},{4,12},{8,0},{12,4},{16,24},{20,28},{24,16},{28,20},{1,9},{5... | collective-permute-start | bytes 1572872 | tf_op jit(solution)/shard_map/ppermute | solution.py:671
  109.2 1.6 %collective-permute-start.12 = (bf16[2,1,1024,128]{3,2,1,0:T(8,128)(2,1)S(1)}, bf16[2,1,1024,128]{3,2,1,0:T(8,128)(2,1)S(1)}, u32[]{:S(2)}, u32[]{:S(2)}) collective-permute-start(bf16[2,1,1024,128]{3,2,1,0:T(8,128)(2,1)S(1)} %add_convert_fusion), channel_id=1, source_target_pairs={{0,16},{4,20},{8,24},{12,28},{16,0},{20,4},{24,8},{28,12},{1,17},{... | collective-permute-start | bytes 1572872 | tf_op jit(solution)/shard_map/ppermute | solution.py:671
  111.0 10.3 %collective-permute-done.10 = bf16[1,2,1024,128]{3,2,1,0:T(8,128)(2,1)S(1)} collective-permute-done((bf16[1,2,1024,128]{3,2,1,0:T(8,128)(2,1)S(1)}, bf16[1,2,1024,128]{3,2,1,0:T(8,128)(2,1)S(1)}, u32[]{:S(2)}, u32[]{:S(2)}) %collective-permute-start.10) | collective-permute-done | bytes 524320 | tf_op jit(solution)/shard_map/ppermute | solution.py:671
  121.4 1.8 %collective-permute-start.11 = (bf16[1,1,1024,128]{3,2,1,0:T(8,128)(2,1)S(1)}, bf16[1,1,1024,128]{3,2,1,0:T(8,128)(2,1)S(1)}, u32[]{:S(2)}, u32[]{:S(2)}) collective-permute-start(bf16[1,1,1024,128]{3,2,1,0:T(8,128)(2,1)S(1)} %add_convert_fusion.4), channel_id=1, source_target_pairs={{0,16},{4,20},{8,24},{12,28},{16,0},{20,4},{24,8},{28,12},{1,17},{... | collective-permute-start | bytes 786440 | tf_op jit(solution)/shard_map/ppermute | solution.py:671
  123.3 1.6 %collective-permute-start.13 = (bf16[1,1,1024,128]{3,2,1,0:T(8,128)(2,1)S(1)}, bf16[1,1,1024,128]{3,2,1,0:T(8,128)(2,1)S(1)}, u32[]{:S(2)}, u32[]{:S(2)}) collective-permute-start(bf16[1,1,1024,128]{3,2,1,0:T(8,128)(2,1)S(1)} %add_convert_fusion.3), channel_id=1, source_target_pairs={{0,8},{4,12},{8,0},{12,4},{16,24},{20,28},{24,16},{28,20},{1,9},{5... | collective-permute-start | bytes 786440 | tf_op jit(solution)/shard_map/ppermute | solution.py:671
  124.9 4.1 %collective-permute-done.11 = bf16[1,1,1024,128]{3,2,1,0:T(8,128)(2,1)S(1)} collective-permute-done((bf16[1,1,1024,128]{3,2,1,0:T(8,128)(2,1)S(1)}, bf16[1,1,1024,128]{3,2,1,0:T(8,128)(2,1)S(1)}, u32[]{:S(2)}, u32[]{:S(2)}) %collective-permute-start.11) | collective-permute-done | bytes 262176 | tf_op jit(solution)/shard_map/ppermute | solution.py:671
  129.0 1.6 %collective-permute-done.13 = bf16[1,1,1024,128]{3,2,1,0:T(8,128)(2,1)S(1)} collective-permute-done((bf16[1,1,1024,128]{3,2,1,0:T(8,128)(2,1)S(1)}, bf16[1,1,1024,128]{3,2,1,0:T(8,128)(2,1)S(1)}, u32[]{:S(2)}, u32[]{:S(2)}) %collective-permute-start.13) | collective-permute-done | bytes 262176 | tf_op jit(solution)/shard_map/ppermute | solution.py:671
  132.0 5.2 %collective-permute-done.14 = bf16[2,512,128]{2,1,0:T(8,128)(2,1)S(1)} collective-permute-done((bf16[2,512,128]{2,1,0:T(8,128)(2,1)S(1)}, bf16[2,512,128]{2,1,0:T(8,128)(2,1)S(1)}, u32[]{:S(2)}, u32[]{:S(2)}) %collective-permute-start.14) | collective-permute-done | bytes 262176 | tf_op jit(solution)/shard_map/ppermute | solution.py:671
  137.3 3.4 %collective-permute-start.15 = (bf16[2,256,128]{2,1,0:T(8,128)(2,1)S(1)}, bf16[2,256,128]{2,1,0:T(8,128)(2,1)S(1)}, u32[]{:S(2)}, u32[]{:S(2)}) collective-permute-start(bf16[2,256,128]{2,1,0:T(8,128)(2,1)S(1)} %add_convert_fusion.5), channel_id=1, source_target_pairs={{0,2},{1,3},{2,0},{3,1},{4,6},{5,7},{6,4},{7,5},{8,10},{9,11},{10,... | collective-permute-start | bytes 393224 | tf_op jit(solution)/shard_map/ppermute | solution.py:671
  140.7 4.4 %collective-permute-done.15 = bf16[2,256,128]{2,1,0:T(8,128)(2,1)S(1)} collective-permute-done((bf16[2,256,128]{2,1,0:T(8,128)(2,1)S(1)}, bf16[2,256,128]{2,1,0:T(8,128)(2,1)S(1)}, u32[]{:S(2)}, u32[]{:S(2)}) %collective-permute-start.15) | collective-permute-done | bytes 131104 | tf_op jit(solution)/shard_map/ppermute | solution.py:671
  147.1 1.3 collective-permute-start.17
  149.3 2.5 %collective-permute-done.16 = bf16[256,256]{1,0:T(8,128)(2,1)S(1)} collective-permute-done((bf16[256,256]{1,0:T(8,128)(2,1)S(1)}, bf16[256,256]{1,0:T(8,128)(2,1)S(1)}, u32[]{:S(2)}, u32[]{:S(2)}) %collective-permute-start.16) | collective-permute-done | bytes 131104 | tf_op jit(solution)/shard_map/ppermute | solution.py:671
  151.8 1.3 collective-permute-done.17
  153.6 1.9 %collective-permute-done.19 = bf16[4,256,256]{2,1,0:T(8,128)(2,1)S(1)} collective-permute-done((bf16[4,256,256]{2,1,0:T(8,128)(2,1)S(1)}, bf16[4,256,256]{2,1,0:T(8,128)(2,1)S(1)}, u32[]{:S(2)}, u32[]{:S(2)}) %collective-permute-start.19) | collective-permute-done | bytes 524320 | tf_op jit(solution)/shard_map/ppermute | solution.py:671
  (59 shorter events, 10.1 us)
Async XLA Ops:
  1.2 37.0 %copy-start.1 = (s32[512,2]{0,1:T(2,128)S(1)}, s32[512,2]{0,1:T(2,128)}, u32[]{:S(2)}) copy-start(s32[512,2]{0,1:T(2,128)} %param.8) | copy-start | bytes 12292
  32.4 21.9 %copy-start.2 = (s32[2]{0:T(128)S(1)}, s32[2]{0:T(128)}, u32[]{:S(2)}) copy-start(s32[2]{0:T(128)} %pad_add_fusion.here_ref) | copy-start | bytes 28
  32.4 21.9 %copy-start.3 = (s32[320,512]{1,0:T(8,128)S(1)}, s32[320,512]{1,0:T(8,128)}, u32[]{:S(2)}) copy-start(s32[320,512]{1,0:T(8,128)} %index_ref.1) | copy-start | bytes 1966084
  32.4 21.9 %copy-start.4 = (f32[320,512]{1,0:T(8,128)S(1)}, f32[320,512]{1,0:T(8,128)}, u32[]{:S(2)}) copy-start(f32[320,512]{1,0:T(8,128)} %frac_ref.1) | copy-start | bytes 1966084
  32.4 29.1 %collective-permute-start = (bf16[512,10240]{1,0:T(8,128)(2,1)}, bf16[512,10240]{1,0:T(8,128)(2,1)}, u32[]{:S(2)}, u32[]{:S(2)}) collective-permute-start(bf16[512,10240]{1,0:T(8,128)(2,1)} %get-tuple-element.33), channel_id=1, source_target_pairs={{0,4},{4,0},{8,12},{12,8},{16,20},{20,16},{24,28},{28,24},{1,5},{5... | collective-permute-start | bytes 31457288 | tf_op jit(solution)/shard_map/ppermute | solution.py:671
  32.9 12.5 %collective-permute-start.1 = (f32[128,256]{1,0:T(8,128)}, f32[128,256]{1,0:T(8,128)S(1)}, u32[]{:S(2)}, u32[]{:S(2)}) collective-permute-start(f32[128,256]{1,0:T(8,128)} %get-tuple-element.36), channel_id=1, source_target_pairs={{0,1},{1,0},{2,3},{3,2},{4,5},{5,4},{6,7},{7,6},{8,9},{9,8},{10,11... | collective-permute-start | bytes 393224 | tf_op jit(solution)/shard_map/ppermute | solution.py:671
  35.6 13.1 %collective-permute-start.2 = (f32[128,256]{1,0:T(8,128)}, f32[128,256]{1,0:T(8,128)S(1)}, u32[]{:S(2)}, u32[]{:S(2)}) collective-permute-start(f32[128,256]{1,0:T(8,128)} %get-tuple-element.37), channel_id=1, source_target_pairs={{0,2},{1,3},{2,0},{3,1},{4,6},{5,7},{6,4},{7,5},{8,10},{9,11},{10,... | collective-permute-start | bytes 393224 | tf_op jit(solution)/shard_map/ppermute | solution.py:671
  38.2 10.5 %collective-permute-start.3 = (f32[128,256]{1,0:T(8,128)}, f32[128,256]{1,0:T(8,128)S(1)}, u32[]{:S(2)}, u32[]{:S(2)}) collective-permute-start(f32[128,256]{1,0:T(8,128)} %get-tuple-element.38), channel_id=1, source_target_pairs={{0,3},{1,2},{2,1},{3,0},{4,7},{5,6},{6,5},{7,4},{8,11},{9,10},{10,... | collective-permute-start | bytes 393224 | tf_op jit(solution)/shard_map/ppermute | solution.py:671
  38.2 10.7 %collective-permute-start.4 = (s32[2,512]{1,0:T(2,128)S(1)}, s32[2,512]{1,0:T(2,128)S(1)}, u32[]{:S(2)}, u32[]{:S(2)}) collective-permute-start(s32[2,512]{1,0:T(2,128)S(1)} %bitcast.47), channel_id=1, source_target_pairs={{0,4},{4,0},{8,12},{12,8},{16,20},{20,16},{24,28},{28,24},{1,5},{5... | collective-permute-start | bytes 12296 | tf_op jit(solution)/shard_map/ppermute | solution.py:671
  49.0 10.9 %collective-permute-start.7 = (bf16[128,256]{1,0:T(8,128)(2,1)S(1)}, bf16[128,256]{1,0:T(8,128)(2,1)S(1)}, u32[]{:S(2)}, u32[]{:S(2)}) collective-permute-start(bf16[128,256]{1,0:T(8,128)(2,1)S(1)} %shard_map.88.rest_0_), channel_id=1, source_target_pairs={{0,3},{1,2},{2,1},{3,0},{4,7},{5,6},{6,5},{7,4},{8,11},{9,10},{10,... | collective-permute-start | bytes 196616 | tf_op jit(solution)/shard_map/ppermute | solution.py:671
  53.7 6.2 %collective-permute-start.6 = (bf16[128,256]{1,0:T(8,128)(2,1)S(1)}, bf16[128,256]{1,0:T(8,128)(2,1)S(1)}, u32[]{:S(2)}, u32[]{:S(2)}) collective-permute-start(bf16[128,256]{1,0:T(8,128)(2,1)S(1)} %shard_map.88.rest_0_), channel_id=1, source_target_pairs={{0,2},{1,3},{2,0},{3,1},{4,6},{5,7},{6,4},{7,5},{8,10},{9,11},{10,... | collective-permute-start | bytes 196616 | tf_op jit(solution)/shard_map/ppermute | solution.py:671
  53.7 6.2 %collective-permute-start.5 = (bf16[128,256]{1,0:T(8,128)(2,1)S(1)}, bf16[128,256]{1,0:T(8,128)(2,1)S(1)}, u32[]{:S(2)}, u32[]{:S(2)}) collective-permute-start(bf16[128,256]{1,0:T(8,128)(2,1)S(1)} %shard_map.88.rest_0_), channel_id=1, source_target_pairs={{0,1},{1,0},{2,3},{3,2},{4,5},{5,4},{6,7},{7,6},{8,9},{9,8},{10,11... | collective-permute-start | bytes 196616 | tf_op jit(solution)/shard_map/ppermute | solution.py:671
  60.0 1.6 %collective-permute-start.8 = (bf16[4,128,256]{2,1,0:T(8,128)(2,1)S(1)}, bf16[4,128,256]{2,1,0:T(8,128)(2,1)S(1)}, u32[]{:S(2)}, u32[]{:S(2)}) collective-permute-start(bf16[4,128,256]{2,1,0:T(8,128)(2,1)S(1)} %pad_maximum_fusion.1), channel_id=1, source_target_pairs={{0,4},{4,0},{8,12},{12,8},{16,20},{20,16},{24,28},{28,24},{1,5},{5... | collective-permute-start | bytes 786440 | tf_op jit(solution)/shard_map/ppermute | solution.py:671
  102.9 4.2 %collective-permute-start.9 = (bf16[2,4096,128]{2,1,0:T(8,128)(2,1)S(1)}, bf16[2,4096,128]{2,1,0:T(8,128)(2,1)S(1)}, u32[]{:S(2)}, u32[]{:S(2)}) collective-permute-start(bf16[2,4096,128]{2,1,0:T(8,128)(2,1)S(1)} %get-tuple-element.45), channel_id=1, source_target_pairs={{0,4},{4,0},{8,12},{12,8},{16,20},{20,16},{24,28},{28,24},{1,5},{5... | collective-permute-start | bytes 6291464 | tf_op jit(solution)/shard_map/ppermute | solution.py:671
  107.3 14.0 %collective-permute-start.10 = (bf16[1,2,1024,128]{3,2,1,0:T(8,128)(2,1)S(1)}, bf16[1,2,1024,128]{3,2,1,0:T(8,128)(2,1)S(1)}, u32[]{:S(2)}, u32[]{:S(2)}) collective-permute-start(bf16[1,2,1024,128]{3,2,1,0:T(8,128)(2,1)S(1)} %bitcast.66), channel_id=1, source_target_pairs={{0,8},{4,12},{8,0},{12,4},{16,24},{20,28},{24,16},{28,20},{1,9},{5... | collective-permute-start | bytes 1572872 | tf_op jit(solution)/shard_map/ppermute | solution.py:671
  109.2 14.0 %collective-permute-start.12 = (bf16[2,1,1024,128]{3,2,1,0:T(8,128)(2,1)S(1)}, bf16[2,1,1024,128]{3,2,1,0:T(8,128)(2,1)S(1)}, u32[]{:S(2)}, u32[]{:S(2)}) collective-permute-start(bf16[2,1,1024,128]{3,2,1,0:T(8,128)(2,1)S(1)} %add_convert_fusion), channel_id=1, source_target_pairs={{0,16},{4,20},{8,24},{12,28},{16,0},{20,4},{24,8},{28,12},{1,17},{... | collective-permute-start | bytes 1572872 | tf_op jit(solution)/shard_map/ppermute | solution.py:671
  121.4 7.6 %collective-permute-start.11 = (bf16[1,1,1024,128]{3,2,1,0:T(8,128)(2,1)S(1)}, bf16[1,1,1024,128]{3,2,1,0:T(8,128)(2,1)S(1)}, u32[]{:S(2)}, u32[]{:S(2)}) collective-permute-start(bf16[1,1,1024,128]{3,2,1,0:T(8,128)(2,1)S(1)} %add_convert_fusion.4), channel_id=1, source_target_pairs={{0,16},{4,20},{8,24},{12,28},{16,0},{20,4},{24,8},{28,12},{1,17},{... | collective-permute-start | bytes 786440 | tf_op jit(solution)/shard_map/ppermute | solution.py:671
  123.3 7.3 %collective-permute-start.13 = (bf16[1,1,1024,128]{3,2,1,0:T(8,128)(2,1)S(1)}, bf16[1,1,1024,128]{3,2,1,0:T(8,128)(2,1)S(1)}, u32[]{:S(2)}, u32[]{:S(2)}) collective-permute-start(bf16[1,1,1024,128]{3,2,1,0:T(8,128)(2,1)S(1)} %add_convert_fusion.3), channel_id=1, source_target_pairs={{0,8},{4,12},{8,0},{12,4},{16,24},{20,28},{24,16},{28,20},{1,9},{5... | collective-permute-start | bytes 786440 | tf_op jit(solution)/shard_map/ppermute | solution.py:671
  130.8 6.4 %collective-permute-start.14 = (bf16[2,512,128]{2,1,0:T(8,128)(2,1)S(1)}, bf16[2,512,128]{2,1,0:T(8,128)(2,1)S(1)}, u32[]{:S(2)}, u32[]{:S(2)}) collective-permute-start(bf16[2,512,128]{2,1,0:T(8,128)(2,1)S(1)} %add_convert_fusion.2), channel_id=1, source_target_pairs={{0,1},{1,0},{2,3},{3,2},{4,5},{5,4},{6,7},{7,6},{8,9},{9,8},{10,11... | collective-permute-start | bytes 786440 | tf_op jit(solution)/shard_map/ppermute | solution.py:671
  137.3 7.7 %collective-permute-start.15 = (bf16[2,256,128]{2,1,0:T(8,128)(2,1)S(1)}, bf16[2,256,128]{2,1,0:T(8,128)(2,1)S(1)}, u32[]{:S(2)}, u32[]{:S(2)}) collective-permute-start(bf16[2,256,128]{2,1,0:T(8,128)(2,1)S(1)} %add_convert_fusion.5), channel_id=1, source_target_pairs={{0,2},{1,3},{2,0},{3,1},{4,6},{5,7},{6,4},{7,5},{8,10},{9,11},{10,... | collective-permute-start | bytes 393224 | tf_op jit(solution)/shard_map/ppermute | solution.py:671
  145.9 6.0 %collective-permute-start.16 = (bf16[256,256]{1,0:T(8,128)(2,1)S(1)}, bf16[256,256]{1,0:T(8,128)(2,1)S(1)}, u32[]{:S(2)}, u32[]{:S(2)}) collective-permute-start(bf16[256,256]{1,0:T(8,128)(2,1)S(1)} %get-tuple-element.46), channel_id=1, source_target_pairs={{0,24},{4,28},{8,16},{12,20},{16,8},{20,12},{24,0},{28,4},{1,25},{... | collective-permute-start | bytes 393224 | tf_op jit(solution)/shard_map/ppermute | solution.py:671
  147.1 6.0 %collective-permute-start.17 = (bf16[256,256]{1,0:T(8,128)(2,1)S(1)}, bf16[256,256]{1,0:T(8,128)(2,1)S(1)}, u32[]{:S(2)}, u32[]{:S(2)}) collective-permute-start(bf16[256,256]{1,0:T(8,128)(2,1)S(1)} %get-tuple-element.46), channel_id=1, source_target_pairs={{0,16},{4,20},{8,24},{12,28},{16,0},{20,4},{24,8},{28,12},{1,17},{... | collective-permute-start | bytes 393224 | tf_op jit(solution)/shard_map/ppermute | solution.py:671
  148.4 5.0 %collective-permute-start.18 = (bf16[256,256]{1,0:T(8,128)(2,1)S(1)}, bf16[256,256]{1,0:T(8,128)(2,1)S(1)}, u32[]{:S(2)}, u32[]{:S(2)}) collective-permute-start(bf16[256,256]{1,0:T(8,128)(2,1)S(1)} %get-tuple-element.46), channel_id=1, source_target_pairs={{0,8},{4,12},{8,0},{12,4},{16,24},{20,28},{24,16},{28,20},{1,9},{5... | collective-permute-start | bytes 393224 | tf_op jit(solution)/shard_map/ppermute | solution.py:671
  153.6 2.0 %collective-permute-start.19 = (bf16[4,256,256]{2,1,0:T(8,128)(2,1)S(1)}, bf16[4,256,256]{2,1,0:T(8,128)(2,1)S(1)}, u32[]{:S(2)}, u32[]{:S(2)}) collective-permute-start(bf16[4,256,256]{2,1,0:T(8,128)(2,1)S(1)} %get-tuple-element.49), channel_id=1, source_target_pairs={{0,4},{4,0},{8,12},{12,8},{16,20},{20,16},{24,28},{28,24},{1,5},{5... | collective-permute-start | bytes 1572872 | tf_op jit(solution)/shard_map/ppermute | solution.py:671
  (4 other events, 42.9 us)

commit v12 on v11

--- a/solution.py
+++ b/solution.py
@@ -32,7 +32,7 @@
 def score_kernel(here_ref, noise_ref, blk_ref, *rest):
     x_refs, r_refs = rest[:STREAMS], rest[STREAMS : 2 * STREAMS]
     keep_ref, send_ref = rest[2 * STREAMS : 2 * STREAMS + 2]
-    out_refs = rest[2 * STREAMS + 2 : -8]
+    out_ref = rest[2 * STREAMS + 2]
     flat_a, flat_b, w_a, w_b, acc_ref, perm_ref, cols_ref, sem = rest[-8:]
     step = pl.program_id(0)
     steps = pl.num_programs(0) - 1
@@ -145,17 +145,16 @@
     def finish(last_flat, last_w):
         for h in range(2):
             product(last_flat[h], last_w[h])
-        me = here_ref[1]
-        share = particles // len(out_refs)
-        for k, out_ref in enumerate(out_refs):
-            at = pl.multiple_of((me ^ k) * share, share)
+        share = out_ref.shape[1]
+        for k in range(out_ref.shape[0]):
+            rows = slice(k * share, (k + 1) * share)
             for j in range(2):
-                wanted = cols_ref[j, pl.ds(at, share), :]
+                wanted = cols_ref[j, rows, :]
                 chosen = jnp.zeros((share, OB), F32)
                 for b in range(orients // OB):
-                    value = acc_ref[pl.ds(at, share), b * OB : (b + 1) * OB]
+                    value = acc_ref[rows, b * OB : (b + 1) * OB]
                     chosen = jnp.where(wanted == b, value, chosen)
-                out_ref[:, j * OB : (j + 1) * OB] = chosen
+                out_ref[k, :, j * OB : (j + 1) * OB] = chosen
         wait_out(flat_a, 0)
 
         @pl.when(steps > 1)
@@ -183,7 +182,7 @@
         score_kernel,
         grid=(steps + 1,),
         out_shape=[jax.ShapeDtypeStruct((count, groups // 2 * width), BF16)] * 2
-        + [jax.ShapeDtypeStruct((share, 2 * OB), F32)] * slab_size,
+        + [jax.ShapeDtypeStruct((slab_size, share, 2 * OB), F32)],
         in_specs=[
             smem,
             smem,
@@ -197,7 +196,7 @@
             for s in range(STREAMS)
         ],
         out_specs=[pl.BlockSpec(memory_space=pl.ANY)] * 2
-        + [pl.BlockSpec((share, 2 * OB), lambda i: (0, 0))] * slab_size,
+        + [pl.BlockSpec((slab_size, share, 2 * OB), lambda i: (0, 0, 0))],
         scratch_shapes=[
             pltpu.VMEM((2, count, gb // 2 * width), BF16),
             pltpu.VMEM((2, count, gb // 2 * width), BF16),
@@ -217,22 +216,23 @@
     )(here, inv_noise, blocks, *[particles] * STREAMS, *[references] * STREAMS)
 
 
-def softmax_kernel(*refs):
-    *parts, out_ref = refs
-    total = parts[0][...]
-    for part in parts[1:]:
-        total = total + part[...]
+def softmax_kernel(parts_ref, out_ref):
+    total = parts_ref[0]
+    for k in range(1, parts_ref.shape[0]):
+        total = total + parts_ref[k]
     highest = jnp.max(total, axis=1, keepdims=True)
     weights = jnp.exp(total - highest)
-    out_ref[...] = (weights / jnp.sum(weights, axis=1, keepdims=True)).astype(BF16)
+    post = (weights / jnp.sum(weights, axis=1, keepdims=True)).astype(BF16)
+    for k in range(out_ref.shape[0]):
+        out_ref[k] = post
 
 
 def softmax_call(parts):
     return pl.pallas_call(
         softmax_kernel,
-        out_shape=jax.ShapeDtypeStruct(parts[0].shape, BF16),
+        out_shape=jax.ShapeDtypeStruct(parts.shape, BF16),
         compiler_params=pltpu.CompilerParams(vmem_limit_bytes=8 * MB),
-    )(*parts)
+    )(parts)
 
 
 def own_row(here_ref, local, per):
@@ -253,9 +253,9 @@
 
     @pl.when(step == 0)
     def _():
-        off = dest_ref[...] ^ (here_ref[0] * slab_size + here_ref[1])
+        off = dest_ref[...] ^ (here_ref[0] * slab_size)
         place = jnp.zeros_like(off)
-        for bit in list(range(slab_log, slab_log + dom_log)) + list(range(slab_log)):
+        for bit in list(range(slab_log, slab_log + dom_log)) + list(range(slab_log))[::-1]:
             place = place * 2 + (lax.shift_right_logical(off, bit) & 1)
         place_ref[...] = place
 
@@ -431,9 +431,9 @@
 
 
 def insert_kernel(
-    me_ref, addr_ref, item_ref, x_ref, y_ref, pos_ref, meta_ref, blk_ref, more_blk_ref, *rest
+    addr_ref, item_ref, x_ref, y_ref, pos_ref, meta_ref, blk_ref, more_blk_ref, *rest
 ):
-    *post_refs, more_ref, send_ref, keep_ref = rest[:-10]
+    post_ref, more_ref, send_ref, keep_ref = rest[:-10]
     post_t, spread_ref, cols_ref, slice_a, slice_b, buf_s, buf_m, volume, stage, sem = rest[-10:]
     step = pl.program_id(0)
     count = x_ref.shape[0]
@@ -442,26 +442,24 @@
     parts = orients // half
     gb = units // parts
     width = x_ref.shape[1] // gb
-    share = count // len(post_refs)
+    share = post_ref.shape[1]
     lanes = addr_ref.shape[2]
 
     @pl.when(step == 0)
     def _():
         volume[...] = jnp.zeros_like(volume)
-        me = me_ref[0]
-        others = [more_ref.at[k] for k in range(len(post_refs))]
-        for who, (lists, pieces) in enumerate(((blk_ref, post_refs), (more_blk_ref, others))):
+        for who, (lists, pieces) in enumerate(((blk_ref, post_ref), (more_blk_ref, more_ref))):
             spread_columns(lists, cols_ref)
-            for k, post_ref in enumerate(pieces):
-                at = pl.multiple_of((me ^ k) * share, share)
-                post = post_ref[...].astype(F32)
-                first = cols_ref[0, pl.ds(at, share), :]
-                second = cols_ref[1, pl.ds(at, share), :]
+            for k in range(pieces.shape[0]):
+                at = slice(k * share, (k + 1) * share)
+                post = pieces[k].astype(F32)
+                first = cols_ref[0, at, :]
+                second = cols_ref[1, at, :]
                 for b in range(orients // OB):
                     spread = jnp.where(
                         first == b, post[:, :OB], jnp.where(second == b, post[:, OB:], 0.0)
                     )
-                    spread_ref[pl.ds(at, share), b * OB : (b + 1) * OB] = spread
+                    spread_ref[at, b * OB : (b + 1) * OB] = spread
             for b in range(orients // OB):
                 rows = slice(b * OB, (b + 1) * OB)
                 post_t[rows, who * count : (who + 1) * count] = spread_ref[:, rows].T.astype(BF16)
@@ -614,16 +612,14 @@
     return best
 
 
-def insert_call(me, addr, items, flats, pos, meta, blocks, posts, more, orients, owners):
+def insert_call(addr, items, flats, pos, meta, blocks, posts, orients, owners):
     count, length = flats[0].shape
     steps, units, half = pos.shape
     gb = units * half // orients
     width = length // (steps * gb)
     total = owners * RD
-    share = posts[0].shape[0]
     rows = units * sort_sizes(half, owners)[0] + RD + 8
     limit = total * width * 4 // MB + 30
-    smem = pl.BlockSpec(memory_space=pltpu.SMEM)
     block = lambda shape, **kw: pl.BlockSpec(
         (1,) + shape[1:], lambda i: (i,) + (0,) * (len(shape) - 1), **kw
     )
@@ -632,7 +628,6 @@
         grid=(steps,),
         out_shape=[jax.ShapeDtypeStruct((2, total // 2, OB), BF16)] * 2,
         in_specs=[
-            smem,
             block(addr.shape, memory_space=pltpu.SMEM),
             block(items.shape, memory_space=pltpu.SMEM),
             pl.BlockSpec((count, gb * width), lambda i: (0, i)),
@@ -642,8 +637,7 @@
             pl.BlockSpec((2, count), lambda i: (0, 0)),
             pl.BlockSpec((2, count), lambda i: (0, 0)),
         ]
-        + [pl.BlockSpec((share, 2 * OB), lambda i: (0, 0))] * len(posts)
-        + [pl.BlockSpec(more.shape, lambda i: (0, 0, 0))],
+        + [pl.BlockSpec(posts[0].shape, lambda i: (0, 0, 0))] * 2,
         out_specs=[pl.BlockSpec(memory_space=pl.ANY)] * 2,
         scratch_shapes=[
             pltpu.VMEM((orients, 2 * count), BF16),
@@ -663,7 +657,7 @@
             bytes_accessed=2 * count * length,
             transcendentals=0,
         ),
-    )(me, addr, items, *flats, pos, meta, *blocks, *posts, more)
+    )(addr, items, *flats, pos, meta, *blocks, *posts)
 
 
 def flip(value, axis, bit):
@@ -680,30 +674,27 @@
     dom_pos = lax.axis_index("dom")
     slab_pos = lax.axis_index("slab")
     here = jnp.stack([dom_pos, slab_pos]).astype(jnp.int32)
-    slab_me = here[1:]
     dom_bits = [1 << i for i in range((dom_size - 1).bit_length())]
-    slab_bits = [1 << i for i in range((slab_size - 1).bit_length())]
+    swap = lambda value, axis: lax.all_to_all(value, "slab", axis, axis, tiled=True)
 
     blocks = blocks.T
-    kept, sent, *scores = score_call(here, inv_noise, particles, references, blocks, slab_size)
+    kept, sent, scores = score_call(here, inv_noise, particles, references, blocks, slab_size)
     gb = insert_block(groups // 2, orients, devices, particles.shape[0], width)
-    here, own = lax.optimization_barrier((here, scores[0]))
+    here, scores, sent = lax.optimization_barrier((here, scores, sent))
     plan = plan_call(here, destination, groups, gb, (dom_size, slab_size))
-    own, *plan = lax.optimization_barrier((own, *plan))
+    flats = [kept, flip(sent, "dom", dom_bits[0])]
+    more_blocks = flip(blocks, "dom", dom_bits[0])
+    parts = swap(scores, 0)
+    parts, more_blocks, later, *plan = lax.optimization_barrier(
+        (parts, more_blocks, here, *plan)
+    )
     pos, addr, items = plan
-    parts = [own] + [flip(scores[k], "slab", k) for k in range(1, slab_size)]
-    flats = [kept, flip(sent, "dom", dom_bits[0])]
-    post = softmax_call(parts)
-    more_blocks = flip(blocks, "dom", dom_bits[0])
-    post, more_blocks, later = lax.optimization_barrier((post, more_blocks, here))
     meta = meta_call(later, row_index, fraction, pos, devices)
-    posts = [post] + [flip(post, "slab", k) for k in range(1, slab_size)]
-    pile, meta = lax.optimization_barrier((jnp.stack(posts), meta))
-    more = flip(pile, "dom", dom_bits[0])
+    post = swap(softmax_call(parts), 0)
+    post, meta = lax.optimization_barrier((post, meta))
+    posts = [post, flip(post, "dom", dom_bits[0])]
     lists = [blocks, more_blocks]
-    send, keep = insert_call(
-        slab_me, addr, items, flats, pos, meta, lists, posts, more, orients, devices
-    )
+    send, keep = insert_call(addr, items, flats, pos, meta, lists, posts, orients, devices)
 
     def added(terms):
         return functools.reduce(jnp.add, [term.astype(F32) for term in terms])
@@ -726,9 +717,11 @@
             axis = stage if part == 0 else len(rest) - 1 - stage
             columns[part] = halve(columns[part], "dom", axis, rest[axis])
     terms = [jnp.stack([t.reshape(slab_size * RD, OB) for t in pair]) for pair in zip(*columns)]
-    for bit in slab_bits:
-        terms = halve(terms, "slab", 1, bit)
-    volume = jnp.concatenate([added([term[part] for term in terms]) for part in range(2)], axis=1)
+    pieces = added(terms).astype(BF16).reshape(2, slab_size, RD, OB)
+    pieces = swap(pieces, 1)
+    volume = jnp.concatenate(
+        [added([pieces[part, k] for k in range(slab_size)]) for part in range(2)], axis=1
+    )
 
     own = volume.astype(BF16)
     plane = [own] + [flip(own, "dom", 2 * k) for k in range(1, dom_size // 2)]

time: 156 us -> 165 us (1.058)
  blocking collectives: 0 us -> 16.1 us
  starting transfers between devices: 26.2 us -> 20.5 us
  waiting for transfers between devices: 40.2 us -> 36.6 us
  local copies, waits for them, and re-layouts: 2.28 us -> 4.63 us
  Pallas kernels: 84.6 us -> 82.7 us
    all_to_all x0 -> x1, blocking collectives: none -> 16.1 us  [shards(): lax.all_to_all(value, 'slab', axis, axis, tiled=True)]
    ppermute x20 -> x12, starting transfers between devices: 26.2 us -> 10.9 us  [flip(): return lax.ppermute(value, axis, [(i, i ^ bit) for i in range(size)])]
    ppermute x20 -> x12, waiting for transfers between devices: 40.2 us -> 30 us  [flip(): return lax.ppermute(value, axis, [(i, i ^ bit) for i in range(size)])]
    all_to_all x0 -> x2, starting transfers between devices: none -> 9.61 us  [shards(): lax.all_to_all(value, 'slab', axis, axis, tiled=True)]
    all_to_all x0 -> x2, waiting for transfers between devices: none -> 6.56 us  [shards(): lax.all_to_all(value, 'slab', axis, axis, tiled=True)]
    unnamed x16 -> x20, local copies, waits for them, and re-layouts: 0.93 us -> 4.31 us
    pallas_call x1, Pallas kernels: 41.3 us -> 38.6 us  [insert_call(): pl.pallas_call(insert_kernel, grid=(steps,), out_shape=[jax.ShapeDtypeStr...]
  transfers between devices with their start and end apart: 20 -> 14, of which waited for: 12 -> 12; matrix products, arithmetic and copies ran while one was open for 0% -> 0% of each run, Pallas kernels for 8% -> 8%
where the time goes in v12:
time: 165 us
  Pallas kernels  82.7 us (50%)
  waiting for transfers between devices  36.6 us (22%)
  starting transfers between devices  20.5 us (12%)
  blocking collectives  16.1 us (10%)
  local copies, waits for them, and re-layouts  4.63 us (3%)
  other arithmetic  3.43 us (2%)
    pallas_call x1, Pallas kernels, insert_call(): pl.pallas_call(insert_kernel, grid=(steps,), out_shape=[jax.ShapeDtypeStr...  38.6 us
    pallas_call x1, Pallas kernels, score_call(): pl.pallas_call(score_kernel, grid=(steps + 1,), out_shape=[jax.ShapeDtype...  31.1 us
    ppermute x12, waiting for transfers between devices, flip(): return lax.ppermute(value, axis, [(i, i ^ bit) for i in range(size)])  30 us
    all_to_all x1, blocking collectives, shards(): lax.all_to_all(value, 'slab', axis, axis, tiled=True)  16.1 us
    ppermute x12, starting transfers between devices, flip(): return lax.ppermute(value, axis, [(i, i ^ bit) for i in range(size)])  10.9 us
    all_to_all x2, starting transfers between devices, shards(): lax.all_to_all(value, 'slab', axis, axis, tiled=True)  9.61 us
    pallas_call x1, Pallas kernels, plan_call(): pl.pallas_call(functools.partial(plan_kernel, sizes=mesh_sizes, per=group...  7.4 us
    all_to_all x2, waiting for transfers between devices, shards(): lax.all_to_all(value, 'slab', axis, axis, tiled=True)  6.56 us
  transfers between devices with their start and end apart: 14, of which 12 were waited for; matrix products, arithmetic and copies ran while one was open for 0% of the time, Pallas kernels for 8%

profile of v12, /device:TPU:0, one launch (start us, length us, event | category | flops | bytes accessed | tf_op | source)
XLA Modules:
  0.0 164.7 jit_solution(4864887477697628401)
XLA Ops:
  1.3 31.1 %shard_map.86 = (bf16[512,10240]{1,0:T(8,128)(2,1)}, bf16[512,10240]{1,0:T(8,128)(2,1)}, f32[4,128,256]{2,1,0:T(8,128)}) custom-call(s32[2]{0:T(128)} %pad_add_fusion.here_ref, f32[80]{0:T(128)} %noise_ref.1, s32[2,512]{1,0:T(2,128)} %bitcast.64, bf16[512,80,256]{2,1,0:T(8,128)(2,1)} %rest_3_.1, bf16[512,80,256]{2,1,0:T(8,128)(2,1)} %rest_3_.1, ...), custom_call_target="tpu_custom_call" | custom-call | flops 21474836480 | bytes 62914560 | tf_op jit(solution)/shard_map/pallas_call | solution.py:181
  32.9 5.9 %all-to-all-start = ((f32[4,128,256]{2,1,0:T(8,128)}), f32[4,128,256]{2,1,0:T(8,128)S(1)}, u32[]{:S(2)}, u32[]{:S(2)}) async-start(f32[4,128,256]{2,1,0:T(8,128)} %get-tuple-element.23), calls=%async_computation | async-start | bytes 1048576 | tf_op jit(solution)/shard_map/all_to_all | solution.py:678
  39.1 7.4 %shard_map.87 = (s32[4,20,256]{2,1,0:T(8,128)}, s32[4,20,128]{2,1,0:T(8,128)}, s32[4,5,128]{2,1,0:T(8,128)}) custom-call(s32[2]{0:T(128)} %pad_add_fusion.here_ref, s32[320,512]{1,0:T(8,128)} %dest_ref.1), custom_call_target="tpu_custom_call" | custom-call | flops 1342177280 | bytes 327680 | tf_op jit(solution)/shard_map/pallas_call | solution.py:385
  46.5 2.2 %collective-permute-done.more_blk_ref = s32[2,512]{1,0:T(2,128)S(1)} collective-permute-done((s32[2,512]{1,0:T(2,128)S(1)}, s32[2,512]{1,0:T(2,128)S(1)}, u32[]{:S(2)}, u32[]{:S(2)}) %collective-permute-start) | collective-permute-done | bytes 4128 | tf_op jit(solution)/shard_map/ppermute | solution.py:665
  48.7 5.2 %all-to-all-done.parts_ref = f32[4,128,256]{2,1,0:T(8,128)S(1)} async-done(((f32[4,128,256]{2,1,0:T(8,128)}), f32[4,128,256]{2,1,0:T(8,128)S(1)}, u32[]{:S(2)}, u32[]{:S(2)}) %all-to-all-start) | async-done | bytes 524320 | tf_op jit(solution)/shard_map/all_to_all | solution.py:678
  54.8 3.7 %all-to-all-start.1 = ((bf16[4,128,256]{2,1,0:T(8,128)(2,1)}), bf16[4,128,256]{2,1,0:T(8,128)(2,1)S(1)}, u32[]{:S(2)}, u32[]{:S(2)}) async-start(bf16[4,128,256]{2,1,0:T(8,128)(2,1)} %shard_map.88), calls=%async_computation.1 | async-start | bytes 524288 | tf_op jit(solution)/shard_map/all_to_all | solution.py:678
  59.5 4.7 %shard_map.89.meta_ref = f32[4,20,72,128]{3,2,1,0:T(8,128)S(1)} custom-call(s32[2]{0:T(128)S(1)} %copy-done.1, s32[320,512]{1,0:T(8,128)S(1)} %copy-done.2, f32[320,512]{1,0:T(8,128)S(1)} %copy-done.3, s32[4,20,256]{2,1,0:T(8,128)S(1)} %copy-done.6), custom_call_target="tpu_custom_call" | custom-call | flops 1509949440 | bytes 5898240 | tf_op jit(solution)/shard_map/pallas_call | solution.py:415
  64.2 1.6 copy-done.4
  65.8 1.3 all-to-all-done.1.rest_0_
  67.1 1.5 collective-permute-done.2.rest_1_
  68.6 1.8 %copy-done.5 = f32[4,20,72,128]{3,2,1,0:T(8,128)S(1)} copy-done((f32[4,20,72,128]{3,2,1,0:T(8,128)S(1)}, f32[4,20,72,128]{3,2,1,0:T(8,128)}, u32[]{:S(2)}) %copy-start.5) | copy-done | bytes 2949144
  70.5 38.6 %shard_map.90 = (bf16[2,4096,128]{2,1,0:T(8,128)(2,1)S(1)}, bf16[2,4096,128]{2,1,0:T(8,128)(2,1)S(1)}) custom-call(s32[4,20,128]{2,1,0:T(8,128)S(1)} %copy-done.8, s32[4,5,128]{2,1,0:T(8,128)S(1)} %copy-done.9, bf16[512,10240]{1,0:T(8,128)(2,1)} %get-tuple-element.30.x_ref, bf16[512,10240]{1,0:T(8,128)(2,1)} %collective-permute-done.1.y_ref, ...), custom_call_target="tpu_custom_call" | custom-call | flops 21474836480 | bytes 10485760 | tf_op jit(solution)/shard_map/pallas_call | solution.py:626
  109.3 4.0 %collective-permute-done.3 = bf16[2,4096,128]{2,1,0:T(8,128)(2,1)S(1)} collective-permute-done((bf16[2,4096,128]{2,1,0:T(8,128)(2,1)S(1)}, bf16[2,4096,128]{2,1,0:T(8,128)(2,1)S(1)}, u32[]{:S(2)}, u32[]{:S(2)}) %collective-permute-start.3) | collective-permute-done | bytes 2097184 | tf_op jit(solution)/shard_map/ppermute | solution.py:665
  113.5 1.6 collective-permute-start.5
  115.2 1.6 collective-permute-start.4
  116.9 10.6 %collective-permute-done.5 = bf16[2,1,1024,128]{3,2,1,0:T(8,128)(2,1)S(1)} collective-permute-done((bf16[2,1,1024,128]{3,2,1,0:T(8,128)(2,1)S(1)}, bf16[2,1,1024,128]{3,2,1,0:T(8,128)(2,1)S(1)}, u32[]{:S(2)}, u32[]{:S(2)}) %collective-permute-start.5) | collective-permute-done | bytes 524320 | tf_op jit(solution)/shard_map/ppermute | solution.py:665
  127.7 1.6 collective-permute-start.7
  129.4 1.6 collective-permute-start.6
  131.1 4.1 %collective-permute-done.7 = bf16[1,1,1024,128]{3,2,1,0:T(8,128)(2,1)S(1)} collective-permute-done((bf16[1,1,1024,128]{3,2,1,0:T(8,128)(2,1)S(1)}, bf16[1,1,1024,128]{3,2,1,0:T(8,128)(2,1)S(1)}, u32[]{:S(2)}, u32[]{:S(2)}) %collective-permute-start.7) | collective-permute-done | bytes 262176 | tf_op jit(solution)/shard_map/ppermute | solution.py:665
  135.3 1.4 collective-permute-done.6
  137.0 16.1 %all_to_all.15 = bf16[2,4,256,128]{3,2,0,1:T(8,128)(2,1)S(1)} all-to-all(bf16[2,4,256,128]{3,2,0,1:T(8,128)(2,1)S(1)} %add_convert_fusion), channel_id=1, replica_groups=mesh['dom'=8,'slab'=4] {'slab'}, dimensions={1} | all-to-all | bytes 1048576 | tf_op jit(solution)/shard_map/all_to_all | solution.py:678
  153.8 1.5 collective-permute-start.8
  157.3 2.8 %collective-permute-done.8 = bf16[256,256]{1,0:T(8,128)(2,1)S(1)} collective-permute-done((bf16[256,256]{1,0:T(8,128)(2,1)S(1)}, bf16[256,256]{1,0:T(8,128)(2,1)S(1)}, u32[]{:S(2)}, u32[]{:S(2)}) %collective-permute-start.8) | collective-permute-done | bytes 131104 | tf_op jit(solution)/shard_map/ppermute | solution.py:665
  161.8 1.9 %collective-permute-done.11 = bf16[4,256,256]{2,1,0:T(8,128)(2,1)S(1)} collective-permute-done((bf16[4,256,256]{2,1,0:T(8,128)(2,1)S(1)}, bf16[4,256,256]{2,1,0:T(8,128)(2,1)S(1)}, u32[]{:S(2)}, u32[]{:S(2)}) %collective-permute-start.11) | collective-permute-done | bytes 524320 | tf_op jit(solution)/shard_map/ppermute | solution.py:665
  (51 shorter events, 10.0 us)
Async XLA Ops:
  1.3 37.5 %copy-start = (s32[512,2]{0,1:T(2,128)S(1)}, s32[512,2]{0,1:T(2,128)}, u32[]{:S(2)}) copy-start(s32[512,2]{0,1:T(2,128)} %param.8) | copy-start | bytes 12292
  32.4 36.3 %collective-permute-start.1 = (bf16[512,10240]{1,0:T(8,128)(2,1)}, bf16[512,10240]{1,0:T(8,128)(2,1)}, u32[]{:S(2)}, u32[]{:S(2)}) collective-permute-start(bf16[512,10240]{1,0:T(8,128)(2,1)} %get-tuple-element.31), channel_id=1, source_target_pairs={{0,4},{4,0},{8,12},{12,8},{16,20},{20,16},{24,28},{28,24},{1,5},{5... | collective-permute-start | bytes 31457288 | tf_op jit(solution)/shard_map/ppermute | solution.py:665
  32.9 21.0 %all-to-all-start = ((f32[4,128,256]{2,1,0:T(8,128)}), f32[4,128,256]{2,1,0:T(8,128)S(1)}, u32[]{:S(2)}, u32[]{:S(2)}) async-start(f32[4,128,256]{2,1,0:T(8,128)} %get-tuple-element.23), calls=%async_computation | async-start | bytes 1048576 | tf_op jit(solution)/shard_map/all_to_all | solution.py:678
  38.8 19.8 %copy-start.1 = (s32[2]{0:T(128)S(1)}, s32[2]{0:T(128)}, u32[]{:S(2)}) copy-start(s32[2]{0:T(128)} %pad_add_fusion.here_ref) | copy-start | bytes 28
  38.8 19.8 %copy-start.2 = (s32[320,512]{1,0:T(8,128)S(1)}, s32[320,512]{1,0:T(8,128)}, u32[]{:S(2)}) copy-start(s32[320,512]{1,0:T(8,128)} %index_ref.1) | copy-start | bytes 1966084
  38.8 19.8 %copy-start.3 = (f32[320,512]{1,0:T(8,128)S(1)}, f32[320,512]{1,0:T(8,128)}, u32[]{:S(2)}) copy-start(f32[320,512]{1,0:T(8,128)} %frac_ref.1) | copy-start | bytes 1966084
  38.8 9.9 %collective-permute-start = (s32[2,512]{1,0:T(2,128)S(1)}, s32[2,512]{1,0:T(2,128)S(1)}, u32[]{:S(2)}, u32[]{:S(2)}) collective-permute-start(s32[2,512]{1,0:T(2,128)S(1)} %bitcast.65), channel_id=1, source_target_pairs={{0,4},{4,0},{8,12},{12,8},{16,20},{20,16},{24,28},{28,24},{1,5},{5... | collective-permute-start | bytes 12296 | tf_op jit(solution)/shard_map/ppermute | solution.py:665
  54.8 13.8 %copy-start.7 = (s32[4,20,256]{2,1,0:T(8,128)S(1)}, s32[4,20,256]{2,1,0:T(8,128)}, u32[]{:S(2)}) copy-start(s32[4,20,256]{2,1,0:T(8,128)} %get-tuple-element.32.pos_ref) | copy-start | bytes 245764
  54.8 13.8 %copy-start.8 = (s32[4,20,128]{2,1,0:T(8,128)S(1)}, s32[4,20,128]{2,1,0:T(8,128)}, u32[]{:S(2)}) copy-start(s32[4,20,128]{2,1,0:T(8,128)} %get-tuple-element.28.addr_ref) | copy-start | bytes 122884
  54.8 13.8 %copy-start.9 = (s32[4,5,128]{2,1,0:T(8,128)S(1)}, s32[4,5,128]{2,1,0:T(8,128)}, u32[]{:S(2)}) copy-start(s32[4,5,128]{2,1,0:T(8,128)} %get-tuple-element.29.item_ref) | copy-start | bytes 30724
  54.8 12.3 %all-to-all-start.1 = ((bf16[4,128,256]{2,1,0:T(8,128)(2,1)}), bf16[4,128,256]{2,1,0:T(8,128)(2,1)S(1)}, u32[]{:S(2)}, u32[]{:S(2)}) async-start(bf16[4,128,256]{2,1,0:T(8,128)(2,1)} %shard_map.88), calls=%async_computation.1 | async-start | bytes 524288 | tf_op jit(solution)/shard_map/all_to_all | solution.py:678
  58.6 0.9 copy-start.6
  64.2 1.6 copy-start.4
  67.1 1.5 collective-permute-start.2
  68.6 1.8 %copy-start.5 = (f32[4,20,72,128]{3,2,1,0:T(8,128)S(1)}, f32[4,20,72,128]{3,2,1,0:T(8,128)}, u32[]{:S(2)}) copy-start(f32[4,20,72,128]{3,2,1,0:T(8,128)} %copy-done.4) | copy-start | bytes 8847364
  109.1 4.2 %collective-permute-start.3 = (bf16[2,4096,128]{2,1,0:T(8,128)(2,1)S(1)}, bf16[2,4096,128]{2,1,0:T(8,128)(2,1)S(1)}, u32[]{:S(2)}, u32[]{:S(2)}) collective-permute-start(bf16[2,4096,128]{2,1,0:T(8,128)(2,1)S(1)} %get-tuple-element.39), channel_id=1, source_target_pairs={{0,4},{4,0},{8,12},{12,8},{16,20},{20,16},{24,28},{28,24},{1,5},{5... | collective-permute-start | bytes 6291464 | tf_op jit(solution)/shard_map/ppermute | solution.py:665
  113.5 14.0 %collective-permute-start.5 = (bf16[2,1,1024,128]{3,2,1,0:T(8,128)(2,1)S(1)}, bf16[2,1,1024,128]{3,2,1,0:T(8,128)(2,1)S(1)}, u32[]{:S(2)}, u32[]{:S(2)}) collective-permute-start(bf16[2,1,1024,128]{3,2,1,0:T(8,128)(2,1)S(1)} %add_convert_fusion.1), channel_id=1, source_target_pairs={{0,16},{4,20},{8,24},{12,28},{16,0},{20,4},{24,8},{28,12},{1,17},{... | collective-permute-start | bytes 1572872 | tf_op jit(solution)/shard_map/ppermute | solution.py:665
  115.2 14.0 %collective-permute-start.4 = (bf16[1,2,1024,128]{3,2,1,0:T(8,128)(2,1)S(1)}, bf16[1,2,1024,128]{3,2,1,0:T(8,128)(2,1)S(1)}, u32[]{:S(2)}, u32[]{:S(2)}) collective-permute-start(bf16[1,2,1024,128]{3,2,1,0:T(8,128)(2,1)S(1)} %bitcast.84), channel_id=1, source_target_pairs={{0,8},{4,12},{8,0},{12,4},{16,24},{20,28},{24,16},{28,20},{1,9},{5... | collective-permute-start | bytes 1572872 | tf_op jit(solution)/shard_map/ppermute | solution.py:665
  127.7 7.6 %collective-permute-start.7 = (bf16[1,1,1024,128]{3,2,1,0:T(8,128)(2,1)S(1)}, bf16[1,1,1024,128]{3,2,1,0:T(8,128)(2,1)S(1)}, u32[]{:S(2)}, u32[]{:S(2)}) collective-permute-start(bf16[1,1,1024,128]{3,2,1,0:T(8,128)(2,1)S(1)} %add_convert_fusion.3), channel_id=1, source_target_pairs={{0,8},{4,12},{8,0},{12,4},{16,24},{20,28},{24,16},{28,20},{1,9},{5... | collective-permute-start | bytes 786440 | tf_op jit(solution)/shard_map/ppermute | solution.py:665
  129.4 7.3 %collective-permute-start.6 = (bf16[1,1,1024,128]{3,2,1,0:T(8,128)(2,1)S(1)}, bf16[1,1,1024,128]{3,2,1,0:T(8,128)(2,1)S(1)}, u32[]{:S(2)}, u32[]{:S(2)}) collective-permute-start(bf16[1,1,1024,128]{3,2,1,0:T(8,128)(2,1)S(1)} %add_convert_fusion.4), channel_id=1, source_target_pairs={{0,16},{4,20},{8,24},{12,28},{16,0},{20,4},{24,8},{28,12},{1,17},{... | collective-permute-start | bytes 786440 | tf_op jit(solution)/shard_map/ppermute | solution.py:665
  153.8 6.3 %collective-permute-start.8 = (bf16[256,256]{1,0:T(8,128)(2,1)S(1)}, bf16[256,256]{1,0:T(8,128)(2,1)S(1)}, u32[]{:S(2)}, u32[]{:S(2)}) collective-permute-start(bf16[256,256]{1,0:T(8,128)(2,1)S(1)} %get-tuple-element.40), channel_id=1, source_target_pairs={{0,24},{4,28},{8,16},{12,20},{16,8},{20,12},{24,0},{28,4},{1,25},{... | collective-permute-start | bytes 393224 | tf_op jit(solution)/shard_map/ppermute | solution.py:665
  155.3 6.1 %collective-permute-start.9 = (bf16[256,256]{1,0:T(8,128)(2,1)S(1)}, bf16[256,256]{1,0:T(8,128)(2,1)S(1)}, u32[]{:S(2)}, u32[]{:S(2)}) collective-permute-start(bf16[256,256]{1,0:T(8,128)(2,1)S(1)} %get-tuple-element.40), channel_id=1, source_target_pairs={{0,16},{4,20},{8,24},{12,28},{16,0},{20,4},{24,8},{28,12},{1,17},{... | collective-permute-start | bytes 393224 | tf_op jit(solution)/shard_map/ppermute | solution.py:665
  156.5 5.0 %collective-permute-start.10 = (bf16[256,256]{1,0:T(8,128)(2,1)S(1)}, bf16[256,256]{1,0:T(8,128)(2,1)S(1)}, u32[]{:S(2)}, u32[]{:S(2)}) collective-permute-start(bf16[256,256]{1,0:T(8,128)(2,1)S(1)} %get-tuple-element.40), channel_id=1, source_target_pairs={{0,8},{4,12},{8,0},{12,4},{16,24},{20,28},{24,16},{28,20},{1,9},{5... | collective-permute-start | bytes 393224 | tf_op jit(solution)/shard_map/ppermute | solution.py:665
  161.7 2.0 %collective-permute-start.11 = (bf16[4,256,256]{2,1,0:T(8,128)(2,1)S(1)}, bf16[4,256,256]{2,1,0:T(8,128)(2,1)S(1)}, u32[]{:S(2)}, u32[]{:S(2)}) collective-permute-start(bf16[4,256,256]{2,1,0:T(8,128)(2,1)S(1)} %get-tuple-element.43), channel_id=1, source_target_pairs={{0,4},{4,0},{8,12},{12,8},{16,20},{20,16},{24,28},{28,24},{1,5},{5... | collective-permute-start | bytes 1572872 | tf_op jit(solution)/shard_map/ppermute | solution.py:665

commit v13 on v11

--- a/solution.py
+++ b/solution.py
@@ -40,7 +40,8 @@
     particles, orients = acc_ref.shape
     side = 16 * gb
     per = gb // 2
-    core = here_ref[0] & 1
+    slabs = len(out_refs)
+    core = lax.div(here_ref[0], slabs) & 1
     rounds = 4
 
     def copies(flat_ref, slot, at_step, swap):
@@ -90,12 +91,12 @@
             rows = particles // STREAMS
             for t in range(rows // 16 // rounds):
                 job = (x_refs[s], i * (rows // 16 // rounds) + t, s * rows, flat_ref)
-                if (s * (rows // 16 // rounds) + t) % 4:
+                if (s * (rows // 16 // rounds) + t) % 2:
                     turns.append(job)
                 else:
                     jobs.append(job + (False,))
-        for at in range(0, len(jobs), 5):
-            regroup(jobs[at : at + 5])
+        for at in range(0, len(jobs), 6):
+            regroup(jobs[at : at + 6])
         for job in turns:
             turn(*job)
 
@@ -145,7 +146,7 @@
     def finish(last_flat, last_w):
         for h in range(2):
             product(last_flat[h], last_w[h])
-        me = here_ref[1]
+        me = lax.rem(here_ref[0], slabs)
         share = particles // len(out_refs)
         for k, out_ref in enumerate(out_refs):
             at = pl.multiple_of((me ^ k) * share, share)
@@ -235,8 +236,9 @@
     )(*parts)
 
 
-def own_row(here_ref, local, per):
-    return lax.div(local, per) * (2 * per) + (here_ref[0] & 1) * per + lax.rem(local, per)
+def own_row(here_ref, local, per, slabs):
+    core = lax.div(here_ref[0], slabs) & 1
+    return lax.div(local, per) * (2 * per) + core * per + lax.rem(local, per)
 
 
 def plan_kernel(
@@ -253,7 +255,7 @@
 
     @pl.when(step == 0)
     def _():
-        off = dest_ref[...] ^ (here_ref[0] * slab_size + here_ref[1])
+        off = dest_ref[...] ^ here_ref[0]
         place = jnp.zeros_like(off)
         for bit in list(range(slab_log, slab_log + dom_log)) + list(range(slab_log)):
             place = place * 2 + (lax.shift_right_logical(off, bit) & 1)
@@ -262,7 +264,7 @@
     owner = lax.broadcasted_iota(jnp.int32, (owners, 1), 0)
     for u in range(units):
         g, h = u // parts, u % parts
-        at = pl.ds(own_row(here_ref, step * gb + g, per), 1)
+        at = pl.ds(own_row(here_ref, step * gb + g, per, slab_size), 1)
         line = place_ref[at, h * half : (h + 1) * half]
         hot = jnp.where(line == owner, 1.0, 0.0)
         hot_ref[u * owners : (u + 1) * owners, :] = hot.astype(BF16)
@@ -327,7 +329,7 @@
         item_ref[0, i : i + 1, :] = value.astype(jnp.int32)
 
 
-def meta_kernel(here_ref, index_ref, frac_ref, pos_ref, meta_ref, *, per):
+def meta_kernel(here_ref, index_ref, frac_ref, pos_ref, meta_ref, *, per, slabs):
     step = pl.program_id(0)
     _, units, half = pos_ref.shape
     parts = index_ref.shape[1] // half
@@ -339,7 +341,7 @@
     one, none = jnp.bfloat16(1.0), jnp.bfloat16(0.0)
     for u in range(units):
         g, h = u // parts, u % parts
-        line = pl.ds(own_row(here_ref, step * gb + g, per), 1)
+        line = pl.ds(own_row(here_ref, step * gb + g, per, slabs), 1)
         span = slice(h * half, (h + 1) * half)
         pos = pos_ref[0, u : u + 1, :]
         here = lane_of == low(pos & 7)
@@ -387,7 +389,11 @@
         grid_spec=pltpu.PrefetchScalarGridSpec(
             num_scalar_prefetch=1,
             grid=(steps,),
-            in_specs=[pl.BlockSpec((groups, orients), lambda i, here: (here[1], 0))],
+            in_specs=[
+                pl.BlockSpec(
+                    (groups, orients), lambda i, here: (lax.rem(here[0], mesh_sizes[1]), 0)
+                )
+            ],
             out_specs=[planned(shape) for shape in shapes],
             scratch_shapes=[
                 pltpu.VMEM((groups, orients), jnp.int32),
@@ -405,15 +411,15 @@
     )(here, destination)
 
 
-def meta_call(here, row_index, fraction, pos, owners):
+def meta_call(here, row_index, fraction, pos, owners, slabs):
     steps, units, half = pos.shape
     orients = row_index.shape[1]
     groups = 2 * steps * units * half // orients
     blocks = sort_sizes(half, owners)[2]
     shape = (steps, units, blocks, OB)
-    table = pl.BlockSpec((groups, orients), lambda i, here: (here[1], 0))
+    table = pl.BlockSpec((groups, orients), lambda i, here: (lax.rem(here[0], slabs), 0))
     return pl.pallas_call(
-        functools.partial(meta_kernel, per=group_block(groups) // 2),
+        functools.partial(meta_kernel, per=group_block(groups) // 2, slabs=slabs),
         grid_spec=pltpu.PrefetchScalarGridSpec(
             num_scalar_prefetch=1,
             grid=(steps,),
@@ -431,10 +437,10 @@
 
 
 def insert_kernel(
-    me_ref, addr_ref, item_ref, x_ref, y_ref, pos_ref, meta_ref, blk_ref, more_blk_ref, *rest
+    addr_ref, item_ref, x_ref, y_ref, pos_ref, meta_ref, blk_ref, more_blk_ref, *rest
 ):
-    *post_refs, more_ref, send_ref, keep_ref = rest[:-10]
-    post_t, spread_ref, cols_ref, slice_a, slice_b, buf_s, buf_m, volume, stage, sem = rest[-10:]
+    post_ref, more_ref, send_ref, keep_ref = rest[:-8]
+    post_t, slice_a, slice_b, buf_s, buf_m, volume, stage, sem = rest[-8:]
     step = pl.program_id(0)
     count = x_ref.shape[0]
     orients = post_t.shape[0]
@@ -442,29 +448,24 @@
     parts = orients // half
     gb = units // parts
     width = x_ref.shape[1] // gb
-    share = count // len(post_refs)
+    share = post_ref.shape[1]
     lanes = addr_ref.shape[2]
 
     @pl.when(step == 0)
     def _():
         volume[...] = jnp.zeros_like(volume)
-        me = me_ref[0]
-        others = [more_ref.at[k] for k in range(len(post_refs))]
-        for who, (lists, pieces) in enumerate(((blk_ref, post_refs), (more_blk_ref, others))):
-            spread_columns(lists, cols_ref)
-            for k, post_ref in enumerate(pieces):
-                at = pl.multiple_of((me ^ k) * share, share)
-                post = post_ref[...].astype(F32)
-                first = cols_ref[0, pl.ds(at, share), :]
-                second = cols_ref[1, pl.ds(at, share), :]
+        for who, (lists, pieces) in enumerate(((blk_ref, post_ref), (more_blk_ref, more_ref))):
+            for k in range(pieces.shape[0]):
+                lanes = slice(k * share, (k + 1) * share)
+                turned = pieces[k].astype(F32).T
                 for b in range(orients // OB):
-                    spread = jnp.where(
-                        first == b, post[:, :OB], jnp.where(second == b, post[:, OB:], 0.0)
+                    value = jnp.where(
+                        lists[0:1, lanes] == b,
+                        turned[:OB],
+                        jnp.where(lists[1:2, lanes] == b, turned[OB:], 0.0),
                     )
-                    spread_ref[pl.ds(at, share), b * OB : (b + 1) * OB] = spread
-            for b in range(orients // OB):
-                rows = slice(b * OB, (b + 1) * OB)
-                post_t[rows, who * count : (who + 1) * count] = spread_ref[:, rows].T.astype(BF16)
+                    at = slice(who * count + k * share, who * count + (k + 1) * share)
+                    post_t[b * OB : (b + 1) * OB, at] = value.astype(BF16)
 
     tail = pl.ds(pl.multiple_of(item_ref[0, 4, 0] * 8, 8), RD)
     buf_s[tail, :] = jnp.zeros((RD, width), F32)
@@ -614,16 +615,14 @@
     return best
 
 
-def insert_call(me, addr, items, flats, pos, meta, blocks, posts, more, orients, owners):
+def insert_call(addr, items, flats, pos, meta, blocks, posts, orients, owners):
     count, length = flats[0].shape
     steps, units, half = pos.shape
     gb = units * half // orients
     width = length // (steps * gb)
     total = owners * RD
-    share = posts[0].shape[0]
     rows = units * sort_sizes(half, owners)[0] + RD + 8
     limit = total * width * 4 // MB + 30
-    smem = pl.BlockSpec(memory_space=pltpu.SMEM)
     block = lambda shape, **kw: pl.BlockSpec(
         (1,) + shape[1:], lambda i: (i,) + (0,) * (len(shape) - 1), **kw
     )
@@ -632,7 +631,6 @@
         grid=(steps,),
         out_shape=[jax.ShapeDtypeStruct((2, total // 2, OB), BF16)] * 2,
         in_specs=[
-            smem,
             block(addr.shape, memory_space=pltpu.SMEM),
             block(items.shape, memory_space=pltpu.SMEM),
             pl.BlockSpec((count, gb * width), lambda i: (0, i)),
@@ -642,13 +640,10 @@
             pl.BlockSpec((2, count), lambda i: (0, 0)),
             pl.BlockSpec((2, count), lambda i: (0, 0)),
         ]
-        + [pl.BlockSpec((share, 2 * OB), lambda i: (0, 0))] * len(posts)
-        + [pl.BlockSpec(more.shape, lambda i: (0, 0, 0))],
+        + [pl.BlockSpec(posts[0].shape, lambda i: (0, 0, 0))] * 2,
         out_specs=[pl.BlockSpec(memory_space=pl.ANY)] * 2,
         scratch_shapes=[
             pltpu.VMEM((orients, 2 * count), BF16),
-            pltpu.VMEM((count, orients), F32),
-            pltpu.VMEM((2, count, OB), F32),
             pltpu.VMEM((orients, group_pair(gb) * width), BF16),
             pltpu.VMEM((orients, group_pair(gb) * width), BF16),
             pltpu.VMEM((rows, width), F32),
@@ -663,7 +658,7 @@
             bytes_accessed=2 * count * length,
             transcendentals=0,
         ),
-    )(me, addr, items, *flats, pos, meta, *blocks, *posts, more)
+    )(addr, items, *flats, pos, meta, *blocks, *posts)
 
 
 def flip(value, axis, bit):
@@ -679,8 +674,7 @@
     devices = dom_size * slab_size
     dom_pos = lax.axis_index("dom")
     slab_pos = lax.axis_index("slab")
-    here = jnp.stack([dom_pos, slab_pos]).astype(jnp.int32)
-    slab_me = here[1:]
+    here = lax.axis_index(("dom", "slab")).astype(jnp.int32).reshape(1)
     dom_bits = [1 << i for i in range((dom_size - 1).bit_length())]
     slab_bits = [1 << i for i in range((slab_size - 1).bit_length())]
 
@@ -696,14 +690,18 @@
     post = softmax_call(parts)
     more_blocks = flip(blocks, "dom", dom_bits[0])
     post, more_blocks, later = lax.optimization_barrier((post, more_blocks, here))
-    meta = meta_call(later, row_index, fraction, pos, devices)
+    meta = meta_call(later, row_index, fraction, pos, devices, slab_size)
     posts = [post] + [flip(post, "slab", k) for k in range(1, slab_size)]
-    pile, meta = lax.optimization_barrier((jnp.stack(posts), meta))
-    more = flip(pile, "dom", dom_bits[0])
+    ordered = []
+    for k in range(slab_size):
+        value = posts[0]
+        for j in range(1, slab_size):
+            value = jnp.where(slab_pos ^ j == k, posts[j], value)
+        ordered.append(value)
+    pile, meta = lax.optimization_barrier((jnp.stack(ordered), meta))
+    posts = [pile, flip(pile, "dom", dom_bits[0])]
     lists = [blocks, more_blocks]
-    send, keep = insert_call(
-        slab_me, addr, items, flats, pos, meta, lists, posts, more, orients, devices
-    )
+    send, keep = insert_call(addr, items, flats, pos, meta, lists, posts, orients, devices)
 
     def added(terms):
         return functools.reduce(jnp.add, [term.astype(F32) for term in terms])

time: 156 us -> 157 us (level)
  waiting for transfers between devices: 40.2 us -> 43.8 us
  starting transfers between devices: 26.2 us -> 24.1 us
    ppermute x20, waiting for transfers between devices: 40.2 us -> 43.8 us  [flip(): return lax.ppermute(value, axis, [(i, i ^ bit) for i in range(size)])]
    pallas_call x1, Pallas kernels: 31.1 us -> 33.7 us  [score_call(): pl.pallas_call(score_kernel, grid=(steps + 1,), out_shape=[jax.ShapeDtype...]
    ppermute x20, starting transfers between devices: 26.2 us -> 24.1 us  [flip(): return lax.ppermute(value, axis, [(i, i ^ bit) for i in range(size)])]
  transfers between devices with their start and end apart: 20 -> 20, of which waited for: 12 -> 13; matrix products, arithmetic and copies ran while one was open for 0% -> 0% of each run, Pallas kernels for 8% -> 7%
where the time goes in v13:
time: 157 us; the launch traced here: 158 us
  Pallas kernels  85.1 us (54%)
  waiting for transfers between devices  43.8 us (28%)
  starting transfers between devices  24.1 us (15%)
  local copies, waits for them, and re-layouts  2.28 us (1%)
  other arithmetic  1.95 us (1%)
    ppermute x20, waiting for transfers between devices, flip(): return lax.ppermute(value, axis, [(i, i ^ bit) for i in range(size)])  43.8 us
    pallas_call x1, Pallas kernels, insert_call(): pl.pallas_call(insert_kernel, grid=(steps,), out_shape=[jax.ShapeDtypeStr...  40.5 us
    pallas_call x1, Pallas kernels, score_call(): pl.pallas_call(score_kernel, grid=(steps + 1,), out_shape=[jax.ShapeDtype...  33.7 us
    ppermute x20, starting transfers between devices, flip(): return lax.ppermute(value, axis, [(i, i ^ bit) for i in range(size)])  24.1 us
    pallas_call x1, Pallas kernels, plan_call(): pl.pallas_call(functools.partial(plan_kernel, sizes=mesh_sizes, per=group...  6.62 us
    pallas_call x1, Pallas kernels, meta_call(): pl.pallas_call(functools.partial(meta_kernel, per=group_block(groups) //...  4.08 us
  transfers between devices with their start and end apart: 20, of which 13 were waited for; matrix products, arithmetic and copies ran while one was open for 0% of the time, Pallas kernels for 7%

profile of v13, /device:TPU:0, one launch (start us, length us, event | category | flops | bytes accessed | tf_op | source)
XLA Modules:
  0.0 158.1 jit_solution(16018399361119043947)
XLA Ops:
  0.6 33.7 %shard_map.86 = (bf16[512,10240]{1,0:T(8,128)(2,1)}, bf16[512,10240]{1,0:T(8,128)(2,1)}, f32[128,256]{1,0:T(8,128)}, f32[128,256]{1,0:T(8,128)}, f32[128,256]{1,0:T(8,128)}, /*index=5*/f32[128,256]{1,0:T(8,128)}) custom-call(s32[1]{0:T(128)} %bitcast.here_ref, f32[80]{0:T(128)} %noise_ref.1, s32[2,512]{1,0:T(2,128)} %bitcast.45, ...), custom_call_target="tpu_custom_call" | custom-call | flops 21474836480 | bytes 62914560 | tf_op jit(solution)/shard_map/pallas_call | solution.py:183
  35.0 2.6 %collective-permute-start.1 = (f32[128,256]{1,0:T(8,128)}, f32[128,256]{1,0:T(8,128)S(1)}, u32[]{:S(2)}, u32[]{:S(2)}) collective-permute-start(f32[128,256]{1,0:T(8,128)} %get-tuple-element.36), channel_id=1, source_target_pairs={{0,1},{1,0},{2,3},{3,2},{4,5},{5,4},{6,7},{7,6},{8,9},{9,8},{10,11... | collective-permute-start | bytes 393224 | tf_op jit(solution)/shard_map/ppermute | solution.py:666
  37.6 2.6 %collective-permute-start.2 = (f32[128,256]{1,0:T(8,128)}, f32[128,256]{1,0:T(8,128)S(1)}, u32[]{:S(2)}, u32[]{:S(2)}) collective-permute-start(f32[128,256]{1,0:T(8,128)} %get-tuple-element.37), channel_id=1, source_target_pairs={{0,2},{1,3},{2,0},{3,1},{4,6},{5,7},{6,4},{7,5},{8,10},{9,11},{10,... | collective-permute-start | bytes 393224 | tf_op jit(solution)/shard_map/ppermute | solution.py:666
  40.2 6.6 %shard_map.87 = (s32[4,20,256]{2,1,0:T(8,128)}, s32[4,20,128]{2,1,0:T(8,128)}, s32[4,5,128]{2,1,0:T(8,128)}) custom-call(s32[1]{0:T(128)} %bitcast.here_ref, s32[320,512]{1,0:T(8,128)} %dest_ref.1), custom_call_target="tpu_custom_call" | custom-call | flops 1342177280 | bytes 327680 | tf_op jit(solution)/shard_map/pallas_call | solution.py:387
  46.8 3.9 %collective-permute-done.2.refs_2_ = f32[128,256]{1,0:T(8,128)S(1)} collective-permute-done((f32[128,256]{1,0:T(8,128)}, f32[128,256]{1,0:T(8,128)S(1)}, u32[]{:S(2)}, u32[]{:S(2)}) %collective-permute-start.2) | collective-permute-done | bytes 131104 | tf_op jit(solution)/shard_map/ppermute | solution.py:666
  51.0 4.8 %collective-permute-start.5 = (bf16[128,256]{1,0:T(8,128)(2,1)S(1)}, bf16[128,256]{1,0:T(8,128)(2,1)S(1)}, u32[]{:S(2)}, u32[]{:S(2)}) collective-permute-start(bf16[128,256]{1,0:T(8,128)(2,1)S(1)} %shard_map.88), channel_id=1, source_target_pairs={{0,3},{1,2},{2,1},{3,0},{4,7},{5,6},{6,5},{7,4},{8,11},{9,10},{10,... | collective-permute-start | bytes 196616 | tf_op jit(solution)/shard_map/ppermute | solution.py:666
  57.2 4.1 %shard_map.89.meta_ref = f32[4,20,72,128]{3,2,1,0:T(8,128)S(1)} custom-call(s32[1]{0:T(128)} %bitcast.here_ref, s32[320,512]{1,0:T(8,128)S(1)} %copy-done.2, f32[320,512]{1,0:T(8,128)S(1)} %copy-done.3, s32[4,20,256]{2,1,0:T(8,128)S(1)} %copy-done.4), custom_call_target="tpu_custom_call" | custom-call | flops 1509949440 | bytes 5898240 | tf_op jit(solution)/shard_map/pallas_call | solution.py:421
  61.8 1.5 collective-permute-done.8.rest_1_
  63.3 40.5 %shard_map.90 = (bf16[2,4096,128]{2,1,0:T(8,128)(2,1)S(1)}, bf16[2,4096,128]{2,1,0:T(8,128)(2,1)S(1)}) custom-call(s32[4,20,128]{2,1,0:T(8,128)S(1)} %copy-done.6, s32[4,5,128]{2,1,0:T(8,128)S(1)} %copy-done.7, bf16[512,10240]{1,0:T(8,128)(2,1)} %get-tuple-element.32.x_ref, bf16[512,10240]{1,0:T(8,128)(2,1)} %collective-permute-done.y_ref, ...), custom_call_target="tpu_custom_call" | custom-call | flops 21474836480 | bytes 10485760 | tf_op jit(solution)/shard_map/pallas_call | solution.py:629
  104.4 3.7 %collective-permute-done.9 = bf16[2,4096,128]{2,1,0:T(8,128)(2,1)S(1)} collective-permute-done((bf16[2,4096,128]{2,1,0:T(8,128)(2,1)S(1)}, bf16[2,4096,128]{2,1,0:T(8,128)(2,1)S(1)}, u32[]{:S(2)}, u32[]{:S(2)}) %collective-permute-start.9) | collective-permute-done | bytes 2097184 | tf_op jit(solution)/shard_map/ppermute | solution.py:666
  108.2 1.6 %collective-permute-start.10 = (bf16[1,2,1024,128]{3,2,1,0:T(8,128)(2,1)S(1)}, bf16[1,2,1024,128]{3,2,1,0:T(8,128)(2,1)S(1)}, u32[]{:S(2)}, u32[]{:S(2)}) collective-permute-start(bf16[1,2,1024,128]{3,2,1,0:T(8,128)(2,1)S(1)} %bitcast.65), channel_id=1, source_target_pairs={{0,8},{4,12},{8,0},{12,4},{16,24},{20,28},{24,16},{28,20},{1,9},{5... | collective-permute-start | bytes 1572872 | tf_op jit(solution)/shard_map/ppermute | solution.py:666
  110.0 1.5 collective-permute-start.12
  111.7 10.8 %collective-permute-done.10 = bf16[1,2,1024,128]{3,2,1,0:T(8,128)(2,1)S(1)} collective-permute-done((bf16[1,2,1024,128]{3,2,1,0:T(8,128)(2,1)S(1)}, bf16[1,2,1024,128]{3,2,1,0:T(8,128)(2,1)S(1)}, u32[]{:S(2)}, u32[]{:S(2)}) %collective-permute-start.10) | collective-permute-done | bytes 524320 | tf_op jit(solution)/shard_map/ppermute | solution.py:666
  122.6 1.5 collective-permute-start.11
  124.2 1.6 collective-permute-start.13
  125.8 4.6 %collective-permute-done.11 = bf16[1,1,1024,128]{3,2,1,0:T(8,128)(2,1)S(1)} collective-permute-done((bf16[1,1,1024,128]{3,2,1,0:T(8,128)(2,1)S(1)}, bf16[1,1,1024,128]{3,2,1,0:T(8,128)(2,1)S(1)}, u32[]{:S(2)}, u32[]{:S(2)}) %collective-permute-start.11) | collective-permute-done | bytes 262176 | tf_op jit(solution)/shard_map/ppermute | solution.py:666
  130.4 1.4 collective-permute-done.13
  132.7 5.8 %collective-permute-done.14 = bf16[2,512,128]{2,1,0:T(8,128)(2,1)S(1)} collective-permute-done((bf16[2,512,128]{2,1,0:T(8,128)(2,1)S(1)}, bf16[2,512,128]{2,1,0:T(8,128)(2,1)S(1)}, u32[]{:S(2)}, u32[]{:S(2)}) %collective-permute-start.14) | collective-permute-done | bytes 262176 | tf_op jit(solution)/shard_map/ppermute | solution.py:666
  138.6 1.9 %collective-permute-start.15 = (bf16[2,256,128]{2,1,0:T(8,128)(2,1)S(1)}, bf16[2,256,128]{2,1,0:T(8,128)(2,1)S(1)}, u32[]{:S(2)}, u32[]{:S(2)}) collective-permute-start(bf16[2,256,128]{2,1,0:T(8,128)(2,1)S(1)} %add_convert_fusion.5), channel_id=1, source_target_pairs={{0,2},{1,3},{2,0},{3,1},{4,6},{5,7},{6,4},{7,5},{8,10},{9,11},{10,... | collective-permute-start | bytes 393224 | tf_op jit(solution)/shard_map/ppermute | solution.py:666
  140.5 5.4 %collective-permute-done.15 = bf16[2,256,128]{2,1,0:T(8,128)(2,1)S(1)} collective-permute-done((bf16[2,256,128]{2,1,0:T(8,128)(2,1)S(1)}, bf16[2,256,128]{2,1,0:T(8,128)(2,1)S(1)}, u32[]{:S(2)}, u32[]{:S(2)}) %collective-permute-start.15) | collective-permute-done | bytes 131104 | tf_op jit(solution)/shard_map/ppermute | solution.py:666
  146.8 1.5 collective-permute-start.16
  148.3 1.5 collective-permute-start.17
  150.3 2.5 %collective-permute-done.16 = bf16[256,256]{1,0:T(8,128)(2,1)S(1)} collective-permute-done((bf16[256,256]{1,0:T(8,128)(2,1)S(1)}, bf16[256,256]{1,0:T(8,128)(2,1)S(1)}, u32[]{:S(2)}, u32[]{:S(2)}) %collective-permute-start.16) | collective-permute-done | bytes 131104 | tf_op jit(solution)/shard_map/ppermute | solution.py:666
  155.0 1.9 %collective-permute-done.19 = bf16[4,256,256]{2,1,0:T(8,128)(2,1)S(1)} collective-permute-done((bf16[4,256,256]{2,1,0:T(8,128)(2,1)S(1)}, bf16[4,256,256]{2,1,0:T(8,128)(2,1)S(1)}, u32[]{:S(2)}, u32[]{:S(2)}) %collective-permute-start.19) | collective-permute-done | bytes 524320 | tf_op jit(solution)/shard_map/ppermute | solution.py:666
  (59 shorter events, 9.8 us)
Async XLA Ops:
  0.6 39.6 %copy-start.1 = (s32[512,2]{0,1:T(2,128)S(1)}, s32[512,2]{0,1:T(2,128)}, u32[]{:S(2)}) copy-start(s32[512,2]{0,1:T(2,128)} %param.8) | copy-start | bytes 12292
  34.4 16.3 %copy-start = (f32[128,256]{1,0:T(8,128)S(1)}, f32[128,256]{1,0:T(8,128)}, u32[]{:S(2)}) copy-start(f32[128,256]{1,0:T(8,128)} %get-tuple-element.35.refs_0_) | copy-start | bytes 393220
  34.4 21.9 %copy-start.2 = (s32[320,512]{1,0:T(8,128)S(1)}, s32[320,512]{1,0:T(8,128)}, u32[]{:S(2)}) copy-start(s32[320,512]{1,0:T(8,128)} %index_ref.1) | copy-start | bytes 1966084
  34.4 21.9 %copy-start.3 = (f32[320,512]{1,0:T(8,128)S(1)}, f32[320,512]{1,0:T(8,128)}, u32[]{:S(2)}) copy-start(f32[320,512]{1,0:T(8,128)} %frac_ref.1) | copy-start | bytes 1966084
  34.4 28.9 %collective-permute-start = (bf16[512,10240]{1,0:T(8,128)(2,1)}, bf16[512,10240]{1,0:T(8,128)(2,1)}, u32[]{:S(2)}, u32[]{:S(2)}) collective-permute-start(bf16[512,10240]{1,0:T(8,128)(2,1)} %get-tuple-element.33), channel_id=1, source_target_pairs={{0,4},{4,0},{8,12},{12,8},{16,20},{20,16},{24,28},{28,24},{1,5},{5... | collective-permute-start | bytes 31457288 | tf_op jit(solution)/shard_map/ppermute | solution.py:666
  35.0 11.9 %collective-permute-start.1 = (f32[128,256]{1,0:T(8,128)}, f32[128,256]{1,0:T(8,128)S(1)}, u32[]{:S(2)}, u32[]{:S(2)}) collective-permute-start(f32[128,256]{1,0:T(8,128)} %get-tuple-element.36), channel_id=1, source_target_pairs={{0,1},{1,0},{2,3},{3,2},{4,5},{5,4},{6,7},{7,6},{8,9},{9,8},{10,11... | collective-permute-start | bytes 393224 | tf_op jit(solution)/shard_map/ppermute | solution.py:666
  37.6 13.1 %collective-permute-start.2 = (f32[128,256]{1,0:T(8,128)}, f32[128,256]{1,0:T(8,128)S(1)}, u32[]{:S(2)}, u32[]{:S(2)}) collective-permute-start(f32[128,256]{1,0:T(8,128)} %get-tuple-element.37), channel_id=1, source_target_pairs={{0,2},{1,3},{2,0},{3,1},{4,6},{5,7},{6,4},{7,5},{8,10},{9,11},{10,... | collective-permute-start | bytes 393224 | tf_op jit(solution)/shard_map/ppermute | solution.py:666
  40.2 10.5 %collective-permute-start.3 = (f32[128,256]{1,0:T(8,128)}, f32[128,256]{1,0:T(8,128)S(1)}, u32[]{:S(2)}, u32[]{:S(2)}) collective-permute-start(f32[128,256]{1,0:T(8,128)} %get-tuple-element.38), channel_id=1, source_target_pairs={{0,3},{1,2},{2,1},{3,0},{4,7},{5,6},{6,5},{7,4},{8,11},{9,10},{10,... | collective-permute-start | bytes 393224 | tf_op jit(solution)/shard_map/ppermute | solution.py:666
  40.2 10.8 %collective-permute-start.4 = (s32[2,512]{1,0:T(2,128)S(1)}, s32[2,512]{1,0:T(2,128)S(1)}, u32[]{:S(2)}, u32[]{:S(2)}) collective-permute-start(s32[2,512]{1,0:T(2,128)S(1)} %bitcast.46), channel_id=1, source_target_pairs={{0,4},{4,0},{8,12},{12,8},{16,20},{20,16},{24,28},{28,24},{1,5},{5... | collective-permute-start | bytes 12296 | tf_op jit(solution)/shard_map/ppermute | solution.py:666
  51.0 10.3 %collective-permute-start.5 = (bf16[128,256]{1,0:T(8,128)(2,1)S(1)}, bf16[128,256]{1,0:T(8,128)(2,1)S(1)}, u32[]{:S(2)}, u32[]{:S(2)}) collective-permute-start(bf16[128,256]{1,0:T(8,128)(2,1)S(1)} %shard_map.88), channel_id=1, source_target_pairs={{0,3},{1,2},{2,1},{3,0},{4,7},{5,6},{6,5},{7,4},{8,11},{9,10},{10,... | collective-permute-start | bytes 196616 | tf_op jit(solution)/shard_map/ppermute | solution.py:666
  55.7 5.9 %collective-permute-start.6 = (bf16[128,256]{1,0:T(8,128)(2,1)S(1)}, bf16[128,256]{1,0:T(8,128)(2,1)S(1)}, u32[]{:S(2)}, u32[]{:S(2)}) collective-permute-start(bf16[128,256]{1,0:T(8,128)(2,1)S(1)} %shard_map.88), channel_id=1, source_target_pairs={{0,2},{1,3},{2,0},{3,1},{4,6},{5,7},{6,4},{7,5},{8,10},{9,11},{10,... | collective-permute-start | bytes 196616 | tf_op jit(solution)/shard_map/ppermute | solution.py:666
  55.7 5.9 %collective-permute-start.7 = (bf16[128,256]{1,0:T(8,128)(2,1)S(1)}, bf16[128,256]{1,0:T(8,128)(2,1)S(1)}, u32[]{:S(2)}, u32[]{:S(2)}) collective-permute-start(bf16[128,256]{1,0:T(8,128)(2,1)S(1)} %shard_map.88), channel_id=1, source_target_pairs={{0,1},{1,0},{2,3},{3,2},{4,5},{5,4},{6,7},{7,6},{8,9},{9,8},{10,11... | collective-permute-start | bytes 196616 | tf_op jit(solution)/shard_map/ppermute | solution.py:666
  61.7 1.6 %collective-permute-start.8 = (bf16[4,128,256]{2,1,0:T(8,128)(2,1)S(1)}, bf16[4,128,256]{2,1,0:T(8,128)(2,1)S(1)}, u32[]{:S(2)}, u32[]{:S(2)}) collective-permute-start(bf16[4,128,256]{2,1,0:T(8,128)(2,1)S(1)} %pad_maximum_fusion.1.rest_0_), channel_id=1, source_target_pairs={{0,4},{4,0},{8,12},{12,8},{16,20},{20,16},{24,28},{28,24},{1,5},{5... | collective-permute-start | bytes 786440 | tf_op jit(solution)/shard_map/ppermute | solution.py:666
  103.8 4.2 %collective-permute-start.9 = (bf16[2,4096,128]{2,1,0:T(8,128)(2,1)S(1)}, bf16[2,4096,128]{2,1,0:T(8,128)(2,1)S(1)}, u32[]{:S(2)}, u32[]{:S(2)}) collective-permute-start(bf16[2,4096,128]{2,1,0:T(8,128)(2,1)S(1)} %get-tuple-element.45), channel_id=1, source_target_pairs={{0,4},{4,0},{8,12},{12,8},{16,20},{20,16},{24,28},{28,24},{1,5},{5... | collective-permute-start | bytes 6291464 | tf_op jit(solution)/shard_map/ppermute | solution.py:666
  108.2 14.3 %collective-permute-start.10 = (bf16[1,2,1024,128]{3,2,1,0:T(8,128)(2,1)S(1)}, bf16[1,2,1024,128]{3,2,1,0:T(8,128)(2,1)S(1)}, u32[]{:S(2)}, u32[]{:S(2)}) collective-permute-start(bf16[1,2,1024,128]{3,2,1,0:T(8,128)(2,1)S(1)} %bitcast.65), channel_id=1, source_target_pairs={{0,8},{4,12},{8,0},{12,4},{16,24},{20,28},{24,16},{28,20},{1,9},{5... | collective-permute-start | bytes 1572872 | tf_op jit(solution)/shard_map/ppermute | solution.py:666
  110.0 14.1 %collective-permute-start.12 = (bf16[2,1,1024,128]{3,2,1,0:T(8,128)(2,1)S(1)}, bf16[2,1,1024,128]{3,2,1,0:T(8,128)(2,1)S(1)}, u32[]{:S(2)}, u32[]{:S(2)}) collective-permute-start(bf16[2,1,1024,128]{3,2,1,0:T(8,128)(2,1)S(1)} %add_convert_fusion), channel_id=1, source_target_pairs={{0,16},{4,20},{8,24},{12,28},{16,0},{20,4},{24,8},{28,12},{1,17},{... | collective-permute-start | bytes 1572872 | tf_op jit(solution)/shard_map/ppermute | solution.py:666
  122.6 7.8 %collective-permute-start.11 = (bf16[1,1,1024,128]{3,2,1,0:T(8,128)(2,1)S(1)}, bf16[1,1,1024,128]{3,2,1,0:T(8,128)(2,1)S(1)}, u32[]{:S(2)}, u32[]{:S(2)}) collective-permute-start(bf16[1,1,1024,128]{3,2,1,0:T(8,128)(2,1)S(1)} %add_convert_fusion.4), channel_id=1, source_target_pairs={{0,16},{4,20},{8,24},{12,28},{16,0},{20,4},{24,8},{28,12},{1,17},{... | collective-permute-start | bytes 786440 | tf_op jit(solution)/shard_map/ppermute | solution.py:666
  124.2 7.5 %collective-permute-start.13 = (bf16[1,1,1024,128]{3,2,1,0:T(8,128)(2,1)S(1)}, bf16[1,1,1024,128]{3,2,1,0:T(8,128)(2,1)S(1)}, u32[]{:S(2)}, u32[]{:S(2)}) collective-permute-start(bf16[1,1,1024,128]{3,2,1,0:T(8,128)(2,1)S(1)} %add_convert_fusion.3), channel_id=1, source_target_pairs={{0,8},{4,12},{8,0},{12,4},{16,24},{20,28},{24,16},{28,20},{1,9},{5... | collective-permute-start | bytes 786440 | tf_op jit(solution)/shard_map/ppermute | solution.py:666
  131.9 6.6 %collective-permute-start.14 = (bf16[2,512,128]{2,1,0:T(8,128)(2,1)S(1)}, bf16[2,512,128]{2,1,0:T(8,128)(2,1)S(1)}, u32[]{:S(2)}, u32[]{:S(2)}) collective-permute-start(bf16[2,512,128]{2,1,0:T(8,128)(2,1)S(1)} %add_convert_fusion.2), channel_id=1, source_target_pairs={{0,1},{1,0},{2,3},{3,2},{4,5},{5,4},{6,7},{7,6},{8,9},{9,8},{10,11... | collective-permute-start | bytes 786440 | tf_op jit(solution)/shard_map/ppermute | solution.py:666
  138.6 7.3 %collective-permute-start.15 = (bf16[2,256,128]{2,1,0:T(8,128)(2,1)S(1)}, bf16[2,256,128]{2,1,0:T(8,128)(2,1)S(1)}, u32[]{:S(2)}, u32[]{:S(2)}) collective-permute-start(bf16[2,256,128]{2,1,0:T(8,128)(2,1)S(1)} %add_convert_fusion.5), channel_id=1, source_target_pairs={{0,2},{1,3},{2,0},{3,1},{4,6},{5,7},{6,4},{7,5},{8,10},{9,11},{10,... | collective-permute-start | bytes 393224 | tf_op jit(solution)/shard_map/ppermute | solution.py:666
  146.8 6.0 %collective-permute-start.16 = (bf16[256,256]{1,0:T(8,128)(2,1)S(1)}, bf16[256,256]{1,0:T(8,128)(2,1)S(1)}, u32[]{:S(2)}, u32[]{:S(2)}) collective-permute-start(bf16[256,256]{1,0:T(8,128)(2,1)S(1)} %get-tuple-element.46), channel_id=1, source_target_pairs={{0,24},{4,28},{8,16},{12,20},{16,8},{20,12},{24,0},{28,4},{1,25},{... | collective-permute-start | bytes 393224 | tf_op jit(solution)/shard_map/ppermute | solution.py:666
  148.3 5.8 %collective-permute-start.17 = (bf16[256,256]{1,0:T(8,128)(2,1)S(1)}, bf16[256,256]{1,0:T(8,128)(2,1)S(1)}, u32[]{:S(2)}, u32[]{:S(2)}) collective-permute-start(bf16[256,256]{1,0:T(8,128)(2,1)S(1)} %get-tuple-element.46), channel_id=1, source_target_pairs={{0,16},{4,20},{8,24},{12,28},{16,0},{20,4},{24,8},{28,12},{1,17},{... | collective-permute-start | bytes 393224 | tf_op jit(solution)/shard_map/ppermute | solution.py:666
  149.7 5.0 %collective-permute-start.18 = (bf16[256,256]{1,0:T(8,128)(2,1)S(1)}, bf16[256,256]{1,0:T(8,128)(2,1)S(1)}, u32[]{:S(2)}, u32[]{:S(2)}) collective-permute-start(bf16[256,256]{1,0:T(8,128)(2,1)S(1)} %get-tuple-element.46), channel_id=1, source_target_pairs={{0,8},{4,12},{8,0},{12,4},{16,24},{20,28},{24,16},{28,20},{1,9},{5... | collective-permute-start | bytes 393224 | tf_op jit(solution)/shard_map/ppermute | solution.py:666
  154.9 2.0 %collective-permute-start.19 = (bf16[4,256,256]{2,1,0:T(8,128)(2,1)S(1)}, bf16[4,256,256]{2,1,0:T(8,128)(2,1)S(1)}, u32[]{:S(2)}, u32[]{:S(2)}) collective-permute-start(bf16[4,256,256]{2,1,0:T(8,128)(2,1)S(1)} %get-tuple-element.49), channel_id=1, source_target_pairs={{0,4},{4,0},{8,12},{12,8},{16,20},{20,16},{24,28},{28,24},{1,5},{5... | collective-permute-start | bytes 1572872 | tf_op jit(solution)/shard_map/ppermute | solution.py:666
  (4 other events, 38.6 us)

commit v14 on v13

--- a/solution.py
+++ b/solution.py
@@ -76,27 +76,27 @@
                 at = pl.ds(pl.multiple_of(base + first * 16, 16), 16)
                 goal_ref[g // per, at, lanes] = part.astype(BF16)
 
-    def turn(src_ref, first, base, goal_ref):
+    def turn(src_ref, first, base, goal_ref, scaled):
         turned = jnp.swapaxes(src_ref[pl.ds(first * 16, 16)], 0, 1)
         at = pl.ds(pl.multiple_of(base + first * 16, 16), 16)
         for g in range(gb):
-            goal_ref[g // per, at, g % per * width : (g % per + 1) * width] = turned[g]
+            part = turned[g]
+            if scaled:
+                part = (part.astype(F32) * noise_ref[step * gb + g]).astype(BF16)
+            goal_ref[g // per, at, g % per * width : (g % per + 1) * width] = part
 
     def tiles(i, flat_ref, w_ref):
         jobs, turns = [], []
         for s in range(STREAMS):
             rows = orients // STREAMS
             for t in range(rows // 16 // rounds):
-                jobs.append((r_refs[s], i * (rows // 16 // rounds) + t, s * rows, w_ref, True))
+                job = (r_refs[s], i * (rows // 16 // rounds) + t, s * rows, w_ref, True)
+                (turns if t % 2 else jobs).append(job)
             rows = particles // STREAMS
             for t in range(rows // 16 // rounds):
-                job = (x_refs[s], i * (rows // 16 // rounds) + t, s * rows, flat_ref)
-                if (s * (rows // 16 // rounds) + t) % 2:
-                    turns.append(job)
-                else:
-                    jobs.append(job + (False,))
-        for at in range(0, len(jobs), 6):
-            regroup(jobs[at : at + 6])
+                job = (x_refs[s], i * (rows // 16 // rounds) + t, s * rows, flat_ref, False)
+                turns.append(job)
+        regroup(jobs)
         for job in turns:
             turn(*job)
 

time: 157 us -> 157 us (level)
  no operation moved by 1% of the time
where the time goes in v14:
time: 157 us
  Pallas kernels  84.6 us (54%)
  waiting for transfers between devices  42.5 us (27%)
  starting transfers between devices  24.7 us (16%)
  local copies, waits for them, and re-layouts  2.28 us (1%)
  other arithmetic  1.95 us (1%)
    ppermute x20, waiting for transfers between devices, flip(): return lax.ppermute(value, axis, [(i, i ^ bit) for i in range(size)])  42.5 us
    pallas_call x1, Pallas kernels, insert_call(): pl.pallas_call(insert_kernel, grid=(steps,), out_shape=[jax.ShapeDtypeStr...  40.5 us
    pallas_call x1, Pallas kernels, score_call(): pl.pallas_call(score_kernel, grid=(steps + 1,), out_shape=[jax.ShapeDtype...  33.2 us
    ppermute x20, starting transfers between devices, flip(): return lax.ppermute(value, axis, [(i, i ^ bit) for i in range(size)])  24.7 us
    pallas_call x1, Pallas kernels, plan_call(): pl.pallas_call(functools.partial(plan_kernel, sizes=mesh_sizes, per=group...  6.62 us
    pallas_call x1, Pallas kernels, meta_call(): pl.pallas_call(functools.partial(meta_kernel, per=group_block(groups) //...  4.08 us
  transfers between devices with their start and end apart: 20, of which 13 were waited for; matrix products, arithmetic and copies ran while one was open for 0% of the time, Pallas kernels for 7%

profile of v14, /device:TPU:0, one launch (start us, length us, event | category | flops | bytes accessed | tf_op | source)
XLA Modules:
  0.0 157.0 jit_solution(6394660457440266955)
XLA Ops:
  0.6 33.2 %shard_map.86 = (bf16[512,10240]{1,0:T(8,128)(2,1)}, bf16[512,10240]{1,0:T(8,128)(2,1)}, f32[128,256]{1,0:T(8,128)}, f32[128,256]{1,0:T(8,128)}, f32[128,256]{1,0:T(8,128)}, /*index=5*/f32[128,256]{1,0:T(8,128)}) custom-call(s32[1]{0:T(128)} %bitcast.here_ref, f32[80]{0:T(128)} %noise_ref.1, s32[2,512]{1,0:T(2,128)} %bitcast.45, ...), custom_call_target="tpu_custom_call" | custom-call | flops 21474836480 | bytes 62914560 | tf_op jit(solution)/shard_map/pallas_call | solution.py:183
  34.5 2.7 %collective-permute-start.1 = (f32[128,256]{1,0:T(8,128)}, f32[128,256]{1,0:T(8,128)S(1)}, u32[]{:S(2)}, u32[]{:S(2)}) collective-permute-start(f32[128,256]{1,0:T(8,128)} %get-tuple-element.36), channel_id=1, source_target_pairs={{0,1},{1,0},{2,3},{3,2},{4,5},{5,4},{6,7},{7,6},{8,9},{9,8},{10,11... | collective-permute-start | bytes 393224 | tf_op jit(solution)/shard_map/ppermute | solution.py:666
  37.1 2.5 %collective-permute-start.2 = (f32[128,256]{1,0:T(8,128)}, f32[128,256]{1,0:T(8,128)S(1)}, u32[]{:S(2)}, u32[]{:S(2)}) collective-permute-start(f32[128,256]{1,0:T(8,128)} %get-tuple-element.37), channel_id=1, source_target_pairs={{0,2},{1,3},{2,0},{3,1},{4,6},{5,7},{6,4},{7,5},{8,10},{9,11},{10,... | collective-permute-start | bytes 393224 | tf_op jit(solution)/shard_map/ppermute | solution.py:666
  39.7 6.6 %shard_map.87 = (s32[4,20,256]{2,1,0:T(8,128)}, s32[4,20,128]{2,1,0:T(8,128)}, s32[4,5,128]{2,1,0:T(8,128)}) custom-call(s32[1]{0:T(128)} %bitcast.here_ref, s32[320,512]{1,0:T(8,128)} %dest_ref.1), custom_call_target="tpu_custom_call" | custom-call | flops 1342177280 | bytes 327680 | tf_op jit(solution)/shard_map/pallas_call | solution.py:387
  46.3 3.9 %collective-permute-done.2.refs_2_ = f32[128,256]{1,0:T(8,128)S(1)} collective-permute-done((f32[128,256]{1,0:T(8,128)}, f32[128,256]{1,0:T(8,128)S(1)}, u32[]{:S(2)}, u32[]{:S(2)}) %collective-permute-start.2) | collective-permute-done | bytes 131104 | tf_op jit(solution)/shard_map/ppermute | solution.py:666
  50.5 4.7 %collective-permute-start.5 = (bf16[128,256]{1,0:T(8,128)(2,1)S(1)}, bf16[128,256]{1,0:T(8,128)(2,1)S(1)}, u32[]{:S(2)}, u32[]{:S(2)}) collective-permute-start(bf16[128,256]{1,0:T(8,128)(2,1)S(1)} %shard_map.88), channel_id=1, source_target_pairs={{0,3},{1,2},{2,1},{3,0},{4,7},{5,6},{6,5},{7,4},{8,11},{9,10},{10,... | collective-permute-start | bytes 196616 | tf_op jit(solution)/shard_map/ppermute | solution.py:666
  56.7 4.1 %shard_map.89.meta_ref = f32[4,20,72,128]{3,2,1,0:T(8,128)S(1)} custom-call(s32[1]{0:T(128)} %bitcast.here_ref, s32[320,512]{1,0:T(8,128)S(1)} %copy-done.2, f32[320,512]{1,0:T(8,128)S(1)} %copy-done.3, s32[4,20,256]{2,1,0:T(8,128)S(1)} %copy-done.4), custom_call_target="tpu_custom_call" | custom-call | flops 1509949440 | bytes 5898240 | tf_op jit(solution)/shard_map/pallas_call | solution.py:421
  61.3 1.5 collective-permute-done.8.rest_1_
  62.8 40.5 %shard_map.90 = (bf16[2,4096,128]{2,1,0:T(8,128)(2,1)S(1)}, bf16[2,4096,128]{2,1,0:T(8,128)(2,1)S(1)}) custom-call(s32[4,20,128]{2,1,0:T(8,128)S(1)} %copy-done.6, s32[4,5,128]{2,1,0:T(8,128)S(1)} %copy-done.7, bf16[512,10240]{1,0:T(8,128)(2,1)} %get-tuple-element.32.x_ref, bf16[512,10240]{1,0:T(8,128)(2,1)} %collective-permute-done.y_ref, ...), custom_call_target="tpu_custom_call" | custom-call | flops 21474836480 | bytes 10485760 | tf_op jit(solution)/shard_map/pallas_call | solution.py:629
  103.6 3.9 %collective-permute-done.9 = bf16[2,4096,128]{2,1,0:T(8,128)(2,1)S(1)} collective-permute-done((bf16[2,4096,128]{2,1,0:T(8,128)(2,1)S(1)}, bf16[2,4096,128]{2,1,0:T(8,128)(2,1)S(1)}, u32[]{:S(2)}, u32[]{:S(2)}) %collective-permute-start.9) | collective-permute-done | bytes 2097184 | tf_op jit(solution)/shard_map/ppermute | solution.py:666
  107.7 1.5 collective-permute-start.10
  109.5 1.5 collective-permute-start.12
  111.1 10.6 %collective-permute-done.10 = bf16[1,2,1024,128]{3,2,1,0:T(8,128)(2,1)S(1)} collective-permute-done((bf16[1,2,1024,128]{3,2,1,0:T(8,128)(2,1)S(1)}, bf16[1,2,1024,128]{3,2,1,0:T(8,128)(2,1)S(1)}, u32[]{:S(2)}, u32[]{:S(2)}) %collective-permute-start.10) | collective-permute-done | bytes 524320 | tf_op jit(solution)/shard_map/ppermute | solution.py:666
  121.8 1.6 %collective-permute-start.11 = (bf16[1,1,1024,128]{3,2,1,0:T(8,128)(2,1)S(1)}, bf16[1,1,1024,128]{3,2,1,0:T(8,128)(2,1)S(1)}, u32[]{:S(2)}, u32[]{:S(2)}) collective-permute-start(bf16[1,1,1024,128]{3,2,1,0:T(8,128)(2,1)S(1)} %add_convert_fusion.4), channel_id=1, source_target_pairs={{0,16},{4,20},{8,24},{12,28},{16,0},{20,4},{24,8},{28,12},{1,17},{... | collective-permute-start | bytes 786440 | tf_op jit(solution)/shard_map/ppermute | solution.py:666
  123.6 1.5 collective-permute-start.13
  125.1 4.3 %collective-permute-done.11 = bf16[1,1,1024,128]{3,2,1,0:T(8,128)(2,1)S(1)} collective-permute-done((bf16[1,1,1024,128]{3,2,1,0:T(8,128)(2,1)S(1)}, bf16[1,1,1024,128]{3,2,1,0:T(8,128)(2,1)S(1)}, u32[]{:S(2)}, u32[]{:S(2)}) %collective-permute-start.11) | collective-permute-done | bytes 262176 | tf_op jit(solution)/shard_map/ppermute | solution.py:666
  129.4 1.5 collective-permute-done.13
  132.2 5.2 %collective-permute-done.14 = bf16[2,512,128]{2,1,0:T(8,128)(2,1)S(1)} collective-permute-done((bf16[2,512,128]{2,1,0:T(8,128)(2,1)S(1)}, bf16[2,512,128]{2,1,0:T(8,128)(2,1)S(1)}, u32[]{:S(2)}, u32[]{:S(2)}) %collective-permute-start.14) | collective-permute-done | bytes 262176 | tf_op jit(solution)/shard_map/ppermute | solution.py:666
  137.6 2.5 %collective-permute-start.15 = (bf16[2,256,128]{2,1,0:T(8,128)(2,1)S(1)}, bf16[2,256,128]{2,1,0:T(8,128)(2,1)S(1)}, u32[]{:S(2)}, u32[]{:S(2)}) collective-permute-start(bf16[2,256,128]{2,1,0:T(8,128)(2,1)S(1)} %add_convert_fusion.5), channel_id=1, source_target_pairs={{0,2},{1,3},{2,0},{3,1},{4,6},{5,7},{6,4},{7,5},{8,10},{9,11},{10,... | collective-permute-start | bytes 393224 | tf_op jit(solution)/shard_map/ppermute | solution.py:666
  140.1 4.8 %collective-permute-done.15 = bf16[2,256,128]{2,1,0:T(8,128)(2,1)S(1)} collective-permute-done((bf16[2,256,128]{2,1,0:T(8,128)(2,1)S(1)}, bf16[2,256,128]{2,1,0:T(8,128)(2,1)S(1)}, u32[]{:S(2)}, u32[]{:S(2)}) %collective-permute-start.15) | collective-permute-done | bytes 131104 | tf_op jit(solution)/shard_map/ppermute | solution.py:666
  145.7 1.4 collective-permute-start.16
  147.1 1.5 collective-permute-start.17
  149.2 2.5 %collective-permute-done.16 = bf16[256,256]{1,0:T(8,128)(2,1)S(1)} collective-permute-done((bf16[256,256]{1,0:T(8,128)(2,1)S(1)}, bf16[256,256]{1,0:T(8,128)(2,1)S(1)}, u32[]{:S(2)}, u32[]{:S(2)}) %collective-permute-start.16) | collective-permute-done | bytes 131104 | tf_op jit(solution)/shard_map/ppermute | solution.py:666
  153.9 1.9 %collective-permute-done.19 = bf16[4,256,256]{2,1,0:T(8,128)(2,1)S(1)} collective-permute-done((bf16[4,256,256]{2,1,0:T(8,128)(2,1)S(1)}, bf16[4,256,256]{2,1,0:T(8,128)(2,1)S(1)}, u32[]{:S(2)}, u32[]{:S(2)}) %collective-permute-start.19) | collective-permute-done | bytes 524320 | tf_op jit(solution)/shard_map/ppermute | solution.py:666
  (59 shorter events, 9.9 us)
Async XLA Ops:
  0.6 39.0 %copy-start.1 = (s32[512,2]{0,1:T(2,128)S(1)}, s32[512,2]{0,1:T(2,128)}, u32[]{:S(2)}) copy-start(s32[512,2]{0,1:T(2,128)} %param.8) | copy-start | bytes 12292
  33.9 16.4 %copy-start = (f32[128,256]{1,0:T(8,128)S(1)}, f32[128,256]{1,0:T(8,128)}, u32[]{:S(2)}) copy-start(f32[128,256]{1,0:T(8,128)} %get-tuple-element.35.refs_0_) | copy-start | bytes 393220
  33.9 21.9 %copy-start.2 = (s32[320,512]{1,0:T(8,128)S(1)}, s32[320,512]{1,0:T(8,128)}, u32[]{:S(2)}) copy-start(s32[320,512]{1,0:T(8,128)} %index_ref.1) | copy-start | bytes 1966084
  33.9 21.9 %copy-start.3 = (f32[320,512]{1,0:T(8,128)S(1)}, f32[320,512]{1,0:T(8,128)}, u32[]{:S(2)}) copy-start(f32[320,512]{1,0:T(8,128)} %frac_ref.1) | copy-start | bytes 1966084
  33.9 28.9 %collective-permute-start = (bf16[512,10240]{1,0:T(8,128)(2,1)}, bf16[512,10240]{1,0:T(8,128)(2,1)}, u32[]{:S(2)}, u32[]{:S(2)}) collective-permute-start(bf16[512,10240]{1,0:T(8,128)(2,1)} %get-tuple-element.33), channel_id=1, source_target_pairs={{0,4},{4,0},{8,12},{12,8},{16,20},{20,16},{24,28},{28,24},{1,5},{5... | collective-permute-start | bytes 31457288 | tf_op jit(solution)/shard_map/ppermute | solution.py:666
  34.5 11.9 %collective-permute-start.1 = (f32[128,256]{1,0:T(8,128)}, f32[128,256]{1,0:T(8,128)S(1)}, u32[]{:S(2)}, u32[]{:S(2)}) collective-permute-start(f32[128,256]{1,0:T(8,128)} %get-tuple-element.36), channel_id=1, source_target_pairs={{0,1},{1,0},{2,3},{3,2},{4,5},{5,4},{6,7},{7,6},{8,9},{9,8},{10,11... | collective-permute-start | bytes 393224 | tf_op jit(solution)/shard_map/ppermute | solution.py:666
  37.1 13.1 %collective-permute-start.2 = (f32[128,256]{1,0:T(8,128)}, f32[128,256]{1,0:T(8,128)S(1)}, u32[]{:S(2)}, u32[]{:S(2)}) collective-permute-start(f32[128,256]{1,0:T(8,128)} %get-tuple-element.37), channel_id=1, source_target_pairs={{0,2},{1,3},{2,0},{3,1},{4,6},{5,7},{6,4},{7,5},{8,10},{9,11},{10,... | collective-permute-start | bytes 393224 | tf_op jit(solution)/shard_map/ppermute | solution.py:666
  39.7 10.6 %collective-permute-start.3 = (f32[128,256]{1,0:T(8,128)}, f32[128,256]{1,0:T(8,128)S(1)}, u32[]{:S(2)}, u32[]{:S(2)}) collective-permute-start(f32[128,256]{1,0:T(8,128)} %get-tuple-element.38), channel_id=1, source_target_pairs={{0,3},{1,2},{2,1},{3,0},{4,7},{5,6},{6,5},{7,4},{8,11},{9,10},{10,... | collective-permute-start | bytes 393224 | tf_op jit(solution)/shard_map/ppermute | solution.py:666
  39.7 10.8 %collective-permute-start.4 = (s32[2,512]{1,0:T(2,128)S(1)}, s32[2,512]{1,0:T(2,128)S(1)}, u32[]{:S(2)}, u32[]{:S(2)}) collective-permute-start(s32[2,512]{1,0:T(2,128)S(1)} %bitcast.46), channel_id=1, source_target_pairs={{0,4},{4,0},{8,12},{12,8},{16,20},{20,16},{24,28},{28,24},{1,5},{5... | collective-permute-start | bytes 12296 | tf_op jit(solution)/shard_map/ppermute | solution.py:666
  50.5 10.3 %collective-permute-start.5 = (bf16[128,256]{1,0:T(8,128)(2,1)S(1)}, bf16[128,256]{1,0:T(8,128)(2,1)S(1)}, u32[]{:S(2)}, u32[]{:S(2)}) collective-permute-start(bf16[128,256]{1,0:T(8,128)(2,1)S(1)} %shard_map.88), channel_id=1, source_target_pairs={{0,3},{1,2},{2,1},{3,0},{4,7},{5,6},{6,5},{7,4},{8,11},{9,10},{10,... | collective-permute-start | bytes 196616 | tf_op jit(solution)/shard_map/ppermute | solution.py:666
  55.2 5.9 %collective-permute-start.6 = (bf16[128,256]{1,0:T(8,128)(2,1)S(1)}, bf16[128,256]{1,0:T(8,128)(2,1)S(1)}, u32[]{:S(2)}, u32[]{:S(2)}) collective-permute-start(bf16[128,256]{1,0:T(8,128)(2,1)S(1)} %shard_map.88), channel_id=1, source_target_pairs={{0,2},{1,3},{2,0},{3,1},{4,6},{5,7},{6,4},{7,5},{8,10},{9,11},{10,... | collective-permute-start | bytes 196616 | tf_op jit(solution)/shard_map/ppermute | solution.py:666
  55.2 5.9 %collective-permute-start.7 = (bf16[128,256]{1,0:T(8,128)(2,1)S(1)}, bf16[128,256]{1,0:T(8,128)(2,1)S(1)}, u32[]{:S(2)}, u32[]{:S(2)}) collective-permute-start(bf16[128,256]{1,0:T(8,128)(2,1)S(1)} %shard_map.88), channel_id=1, source_target_pairs={{0,1},{1,0},{2,3},{3,2},{4,5},{5,4},{6,7},{7,6},{8,9},{9,8},{10,11... | collective-permute-start | bytes 196616 | tf_op jit(solution)/shard_map/ppermute | solution.py:666
  61.2 1.6 %collective-permute-start.8 = (bf16[4,128,256]{2,1,0:T(8,128)(2,1)S(1)}, bf16[4,128,256]{2,1,0:T(8,128)(2,1)S(1)}, u32[]{:S(2)}, u32[]{:S(2)}) collective-permute-start(bf16[4,128,256]{2,1,0:T(8,128)(2,1)S(1)} %pad_maximum_fusion.1.rest_0_), channel_id=1, source_target_pairs={{0,4},{4,0},{8,12},{12,8},{16,20},{20,16},{24,28},{28,24},{1,5},{5... | collective-permute-start | bytes 786440 | tf_op jit(solution)/shard_map/ppermute | solution.py:666
  103.3 4.2 %collective-permute-start.9 = (bf16[2,4096,128]{2,1,0:T(8,128)(2,1)S(1)}, bf16[2,4096,128]{2,1,0:T(8,128)(2,1)S(1)}, u32[]{:S(2)}, u32[]{:S(2)}) collective-permute-start(bf16[2,4096,128]{2,1,0:T(8,128)(2,1)S(1)} %get-tuple-element.45), channel_id=1, source_target_pairs={{0,4},{4,0},{8,12},{12,8},{16,20},{20,16},{24,28},{28,24},{1,5},{5... | collective-permute-start | bytes 6291464 | tf_op jit(solution)/shard_map/ppermute | solution.py:666
  107.7 14.0 %collective-permute-start.10 = (bf16[1,2,1024,128]{3,2,1,0:T(8,128)(2,1)S(1)}, bf16[1,2,1024,128]{3,2,1,0:T(8,128)(2,1)S(1)}, u32[]{:S(2)}, u32[]{:S(2)}) collective-permute-start(bf16[1,2,1024,128]{3,2,1,0:T(8,128)(2,1)S(1)} %bitcast.65), channel_id=1, source_target_pairs={{0,8},{4,12},{8,0},{12,4},{16,24},{20,28},{24,16},{28,20},{1,9},{5... | collective-permute-start | bytes 1572872 | tf_op jit(solution)/shard_map/ppermute | solution.py:666
  109.5 14.0 %collective-permute-start.12 = (bf16[2,1,1024,128]{3,2,1,0:T(8,128)(2,1)S(1)}, bf16[2,1,1024,128]{3,2,1,0:T(8,128)(2,1)S(1)}, u32[]{:S(2)}, u32[]{:S(2)}) collective-permute-start(bf16[2,1,1024,128]{3,2,1,0:T(8,128)(2,1)S(1)} %add_convert_fusion), channel_id=1, source_target_pairs={{0,16},{4,20},{8,24},{12,28},{16,0},{20,4},{24,8},{28,12},{1,17},{... | collective-permute-start | bytes 1572872 | tf_op jit(solution)/shard_map/ppermute | solution.py:666
  121.8 7.6 %collective-permute-start.11 = (bf16[1,1,1024,128]{3,2,1,0:T(8,128)(2,1)S(1)}, bf16[1,1,1024,128]{3,2,1,0:T(8,128)(2,1)S(1)}, u32[]{:S(2)}, u32[]{:S(2)}) collective-permute-start(bf16[1,1,1024,128]{3,2,1,0:T(8,128)(2,1)S(1)} %add_convert_fusion.4), channel_id=1, source_target_pairs={{0,16},{4,20},{8,24},{12,28},{16,0},{20,4},{24,8},{28,12},{1,17},{... | collective-permute-start | bytes 786440 | tf_op jit(solution)/shard_map/ppermute | solution.py:666
  123.6 7.3 %collective-permute-start.13 = (bf16[1,1,1024,128]{3,2,1,0:T(8,128)(2,1)S(1)}, bf16[1,1,1024,128]{3,2,1,0:T(8,128)(2,1)S(1)}, u32[]{:S(2)}, u32[]{:S(2)}) collective-permute-start(bf16[1,1,1024,128]{3,2,1,0:T(8,128)(2,1)S(1)} %add_convert_fusion.3), channel_id=1, source_target_pairs={{0,8},{4,12},{8,0},{12,4},{16,24},{20,28},{24,16},{28,20},{1,9},{5... | collective-permute-start | bytes 786440 | tf_op jit(solution)/shard_map/ppermute | solution.py:666
  131.0 6.4 %collective-permute-start.14 = (bf16[2,512,128]{2,1,0:T(8,128)(2,1)S(1)}, bf16[2,512,128]{2,1,0:T(8,128)(2,1)S(1)}, u32[]{:S(2)}, u32[]{:S(2)}) collective-permute-start(bf16[2,512,128]{2,1,0:T(8,128)(2,1)S(1)} %add_convert_fusion.2), channel_id=1, source_target_pairs={{0,1},{1,0},{2,3},{3,2},{4,5},{5,4},{6,7},{7,6},{8,9},{9,8},{10,11... | collective-permute-start | bytes 786440 | tf_op jit(solution)/shard_map/ppermute | solution.py:666
  137.6 7.3 %collective-permute-start.15 = (bf16[2,256,128]{2,1,0:T(8,128)(2,1)S(1)}, bf16[2,256,128]{2,1,0:T(8,128)(2,1)S(1)}, u32[]{:S(2)}, u32[]{:S(2)}) collective-permute-start(bf16[2,256,128]{2,1,0:T(8,128)(2,1)S(1)} %add_convert_fusion.5), channel_id=1, source_target_pairs={{0,2},{1,3},{2,0},{3,1},{4,6},{5,7},{6,4},{7,5},{8,10},{9,11},{10,... | collective-permute-start | bytes 393224 | tf_op jit(solution)/shard_map/ppermute | solution.py:666
  145.7 6.0 %collective-permute-start.16 = (bf16[256,256]{1,0:T(8,128)(2,1)S(1)}, bf16[256,256]{1,0:T(8,128)(2,1)S(1)}, u32[]{:S(2)}, u32[]{:S(2)}) collective-permute-start(bf16[256,256]{1,0:T(8,128)(2,1)S(1)} %get-tuple-element.46), channel_id=1, source_target_pairs={{0,24},{4,28},{8,16},{12,20},{16,8},{20,12},{24,0},{28,4},{1,25},{... | collective-permute-start | bytes 393224 | tf_op jit(solution)/shard_map/ppermute | solution.py:666
  147.1 5.9 %collective-permute-start.17 = (bf16[256,256]{1,0:T(8,128)(2,1)S(1)}, bf16[256,256]{1,0:T(8,128)(2,1)S(1)}, u32[]{:S(2)}, u32[]{:S(2)}) collective-permute-start(bf16[256,256]{1,0:T(8,128)(2,1)S(1)} %get-tuple-element.46), channel_id=1, source_target_pairs={{0,16},{4,20},{8,24},{12,28},{16,0},{20,4},{24,8},{28,12},{1,17},{... | collective-permute-start | bytes 393224 | tf_op jit(solution)/shard_map/ppermute | solution.py:666
  148.6 5.0 %collective-permute-start.18 = (bf16[256,256]{1,0:T(8,128)(2,1)S(1)}, bf16[256,256]{1,0:T(8,128)(2,1)S(1)}, u32[]{:S(2)}, u32[]{:S(2)}) collective-permute-start(bf16[256,256]{1,0:T(8,128)(2,1)S(1)} %get-tuple-element.46), channel_id=1, source_target_pairs={{0,8},{4,12},{8,0},{12,4},{16,24},{20,28},{24,16},{28,20},{1,9},{5... | collective-permute-start | bytes 393224 | tf_op jit(solution)/shard_map/ppermute | solution.py:666
  153.8 2.0 %collective-permute-start.19 = (bf16[4,256,256]{2,1,0:T(8,128)(2,1)S(1)}, bf16[4,256,256]{2,1,0:T(8,128)(2,1)S(1)}, u32[]{:S(2)}, u32[]{:S(2)}) collective-permute-start(bf16[4,256,256]{2,1,0:T(8,128)(2,1)S(1)} %get-tuple-element.49), channel_id=1, source_target_pairs={{0,4},{4,0},{8,12},{12,8},{16,20},{20,16},{24,28},{28,24},{1,5},{5... | collective-permute-start | bytes 1572872 | tf_op jit(solution)/shard_map/ppermute | solution.py:666
  (4 other events, 38.5 us)

commit v15 on v13

--- a/solution.py
+++ b/solution.py
@@ -69,10 +69,9 @@
         moved = jnp.dot(perm_ref[...], jnp.concatenate(wide, axis=1), preferred_element_type=F32)
         for g in range(gb):
             lanes = slice(g % per * width, (g % per + 1) * width)
-            for t, (_, first, base, goal_ref, scaled) in enumerate(jobs):
+            for t, (_, first, base, goal_ref) in enumerate(jobs):
                 part = moved[g * 16 : (g + 1) * 16, t * width : (t + 1) * width]
-                if scaled:
-                    part = part * noise_ref[step * gb + g]
+                part = part * noise_ref[step * gb + g]
                 at = pl.ds(pl.multiple_of(base + first * 16, 16), 16)
                 goal_ref[g // per, at, lanes] = part.astype(BF16)
 
@@ -87,16 +86,12 @@
         for s in range(STREAMS):
             rows = orients // STREAMS
             for t in range(rows // 16 // rounds):
-                jobs.append((r_refs[s], i * (rows // 16 // rounds) + t, s * rows, w_ref, True))
+                jobs.append((r_refs[s], i * (rows // 16 // rounds) + t, s * rows, w_ref))
             rows = particles // STREAMS
             for t in range(rows // 16 // rounds):
-                job = (x_refs[s], i * (rows // 16 // rounds) + t, s * rows, flat_ref)
-                if (s * (rows // 16 // rounds) + t) % 2:
-                    turns.append(job)
-                else:
-                    jobs.append(job + (False,))
-        for at in range(0, len(jobs), 6):
-            regroup(jobs[at : at + 6])
+                turns.append((x_refs[s], i * (rows // 16 // rounds) + t, s * rows, flat_ref))
+        for at in range(0, len(jobs), 4):
+            regroup(jobs[at : at + 4])
         for job in turns:
             turn(*job)
 

time: 157 us -> 156 us (level)
  waiting for transfers between devices: 43.8 us -> 42.2 us
    ppermute x20, waiting for transfers between devices: 43.8 us -> 42.2 us  [flip(): return lax.ppermute(value, axis, [(i, i ^ bit) for i in range(size)])]
where the time goes in v15:
time: 156 us
  Pallas kernels  83.7 us (54%)
  waiting for transfers between devices  42.2 us (27%)
  starting transfers between devices  25 us (16%)
  local copies, waits for them, and re-layouts  2.28 us (1%)
  other arithmetic  1.95 us (1%)
    ppermute x20, waiting for transfers between devices, flip(): return lax.ppermute(value, axis, [(i, i ^ bit) for i in range(size)])  42.2 us
    pallas_call x1, Pallas kernels, insert_call(): pl.pallas_call(insert_kernel, grid=(steps,), out_shape=[jax.ShapeDtypeStr...  40.4 us
    pallas_call x1, Pallas kernels, score_call(): pl.pallas_call(score_kernel, grid=(steps + 1,), out_shape=[jax.ShapeDtype...  32.3 us
    ppermute x20, starting transfers between devices, flip(): return lax.ppermute(value, axis, [(i, i ^ bit) for i in range(size)])  25 us
    pallas_call x1, Pallas kernels, plan_call(): pl.pallas_call(functools.partial(plan_kernel, sizes=mesh_sizes, per=group...  6.62 us
    pallas_call x1, Pallas kernels, meta_call(): pl.pallas_call(functools.partial(meta_kernel, per=group_block(groups) //...  4.09 us
  transfers between devices with their start and end apart: 20, of which 13 were waited for; matrix products, arithmetic and copies ran while one was open for 0% of the time, Pallas kernels for 7%

profile of v15, /device:TPU:0, one launch (start us, length us, event | category | flops | bytes accessed | tf_op | source)
XLA Modules:
  0.0 156.0 jit_solution(3844749703224620802)
XLA Ops:
  0.6 32.3 %shard_map.86 = (bf16[512,10240]{1,0:T(8,128)(2,1)}, bf16[512,10240]{1,0:T(8,128)(2,1)}, f32[128,256]{1,0:T(8,128)}, f32[128,256]{1,0:T(8,128)}, f32[128,256]{1,0:T(8,128)}, /*index=5*/f32[128,256]{1,0:T(8,128)}) custom-call(s32[1]{0:T(128)} %bitcast.here_ref, f32[80]{0:T(128)} %noise_ref.1, s32[2,512]{1,0:T(2,128)} %bitcast.45, ...), custom_call_target="tpu_custom_call" | custom-call | flops 21474836480 | bytes 62914560 | tf_op jit(solution)/shard_map/pallas_call | solution.py:178
  33.5 2.7 %collective-permute-start.1 = (f32[128,256]{1,0:T(8,128)}, f32[128,256]{1,0:T(8,128)S(1)}, u32[]{:S(2)}, u32[]{:S(2)}) collective-permute-start(f32[128,256]{1,0:T(8,128)} %get-tuple-element.36), channel_id=1, source_target_pairs={{0,1},{1,0},{2,3},{3,2},{4,5},{5,4},{6,7},{7,6},{8,9},{9,8},{10,11... | collective-permute-start | bytes 393224 | tf_op jit(solution)/shard_map/ppermute | solution.py:661
  36.2 2.6 %collective-permute-start.2 = (f32[128,256]{1,0:T(8,128)}, f32[128,256]{1,0:T(8,128)S(1)}, u32[]{:S(2)}, u32[]{:S(2)}) collective-permute-start(f32[128,256]{1,0:T(8,128)} %get-tuple-element.37), channel_id=1, source_target_pairs={{0,2},{1,3},{2,0},{3,1},{4,6},{5,7},{6,4},{7,5},{8,10},{9,11},{10,... | collective-permute-start | bytes 393224 | tf_op jit(solution)/shard_map/ppermute | solution.py:661
  38.8 6.6 %shard_map.87 = (s32[4,20,256]{2,1,0:T(8,128)}, s32[4,20,128]{2,1,0:T(8,128)}, s32[4,5,128]{2,1,0:T(8,128)}) custom-call(s32[1]{0:T(128)} %bitcast.here_ref, s32[320,512]{1,0:T(8,128)} %dest_ref.1), custom_call_target="tpu_custom_call" | custom-call | flops 1342177280 | bytes 327680 | tf_op jit(solution)/shard_map/pallas_call | solution.py:382
  45.4 3.9 %collective-permute-done.2.refs_2_ = f32[128,256]{1,0:T(8,128)S(1)} collective-permute-done((f32[128,256]{1,0:T(8,128)}, f32[128,256]{1,0:T(8,128)S(1)}, u32[]{:S(2)}, u32[]{:S(2)}) %collective-permute-start.2) | collective-permute-done | bytes 131104 | tf_op jit(solution)/shard_map/ppermute | solution.py:661
  49.5 4.8 %collective-permute-start.5 = (bf16[128,256]{1,0:T(8,128)(2,1)S(1)}, bf16[128,256]{1,0:T(8,128)(2,1)S(1)}, u32[]{:S(2)}, u32[]{:S(2)}) collective-permute-start(bf16[128,256]{1,0:T(8,128)(2,1)S(1)} %shard_map.88), channel_id=1, source_target_pairs={{0,3},{1,2},{2,1},{3,0},{4,7},{5,6},{6,5},{7,4},{8,11},{9,10},{10,... | collective-permute-start | bytes 196616 | tf_op jit(solution)/shard_map/ppermute | solution.py:661
  55.8 4.1 %shard_map.89.meta_ref = f32[4,20,72,128]{3,2,1,0:T(8,128)S(1)} custom-call(s32[1]{0:T(128)} %bitcast.here_ref, s32[320,512]{1,0:T(8,128)S(1)} %copy-done.2, f32[320,512]{1,0:T(8,128)S(1)} %copy-done.3, s32[4,20,256]{2,1,0:T(8,128)S(1)} %copy-done.4), custom_call_target="tpu_custom_call" | custom-call | flops 1509949440 | bytes 5898240 | tf_op jit(solution)/shard_map/pallas_call | solution.py:416
  60.4 1.5 collective-permute-done.8.rest_1_
  61.9 40.4 %shard_map.90 = (bf16[2,4096,128]{2,1,0:T(8,128)(2,1)S(1)}, bf16[2,4096,128]{2,1,0:T(8,128)(2,1)S(1)}) custom-call(s32[4,20,128]{2,1,0:T(8,128)S(1)} %copy-done.6, s32[4,5,128]{2,1,0:T(8,128)S(1)} %copy-done.7, bf16[512,10240]{1,0:T(8,128)(2,1)} %get-tuple-element.32.x_ref, bf16[512,10240]{1,0:T(8,128)(2,1)} %collective-permute-done.y_ref, ...), custom_call_target="tpu_custom_call" | custom-call | flops 21474836480 | bytes 10485760 | tf_op jit(solution)/shard_map/pallas_call | solution.py:624
  102.7 3.8 %collective-permute-done.9 = bf16[2,4096,128]{2,1,0:T(8,128)(2,1)S(1)} collective-permute-done((bf16[2,4096,128]{2,1,0:T(8,128)(2,1)S(1)}, bf16[2,4096,128]{2,1,0:T(8,128)(2,1)S(1)}, u32[]{:S(2)}, u32[]{:S(2)}) %collective-permute-start.9) | collective-permute-done | bytes 2097184 | tf_op jit(solution)/shard_map/ppermute | solution.py:661
  106.7 1.6 %collective-permute-start.10 = (bf16[1,2,1024,128]{3,2,1,0:T(8,128)(2,1)S(1)}, bf16[1,2,1024,128]{3,2,1,0:T(8,128)(2,1)S(1)}, u32[]{:S(2)}, u32[]{:S(2)}) collective-permute-start(bf16[1,2,1024,128]{3,2,1,0:T(8,128)(2,1)S(1)} %bitcast.65), channel_id=1, source_target_pairs={{0,8},{4,12},{8,0},{12,4},{16,24},{20,28},{24,16},{28,20},{1,9},{5... | collective-permute-start | bytes 1572872 | tf_op jit(solution)/shard_map/ppermute | solution.py:661
  108.5 1.6 %collective-permute-start.12 = (bf16[2,1,1024,128]{3,2,1,0:T(8,128)(2,1)S(1)}, bf16[2,1,1024,128]{3,2,1,0:T(8,128)(2,1)S(1)}, u32[]{:S(2)}, u32[]{:S(2)}) collective-permute-start(bf16[2,1,1024,128]{3,2,1,0:T(8,128)(2,1)S(1)} %add_convert_fusion), channel_id=1, source_target_pairs={{0,16},{4,20},{8,24},{12,28},{16,0},{20,4},{24,8},{28,12},{1,17},{... | collective-permute-start | bytes 1572872 | tf_op jit(solution)/shard_map/ppermute | solution.py:661
  110.2 10.6 %collective-permute-done.10 = bf16[1,2,1024,128]{3,2,1,0:T(8,128)(2,1)S(1)} collective-permute-done((bf16[1,2,1024,128]{3,2,1,0:T(8,128)(2,1)S(1)}, bf16[1,2,1024,128]{3,2,1,0:T(8,128)(2,1)S(1)}, u32[]{:S(2)}, u32[]{:S(2)}) %collective-permute-start.10) | collective-permute-done | bytes 524320 | tf_op jit(solution)/shard_map/ppermute | solution.py:661
  120.9 1.6 %collective-permute-start.11 = (bf16[1,1,1024,128]{3,2,1,0:T(8,128)(2,1)S(1)}, bf16[1,1,1024,128]{3,2,1,0:T(8,128)(2,1)S(1)}, u32[]{:S(2)}, u32[]{:S(2)}) collective-permute-start(bf16[1,1,1024,128]{3,2,1,0:T(8,128)(2,1)S(1)} %add_convert_fusion.4), channel_id=1, source_target_pairs={{0,16},{4,20},{8,24},{12,28},{16,0},{20,4},{24,8},{28,12},{1,17},{... | collective-permute-start | bytes 786440 | tf_op jit(solution)/shard_map/ppermute | solution.py:661
  122.6 1.5 collective-permute-start.13
  124.2 4.4 %collective-permute-done.11 = bf16[1,1,1024,128]{3,2,1,0:T(8,128)(2,1)S(1)} collective-permute-done((bf16[1,1,1024,128]{3,2,1,0:T(8,128)(2,1)S(1)}, bf16[1,1,1024,128]{3,2,1,0:T(8,128)(2,1)S(1)}, u32[]{:S(2)}, u32[]{:S(2)}) %collective-permute-start.11) | collective-permute-done | bytes 262176 | tf_op jit(solution)/shard_map/ppermute | solution.py:661
  128.6 1.3 collective-permute-done.13
  131.3 5.2 %collective-permute-done.14 = bf16[2,512,128]{2,1,0:T(8,128)(2,1)S(1)} collective-permute-done((bf16[2,512,128]{2,1,0:T(8,128)(2,1)S(1)}, bf16[2,512,128]{2,1,0:T(8,128)(2,1)S(1)}, u32[]{:S(2)}, u32[]{:S(2)}) %collective-permute-start.14) | collective-permute-done | bytes 262176 | tf_op jit(solution)/shard_map/ppermute | solution.py:661
  136.6 2.5 %collective-permute-start.15 = (bf16[2,256,128]{2,1,0:T(8,128)(2,1)S(1)}, bf16[2,256,128]{2,1,0:T(8,128)(2,1)S(1)}, u32[]{:S(2)}, u32[]{:S(2)}) collective-permute-start(bf16[2,256,128]{2,1,0:T(8,128)(2,1)S(1)} %add_convert_fusion.5), channel_id=1, source_target_pairs={{0,2},{1,3},{2,0},{3,1},{4,6},{5,7},{6,4},{7,5},{8,10},{9,11},{10,... | collective-permute-start | bytes 393224 | tf_op jit(solution)/shard_map/ppermute | solution.py:661
  139.2 4.8 %collective-permute-done.15 = bf16[2,256,128]{2,1,0:T(8,128)(2,1)S(1)} collective-permute-done((bf16[2,256,128]{2,1,0:T(8,128)(2,1)S(1)}, bf16[2,256,128]{2,1,0:T(8,128)(2,1)S(1)}, u32[]{:S(2)}, u32[]{:S(2)}) %collective-permute-start.15) | collective-permute-done | bytes 131104 | tf_op jit(solution)/shard_map/ppermute | solution.py:661
  144.8 1.5 collective-permute-start.16
  146.3 1.4 collective-permute-start.17
  148.3 2.5 %collective-permute-done.16 = bf16[256,256]{1,0:T(8,128)(2,1)S(1)} collective-permute-done((bf16[256,256]{1,0:T(8,128)(2,1)S(1)}, bf16[256,256]{1,0:T(8,128)(2,1)S(1)}, u32[]{:S(2)}, u32[]{:S(2)}) %collective-permute-start.16) | collective-permute-done | bytes 131104 | tf_op jit(solution)/shard_map/ppermute | solution.py:661
  152.9 1.9 %collective-permute-done.19 = bf16[4,256,256]{2,1,0:T(8,128)(2,1)S(1)} collective-permute-done((bf16[4,256,256]{2,1,0:T(8,128)(2,1)S(1)}, bf16[4,256,256]{2,1,0:T(8,128)(2,1)S(1)}, u32[]{:S(2)}, u32[]{:S(2)}) %collective-permute-start.19) | collective-permute-done | bytes 524320 | tf_op jit(solution)/shard_map/ppermute | solution.py:661
  (59 shorter events, 10.0 us)
Async XLA Ops:
  0.6 38.1 %copy-start.1 = (s32[512,2]{0,1:T(2,128)S(1)}, s32[512,2]{0,1:T(2,128)}, u32[]{:S(2)}) copy-start(s32[512,2]{0,1:T(2,128)} %param.8) | copy-start | bytes 12292
  33.0 16.3 %copy-start = (f32[128,256]{1,0:T(8,128)S(1)}, f32[128,256]{1,0:T(8,128)}, u32[]{:S(2)}) copy-start(f32[128,256]{1,0:T(8,128)} %get-tuple-element.35.refs_0_) | copy-start | bytes 393220
  33.0 21.9 %copy-start.2 = (s32[320,512]{1,0:T(8,128)S(1)}, s32[320,512]{1,0:T(8,128)}, u32[]{:S(2)}) copy-start(s32[320,512]{1,0:T(8,128)} %index_ref.1) | copy-start | bytes 1966084
  33.0 21.9 %copy-start.3 = (f32[320,512]{1,0:T(8,128)S(1)}, f32[320,512]{1,0:T(8,128)}, u32[]{:S(2)}) copy-start(f32[320,512]{1,0:T(8,128)} %frac_ref.1) | copy-start | bytes 1966084
  33.0 28.9 %collective-permute-start = (bf16[512,10240]{1,0:T(8,128)(2,1)}, bf16[512,10240]{1,0:T(8,128)(2,1)}, u32[]{:S(2)}, u32[]{:S(2)}) collective-permute-start(bf16[512,10240]{1,0:T(8,128)(2,1)} %get-tuple-element.33), channel_id=1, source_target_pairs={{0,4},{4,0},{8,12},{12,8},{16,20},{20,16},{24,28},{28,24},{1,5},{5... | collective-permute-start | bytes 31457288 | tf_op jit(solution)/shard_map/ppermute | solution.py:661
  33.5 11.9 %collective-permute-start.1 = (f32[128,256]{1,0:T(8,128)}, f32[128,256]{1,0:T(8,128)S(1)}, u32[]{:S(2)}, u32[]{:S(2)}) collective-permute-start(f32[128,256]{1,0:T(8,128)} %get-tuple-element.36), channel_id=1, source_target_pairs={{0,1},{1,0},{2,3},{3,2},{4,5},{5,4},{6,7},{7,6},{8,9},{9,8},{10,11... | collective-permute-start | bytes 393224 | tf_op jit(solution)/shard_map/ppermute | solution.py:661
  36.2 13.1 %collective-permute-start.2 = (f32[128,256]{1,0:T(8,128)}, f32[128,256]{1,0:T(8,128)S(1)}, u32[]{:S(2)}, u32[]{:S(2)}) collective-permute-start(f32[128,256]{1,0:T(8,128)} %get-tuple-element.37), channel_id=1, source_target_pairs={{0,2},{1,3},{2,0},{3,1},{4,6},{5,7},{6,4},{7,5},{8,10},{9,11},{10,... | collective-permute-start | bytes 393224 | tf_op jit(solution)/shard_map/ppermute | solution.py:661
  38.8 10.5 %collective-permute-start.3 = (f32[128,256]{1,0:T(8,128)}, f32[128,256]{1,0:T(8,128)S(1)}, u32[]{:S(2)}, u32[]{:S(2)}) collective-permute-start(f32[128,256]{1,0:T(8,128)} %get-tuple-element.38), channel_id=1, source_target_pairs={{0,3},{1,2},{2,1},{3,0},{4,7},{5,6},{6,5},{7,4},{8,11},{9,10},{10,... | collective-permute-start | bytes 393224 | tf_op jit(solution)/shard_map/ppermute | solution.py:661
  38.8 10.8 %collective-permute-start.4 = (s32[2,512]{1,0:T(2,128)S(1)}, s32[2,512]{1,0:T(2,128)S(1)}, u32[]{:S(2)}, u32[]{:S(2)}) collective-permute-start(s32[2,512]{1,0:T(2,128)S(1)} %bitcast.46), channel_id=1, source_target_pairs={{0,4},{4,0},{8,12},{12,8},{16,20},{20,16},{24,28},{28,24},{1,5},{5... | collective-permute-start | bytes 12296 | tf_op jit(solution)/shard_map/ppermute | solution.py:661
  49.5 10.3 %collective-permute-start.5 = (bf16[128,256]{1,0:T(8,128)(2,1)S(1)}, bf16[128,256]{1,0:T(8,128)(2,1)S(1)}, u32[]{:S(2)}, u32[]{:S(2)}) collective-permute-start(bf16[128,256]{1,0:T(8,128)(2,1)S(1)} %shard_map.88), channel_id=1, source_target_pairs={{0,3},{1,2},{2,1},{3,0},{4,7},{5,6},{6,5},{7,4},{8,11},{9,10},{10,... | collective-permute-start | bytes 196616 | tf_op jit(solution)/shard_map/ppermute | solution.py:661
  54.3 5.9 %collective-permute-start.6 = (bf16[128,256]{1,0:T(8,128)(2,1)S(1)}, bf16[128,256]{1,0:T(8,128)(2,1)S(1)}, u32[]{:S(2)}, u32[]{:S(2)}) collective-permute-start(bf16[128,256]{1,0:T(8,128)(2,1)S(1)} %shard_map.88), channel_id=1, source_target_pairs={{0,2},{1,3},{2,0},{3,1},{4,6},{5,7},{6,4},{7,5},{8,10},{9,11},{10,... | collective-permute-start | bytes 196616 | tf_op jit(solution)/shard_map/ppermute | solution.py:661
  54.3 5.9 %collective-permute-start.7 = (bf16[128,256]{1,0:T(8,128)(2,1)S(1)}, bf16[128,256]{1,0:T(8,128)(2,1)S(1)}, u32[]{:S(2)}, u32[]{:S(2)}) collective-permute-start(bf16[128,256]{1,0:T(8,128)(2,1)S(1)} %shard_map.88), channel_id=1, source_target_pairs={{0,1},{1,0},{2,3},{3,2},{4,5},{5,4},{6,7},{7,6},{8,9},{9,8},{10,11... | collective-permute-start | bytes 196616 | tf_op jit(solution)/shard_map/ppermute | solution.py:661
  60.3 1.6 %collective-permute-start.8 = (bf16[4,128,256]{2,1,0:T(8,128)(2,1)S(1)}, bf16[4,128,256]{2,1,0:T(8,128)(2,1)S(1)}, u32[]{:S(2)}, u32[]{:S(2)}) collective-permute-start(bf16[4,128,256]{2,1,0:T(8,128)(2,1)S(1)} %pad_maximum_fusion.1.rest_0_), channel_id=1, source_target_pairs={{0,4},{4,0},{8,12},{12,8},{16,20},{20,16},{24,28},{28,24},{1,5},{5... | collective-permute-start | bytes 786440 | tf_op jit(solution)/shard_map/ppermute | solution.py:661
  102.3 4.2 %collective-permute-start.9 = (bf16[2,4096,128]{2,1,0:T(8,128)(2,1)S(1)}, bf16[2,4096,128]{2,1,0:T(8,128)(2,1)S(1)}, u32[]{:S(2)}, u32[]{:S(2)}) collective-permute-start(bf16[2,4096,128]{2,1,0:T(8,128)(2,1)S(1)} %get-tuple-element.45), channel_id=1, source_target_pairs={{0,4},{4,0},{8,12},{12,8},{16,20},{20,16},{24,28},{28,24},{1,5},{5... | collective-permute-start | bytes 6291464 | tf_op jit(solution)/shard_map/ppermute | solution.py:661
  106.7 14.1 %collective-permute-start.10 = (bf16[1,2,1024,128]{3,2,1,0:T(8,128)(2,1)S(1)}, bf16[1,2,1024,128]{3,2,1,0:T(8,128)(2,1)S(1)}, u32[]{:S(2)}, u32[]{:S(2)}) collective-permute-start(bf16[1,2,1024,128]{3,2,1,0:T(8,128)(2,1)S(1)} %bitcast.65), channel_id=1, source_target_pairs={{0,8},{4,12},{8,0},{12,4},{16,24},{20,28},{24,16},{28,20},{1,9},{5... | collective-permute-start | bytes 1572872 | tf_op jit(solution)/shard_map/ppermute | solution.py:661
  108.5 14.0 %collective-permute-start.12 = (bf16[2,1,1024,128]{3,2,1,0:T(8,128)(2,1)S(1)}, bf16[2,1,1024,128]{3,2,1,0:T(8,128)(2,1)S(1)}, u32[]{:S(2)}, u32[]{:S(2)}) collective-permute-start(bf16[2,1,1024,128]{3,2,1,0:T(8,128)(2,1)S(1)} %add_convert_fusion), channel_id=1, source_target_pairs={{0,16},{4,20},{8,24},{12,28},{16,0},{20,4},{24,8},{28,12},{1,17},{... | collective-permute-start | bytes 1572872 | tf_op jit(solution)/shard_map/ppermute | solution.py:661
  120.9 7.7 %collective-permute-start.11 = (bf16[1,1,1024,128]{3,2,1,0:T(8,128)(2,1)S(1)}, bf16[1,1,1024,128]{3,2,1,0:T(8,128)(2,1)S(1)}, u32[]{:S(2)}, u32[]{:S(2)}) collective-permute-start(bf16[1,1,1024,128]{3,2,1,0:T(8,128)(2,1)S(1)} %add_convert_fusion.4), channel_id=1, source_target_pairs={{0,16},{4,20},{8,24},{12,28},{16,0},{20,4},{24,8},{28,12},{1,17},{... | collective-permute-start | bytes 786440 | tf_op jit(solution)/shard_map/ppermute | solution.py:661
  122.6 7.3 %collective-permute-start.13 = (bf16[1,1,1024,128]{3,2,1,0:T(8,128)(2,1)S(1)}, bf16[1,1,1024,128]{3,2,1,0:T(8,128)(2,1)S(1)}, u32[]{:S(2)}, u32[]{:S(2)}) collective-permute-start(bf16[1,1,1024,128]{3,2,1,0:T(8,128)(2,1)S(1)} %add_convert_fusion.3), channel_id=1, source_target_pairs={{0,8},{4,12},{8,0},{12,4},{16,24},{20,28},{24,16},{28,20},{1,9},{5... | collective-permute-start | bytes 786440 | tf_op jit(solution)/shard_map/ppermute | solution.py:661
  130.1 6.4 %collective-permute-start.14 = (bf16[2,512,128]{2,1,0:T(8,128)(2,1)S(1)}, bf16[2,512,128]{2,1,0:T(8,128)(2,1)S(1)}, u32[]{:S(2)}, u32[]{:S(2)}) collective-permute-start(bf16[2,512,128]{2,1,0:T(8,128)(2,1)S(1)} %add_convert_fusion.2), channel_id=1, source_target_pairs={{0,1},{1,0},{2,3},{3,2},{4,5},{5,4},{6,7},{7,6},{8,9},{9,8},{10,11... | collective-permute-start | bytes 786440 | tf_op jit(solution)/shard_map/ppermute | solution.py:661
  136.6 7.3 %collective-permute-start.15 = (bf16[2,256,128]{2,1,0:T(8,128)(2,1)S(1)}, bf16[2,256,128]{2,1,0:T(8,128)(2,1)S(1)}, u32[]{:S(2)}, u32[]{:S(2)}) collective-permute-start(bf16[2,256,128]{2,1,0:T(8,128)(2,1)S(1)} %add_convert_fusion.5), channel_id=1, source_target_pairs={{0,2},{1,3},{2,0},{3,1},{4,6},{5,7},{6,4},{7,5},{8,10},{9,11},{10,... | collective-permute-start | bytes 393224 | tf_op jit(solution)/shard_map/ppermute | solution.py:661
  144.8 5.9 %collective-permute-start.16 = (bf16[256,256]{1,0:T(8,128)(2,1)S(1)}, bf16[256,256]{1,0:T(8,128)(2,1)S(1)}, u32[]{:S(2)}, u32[]{:S(2)}) collective-permute-start(bf16[256,256]{1,0:T(8,128)(2,1)S(1)} %get-tuple-element.46), channel_id=1, source_target_pairs={{0,24},{4,28},{8,16},{12,20},{16,8},{20,12},{24,0},{28,4},{1,25},{... | collective-permute-start | bytes 393224 | tf_op jit(solution)/shard_map/ppermute | solution.py:661
  146.3 5.8 %collective-permute-start.17 = (bf16[256,256]{1,0:T(8,128)(2,1)S(1)}, bf16[256,256]{1,0:T(8,128)(2,1)S(1)}, u32[]{:S(2)}, u32[]{:S(2)}) collective-permute-start(bf16[256,256]{1,0:T(8,128)(2,1)S(1)} %get-tuple-element.46), channel_id=1, source_target_pairs={{0,16},{4,20},{8,24},{12,28},{16,0},{20,4},{24,8},{28,12},{1,17},{... | collective-permute-start | bytes 393224 | tf_op jit(solution)/shard_map/ppermute | solution.py:661
  147.7 5.0 %collective-permute-start.18 = (bf16[256,256]{1,0:T(8,128)(2,1)S(1)}, bf16[256,256]{1,0:T(8,128)(2,1)S(1)}, u32[]{:S(2)}, u32[]{:S(2)}) collective-permute-start(bf16[256,256]{1,0:T(8,128)(2,1)S(1)} %get-tuple-element.46), channel_id=1, source_target_pairs={{0,8},{4,12},{8,0},{12,4},{16,24},{20,28},{24,16},{28,20},{1,9},{5... | collective-permute-start | bytes 393224 | tf_op jit(solution)/shard_map/ppermute | solution.py:661
  152.8 2.0 %collective-permute-start.19 = (bf16[4,256,256]{2,1,0:T(8,128)(2,1)S(1)}, bf16[4,256,256]{2,1,0:T(8,128)(2,1)S(1)}, u32[]{:S(2)}, u32[]{:S(2)}) collective-permute-start(bf16[4,256,256]{2,1,0:T(8,128)(2,1)S(1)} %get-tuple-element.49), channel_id=1, source_target_pairs={{0,4},{4,0},{8,12},{12,8},{16,20},{20,16},{24,28},{28,24},{1,5},{5... | collective-permute-start | bytes 1572872 | tf_op jit(solution)/shard_map/ppermute | solution.py:661
  (4 other events, 38.6 us)

commit v16 on v13

--- a/solution.py
+++ b/solution.py
@@ -91,12 +91,12 @@
             rows = particles // STREAMS
             for t in range(rows // 16 // rounds):
                 job = (x_refs[s], i * (rows // 16 // rounds) + t, s * rows, flat_ref)
-                if (s * (rows // 16 // rounds) + t) % 2:
+                if (s * (rows // 16 // rounds) + t) % 4:
                     turns.append(job)
                 else:
                     jobs.append(job + (False,))
-        for at in range(0, len(jobs), 6):
-            regroup(jobs[at : at + 6])
+        for at in range(0, len(jobs), 5):
+            regroup(jobs[at : at + 5])
         for job in turns:
             turn(*job)
 

time: 157 us -> 153 us (0.975)
  Pallas kernels: 85.1 us -> 80.5 us
  waiting for transfers between devices: 43.8 us -> 42.2 us
    pallas_call x1, Pallas kernels: 33.7 us -> 31.2 us  [score_call(): pl.pallas_call(score_kernel, grid=(steps + 1,), out_shape=[jax.ShapeDtype...]
    pallas_call x1, Pallas kernels: 40.5 us -> 38.4 us  [insert_call(): pl.pallas_call(insert_kernel, grid=(steps,), out_shape=[jax.ShapeDtypeStr...]
where the time goes in v16:
time: 153 us
  Pallas kernels  80.5 us (53%)
  waiting for transfers between devices  42.2 us (28%)
  starting transfers between devices  25 us (16%)
  local copies, waits for them, and re-layouts  2.28 us (1%)
  other arithmetic  1.95 us (1%)
    ppermute x20, waiting for transfers between devices, flip(): return lax.ppermute(value, axis, [(i, i ^ bit) for i in range(size)])  42.2 us
    pallas_call x1, Pallas kernels, insert_call(): pl.pallas_call(insert_kernel, grid=(steps,), out_shape=[jax.ShapeDtypeStr...  38.4 us
    pallas_call x1, Pallas kernels, score_call(): pl.pallas_call(score_kernel, grid=(steps + 1,), out_shape=[jax.ShapeDtype...  31.2 us
    ppermute x20, starting transfers between devices, flip(): return lax.ppermute(value, axis, [(i, i ^ bit) for i in range(size)])  25 us
    pallas_call x1, Pallas kernels, plan_call(): pl.pallas_call(functools.partial(plan_kernel, sizes=mesh_sizes, per=group...  6.62 us
    pallas_call x1, Pallas kernels, meta_call(): pl.pallas_call(functools.partial(meta_kernel, per=group_block(groups) //...  4.08 us
  transfers between devices with their start and end apart: 20, of which 13 were waited for; matrix products, arithmetic and copies ran while one was open for 0% of the time, Pallas kernels for 7%

profile of v16, /device:TPU:0, one launch (start us, length us, event | category | flops | bytes accessed | tf_op | source)
XLA Modules:
  0.0 152.8 jit_solution(1669672460865913322)
XLA Ops:
  0.6 31.2 %shard_map.86 = (bf16[512,10240]{1,0:T(8,128)(2,1)}, bf16[512,10240]{1,0:T(8,128)(2,1)}, f32[128,256]{1,0:T(8,128)}, f32[128,256]{1,0:T(8,128)}, f32[128,256]{1,0:T(8,128)}, /*index=5*/f32[128,256]{1,0:T(8,128)}) custom-call(s32[1]{0:T(128)} %bitcast.here_ref, f32[80]{0:T(128)} %noise_ref.1, s32[2,512]{1,0:T(2,128)} %bitcast.45, ...), custom_call_target="tpu_custom_call" | custom-call | flops 21474836480 | bytes 62914560 | tf_op jit(solution)/shard_map/pallas_call | solution.py:183
  32.4 2.6 %collective-permute-start.1 = (f32[128,256]{1,0:T(8,128)}, f32[128,256]{1,0:T(8,128)S(1)}, u32[]{:S(2)}, u32[]{:S(2)}) collective-permute-start(f32[128,256]{1,0:T(8,128)} %get-tuple-element.36), channel_id=1, source_target_pairs={{0,1},{1,0},{2,3},{3,2},{4,5},{5,4},{6,7},{7,6},{8,9},{9,8},{10,11... | collective-permute-start | bytes 393224 | tf_op jit(solution)/shard_map/ppermute | solution.py:666
  35.0 2.6 %collective-permute-start.2 = (f32[128,256]{1,0:T(8,128)}, f32[128,256]{1,0:T(8,128)S(1)}, u32[]{:S(2)}, u32[]{:S(2)}) collective-permute-start(f32[128,256]{1,0:T(8,128)} %get-tuple-element.37), channel_id=1, source_target_pairs={{0,2},{1,3},{2,0},{3,1},{4,6},{5,7},{6,4},{7,5},{8,10},{9,11},{10,... | collective-permute-start | bytes 393224 | tf_op jit(solution)/shard_map/ppermute | solution.py:666
  37.6 6.6 %shard_map.87 = (s32[4,20,256]{2,1,0:T(8,128)}, s32[4,20,128]{2,1,0:T(8,128)}, s32[4,5,128]{2,1,0:T(8,128)}) custom-call(s32[1]{0:T(128)} %bitcast.here_ref, s32[320,512]{1,0:T(8,128)} %dest_ref.1), custom_call_target="tpu_custom_call" | custom-call | flops 1342177280 | bytes 327680 | tf_op jit(solution)/shard_map/pallas_call | solution.py:387
  44.3 3.9 %collective-permute-done.2.refs_2_ = f32[128,256]{1,0:T(8,128)S(1)} collective-permute-done((f32[128,256]{1,0:T(8,128)}, f32[128,256]{1,0:T(8,128)S(1)}, u32[]{:S(2)}, u32[]{:S(2)}) %collective-permute-start.2) | collective-permute-done | bytes 131104 | tf_op jit(solution)/shard_map/ppermute | solution.py:666
  48.4 4.8 %collective-permute-start.5 = (bf16[128,256]{1,0:T(8,128)(2,1)S(1)}, bf16[128,256]{1,0:T(8,128)(2,1)S(1)}, u32[]{:S(2)}, u32[]{:S(2)}) collective-permute-start(bf16[128,256]{1,0:T(8,128)(2,1)S(1)} %shard_map.88), channel_id=1, source_target_pairs={{0,3},{1,2},{2,1},{3,0},{4,7},{5,6},{6,5},{7,4},{8,11},{9,10},{10,... | collective-permute-start | bytes 196616 | tf_op jit(solution)/shard_map/ppermute | solution.py:666
  54.6 4.1 %shard_map.89.meta_ref = f32[4,20,72,128]{3,2,1,0:T(8,128)S(1)} custom-call(s32[1]{0:T(128)} %bitcast.here_ref, s32[320,512]{1,0:T(8,128)S(1)} %copy-done.2, f32[320,512]{1,0:T(8,128)S(1)} %copy-done.3, s32[4,20,256]{2,1,0:T(8,128)S(1)} %copy-done.4), custom_call_target="tpu_custom_call" | custom-call | flops 1509949440 | bytes 5898240 | tf_op jit(solution)/shard_map/pallas_call | solution.py:421
  59.2 1.5 collective-permute-done.8.rest_1_
  60.7 38.4 %shard_map.90 = (bf16[2,4096,128]{2,1,0:T(8,128)(2,1)S(1)}, bf16[2,4096,128]{2,1,0:T(8,128)(2,1)S(1)}) custom-call(s32[4,20,128]{2,1,0:T(8,128)S(1)} %copy-done.6, s32[4,5,128]{2,1,0:T(8,128)S(1)} %copy-done.7, bf16[512,10240]{1,0:T(8,128)(2,1)} %get-tuple-element.32.x_ref, bf16[512,10240]{1,0:T(8,128)(2,1)} %collective-permute-done.y_ref, ...), custom_call_target="tpu_custom_call" | custom-call | flops 21474836480 | bytes 10485760 | tf_op jit(solution)/shard_map/pallas_call | solution.py:629
  99.4 3.9 %collective-permute-done.9 = bf16[2,4096,128]{2,1,0:T(8,128)(2,1)S(1)} collective-permute-done((bf16[2,4096,128]{2,1,0:T(8,128)(2,1)S(1)}, bf16[2,4096,128]{2,1,0:T(8,128)(2,1)S(1)}, u32[]{:S(2)}, u32[]{:S(2)}) %collective-permute-start.9) | collective-permute-done | bytes 2097184 | tf_op jit(solution)/shard_map/ppermute | solution.py:666
  103.5 1.5 %collective-permute-start.10 = (bf16[1,2,1024,128]{3,2,1,0:T(8,128)(2,1)S(1)}, bf16[1,2,1024,128]{3,2,1,0:T(8,128)(2,1)S(1)}, u32[]{:S(2)}, u32[]{:S(2)}) collective-permute-start(bf16[1,2,1024,128]{3,2,1,0:T(8,128)(2,1)S(1)} %bitcast.65), channel_id=1, source_target_pairs={{0,8},{4,12},{8,0},{12,4},{16,24},{20,28},{24,16},{28,20},{1,9},{5... | collective-permute-start | bytes 1572872 | tf_op jit(solution)/shard_map/ppermute | solution.py:666
  105.3 1.6 %collective-permute-start.12 = (bf16[2,1,1024,128]{3,2,1,0:T(8,128)(2,1)S(1)}, bf16[2,1,1024,128]{3,2,1,0:T(8,128)(2,1)S(1)}, u32[]{:S(2)}, u32[]{:S(2)}) collective-permute-start(bf16[2,1,1024,128]{3,2,1,0:T(8,128)(2,1)S(1)} %add_convert_fusion), channel_id=1, source_target_pairs={{0,16},{4,20},{8,24},{12,28},{16,0},{20,4},{24,8},{28,12},{1,17},{... | collective-permute-start | bytes 1572872 | tf_op jit(solution)/shard_map/ppermute | solution.py:666
  107.0 10.6 %collective-permute-done.10 = bf16[1,2,1024,128]{3,2,1,0:T(8,128)(2,1)S(1)} collective-permute-done((bf16[1,2,1024,128]{3,2,1,0:T(8,128)(2,1)S(1)}, bf16[1,2,1024,128]{3,2,1,0:T(8,128)(2,1)S(1)}, u32[]{:S(2)}, u32[]{:S(2)}) %collective-permute-start.10) | collective-permute-done | bytes 524320 | tf_op jit(solution)/shard_map/ppermute | solution.py:666
  117.7 1.6 %collective-permute-start.11 = (bf16[1,1,1024,128]{3,2,1,0:T(8,128)(2,1)S(1)}, bf16[1,1,1024,128]{3,2,1,0:T(8,128)(2,1)S(1)}, u32[]{:S(2)}, u32[]{:S(2)}) collective-permute-start(bf16[1,1,1024,128]{3,2,1,0:T(8,128)(2,1)S(1)} %add_convert_fusion.4), channel_id=1, source_target_pairs={{0,16},{4,20},{8,24},{12,28},{16,0},{20,4},{24,8},{28,12},{1,17},{... | collective-permute-start | bytes 786440 | tf_op jit(solution)/shard_map/ppermute | solution.py:666
  119.3 1.6 %collective-permute-start.13 = (bf16[1,1,1024,128]{3,2,1,0:T(8,128)(2,1)S(1)}, bf16[1,1,1024,128]{3,2,1,0:T(8,128)(2,1)S(1)}, u32[]{:S(2)}, u32[]{:S(2)}) collective-permute-start(bf16[1,1,1024,128]{3,2,1,0:T(8,128)(2,1)S(1)} %add_convert_fusion.3), channel_id=1, source_target_pairs={{0,8},{4,12},{8,0},{12,4},{16,24},{20,28},{24,16},{28,20},{1,9},{5... | collective-permute-start | bytes 786440 | tf_op jit(solution)/shard_map/ppermute | solution.py:666
  121.0 4.3 %collective-permute-done.11 = bf16[1,1,1024,128]{3,2,1,0:T(8,128)(2,1)S(1)} collective-permute-done((bf16[1,1,1024,128]{3,2,1,0:T(8,128)(2,1)S(1)}, bf16[1,1,1024,128]{3,2,1,0:T(8,128)(2,1)S(1)}, u32[]{:S(2)}, u32[]{:S(2)}) %collective-permute-start.11) | collective-permute-done | bytes 262176 | tf_op jit(solution)/shard_map/ppermute | solution.py:666
  125.2 1.4 collective-permute-done.13
  128.0 5.2 %collective-permute-done.14 = bf16[2,512,128]{2,1,0:T(8,128)(2,1)S(1)} collective-permute-done((bf16[2,512,128]{2,1,0:T(8,128)(2,1)S(1)}, bf16[2,512,128]{2,1,0:T(8,128)(2,1)S(1)}, u32[]{:S(2)}, u32[]{:S(2)}) %collective-permute-start.14) | collective-permute-done | bytes 262176 | tf_op jit(solution)/shard_map/ppermute | solution.py:666
  133.3 2.5 %collective-permute-start.15 = (bf16[2,256,128]{2,1,0:T(8,128)(2,1)S(1)}, bf16[2,256,128]{2,1,0:T(8,128)(2,1)S(1)}, u32[]{:S(2)}, u32[]{:S(2)}) collective-permute-start(bf16[2,256,128]{2,1,0:T(8,128)(2,1)S(1)} %add_convert_fusion.5), channel_id=1, source_target_pairs={{0,2},{1,3},{2,0},{3,1},{4,6},{5,7},{6,4},{7,5},{8,10},{9,11},{10,... | collective-permute-start | bytes 393224 | tf_op jit(solution)/shard_map/ppermute | solution.py:666
  135.9 4.8 %collective-permute-done.15 = bf16[2,256,128]{2,1,0:T(8,128)(2,1)S(1)} collective-permute-done((bf16[2,256,128]{2,1,0:T(8,128)(2,1)S(1)}, bf16[2,256,128]{2,1,0:T(8,128)(2,1)S(1)}, u32[]{:S(2)}, u32[]{:S(2)}) %collective-permute-start.15) | collective-permute-done | bytes 131104 | tf_op jit(solution)/shard_map/ppermute | solution.py:666
  141.5 1.4 collective-permute-start.16
  142.9 1.5 collective-permute-start.17
  145.0 2.5 %collective-permute-done.16 = bf16[256,256]{1,0:T(8,128)(2,1)S(1)} collective-permute-done((bf16[256,256]{1,0:T(8,128)(2,1)S(1)}, bf16[256,256]{1,0:T(8,128)(2,1)S(1)}, u32[]{:S(2)}, u32[]{:S(2)}) %collective-permute-start.16) | collective-permute-done | bytes 131104 | tf_op jit(solution)/shard_map/ppermute | solution.py:666
  149.7 1.9 %collective-permute-done.19 = bf16[4,256,256]{2,1,0:T(8,128)(2,1)S(1)} collective-permute-done((bf16[4,256,256]{2,1,0:T(8,128)(2,1)S(1)}, bf16[4,256,256]{2,1,0:T(8,128)(2,1)S(1)}, u32[]{:S(2)}, u32[]{:S(2)}) %collective-permute-start.19) | collective-permute-done | bytes 524320 | tf_op jit(solution)/shard_map/ppermute | solution.py:666
  (59 shorter events, 9.9 us)
Async XLA Ops:
  0.6 37.0 %copy-start.1 = (s32[512,2]{0,1:T(2,128)S(1)}, s32[512,2]{0,1:T(2,128)}, u32[]{:S(2)}) copy-start(s32[512,2]{0,1:T(2,128)} %param.8) | copy-start | bytes 12292
  31.8 16.3 %copy-start = (f32[128,256]{1,0:T(8,128)S(1)}, f32[128,256]{1,0:T(8,128)}, u32[]{:S(2)}) copy-start(f32[128,256]{1,0:T(8,128)} %get-tuple-element.35.refs_0_) | copy-start | bytes 393220
  31.8 21.9 %copy-start.2 = (s32[320,512]{1,0:T(8,128)S(1)}, s32[320,512]{1,0:T(8,128)}, u32[]{:S(2)}) copy-start(s32[320,512]{1,0:T(8,128)} %index_ref.1) | copy-start | bytes 1966084
  31.8 21.9 %copy-start.3 = (f32[320,512]{1,0:T(8,128)S(1)}, f32[320,512]{1,0:T(8,128)}, u32[]{:S(2)}) copy-start(f32[320,512]{1,0:T(8,128)} %frac_ref.1) | copy-start | bytes 1966084
  31.9 28.9 %collective-permute-start = (bf16[512,10240]{1,0:T(8,128)(2,1)}, bf16[512,10240]{1,0:T(8,128)(2,1)}, u32[]{:S(2)}, u32[]{:S(2)}) collective-permute-start(bf16[512,10240]{1,0:T(8,128)(2,1)} %get-tuple-element.33), channel_id=1, source_target_pairs={{0,4},{4,0},{8,12},{12,8},{16,20},{20,16},{24,28},{28,24},{1,5},{5... | collective-permute-start | bytes 31457288 | tf_op jit(solution)/shard_map/ppermute | solution.py:666
  32.4 11.9 %collective-permute-start.1 = (f32[128,256]{1,0:T(8,128)}, f32[128,256]{1,0:T(8,128)S(1)}, u32[]{:S(2)}, u32[]{:S(2)}) collective-permute-start(f32[128,256]{1,0:T(8,128)} %get-tuple-element.36), channel_id=1, source_target_pairs={{0,1},{1,0},{2,3},{3,2},{4,5},{5,4},{6,7},{7,6},{8,9},{9,8},{10,11... | collective-permute-start | bytes 393224 | tf_op jit(solution)/shard_map/ppermute | solution.py:666
  35.0 13.1 %collective-permute-start.2 = (f32[128,256]{1,0:T(8,128)}, f32[128,256]{1,0:T(8,128)S(1)}, u32[]{:S(2)}, u32[]{:S(2)}) collective-permute-start(f32[128,256]{1,0:T(8,128)} %get-tuple-element.37), channel_id=1, source_target_pairs={{0,2},{1,3},{2,0},{3,1},{4,6},{5,7},{6,4},{7,5},{8,10},{9,11},{10,... | collective-permute-start | bytes 393224 | tf_op jit(solution)/shard_map/ppermute | solution.py:666
  37.6 10.5 %collective-permute-start.3 = (f32[128,256]{1,0:T(8,128)}, f32[128,256]{1,0:T(8,128)S(1)}, u32[]{:S(2)}, u32[]{:S(2)}) collective-permute-start(f32[128,256]{1,0:T(8,128)} %get-tuple-element.38), channel_id=1, source_target_pairs={{0,3},{1,2},{2,1},{3,0},{4,7},{5,6},{6,5},{7,4},{8,11},{9,10},{10,... | collective-permute-start | bytes 393224 | tf_op jit(solution)/shard_map/ppermute | solution.py:666
  37.6 10.7 %collective-permute-start.4 = (s32[2,512]{1,0:T(2,128)S(1)}, s32[2,512]{1,0:T(2,128)S(1)}, u32[]{:S(2)}, u32[]{:S(2)}) collective-permute-start(s32[2,512]{1,0:T(2,128)S(1)} %bitcast.46), channel_id=1, source_target_pairs={{0,4},{4,0},{8,12},{12,8},{16,20},{20,16},{24,28},{28,24},{1,5},{5... | collective-permute-start | bytes 12296 | tf_op jit(solution)/shard_map/ppermute | solution.py:666
  48.4 10.3 %collective-permute-start.5 = (bf16[128,256]{1,0:T(8,128)(2,1)S(1)}, bf16[128,256]{1,0:T(8,128)(2,1)S(1)}, u32[]{:S(2)}, u32[]{:S(2)}) collective-permute-start(bf16[128,256]{1,0:T(8,128)(2,1)S(1)} %shard_map.88), channel_id=1, source_target_pairs={{0,3},{1,2},{2,1},{3,0},{4,7},{5,6},{6,5},{7,4},{8,11},{9,10},{10,... | collective-permute-start | bytes 196616 | tf_op jit(solution)/shard_map/ppermute | solution.py:666
  53.1 5.9 %collective-permute-start.6 = (bf16[128,256]{1,0:T(8,128)(2,1)S(1)}, bf16[128,256]{1,0:T(8,128)(2,1)S(1)}, u32[]{:S(2)}, u32[]{:S(2)}) collective-permute-start(bf16[128,256]{1,0:T(8,128)(2,1)S(1)} %shard_map.88), channel_id=1, source_target_pairs={{0,2},{1,3},{2,0},{3,1},{4,6},{5,7},{6,4},{7,5},{8,10},{9,11},{10,... | collective-permute-start | bytes 196616 | tf_op jit(solution)/shard_map/ppermute | solution.py:666
  53.1 5.9 %collective-permute-start.7 = (bf16[128,256]{1,0:T(8,128)(2,1)S(1)}, bf16[128,256]{1,0:T(8,128)(2,1)S(1)}, u32[]{:S(2)}, u32[]{:S(2)}) collective-permute-start(bf16[128,256]{1,0:T(8,128)(2,1)S(1)} %shard_map.88), channel_id=1, source_target_pairs={{0,1},{1,0},{2,3},{3,2},{4,5},{5,4},{6,7},{7,6},{8,9},{9,8},{10,11... | collective-permute-start | bytes 196616 | tf_op jit(solution)/shard_map/ppermute | solution.py:666
  59.1 1.6 %collective-permute-start.8 = (bf16[4,128,256]{2,1,0:T(8,128)(2,1)S(1)}, bf16[4,128,256]{2,1,0:T(8,128)(2,1)S(1)}, u32[]{:S(2)}, u32[]{:S(2)}) collective-permute-start(bf16[4,128,256]{2,1,0:T(8,128)(2,1)S(1)} %pad_maximum_fusion.1.rest_0_), channel_id=1, source_target_pairs={{0,4},{4,0},{8,12},{12,8},{16,20},{20,16},{24,28},{28,24},{1,5},{5... | collective-permute-start | bytes 786440 | tf_op jit(solution)/shard_map/ppermute | solution.py:666
  99.1 4.2 %collective-permute-start.9 = (bf16[2,4096,128]{2,1,0:T(8,128)(2,1)S(1)}, bf16[2,4096,128]{2,1,0:T(8,128)(2,1)S(1)}, u32[]{:S(2)}, u32[]{:S(2)}) collective-permute-start(bf16[2,4096,128]{2,1,0:T(8,128)(2,1)S(1)} %get-tuple-element.45), channel_id=1, source_target_pairs={{0,4},{4,0},{8,12},{12,8},{16,20},{20,16},{24,28},{28,24},{1,5},{5... | collective-permute-start | bytes 6291464 | tf_op jit(solution)/shard_map/ppermute | solution.py:666
  103.5 14.0 %collective-permute-start.10 = (bf16[1,2,1024,128]{3,2,1,0:T(8,128)(2,1)S(1)}, bf16[1,2,1024,128]{3,2,1,0:T(8,128)(2,1)S(1)}, u32[]{:S(2)}, u32[]{:S(2)}) collective-permute-start(bf16[1,2,1024,128]{3,2,1,0:T(8,128)(2,1)S(1)} %bitcast.65), channel_id=1, source_target_pairs={{0,8},{4,12},{8,0},{12,4},{16,24},{20,28},{24,16},{28,20},{1,9},{5... | collective-permute-start | bytes 1572872 | tf_op jit(solution)/shard_map/ppermute | solution.py:666
  105.3 13.9 %collective-permute-start.12 = (bf16[2,1,1024,128]{3,2,1,0:T(8,128)(2,1)S(1)}, bf16[2,1,1024,128]{3,2,1,0:T(8,128)(2,1)S(1)}, u32[]{:S(2)}, u32[]{:S(2)}) collective-permute-start(bf16[2,1,1024,128]{3,2,1,0:T(8,128)(2,1)S(1)} %add_convert_fusion), channel_id=1, source_target_pairs={{0,16},{4,20},{8,24},{12,28},{16,0},{20,4},{24,8},{28,12},{1,17},{... | collective-permute-start | bytes 1572872 | tf_op jit(solution)/shard_map/ppermute | solution.py:666
  117.7 7.6 %collective-permute-start.11 = (bf16[1,1,1024,128]{3,2,1,0:T(8,128)(2,1)S(1)}, bf16[1,1,1024,128]{3,2,1,0:T(8,128)(2,1)S(1)}, u32[]{:S(2)}, u32[]{:S(2)}) collective-permute-start(bf16[1,1,1024,128]{3,2,1,0:T(8,128)(2,1)S(1)} %add_convert_fusion.4), channel_id=1, source_target_pairs={{0,16},{4,20},{8,24},{12,28},{16,0},{20,4},{24,8},{28,12},{1,17},{... | collective-permute-start | bytes 786440 | tf_op jit(solution)/shard_map/ppermute | solution.py:666
  119.3 7.3 %collective-permute-start.13 = (bf16[1,1,1024,128]{3,2,1,0:T(8,128)(2,1)S(1)}, bf16[1,1,1024,128]{3,2,1,0:T(8,128)(2,1)S(1)}, u32[]{:S(2)}, u32[]{:S(2)}) collective-permute-start(bf16[1,1,1024,128]{3,2,1,0:T(8,128)(2,1)S(1)} %add_convert_fusion.3), channel_id=1, source_target_pairs={{0,8},{4,12},{8,0},{12,4},{16,24},{20,28},{24,16},{28,20},{1,9},{5... | collective-permute-start | bytes 786440 | tf_op jit(solution)/shard_map/ppermute | solution.py:666
  126.8 6.4 %collective-permute-start.14 = (bf16[2,512,128]{2,1,0:T(8,128)(2,1)S(1)}, bf16[2,512,128]{2,1,0:T(8,128)(2,1)S(1)}, u32[]{:S(2)}, u32[]{:S(2)}) collective-permute-start(bf16[2,512,128]{2,1,0:T(8,128)(2,1)S(1)} %add_convert_fusion.2), channel_id=1, source_target_pairs={{0,1},{1,0},{2,3},{3,2},{4,5},{5,4},{6,7},{7,6},{8,9},{9,8},{10,11... | collective-permute-start | bytes 786440 | tf_op jit(solution)/shard_map/ppermute | solution.py:666
  133.3 7.3 %collective-permute-start.15 = (bf16[2,256,128]{2,1,0:T(8,128)(2,1)S(1)}, bf16[2,256,128]{2,1,0:T(8,128)(2,1)S(1)}, u32[]{:S(2)}, u32[]{:S(2)}) collective-permute-start(bf16[2,256,128]{2,1,0:T(8,128)(2,1)S(1)} %add_convert_fusion.5), channel_id=1, source_target_pairs={{0,2},{1,3},{2,0},{3,1},{4,6},{5,7},{6,4},{7,5},{8,10},{9,11},{10,... | collective-permute-start | bytes 393224 | tf_op jit(solution)/shard_map/ppermute | solution.py:666
  141.5 6.0 %collective-permute-start.16 = (bf16[256,256]{1,0:T(8,128)(2,1)S(1)}, bf16[256,256]{1,0:T(8,128)(2,1)S(1)}, u32[]{:S(2)}, u32[]{:S(2)}) collective-permute-start(bf16[256,256]{1,0:T(8,128)(2,1)S(1)} %get-tuple-element.46), channel_id=1, source_target_pairs={{0,24},{4,28},{8,16},{12,20},{16,8},{20,12},{24,0},{28,4},{1,25},{... | collective-permute-start | bytes 393224 | tf_op jit(solution)/shard_map/ppermute | solution.py:666
  142.9 5.8 %collective-permute-start.17 = (bf16[256,256]{1,0:T(8,128)(2,1)S(1)}, bf16[256,256]{1,0:T(8,128)(2,1)S(1)}, u32[]{:S(2)}, u32[]{:S(2)}) collective-permute-start(bf16[256,256]{1,0:T(8,128)(2,1)S(1)} %get-tuple-element.46), channel_id=1, source_target_pairs={{0,16},{4,20},{8,24},{12,28},{16,0},{20,4},{24,8},{28,12},{1,17},{... | collective-permute-start | bytes 393224 | tf_op jit(solution)/shard_map/ppermute | solution.py:666
  144.4 5.0 %collective-permute-start.18 = (bf16[256,256]{1,0:T(8,128)(2,1)S(1)}, bf16[256,256]{1,0:T(8,128)(2,1)S(1)}, u32[]{:S(2)}, u32[]{:S(2)}) collective-permute-start(bf16[256,256]{1,0:T(8,128)(2,1)S(1)} %get-tuple-element.46), channel_id=1, source_target_pairs={{0,8},{4,12},{8,0},{12,4},{16,24},{20,28},{24,16},{28,20},{1,9},{5... | collective-permute-start | bytes 393224 | tf_op jit(solution)/shard_map/ppermute | solution.py:666
  149.6 2.0 %collective-permute-start.19 = (bf16[4,256,256]{2,1,0:T(8,128)(2,1)S(1)}, bf16[4,256,256]{2,1,0:T(8,128)(2,1)S(1)}, u32[]{:S(2)}, u32[]{:S(2)}) collective-permute-start(bf16[4,256,256]{2,1,0:T(8,128)(2,1)S(1)} %get-tuple-element.49), channel_id=1, source_target_pairs={{0,4},{4,0},{8,12},{12,8},{16,20},{20,16},{24,28},{28,24},{1,5},{5... | collective-permute-start | bytes 1572872 | tf_op jit(solution)/shard_map/ppermute | solution.py:666
  (4 other events, 38.6 us)

commit v17 on v16

--- a/solution.py
+++ b/solution.py
@@ -42,7 +42,7 @@
     per = gb // 2
     slabs = len(out_refs)
     core = lax.div(here_ref[0], slabs) & 1
-    rounds = 4
+    rounds = 2
 
     def copies(flat_ref, slot, at_step, swap):
         lanes = pl.ds(pl.multiple_of(at_step * (per * width), per * width), per * width)

time: 153 us -> 153 us (level)
  no operation moved by 1% of the time
where the time goes in v17:
time: 153 us
  Pallas kernels  80.4 us (53%)
  waiting for transfers between devices  41.9 us (27%)
  starting transfers between devices  25.3 us (17%)
  local copies, waits for them, and re-layouts  2.28 us (1%)
  other arithmetic  1.95 us (1%)
    ppermute x20, waiting for transfers between devices, flip(): return lax.ppermute(value, axis, [(i, i ^ bit) for i in range(size)])  41.9 us
    pallas_call x1, Pallas kernels, insert_call(): pl.pallas_call(insert_kernel, grid=(steps,), out_shape=[jax.ShapeDtypeStr...  38.2 us
    pallas_call x1, Pallas kernels, score_call(): pl.pallas_call(score_kernel, grid=(steps + 1,), out_shape=[jax.ShapeDtype...  31.1 us
    ppermute x20, starting transfers between devices, flip(): return lax.ppermute(value, axis, [(i, i ^ bit) for i in range(size)])  25.3 us
    pallas_call x1, Pallas kernels, plan_call(): pl.pallas_call(functools.partial(plan_kernel, sizes=mesh_sizes, per=group...  6.62 us
    pallas_call x1, Pallas kernels, meta_call(): pl.pallas_call(functools.partial(meta_kernel, per=group_block(groups) //...  4.26 us
  transfers between devices with their start and end apart: 20, of which 13 were waited for; matrix products, arithmetic and copies ran while one was open for 0% of the time, Pallas kernels for 7%

profile of v17, /device:TPU:0, one launch (start us, length us, event | category | flops | bytes accessed | tf_op | source)
XLA Modules:
  0.0 152.7 jit_solution(9354503876332910418)
XLA Ops:
  0.6 31.1 %shard_map.86 = (bf16[512,10240]{1,0:T(8,128)(2,1)}, bf16[512,10240]{1,0:T(8,128)(2,1)}, f32[128,256]{1,0:T(8,128)}, f32[128,256]{1,0:T(8,128)}, f32[128,256]{1,0:T(8,128)}, /*index=5*/f32[128,256]{1,0:T(8,128)}) custom-call(s32[1]{0:T(128)} %bitcast.here_ref, f32[80]{0:T(128)} %noise_ref.1, s32[2,512]{1,0:T(2,128)} %bitcast.45, ...), custom_call_target="tpu_custom_call" | custom-call | flops 21474836480 | bytes 62914560 | tf_op jit(solution)/shard_map/pallas_call | solution.py:183
  32.3 2.7 %collective-permute-start.1 = (f32[128,256]{1,0:T(8,128)}, f32[128,256]{1,0:T(8,128)S(1)}, u32[]{:S(2)}, u32[]{:S(2)}) collective-permute-start(f32[128,256]{1,0:T(8,128)} %get-tuple-element.36), channel_id=1, source_target_pairs={{0,1},{1,0},{2,3},{3,2},{4,5},{5,4},{6,7},{7,6},{8,9},{9,8},{10,11... | collective-permute-start | bytes 393224 | tf_op jit(solution)/shard_map/ppermute | solution.py:666
  34.9 2.6 %collective-permute-start.2 = (f32[128,256]{1,0:T(8,128)}, f32[128,256]{1,0:T(8,128)S(1)}, u32[]{:S(2)}, u32[]{:S(2)}) collective-permute-start(f32[128,256]{1,0:T(8,128)} %get-tuple-element.37), channel_id=1, source_target_pairs={{0,2},{1,3},{2,0},{3,1},{4,6},{5,7},{6,4},{7,5},{8,10},{9,11},{10,... | collective-permute-start | bytes 393224 | tf_op jit(solution)/shard_map/ppermute | solution.py:666
  37.5 6.6 %shard_map.87 = (s32[4,20,256]{2,1,0:T(8,128)}, s32[4,20,128]{2,1,0:T(8,128)}, s32[4,5,128]{2,1,0:T(8,128)}) custom-call(s32[1]{0:T(128)} %bitcast.here_ref, s32[320,512]{1,0:T(8,128)} %dest_ref.1), custom_call_target="tpu_custom_call" | custom-call | flops 1342177280 | bytes 327680 | tf_op jit(solution)/shard_map/pallas_call | solution.py:387
  44.2 3.9 %collective-permute-done.2.refs_2_ = f32[128,256]{1,0:T(8,128)S(1)} collective-permute-done((f32[128,256]{1,0:T(8,128)}, f32[128,256]{1,0:T(8,128)S(1)}, u32[]{:S(2)}, u32[]{:S(2)}) %collective-permute-start.2) | collective-permute-done | bytes 131104 | tf_op jit(solution)/shard_map/ppermute | solution.py:666
  48.3 4.8 %collective-permute-start.5 = (bf16[128,256]{1,0:T(8,128)(2,1)S(1)}, bf16[128,256]{1,0:T(8,128)(2,1)S(1)}, u32[]{:S(2)}, u32[]{:S(2)}) collective-permute-start(bf16[128,256]{1,0:T(8,128)(2,1)S(1)} %shard_map.88), channel_id=1, source_target_pairs={{0,3},{1,2},{2,1},{3,0},{4,7},{5,6},{6,5},{7,4},{8,11},{9,10},{10,... | collective-permute-start | bytes 196616 | tf_op jit(solution)/shard_map/ppermute | solution.py:666
  54.5 4.3 %shard_map.89.meta_ref = f32[4,20,72,128]{3,2,1,0:T(8,128)S(1)} custom-call(s32[1]{0:T(128)} %bitcast.here_ref, s32[320,512]{1,0:T(8,128)S(1)} %copy-done.2, f32[320,512]{1,0:T(8,128)S(1)} %copy-done.3, s32[4,20,256]{2,1,0:T(8,128)S(1)} %copy-done.4), custom_call_target="tpu_custom_call" | custom-call | flops 1509949440 | bytes 5898240 | tf_op jit(solution)/shard_map/pallas_call | solution.py:421
  59.1 1.5 collective-permute-done.8.rest_1_
  60.7 38.2 %shard_map.90 = (bf16[2,4096,128]{2,1,0:T(8,128)(2,1)S(1)}, bf16[2,4096,128]{2,1,0:T(8,128)(2,1)S(1)}) custom-call(s32[4,20,128]{2,1,0:T(8,128)S(1)} %copy-done.6, s32[4,5,128]{2,1,0:T(8,128)S(1)} %copy-done.7, bf16[512,10240]{1,0:T(8,128)(2,1)} %get-tuple-element.32.x_ref, bf16[512,10240]{1,0:T(8,128)(2,1)} %collective-permute-done.y_ref, ...), custom_call_target="tpu_custom_call" | custom-call | flops 21474836480 | bytes 10485760 | tf_op jit(solution)/shard_map/pallas_call | solution.py:629
  99.2 3.9 %collective-permute-done.9 = bf16[2,4096,128]{2,1,0:T(8,128)(2,1)S(1)} collective-permute-done((bf16[2,4096,128]{2,1,0:T(8,128)(2,1)S(1)}, bf16[2,4096,128]{2,1,0:T(8,128)(2,1)S(1)}, u32[]{:S(2)}, u32[]{:S(2)}) %collective-permute-start.9) | collective-permute-done | bytes 2097184 | tf_op jit(solution)/shard_map/ppermute | solution.py:666
  103.2 1.6 %collective-permute-start.10 = (bf16[1,2,1024,128]{3,2,1,0:T(8,128)(2,1)S(1)}, bf16[1,2,1024,128]{3,2,1,0:T(8,128)(2,1)S(1)}, u32[]{:S(2)}, u32[]{:S(2)}) collective-permute-start(bf16[1,2,1024,128]{3,2,1,0:T(8,128)(2,1)S(1)} %bitcast.65), channel_id=1, source_target_pairs={{0,8},{4,12},{8,0},{12,4},{16,24},{20,28},{24,16},{28,20},{1,9},{5... | collective-permute-start | bytes 1572872 | tf_op jit(solution)/shard_map/ppermute | solution.py:666
  105.1 1.6 %collective-permute-start.12 = (bf16[2,1,1024,128]{3,2,1,0:T(8,128)(2,1)S(1)}, bf16[2,1,1024,128]{3,2,1,0:T(8,128)(2,1)S(1)}, u32[]{:S(2)}, u32[]{:S(2)}) collective-permute-start(bf16[2,1,1024,128]{3,2,1,0:T(8,128)(2,1)S(1)} %add_convert_fusion), channel_id=1, source_target_pairs={{0,16},{4,20},{8,24},{12,28},{16,0},{20,4},{24,8},{28,12},{1,17},{... | collective-permute-start | bytes 1572872 | tf_op jit(solution)/shard_map/ppermute | solution.py:666
  106.8 10.5 %collective-permute-done.10 = bf16[1,2,1024,128]{3,2,1,0:T(8,128)(2,1)S(1)} collective-permute-done((bf16[1,2,1024,128]{3,2,1,0:T(8,128)(2,1)S(1)}, bf16[1,2,1024,128]{3,2,1,0:T(8,128)(2,1)S(1)}, u32[]{:S(2)}, u32[]{:S(2)}) %collective-permute-start.10) | collective-permute-done | bytes 524320 | tf_op jit(solution)/shard_map/ppermute | solution.py:666
  117.4 1.7 %collective-permute-start.11 = (bf16[1,1,1024,128]{3,2,1,0:T(8,128)(2,1)S(1)}, bf16[1,1,1024,128]{3,2,1,0:T(8,128)(2,1)S(1)}, u32[]{:S(2)}, u32[]{:S(2)}) collective-permute-start(bf16[1,1,1024,128]{3,2,1,0:T(8,128)(2,1)S(1)} %add_convert_fusion.4), channel_id=1, source_target_pairs={{0,16},{4,20},{8,24},{12,28},{16,0},{20,4},{24,8},{28,12},{1,17},{... | collective-permute-start | bytes 786440 | tf_op jit(solution)/shard_map/ppermute | solution.py:666
  119.2 1.5 %collective-permute-start.13 = (bf16[1,1,1024,128]{3,2,1,0:T(8,128)(2,1)S(1)}, bf16[1,1,1024,128]{3,2,1,0:T(8,128)(2,1)S(1)}, u32[]{:S(2)}, u32[]{:S(2)}) collective-permute-start(bf16[1,1,1024,128]{3,2,1,0:T(8,128)(2,1)S(1)} %add_convert_fusion.3), channel_id=1, source_target_pairs={{0,8},{4,12},{8,0},{12,4},{16,24},{20,28},{24,16},{28,20},{1,9},{5... | collective-permute-start | bytes 786440 | tf_op jit(solution)/shard_map/ppermute | solution.py:666
  120.8 4.2 %collective-permute-done.11 = bf16[1,1,1024,128]{3,2,1,0:T(8,128)(2,1)S(1)} collective-permute-done((bf16[1,1,1024,128]{3,2,1,0:T(8,128)(2,1)S(1)}, bf16[1,1,1024,128]{3,2,1,0:T(8,128)(2,1)S(1)}, u32[]{:S(2)}, u32[]{:S(2)}) %collective-permute-start.11) | collective-permute-done | bytes 262176 | tf_op jit(solution)/shard_map/ppermute | solution.py:666
  125.0 1.5 %collective-permute-done.13 = bf16[1,1,1024,128]{3,2,1,0:T(8,128)(2,1)S(1)} collective-permute-done((bf16[1,1,1024,128]{3,2,1,0:T(8,128)(2,1)S(1)}, bf16[1,1,1024,128]{3,2,1,0:T(8,128)(2,1)S(1)}, u32[]{:S(2)}, u32[]{:S(2)}) %collective-permute-start.13) | collective-permute-done | bytes 262176 | tf_op jit(solution)/shard_map/ppermute | solution.py:666
  127.9 5.1 %collective-permute-done.14 = bf16[2,512,128]{2,1,0:T(8,128)(2,1)S(1)} collective-permute-done((bf16[2,512,128]{2,1,0:T(8,128)(2,1)S(1)}, bf16[2,512,128]{2,1,0:T(8,128)(2,1)S(1)}, u32[]{:S(2)}, u32[]{:S(2)}) %collective-permute-start.14) | collective-permute-done | bytes 262176 | tf_op jit(solution)/shard_map/ppermute | solution.py:666
  133.2 2.6 %collective-permute-start.15 = (bf16[2,256,128]{2,1,0:T(8,128)(2,1)S(1)}, bf16[2,256,128]{2,1,0:T(8,128)(2,1)S(1)}, u32[]{:S(2)}, u32[]{:S(2)}) collective-permute-start(bf16[2,256,128]{2,1,0:T(8,128)(2,1)S(1)} %add_convert_fusion.5), channel_id=1, source_target_pairs={{0,2},{1,3},{2,0},{3,1},{4,6},{5,7},{6,4},{7,5},{8,10},{9,11},{10,... | collective-permute-start | bytes 393224 | tf_op jit(solution)/shard_map/ppermute | solution.py:666
  135.8 4.7 %collective-permute-done.15 = bf16[2,256,128]{2,1,0:T(8,128)(2,1)S(1)} collective-permute-done((bf16[2,256,128]{2,1,0:T(8,128)(2,1)S(1)}, bf16[2,256,128]{2,1,0:T(8,128)(2,1)S(1)}, u32[]{:S(2)}, u32[]{:S(2)}) %collective-permute-start.15) | collective-permute-done | bytes 131104 | tf_op jit(solution)/shard_map/ppermute | solution.py:666
  141.3 1.5 collective-permute-start.16
  142.8 1.5 %collective-permute-start.17 = (bf16[256,256]{1,0:T(8,128)(2,1)S(1)}, bf16[256,256]{1,0:T(8,128)(2,1)S(1)}, u32[]{:S(2)}, u32[]{:S(2)}) collective-permute-start(bf16[256,256]{1,0:T(8,128)(2,1)S(1)} %get-tuple-element.46), channel_id=1, source_target_pairs={{0,16},{4,20},{8,24},{12,28},{16,0},{20,4},{24,8},{28,12},{1,17},{... | collective-permute-start | bytes 393224 | tf_op jit(solution)/shard_map/ppermute | solution.py:666
  144.8 2.5 %collective-permute-done.16 = bf16[256,256]{1,0:T(8,128)(2,1)S(1)} collective-permute-done((bf16[256,256]{1,0:T(8,128)(2,1)S(1)}, bf16[256,256]{1,0:T(8,128)(2,1)S(1)}, u32[]{:S(2)}, u32[]{:S(2)}) %collective-permute-start.16) | collective-permute-done | bytes 131104 | tf_op jit(solution)/shard_map/ppermute | solution.py:666
  149.6 1.9 %collective-permute-done.19 = bf16[4,256,256]{2,1,0:T(8,128)(2,1)S(1)} collective-permute-done((bf16[4,256,256]{2,1,0:T(8,128)(2,1)S(1)}, bf16[4,256,256]{2,1,0:T(8,128)(2,1)S(1)}, u32[]{:S(2)}, u32[]{:S(2)}) %collective-permute-start.19) | collective-permute-done | bytes 524320 | tf_op jit(solution)/shard_map/ppermute | solution.py:666
  (59 shorter events, 9.8 us)
Async XLA Ops:
  0.6 36.9 %copy-start.1 = (s32[512,2]{0,1:T(2,128)S(1)}, s32[512,2]{0,1:T(2,128)}, u32[]{:S(2)}) copy-start(s32[512,2]{0,1:T(2,128)} %param.8) | copy-start | bytes 12292
  31.7 16.3 %copy-start = (f32[128,256]{1,0:T(8,128)S(1)}, f32[128,256]{1,0:T(8,128)}, u32[]{:S(2)}) copy-start(f32[128,256]{1,0:T(8,128)} %get-tuple-element.35.refs_0_) | copy-start | bytes 393220
  31.7 21.9 %copy-start.2 = (s32[320,512]{1,0:T(8,128)S(1)}, s32[320,512]{1,0:T(8,128)}, u32[]{:S(2)}) copy-start(s32[320,512]{1,0:T(8,128)} %index_ref.1) | copy-start | bytes 1966084
  31.8 21.9 %copy-start.3 = (f32[320,512]{1,0:T(8,128)S(1)}, f32[320,512]{1,0:T(8,128)}, u32[]{:S(2)}) copy-start(f32[320,512]{1,0:T(8,128)} %frac_ref.1) | copy-start | bytes 1966084
  31.8 28.9 %collective-permute-start = (bf16[512,10240]{1,0:T(8,128)(2,1)}, bf16[512,10240]{1,0:T(8,128)(2,1)}, u32[]{:S(2)}, u32[]{:S(2)}) collective-permute-start(bf16[512,10240]{1,0:T(8,128)(2,1)} %get-tuple-element.33), channel_id=1, source_target_pairs={{0,4},{4,0},{8,12},{12,8},{16,20},{20,16},{24,28},{28,24},{1,5},{5... | collective-permute-start | bytes 31457288 | tf_op jit(solution)/shard_map/ppermute | solution.py:666
  32.3 11.9 %collective-permute-start.1 = (f32[128,256]{1,0:T(8,128)}, f32[128,256]{1,0:T(8,128)S(1)}, u32[]{:S(2)}, u32[]{:S(2)}) collective-permute-start(f32[128,256]{1,0:T(8,128)} %get-tuple-element.36), channel_id=1, source_target_pairs={{0,1},{1,0},{2,3},{3,2},{4,5},{5,4},{6,7},{7,6},{8,9},{9,8},{10,11... | collective-permute-start | bytes 393224 | tf_op jit(solution)/shard_map/ppermute | solution.py:666
  34.9 13.1 %collective-permute-start.2 = (f32[128,256]{1,0:T(8,128)}, f32[128,256]{1,0:T(8,128)S(1)}, u32[]{:S(2)}, u32[]{:S(2)}) collective-permute-start(f32[128,256]{1,0:T(8,128)} %get-tuple-element.37), channel_id=1, source_target_pairs={{0,2},{1,3},{2,0},{3,1},{4,6},{5,7},{6,4},{7,5},{8,10},{9,11},{10,... | collective-permute-start | bytes 393224 | tf_op jit(solution)/shard_map/ppermute | solution.py:666
  37.5 10.5 %collective-permute-start.3 = (f32[128,256]{1,0:T(8,128)}, f32[128,256]{1,0:T(8,128)S(1)}, u32[]{:S(2)}, u32[]{:S(2)}) collective-permute-start(f32[128,256]{1,0:T(8,128)} %get-tuple-element.38), channel_id=1, source_target_pairs={{0,3},{1,2},{2,1},{3,0},{4,7},{5,6},{6,5},{7,4},{8,11},{9,10},{10,... | collective-permute-start | bytes 393224 | tf_op jit(solution)/shard_map/ppermute | solution.py:666
  37.5 10.7 %collective-permute-start.4 = (s32[2,512]{1,0:T(2,128)S(1)}, s32[2,512]{1,0:T(2,128)S(1)}, u32[]{:S(2)}, u32[]{:S(2)}) collective-permute-start(s32[2,512]{1,0:T(2,128)S(1)} %bitcast.46), channel_id=1, source_target_pairs={{0,4},{4,0},{8,12},{12,8},{16,20},{20,16},{24,28},{28,24},{1,5},{5... | collective-permute-start | bytes 12296 | tf_op jit(solution)/shard_map/ppermute | solution.py:666
  48.3 10.5 %collective-permute-start.5 = (bf16[128,256]{1,0:T(8,128)(2,1)S(1)}, bf16[128,256]{1,0:T(8,128)(2,1)S(1)}, u32[]{:S(2)}, u32[]{:S(2)}) collective-permute-start(bf16[128,256]{1,0:T(8,128)(2,1)S(1)} %shard_map.88), channel_id=1, source_target_pairs={{0,3},{1,2},{2,1},{3,0},{4,7},{5,6},{6,5},{7,4},{8,11},{9,10},{10,... | collective-permute-start | bytes 196616 | tf_op jit(solution)/shard_map/ppermute | solution.py:666
  53.1 5.9 %collective-permute-start.6 = (bf16[128,256]{1,0:T(8,128)(2,1)S(1)}, bf16[128,256]{1,0:T(8,128)(2,1)S(1)}, u32[]{:S(2)}, u32[]{:S(2)}) collective-permute-start(bf16[128,256]{1,0:T(8,128)(2,1)S(1)} %shard_map.88), channel_id=1, source_target_pairs={{0,2},{1,3},{2,0},{3,1},{4,6},{5,7},{6,4},{7,5},{8,10},{9,11},{10,... | collective-permute-start | bytes 196616 | tf_op jit(solution)/shard_map/ppermute | solution.py:666
  53.1 5.9 %collective-permute-start.7 = (bf16[128,256]{1,0:T(8,128)(2,1)S(1)}, bf16[128,256]{1,0:T(8,128)(2,1)S(1)}, u32[]{:S(2)}, u32[]{:S(2)}) collective-permute-start(bf16[128,256]{1,0:T(8,128)(2,1)S(1)} %shard_map.88), channel_id=1, source_target_pairs={{0,1},{1,0},{2,3},{3,2},{4,5},{5,4},{6,7},{7,6},{8,9},{9,8},{10,11... | collective-permute-start | bytes 196616 | tf_op jit(solution)/shard_map/ppermute | solution.py:666
  59.0 1.6 %collective-permute-start.8 = (bf16[4,128,256]{2,1,0:T(8,128)(2,1)S(1)}, bf16[4,128,256]{2,1,0:T(8,128)(2,1)S(1)}, u32[]{:S(2)}, u32[]{:S(2)}) collective-permute-start(bf16[4,128,256]{2,1,0:T(8,128)(2,1)S(1)} %pad_maximum_fusion.1.rest_0_), channel_id=1, source_target_pairs={{0,4},{4,0},{8,12},{12,8},{16,20},{20,16},{24,28},{28,24},{1,5},{5... | collective-permute-start | bytes 786440 | tf_op jit(solution)/shard_map/ppermute | solution.py:666
  98.9 4.2 %collective-permute-start.9 = (bf16[2,4096,128]{2,1,0:T(8,128)(2,1)S(1)}, bf16[2,4096,128]{2,1,0:T(8,128)(2,1)S(1)}, u32[]{:S(2)}, u32[]{:S(2)}) collective-permute-start(bf16[2,4096,128]{2,1,0:T(8,128)(2,1)S(1)} %get-tuple-element.45), channel_id=1, source_target_pairs={{0,4},{4,0},{8,12},{12,8},{16,20},{20,16},{24,28},{28,24},{1,5},{5... | collective-permute-start | bytes 6291464 | tf_op jit(solution)/shard_map/ppermute | solution.py:666
  103.2 14.0 %collective-permute-start.10 = (bf16[1,2,1024,128]{3,2,1,0:T(8,128)(2,1)S(1)}, bf16[1,2,1024,128]{3,2,1,0:T(8,128)(2,1)S(1)}, u32[]{:S(2)}, u32[]{:S(2)}) collective-permute-start(bf16[1,2,1024,128]{3,2,1,0:T(8,128)(2,1)S(1)} %bitcast.65), channel_id=1, source_target_pairs={{0,8},{4,12},{8,0},{12,4},{16,24},{20,28},{24,16},{28,20},{1,9},{5... | collective-permute-start | bytes 1572872 | tf_op jit(solution)/shard_map/ppermute | solution.py:666
  105.1 14.0 %collective-permute-start.12 = (bf16[2,1,1024,128]{3,2,1,0:T(8,128)(2,1)S(1)}, bf16[2,1,1024,128]{3,2,1,0:T(8,128)(2,1)S(1)}, u32[]{:S(2)}, u32[]{:S(2)}) collective-permute-start(bf16[2,1,1024,128]{3,2,1,0:T(8,128)(2,1)S(1)} %add_convert_fusion), channel_id=1, source_target_pairs={{0,16},{4,20},{8,24},{12,28},{16,0},{20,4},{24,8},{28,12},{1,17},{... | collective-permute-start | bytes 1572872 | tf_op jit(solution)/shard_map/ppermute | solution.py:666
  117.4 7.6 %collective-permute-start.11 = (bf16[1,1,1024,128]{3,2,1,0:T(8,128)(2,1)S(1)}, bf16[1,1,1024,128]{3,2,1,0:T(8,128)(2,1)S(1)}, u32[]{:S(2)}, u32[]{:S(2)}) collective-permute-start(bf16[1,1,1024,128]{3,2,1,0:T(8,128)(2,1)S(1)} %add_convert_fusion.4), channel_id=1, source_target_pairs={{0,16},{4,20},{8,24},{12,28},{16,0},{20,4},{24,8},{28,12},{1,17},{... | collective-permute-start | bytes 786440 | tf_op jit(solution)/shard_map/ppermute | solution.py:666
  119.2 7.3 %collective-permute-start.13 = (bf16[1,1,1024,128]{3,2,1,0:T(8,128)(2,1)S(1)}, bf16[1,1,1024,128]{3,2,1,0:T(8,128)(2,1)S(1)}, u32[]{:S(2)}, u32[]{:S(2)}) collective-permute-start(bf16[1,1,1024,128]{3,2,1,0:T(8,128)(2,1)S(1)} %add_convert_fusion.3), channel_id=1, source_target_pairs={{0,8},{4,12},{8,0},{12,4},{16,24},{20,28},{24,16},{28,20},{1,9},{5... | collective-permute-start | bytes 786440 | tf_op jit(solution)/shard_map/ppermute | solution.py:666
  126.6 6.4 %collective-permute-start.14 = (bf16[2,512,128]{2,1,0:T(8,128)(2,1)S(1)}, bf16[2,512,128]{2,1,0:T(8,128)(2,1)S(1)}, u32[]{:S(2)}, u32[]{:S(2)}) collective-permute-start(bf16[2,512,128]{2,1,0:T(8,128)(2,1)S(1)} %add_convert_fusion.2), channel_id=1, source_target_pairs={{0,1},{1,0},{2,3},{3,2},{4,5},{5,4},{6,7},{7,6},{8,9},{9,8},{10,11... | collective-permute-start | bytes 786440 | tf_op jit(solution)/shard_map/ppermute | solution.py:666
  133.2 7.3 %collective-permute-start.15 = (bf16[2,256,128]{2,1,0:T(8,128)(2,1)S(1)}, bf16[2,256,128]{2,1,0:T(8,128)(2,1)S(1)}, u32[]{:S(2)}, u32[]{:S(2)}) collective-permute-start(bf16[2,256,128]{2,1,0:T(8,128)(2,1)S(1)} %add_convert_fusion.5), channel_id=1, source_target_pairs={{0,2},{1,3},{2,0},{3,1},{4,6},{5,7},{6,4},{7,5},{8,10},{9,11},{10,... | collective-permute-start | bytes 393224 | tf_op jit(solution)/shard_map/ppermute | solution.py:666
  141.3 6.0 %collective-permute-start.16 = (bf16[256,256]{1,0:T(8,128)(2,1)S(1)}, bf16[256,256]{1,0:T(8,128)(2,1)S(1)}, u32[]{:S(2)}, u32[]{:S(2)}) collective-permute-start(bf16[256,256]{1,0:T(8,128)(2,1)S(1)} %get-tuple-element.46), channel_id=1, source_target_pairs={{0,24},{4,28},{8,16},{12,20},{16,8},{20,12},{24,0},{28,4},{1,25},{... | collective-permute-start | bytes 393224 | tf_op jit(solution)/shard_map/ppermute | solution.py:666
  142.8 5.8 %collective-permute-start.17 = (bf16[256,256]{1,0:T(8,128)(2,1)S(1)}, bf16[256,256]{1,0:T(8,128)(2,1)S(1)}, u32[]{:S(2)}, u32[]{:S(2)}) collective-permute-start(bf16[256,256]{1,0:T(8,128)(2,1)S(1)} %get-tuple-element.46), channel_id=1, source_target_pairs={{0,16},{4,20},{8,24},{12,28},{16,0},{20,4},{24,8},{28,12},{1,17},{... | collective-permute-start | bytes 393224 | tf_op jit(solution)/shard_map/ppermute | solution.py:666
  144.3 5.0 %collective-permute-start.18 = (bf16[256,256]{1,0:T(8,128)(2,1)S(1)}, bf16[256,256]{1,0:T(8,128)(2,1)S(1)}, u32[]{:S(2)}, u32[]{:S(2)}) collective-permute-start(bf16[256,256]{1,0:T(8,128)(2,1)S(1)} %get-tuple-element.46), channel_id=1, source_target_pairs={{0,8},{4,12},{8,0},{12,4},{16,24},{20,28},{24,16},{28,20},{1,9},{5... | collective-permute-start | bytes 393224 | tf_op jit(solution)/shard_map/ppermute | solution.py:666
  149.5 2.0 %collective-permute-start.19 = (bf16[4,256,256]{2,1,0:T(8,128)(2,1)S(1)}, bf16[4,256,256]{2,1,0:T(8,128)(2,1)S(1)}, u32[]{:S(2)}, u32[]{:S(2)}) collective-permute-start(bf16[4,256,256]{2,1,0:T(8,128)(2,1)S(1)} %get-tuple-element.49), channel_id=1, source_target_pairs={{0,4},{4,0},{8,12},{12,8},{16,20},{20,16},{24,28},{28,24},{1,5},{5... | collective-permute-start | bytes 1572872 | tf_op jit(solution)/shard_map/ppermute | solution.py:666
  (4 other events, 38.6 us)
